TPU v7x, 32 devices: a whole 2x2x4 slice. The times are simulated.
32 devices in a mesh: dom: 8 (over z, y), batch: 4 (over x, core).
Axes of the slice: x: 2, y: 2, z: 4, core: 2. Of those that a mesh axis runs over, the one named last changes fastest.
Arguments:
- activations: bfloat16 [1024, 65536], P('batch', 'dom'), may hold values from 0 to 2
- tile_weights: bfloat16 [4, 512, 512, 128], P(None, 'dom', 'batch'), may hold values from -0.375 to 0.375
- biases: float32 [4, 65536], P(None, 'dom'), may hold values from -2.5 to 2.5
- source_codes: int32 [4, 512, 4], P(None, 'dom'), may hold values from 0 to 67
- send_list: int32 [4, 8, 4], P(None, 'dom'), may hold values from 0 to 63
Outputs:
- result: bfloat16 [1024, 65536], P('batch', 'dom')
All inputs are finite; a program needn't handle non-finite values.
Results may differ from a plain program's by a relative error of at most 0.0062.
Values may be sent and summed in bfloat16 or wider, within the bound.
No kernel may reach another device: no remote copies, remote signals or barrier semaphores. Data moves between devices by JAX's collectives and lax.ppermute only.
A program may use at most 192 MiB of HBM per device.

v0:
```python
import jax
import jax.numpy as jnp
from jax import lax
from jax.sharding import PartitionSpec as P


def shifted(block, axis, distance):
    devices = range(lax.axis_size(axis))
    route = [((i - distance) % len(devices), i) for i in devices]
    return lax.ppermute(block, axis, route)


def body(activations, tile_weights, biases, source_codes, send_list):
    row_count = activations.shape[0]
    tile_width = tile_weights.shape[3]
    block_count = source_codes.shape[1]
    fan_tiles = source_codes.shape[2]
    layer_count = tile_weights.shape[0]
    part_count = lax.axis_size("dom")
    neighbor_offsets = (1, 2, -1, part_count // 2)
    current = activations.reshape(row_count, block_count, tile_width)
    for layer_index in range(layer_count):
        outgoing = jnp.take(current, send_list[layer_index, 0], axis=1)
        received = []
        for slot_index, offset in enumerate(neighbor_offsets):
            received.append(shifted(outgoing[:, slot_index], "dom", offset))
        arrived = jnp.stack(received, axis=1)
        block_pool = jnp.concatenate([current, arrived], axis=1)
        input_panel = jnp.take(block_pool, source_codes[layer_index].reshape(-1), axis=1)
        input_panel = input_panel.reshape(row_count, block_count, fan_tiles * tile_width)
        layer_bias = biases[layer_index].reshape(block_count, tile_width)
        summed = jnp.einsum(
            "rjc,jco->rjo",
            input_panel,
            lax.all_gather(tile_weights[layer_index], "batch", axis=1, tiled=True),
            preferred_element_type=jnp.float32,
        )
        current = jnp.maximum(summed + layer_bias[None], 0.0).astype(jnp.bfloat16)
    return current.reshape(row_count, block_count * tile_width)


def solution(mesh):
    in_specs = (
        P("batch", "dom"),
        P(None, "dom", "batch", None),
        P(None, "dom"),
        P(None, "dom", None),
        P(None, "dom", None),
    )
    out_specs = P("batch", "dom")
    return jax.shard_map(body, mesh=mesh, in_specs=in_specs, out_specs=out_specs, check_vma=False)
```

profile of v0, /device:TPU:0, one launch (start us, length us, event | category | flops | bytes accessed | tf_op | source)
XLA Modules:
  0.0 360.8 jit_solution(5144156712287542177)
XLA Ops:
  6.5 5.7 %fusion.20 = (bf16[1,64,128,128]{3,2,1,0:T(8,128)(2,1)S(1)}, bf16[1,64,128,128]{3,2,1,0:T(8,128)(2,1)}, bf16[1,64,128,128]{3,2,1,0:T(8,128)(2,1)}, bf16[1,64,128,128]{3,2,1,0:T(8,128)(2,1)}) fusion(bf16[4,64,128,128]{3,2,1,0:T(8,128)(2,1)} %param.10), kind=kLoop, calls=%fused_computation.92 | loop fusion | bytes 16777216 | tf_op jit(solution)/shard_map/slice | solution.py:35
  13.8 6.4 %copy.31 = bf16[256,8192]{0,1:T(8,128)(2,1)} copy(bf16[256,8192]{1,0:T(8,128)(2,1)} %param.9) | data formatting | bytes 8388608 | tf_op args[0]
  20.2 6.7 %copy.33 = bf16[256,64,128]{2,0,1:T(8,128)(2,1)} copy(bf16[256,64,128]{0,2,1:T(8,128)(2,1)} %bitcast.145) | data formatting | bytes 8388608 | tf_op jit(solution)/shard_map/reshape | solution.py:21
  26.9 3.0 gather_fusion
  30.0 2.9 collective-permute-start
  34.5 3.2 collective-permute-start.2
  38.5 2.9 copy.51
  41.5 4.7 %constant_dynamic-update-slice_fusion = bf16[256,68,128]{2,0,1:T(8,128)(2,1)} fusion(bf16[256,64,128]{2,0,1:T(8,128)(2,1)} %copy.33), kind=kLoop, calls=%fused_computation.64 | loop fusion | bytes 8388608
  50.4 12.1 %gather_fusion.1 = bf16[256,256,128]{2,1,0:T(8,128)(2,1)} fusion(bf16[256,68,128]{2,0,1:T(8,128)(2,1)} %bitcast_dynamic-update-slice_fusion.12, s32[1024]{0:T(1024)S(1)} %pad_clamp_fusion.6), kind=kCustom, calls=%fused_computation.1.clone | custom fusion | bytes 33555456 | tf_op jit(solution)/shard_map/jit(_take)/gather | solution.py:29
  62.5 14.2 %select_bitcast_fusion.3 = bf16[256,256,128]{2,0,1:T(8,128)(2,1)} fusion(bf16[256,256,128]{2,1,0:T(8,128)(2,1)} %gather_fusion.1, pred[256]{0:T(512)(128)(4,1)S(1)} %compare_and_fusion.6), kind=kLoop, calls=%fused_computation.11 | loop fusion | flops 8388608 | bytes 33554688 | tf_op jit(solution)/shard_map/jit(_take)/select_n | solution.py:29
  76.7 21.4 %copy.34 = bf16[256,256,128]{0,2,1:T(8,128)(2,1)} copy(bf16[256,256,128]{2,0,1:T(8,128)(2,1)} %select_bitcast_fusion.3) | data formatting | bytes 33554432 | tf_op jit(solution)/shard_map/jit(_take)/select_n | solution.py:29
  98.1 13.6 %constant_dynamic-update-slice_fusion.1 = (bf16[256,68,128]{2,0,1:T(8,128)(2,1)}, bf16[256,64,128]{2,0,1:T(8,128)(2,1)}) fusion(f32[64,128]{1,0:T(8,128)S(1)} %bitcast.149, bf16[256,64,512]{0,2,1:T(8,128)(2,1)} %bitcast.140, bf16[1,64,512,128]{3,2,1,0:T(8,128)(2,1)} %all-gather.9.cloned.1.call-done), kind=kOutput, calls=%fused_computation.65 | convolution fusion | flops 2153775104 | bytes 33587200 | tf_op jit(solution)/shard_map/rjc,jco->rjo/dot_general | solution.py:32
  111.7 2.8 gather_fusion.2
  116.2 3.7 %collective-permute-start.6 = (bf16[256,128]{1,0:T(8,128)(2,1)S(1)}, bf16[256,128]{1,0:T(8,128)(2,1)S(1)}, u32[]{:S(2)}, u32[]{:S(2)}) collective-permute-start(bf16[256,128]{1,0:T(8,128)(2,1)S(1)} %get-tuple-element.28), channel_id=1, source_target_pairs={{4,0},{8,4},{12,8},{16,12},{20,16},{24,20},{28,24},{0,28},{5,1},{9... | collective-permute-start | bytes 196616 | tf_op jit(solution)/shard_map/ppermute | solution.py:10
  125.8 12.1 %gather_fusion.3 = bf16[256,256,128]{2,1,0:T(8,128)(2,1)} fusion(bf16[256,68,128]{2,0,1:T(8,128)(2,1)} %bitcast_dynamic-update-slice_fusion.8, s32[1024]{0:T(1024)S(1)} %pad_clamp_fusion.4), kind=kCustom, calls=%fused_computation.5.clone | custom fusion | bytes 33555456 | tf_op jit(solution)/shard_map/jit(_take)/gather | solution.py:29
  137.9 14.7 %select_bitcast_fusion.2 = bf16[256,256,128]{2,0,1:T(8,128)(2,1)} fusion(bf16[256,256,128]{2,1,0:T(8,128)(2,1)} %gather_fusion.3, pred[256]{0:T(512)(128)(4,1)S(1)} %compare_and_fusion.4), kind=kLoop, calls=%fused_computation.10 | loop fusion | flops 8388608 | bytes 33554688 | tf_op jit(solution)/shard_map/jit(_take)/select_n | solution.py:29
  152.6 22.5 %copy.36 = bf16[256,256,128]{0,2,1:T(8,128)(2,1)} copy(bf16[256,256,128]{2,0,1:T(8,128)(2,1)} %select_bitcast_fusion.2) | data formatting | bytes 33554432 | tf_op jit(solution)/shard_map/jit(_take)/select_n | solution.py:29
  175.1 13.6 %constant_dynamic-update-slice_fusion.2 = (bf16[256,68,128]{2,0,1:T(8,128)(2,1)}, bf16[256,64,128]{2,0,1:T(8,128)(2,1)}) fusion(f32[64,128]{1,0:T(8,128)S(1)} %bitcast.148, bf16[256,64,512]{0,2,1:T(8,128)(2,1)} %bitcast.141, bf16[1,64,512,128]{3,2,1,0:T(8,128)(2,1)} %all-gather.11.cloned.1.call-done), kind=kOutput, calls=%fused_computation.66 | convolution fusion | flops 2153775104 | bytes 33587200 | tf_op jit(solution)/shard_map/rjc,jco->rjo/dot_general | solution.py:32
  188.7 2.8 gather_fusion.4
  193.2 4.6 %collective-permute-start.10 = (bf16[256,128]{1,0:T(8,128)(2,1)S(1)}, bf16[256,128]{1,0:T(8,128)(2,1)S(1)}, u32[]{:S(2)}, u32[]{:S(2)}) collective-permute-start(bf16[256,128]{1,0:T(8,128)(2,1)S(1)} %get-tuple-element.24), channel_id=1, source_target_pairs={{4,0},{8,4},{12,8},{16,12},{20,16},{24,20},{28,24},{0,28},{5,1},{9... | collective-permute-start | bytes 196616 | tf_op jit(solution)/shard_map/ppermute | solution.py:10
  203.7 12.9 %gather_fusion.5 = bf16[256,256,128]{2,1,0:T(8,128)(2,1)} fusion(bf16[256,68,128]{2,0,1:T(8,128)(2,1)} %bitcast_dynamic-update-slice_fusion.4, s32[1024]{0:T(1024)S(1)} %pad_clamp_fusion.2), kind=kCustom, calls=%fused_computation.6.clone | custom fusion | bytes 33555456 | tf_op jit(solution)/shard_map/jit(_take)/gather | solution.py:29
  216.6 14.3 %select_bitcast_fusion.1 = bf16[256,256,128]{2,0,1:T(8,128)(2,1)} fusion(bf16[256,256,128]{2,1,0:T(8,128)(2,1)} %gather_fusion.5, pred[256]{0:T(512)(128)(4,1)S(1)} %compare_and_fusion.2), kind=kLoop, calls=%fused_computation.9 | loop fusion | flops 8388608 | bytes 33554688 | tf_op jit(solution)/shard_map/jit(_take)/select_n | solution.py:29
  230.9 22.4 %copy.38 = bf16[256,256,128]{0,2,1:T(8,128)(2,1)} copy(bf16[256,256,128]{2,0,1:T(8,128)(2,1)} %select_bitcast_fusion.1) | data formatting | bytes 33554432 | tf_op jit(solution)/shard_map/jit(_take)/select_n | solution.py:29
  253.3 13.6 %constant_dynamic-update-slice_fusion.3 = (bf16[256,68,128]{2,0,1:T(8,128)(2,1)}, bf16[256,64,128]{2,0,1:T(8,128)(2,1)}) fusion(f32[64,128]{1,0:T(8,128)S(1)} %bitcast.147, bf16[256,64,512]{0,2,1:T(8,128)(2,1)} %bitcast.142, bf16[1,64,512,128]{3,2,1,0:T(8,128)(2,1)} %all-gather.13.cloned.1.call-done), kind=kOutput, calls=%fused_computation.67 | convolution fusion | flops 2153775104 | bytes 33587200 | tf_op jit(solution)/shard_map/rjc,jco->rjo/dot_general | solution.py:32
  266.9 2.8 gather_fusion.6
  269.9 4.9 %collective-permute-start.14 = (bf16[256,128]{1,0:T(8,128)(2,1)S(1)}, bf16[256,128]{1,0:T(8,128)(2,1)S(1)}, u32[]{:S(2)}, u32[]{:S(2)}) collective-permute-start(bf16[256,128]{1,0:T(8,128)(2,1)S(1)} %get-tuple-element.20), channel_id=1, source_target_pairs={{4,0},{8,4},{12,8},{16,12},{20,16},{24,20},{28,24},{0,28},{5,1},{9... | collective-permute-start | bytes 196616 | tf_op jit(solution)/shard_map/ppermute | solution.py:10
  280.9 12.0 %gather_fusion.7 = bf16[256,256,128]{2,1,0:T(8,128)(2,1)} fusion(bf16[256,68,128]{2,0,1:T(8,128)(2,1)} %bitcast_dynamic-update-slice_fusion, s32[1024]{0:T(1024)S(1)} %pad_clamp_fusion), kind=kCustom, calls=%fused_computation.7.clone | custom fusion | bytes 33555456 | tf_op jit(solution)/shard_map/jit(_take)/gather | solution.py:29
  292.9 14.2 %select_bitcast_fusion = bf16[256,256,128]{2,0,1:T(8,128)(2,1)} fusion(bf16[256,256,128]{2,1,0:T(8,128)(2,1)} %gather_fusion.7, pred[256]{0:T(512)(128)(4,1)S(1)} %compare_and_fusion), kind=kLoop, calls=%fused_computation.8 | loop fusion | flops 8388608 | bytes 33554688 | tf_op jit(solution)/shard_map/jit(_take)/select_n | solution.py:29
  307.1 22.4 %copy.40 = bf16[256,256,128]{0,2,1:T(8,128)(2,1)} copy(bf16[256,256,128]{2,0,1:T(8,128)(2,1)} %select_bitcast_fusion) | data formatting | bytes 33554432 | tf_op jit(solution)/shard_map/jit(_take)/select_n | solution.py:29
  329.5 12.1 %fusion.11 = bf16[256,64,128]{2,0,1:T(8,128)(2,1)} fusion(f32[64,128]{1,0:T(8,128)S(1)} %bitcast.146, bf16[256,64,512]{0,2,1:T(8,128)(2,1)} %bitcast.143, bf16[1,64,512,128]{2,3,1,0:T(8,128)(2,1)} %all-gather.15.cloned.1.call-done), kind=kOutput, calls=%fused_computation.27 | convolution fusion | flops 2153775104 | bytes 29392896 | tf_op jit(solution)/shard_map/rjc,jco->rjo/dot_general | solution.py:32
  341.6 6.4 %copy.44 = bf16[256,64,128]{0,2,1:T(8,128)(2,1)} copy(bf16[256,64,128]{2,0,1:T(8,128)(2,1)} %fusion.11) | data formatting | bytes 8388608 | tf_op jit(solution)/shard_map/convert_element_type | solution.py:38
  347.9 6.3 %copy.45 = bf16[256,8192]{1,0:T(8,128)(2,1)} copy(bf16[256,8192]{0,1:T(8,128)(2,1)} %bitcast.144) | data formatting | bytes 8388608 | tf_op jit(solution)/shard_map/reshape | solution.py:39
  (98 shorter events, 29.5 us)
Async XLA Ops:
  6.5 91.6 %all-gather.9.cloned.1.call-start = ((), (), s32[]{:S(2)}) async-start(), calls=%async_computation | async-start | bytes 10485760 | tf_op jit(solution)/shard_map/all_gather | solution.py:35
  12.3 162.8 %all-gather.11.cloned.1.call-start = ((), (), s32[]{:S(2)}) async-start(), calls=%async_computation.1 | async-start | bytes 10485760 | tf_op jit(solution)/shard_map/all_gather | solution.py:35
  13.0 240.3 %all-gather.13.cloned.1.call-start = ((), (), s32[]{:S(2)}) async-start(), calls=%async_computation.2 | async-start | bytes 10485760 | tf_op jit(solution)/shard_map/all_gather | solution.py:35
  13.7 315.8 %all-gather.15.cloned.1.call-start = ((), (), s32[]{:S(2)}) async-start(), calls=%async_computation.3 | async-start | bytes 10485760 | tf_op jit(solution)/shard_map/all_gather | solution.py:35
  20.2 6.7 %copy-start.3 = (s32[4,1,4]{2,1,0:T(1,128)S(1)}, s32[4,1,4]{2,1,0:T(1,128)}, u32[]{:S(2)}) copy-start(s32[4,1,4]{2,1,0:T(1,128)} %param.13) | copy-start | bytes 196
  30.0 17.8 %collective-permute-start = (bf16[256,128]{1,0:T(8,128)(2,1)S(1)}, bf16[256,128]{1,0:T(8,128)(2,1)S(1)}, u32[]{:S(2)}, u32[]{:S(2)}) collective-permute-start(bf16[256,128]{1,0:T(8,128)(2,1)S(1)} %get-tuple-element.34), channel_id=1, source_target_pairs={{28,0},{0,4},{4,8},{8,12},{12,16},{16,20},{20,24},{24,28},{29,1},{... | collective-permute-start | bytes 196616 | tf_op jit(solution)/shard_map/ppermute | solution.py:10
  32.9 15.6 %collective-permute-start.1 = (bf16[256,128]{1,0:T(8,128)(2,1)S(1)}, bf16[256,128]{1,0:T(8,128)(2,1)S(1)}, u32[]{:S(2)}, u32[]{:S(2)}) collective-permute-start(bf16[256,128]{1,0:T(8,128)(2,1)S(1)} %get-tuple-element.33), channel_id=1, source_target_pairs={{24,0},{28,4},{0,8},{4,12},{8,16},{12,20},{16,24},{20,28},{25,1},{... | collective-permute-start | bytes 196616 | tf_op jit(solution)/shard_map/ppermute | solution.py:10
  34.5 14.6 %collective-permute-start.2 = (bf16[256,128]{1,0:T(8,128)(2,1)S(1)}, bf16[256,128]{1,0:T(8,128)(2,1)S(1)}, u32[]{:S(2)}, u32[]{:S(2)}) collective-permute-start(bf16[256,128]{1,0:T(8,128)(2,1)S(1)} %get-tuple-element.32), channel_id=1, source_target_pairs={{4,0},{8,4},{12,8},{16,12},{20,16},{24,20},{28,24},{0,28},{5,1},{9... | collective-permute-start | bytes 196616 | tf_op jit(solution)/shard_map/ppermute | solution.py:10
  37.7 12.1 %collective-permute-start.3 = (bf16[256,128]{1,0:T(8,128)(2,1)S(1)}, bf16[256,128]{1,0:T(8,128)(2,1)S(1)}, u32[]{:S(2)}, u32[]{:S(2)}) collective-permute-start(bf16[256,128]{1,0:T(8,128)(2,1)S(1)} %get-tuple-element.31), channel_id=1, source_target_pairs={{16,0},{20,4},{24,8},{28,12},{0,16},{4,20},{8,24},{12,28},{17,1},{... | collective-permute-start | bytes 196616 | tf_op jit(solution)/shard_map/ppermute | solution.py:10
  41.4 4.7 %copy-start.2 = (s32[4,64,4]{1,2,0:T(4,128)S(1)}, s32[4,64,4]{1,2,0:T(4,128)}, u32[]{:S(2)}) copy-start(s32[4,64,4]{1,2,0:T(4,128)} %param.12) | copy-start | bytes 12292
  41.4 5.7 %copy-start = (f32[4,8192]{1,0:T(4,128)S(1)}, f32[4,8192]{1,0:T(4,128)}, u32[]{:S(2)}) copy-start(f32[4,8192]{1,0:T(4,128)} %param.11) | copy-start | bytes 393220
  114.6 7.9 %collective-permute-start.4 = (bf16[256,128]{1,0:T(8,128)(2,1)S(1)}, bf16[256,128]{1,0:T(8,128)(2,1)S(1)}, u32[]{:S(2)}, u32[]{:S(2)}) collective-permute-start(bf16[256,128]{1,0:T(8,128)(2,1)S(1)} %get-tuple-element.30), channel_id=1, source_target_pairs={{28,0},{0,4},{4,8},{8,12},{12,16},{16,20},{20,24},{24,28},{29,1},{... | collective-permute-start | bytes 196616 | tf_op jit(solution)/shard_map/ppermute | solution.py:10
  115.6 7.5 %collective-permute-start.5 = (bf16[256,128]{1,0:T(8,128)(2,1)S(1)}, bf16[256,128]{1,0:T(8,128)(2,1)S(1)}, u32[]{:S(2)}, u32[]{:S(2)}) collective-permute-start(bf16[256,128]{1,0:T(8,128)(2,1)S(1)} %get-tuple-element.29), channel_id=1, source_target_pairs={{24,0},{28,4},{0,8},{4,12},{8,16},{12,20},{16,24},{20,28},{25,1},{... | collective-permute-start | bytes 196616 | tf_op jit(solution)/shard_map/ppermute | solution.py:10
  116.2 7.5 %collective-permute-start.6 = (bf16[256,128]{1,0:T(8,128)(2,1)S(1)}, bf16[256,128]{1,0:T(8,128)(2,1)S(1)}, u32[]{:S(2)}, u32[]{:S(2)}) collective-permute-start(bf16[256,128]{1,0:T(8,128)(2,1)S(1)} %get-tuple-element.28), channel_id=1, source_target_pairs={{4,0},{8,4},{12,8},{16,12},{20,16},{24,20},{28,24},{0,28},{5,1},{9... | collective-permute-start | bytes 196616 | tf_op jit(solution)/shard_map/ppermute | solution.py:10
  120.0 5.2 %collective-permute-start.7 = (bf16[256,128]{1,0:T(8,128)(2,1)S(1)}, bf16[256,128]{1,0:T(8,128)(2,1)S(1)}, u32[]{:S(2)}, u32[]{:S(2)}) collective-permute-start(bf16[256,128]{1,0:T(8,128)(2,1)S(1)} %get-tuple-element.27), channel_id=1, source_target_pairs={{16,0},{20,4},{24,8},{28,12},{0,16},{4,20},{8,24},{12,28},{17,1},{... | collective-permute-start | bytes 196616 | tf_op jit(solution)/shard_map/ppermute | solution.py:10
  191.6 7.0 %collective-permute-start.8 = (bf16[256,128]{1,0:T(8,128)(2,1)S(1)}, bf16[256,128]{1,0:T(8,128)(2,1)S(1)}, u32[]{:S(2)}, u32[]{:S(2)}) collective-permute-start(bf16[256,128]{1,0:T(8,128)(2,1)S(1)} %get-tuple-element.26), channel_id=1, source_target_pairs={{28,0},{0,4},{4,8},{8,12},{12,16},{16,20},{20,24},{24,28},{29,1},{... | collective-permute-start | bytes 196616 | tf_op jit(solution)/shard_map/ppermute | solution.py:10
  192.8 6.4 %collective-permute-start.9 = (bf16[256,128]{1,0:T(8,128)(2,1)S(1)}, bf16[256,128]{1,0:T(8,128)(2,1)S(1)}, u32[]{:S(2)}, u32[]{:S(2)}) collective-permute-start(bf16[256,128]{1,0:T(8,128)(2,1)S(1)} %get-tuple-element.25), channel_id=1, source_target_pairs={{24,0},{28,4},{0,8},{4,12},{8,16},{12,20},{16,24},{20,28},{25,1},{... | collective-permute-start | bytes 196616 | tf_op jit(solution)/shard_map/ppermute | solution.py:10
  193.2 6.6 %collective-permute-start.10 = (bf16[256,128]{1,0:T(8,128)(2,1)S(1)}, bf16[256,128]{1,0:T(8,128)(2,1)S(1)}, u32[]{:S(2)}, u32[]{:S(2)}) collective-permute-start(bf16[256,128]{1,0:T(8,128)(2,1)S(1)} %get-tuple-element.24), channel_id=1, source_target_pairs={{4,0},{8,4},{12,8},{16,12},{20,16},{24,20},{28,24},{0,28},{5,1},{9... | collective-permute-start | bytes 196616 | tf_op jit(solution)/shard_map/ppermute | solution.py:10
  197.9 5.2 %collective-permute-start.11 = (bf16[256,128]{1,0:T(8,128)(2,1)S(1)}, bf16[256,128]{1,0:T(8,128)(2,1)S(1)}, u32[]{:S(2)}, u32[]{:S(2)}) collective-permute-start(bf16[256,128]{1,0:T(8,128)(2,1)S(1)} %get-tuple-element.23), channel_id=1, source_target_pairs={{16,0},{20,4},{24,8},{28,12},{0,16},{4,20},{8,24},{12,28},{17,1},{... | collective-permute-start | bytes 196616 | tf_op jit(solution)/shard_map/ppermute | solution.py:10
  269.8 7.0 %collective-permute-start.12 = (bf16[256,128]{1,0:T(8,128)(2,1)S(1)}, bf16[256,128]{1,0:T(8,128)(2,1)S(1)}, u32[]{:S(2)}, u32[]{:S(2)}) collective-permute-start(bf16[256,128]{1,0:T(8,128)(2,1)S(1)} %get-tuple-element.22), channel_id=1, source_target_pairs={{28,0},{0,4},{4,8},{8,12},{12,16},{16,20},{20,24},{24,28},{29,1},{... | collective-permute-start | bytes 196616 | tf_op jit(solution)/shard_map/ppermute | solution.py:10
  269.9 7.6 %collective-permute-start.13 = (bf16[256,128]{1,0:T(8,128)(2,1)S(1)}, bf16[256,128]{1,0:T(8,128)(2,1)S(1)}, u32[]{:S(2)}, u32[]{:S(2)}) collective-permute-start(bf16[256,128]{1,0:T(8,128)(2,1)S(1)} %get-tuple-element.21), channel_id=1, source_target_pairs={{24,0},{28,4},{0,8},{4,12},{8,16},{12,20},{16,24},{20,28},{25,1},{... | collective-permute-start | bytes 196616 | tf_op jit(solution)/shard_map/ppermute | solution.py:10
  269.9 8.1 %collective-permute-start.14 = (bf16[256,128]{1,0:T(8,128)(2,1)S(1)}, bf16[256,128]{1,0:T(8,128)(2,1)S(1)}, u32[]{:S(2)}, u32[]{:S(2)}) collective-permute-start(bf16[256,128]{1,0:T(8,128)(2,1)S(1)} %get-tuple-element.20), channel_id=1, source_target_pairs={{4,0},{8,4},{12,8},{16,12},{20,16},{24,20},{28,24},{0,28},{5,1},{9... | collective-permute-start | bytes 196616 | tf_op jit(solution)/shard_map/ppermute | solution.py:10
  274.8 5.4 %collective-permute-start.15 = (bf16[256,128]{1,0:T(8,128)(2,1)S(1)}, bf16[256,128]{1,0:T(8,128)(2,1)S(1)}, u32[]{:S(2)}, u32[]{:S(2)}) collective-permute-start(bf16[256,128]{1,0:T(8,128)(2,1)S(1)} %get-tuple-element.19), channel_id=1, source_target_pairs={{16,0},{20,4},{24,8},{28,12},{0,16},{4,20},{8,24},{12,28},{17,1},{... | collective-permute-start | bytes 196616 | tf_op jit(solution)/shard_map/ppermute | solution.py:10
  307.1 22.4 %copy-start.1 = (f32[1,8192]{1,0:T(1,128)S(1)}, f32[1,8192]{1,0:T(1,128)}, u32[]{:S(2)}) copy-start(f32[1,8192]{1,0:T(1,128)} %get-tuple-element.37) | copy-start | bytes 98308
Sparse Core Ops, SparseCore 0:
  12.4 60.9 all-gather.8
  75.0 58.2 all-gather.10
  134.8 58.2 all-gather.12
  194.6 59.3 all-gather.14
where the time goes:
time: 364 us; the launch traced here: 361 us
  local copies, waits for them, and re-layouts  200 us (55%)
  other arithmetic  57.9 us (16%)
  matrix products  52.9 us (15%)
  starting transfers between devices  27.1 us (7%)
  between operations  13.4 us (4%)
  waiting for transfers between devices  9.67 us (3%)
    select_n x4, local copies, waits for them, and re-layouts, body(): jnp.take(block_pool, source_codes[layer_index].reshape(-1), axis=1)  88.7 us
    select_n x8, other arithmetic, body(): jnp.take(block_pool, source_codes[layer_index].reshape(-1), axis=1)  57.4 us
    dot_general x4, matrix products, body(): jnp.einsum('rjc,jco->rjo', input_panel, lax.all_gather(tile_weights[layer...  52.9 us
    gather x4, local copies, waits for them, and re-layouts, body(): jnp.take(block_pool, source_codes[layer_index].reshape(-1), axis=1)  49.1 us
    ppermute x16, starting transfers between devices, shifted(): return lax.ppermute(block, axis, route)  26.9 us
    unnamed x23, local copies, waits for them, and re-layouts  21.6 us
    gather x4, local copies, waits for them, and re-layouts, body(): outgoing = jnp.take(current, send_list[layer_index, 0], axis=1)  11.4 us
    ppermute x16, waiting for transfers between devices, shifted(): return lax.ppermute(block, axis, route)  8.26 us
  transfers between devices with their start and end apart: 20, of which 6 were waited for; matrix products, arithmetic and copies ran while one was open for 78% of the time, Pallas kernels for 0%

commit v1 on v0

v1 whole, which is shorter than its diff:
```python
import functools

import jax
import jax.numpy as jnp
from jax import lax
from jax.experimental import pallas as pl
from jax.experimental.pallas import tpu as pltpu
from jax.sharding import PartitionSpec as P


def shifted(block, axis, distance):
    devices = range(lax.axis_size(axis))
    route = [((i - distance) % len(devices), i) for i in devices]
    return lax.ppermute(block, axis, route)


def swapped(block, mask):
    route = [(i, i ^ mask) for i in range(lax.axis_size("batch"))]
    return lax.ppermute(block, "batch", route)


def layer_kernel(layer, first, group, blocks, fan, neigh, width, aliased, *refs):
    codes, own = refs[:2]
    refs = refs[2:]
    current, arrived, tiles = refs[0], refs[1 : 1 + neigh], refs[1 + neigh : 1 + neigh + fan]
    refs = refs[1 + neigh + fan :]
    bias = refs[0]
    result, pool, semaphores = refs[2:] if aliased else refs[1:]
    step = pl.program_id(0)

    @pl.when(step == 0)
    def _():
        copies = [pltpu.make_async_copy(current, pool.at[:, : blocks * width], semaphores.at[neigh])]
        for slot in range(neigh):
            place = pl.ds((blocks + slot) * width, width)
            copies.append(pltpu.make_async_copy(arrived[slot], pool.at[:, place], semaphores.at[slot]))
        for copy in copies:
            copy.start()
        for copy in copies:
            copy.wait()

    for g in range(group):
        base = (layer * blocks + first + step * group + g) * fan
        panel = []
        for m in range(fan):
            code = codes[base + (own[0] ^ m)]
            panel.append(pool[:, pl.ds(pl.multiple_of(code * width, width), width)])
        summed = jnp.dot(
            jnp.concatenate(panel, axis=1),
            jnp.concatenate([tile[g] for tile in tiles], axis=0),
            preferred_element_type=jnp.float32,
        )
        columns = slice(g * width, (g + 1) * width)
        summed = summed + bias[layer : layer + 1, columns]
        result[:, columns] = jnp.maximum(summed, 0.0).astype(result.dtype)


def run_blocks(layer, first, count, codes, own, current, arrived, tiles, biases, target):
    rows, neurons = current.shape
    fan, neigh = len(tiles), len(arrived)
    width = tiles[0].shape[2]
    blocks = neurons // width
    group = min(8, count)
    steps = count // group
    offset = first // group
    anywhere = pl.BlockSpec(memory_space=pl.ANY)
    in_specs = [anywhere] * (1 + neigh)
    in_specs += [pl.BlockSpec((group, width, width), lambda i, *_: (i, 0, 0))] * fan
    in_specs += [pl.BlockSpec((biases.shape[0], group * width), lambda i, *_: (0, offset + i))]
    operands = [codes, own, current, *arrived, *tiles, biases]
    aliases = {}
    if target is not None:
        in_specs += [anywhere]
        aliases = {len(operands): 0}
        operands += [target]
    kernel = functools.partial(layer_kernel, layer, first, group, blocks, fan, neigh, width, target is not None)
    return pl.pallas_call(
        kernel,
        out_shape=jax.ShapeDtypeStruct((rows, neurons), current.dtype),
        grid_spec=pltpu.PrefetchScalarGridSpec(
            num_scalar_prefetch=2,
            grid=(steps,),
            in_specs=in_specs,
            out_specs=pl.BlockSpec((rows, group * width), lambda i, *_: (0, offset + i)),
            scratch_shapes=[
                pltpu.VMEM((rows, neurons + neigh * width), current.dtype),
                pltpu.SemaphoreType.DMA((neigh + 1,)),
            ],
        ),
        input_output_aliases=aliases,
        compiler_params=pltpu.CompilerParams(vmem_limit_bytes=40 * 2**20),
        cost_estimate=pl.CostEstimate(
            flops=2 * rows * count * fan * width * width,
            bytes_accessed=2 * (rows * neurons + rows * count * width + count * fan * width * width),
            transcendentals=0,
        ),
    )(*operands)


def body(activations, tile_weights, biases, source_codes, send_list):
    layer_count, block_count, part_rows, width = tile_weights.shape
    fan = source_codes.shape[2]
    part_count = lax.axis_size("dom")
    neighbor_offsets = (1, 2, -1, part_count // 2)
    sharers = width // part_rows
    own = (lax.axis_index("batch") // sharers).reshape(1).astype(jnp.int32)
    codes = source_codes.reshape(-1)
    far = fan // 2

    def local(layer, first, count):
        part = lax.slice(tile_weights, (layer, first, 0, 0), (layer + 1, first + count, part_rows, width))[0]
        if sharers == 1:
            return part
        members = range(lax.axis_size("batch") // sharers)
        groups = [[m * sharers + s for s in range(sharers)] for m in members]
        return lax.all_gather(part, "batch", axis=1, tiled=True, axis_index_groups=groups)

    chunks = [(layer, 0, block_count) for layer in range(layer_count - 1)]
    quarter = block_count // 4
    chunks += [(layer_count - 1, i * quarter, quarter) for i in range(4)]

    in_flight = 2
    sent, ready = [], []
    for index, chunk in enumerate(chunks):
        mine = local(*chunk)
        if index >= in_flight:
            mine, sent[index - in_flight] = lax.optimization_barrier((mine, sent[index - in_flight]))
        crossed = swapped(mine, far * sharers)
        sent.append(crossed)
        ready.append(mine)

    def tiles_of(index):
        held = [ready[index]] + [None] * (fan - 1)
        held[far] = sent[index]
        for bit in range(far.bit_length() - 1):
            for m in range(1 << bit):
                for start in (0, far):
                    held[start + m + (1 << bit)] = swapped(held[start + m], (1 << bit) * sharers)
        return held

    current = activations
    target = None
    for index, (layer, first, count) in enumerate(chunks):
        if first == 0:
            arrived = []
            for slot, offset in enumerate(neighbor_offsets):
                start = send_list[layer, 0, slot] * width
                block = lax.dynamic_slice(current, (0, start), (current.shape[0], width))
                arrived.append(shifted(block, "dom", offset))
            source, target = current, None
        current = target = run_blocks(
            layer, first, count, codes, own, source, arrived, tiles_of(index), biases, target
        )
    return current


def solution(mesh):
    in_specs = (
        P("batch", "dom"),
        P(None, "dom", "batch", None),
        P(None, "dom"),
        P(None, "dom", None),
        P(None, "dom", None),
    )
    out_specs = P("batch", "dom")
    return jax.shard_map(body, mesh=mesh, in_specs=in_specs, out_specs=out_specs, check_vma=False)
```

time: 364 us -> 256 us (0.70)
  local copies, waits for them, and re-layouts: 200 us -> 21.2 us
  waiting for transfers between devices: 9.67 us -> 132 us
  other arithmetic: 57.9 us -> 0 us
  matrix products: 52.9 us -> 0 us
  Pallas kernels: 0 us -> 51.7 us
  starting transfers between devices: 27.1 us -> 40.3 us
    ppermute x0 -> x21, waiting for transfers between devices: none -> 111 us  [swapped(): return lax.ppermute(block, 'batch', route)]
    select_n x4 -> x0, local copies, waits for them, and re-layouts: 88.7 us -> none  [body(): jnp.take(block_pool, source_codes[layer_index].reshape(-1), axis=1)]
    gather x8 -> x0, local copies, waits for them, and re-layouts: 60.5 us -> none  [the longest x4 49.1 us: body(): jnp.take(block_pool, source_codes[layer_index].reshape(-1), axis=1)]
    select_n x12 -> x0, other arithmetic: 57.8 us -> none  [the longest x8 57.4 us: body(): jnp.take(block_pool, source_codes[layer_index].reshape(-1), axis=1)]
    dot_general x4 -> x0, matrix products: 52.9 us -> none  [body(): jnp.einsum('rjc,jco->rjo', input_panel, lax.all_gather(tile_weights[layer...]
    pallas_call x0 -> x7, Pallas kernels: none -> 51.7 us  [run_blocks(): pl.pallas_call(kernel, out_shape=jax.ShapeDtypeStruct((rows, neurons), cu...]
    unnamed x23 -> x15, local copies, waits for them, and re-layouts: 21.6 us -> 7.81 us
    ppermute x16, waiting for transfers between devices: 8.26 us -> 21 us  [shifted(): return lax.ppermute(block, axis, route)]
  transfers between devices with their start and end apart: 20 -> 37, of which waited for: 6 -> 13; matrix products, arithmetic and copies ran while one was open for 78% -> 3% of each run, Pallas kernels for 0% -> 19%
where the time goes in v1:
time: 256 us; the launch traced here: 255 us
  waiting for transfers between devices  132 us (52%)
  Pallas kernels  51.7 us (20%)
  starting transfers between devices  40.3 us (16%)
  local copies, waits for them, and re-layouts  21.2 us (8%)
  between operations  10.3 us (4%)
    ppermute x21, waiting for transfers between devices, swapped(): return lax.ppermute(block, 'batch', route)  111 us
    pallas_call x7, Pallas kernels, run_blocks(): pl.pallas_call(kernel, out_shape=jax.ShapeDtypeStruct((rows, neurons), cu...  51.7 us
    ppermute x16, starting transfers between devices, shifted(): return lax.ppermute(block, axis, route)  28.4 us
    ppermute x16, waiting for transfers between devices, shifted(): return lax.ppermute(block, axis, route)  21 us
    ppermute x21, starting transfers between devices, swapped(): return lax.ppermute(block, 'batch', route)  11.9 us
    squeeze x2, local copies, waits for them, and re-layouts, local(): lax.slice(tile_weights, (layer, first, 0, 0), (layer + 1, first + count,...  9.84 us
    unnamed x15, local copies, waits for them, and re-layouts  7.81 us
  transfers between devices with their start and end apart: 37, of which 13 were waited for; matrix products, arithmetic and copies ran while one was open for 3% of the time, Pallas kernels for 19%

profile of v1, /device:TPU:0, one launch (start us, length us, event | category | flops | bytes accessed | tf_op | source)
XLA Modules:
  0.0 255.1 jit_solution(6519140990651760100)
XLA Ops:
  0.0 7.1 %slice_bitcast_fusion = (bf16[64,128,128]{2,1,0:T(8,128)(2,1)}, bf16[64,128,128]{2,1,0:T(8,128)(2,1)S(1)}, bf16[64,128,128]{2,1,0:T(8,128)(2,1)}) fusion(bf16[4,64,128,128]{3,2,1,0:T(8,128)(2,1)} %param.6), kind=kLoop, calls=%fused_computation | loop fusion | bytes 12582912 | tf_op jit(solution)/shard_map/squeeze | solution.py:111
  7.1 2.9 %collective-permute-start.5 = (bf16[64,128,128]{2,1,0:T(8,128)(2,1)}, bf16[64,128,128]{2,1,0:T(8,128)(2,1)S(1)}, u32[]{:S(2)}, u32[]{:S(2)}) collective-permute-start(bf16[64,128,128]{2,1,0:T(8,128)(2,1)} %get-tuple-element.31.refs_7_), channel_id=1, source_target_pairs={{0,2},{1,3},{2,0},{3,1},{4,6},{5,7},{6,4},{7,5},{8,10},{9,11},{10,... | collective-permute-start | bytes 6291464 | tf_op jit(solution)/shard_map/ppermute | solution.py:19
  10.1 46.6 %collective-permute-done.5.refs_9_ = bf16[64,128,128]{2,1,0:T(8,128)(2,1)S(1)} collective-permute-done((bf16[64,128,128]{2,1,0:T(8,128)(2,1)}, bf16[64,128,128]{2,1,0:T(8,128)(2,1)S(1)}, u32[]{:S(2)}, u32[]{:S(2)}) %collective-permute-start.5) | collective-permute-done | bytes 2097184 | tf_op jit(solution)/shard_map/ppermute | solution.py:19
  58.1 2.1 collective-permute-start.19
  64.6 1.6 collective-permute-start
  66.1 1.6 collective-permute-start.1
  67.7 4.5 %collective-permute-done.refs_3_ = bf16[256,128]{1,0:T(8,128)(2,1)S(1)} collective-permute-done((bf16[256,128]{1,0:T(8,128)(2,1)S(1)}, bf16[256,128]{1,0:T(8,128)(2,1)S(1)}, u32[]{:S(2)}, u32[]{:S(2)}) %collective-permute-start) | collective-permute-done | bytes 65568 | tf_op jit(solution)/shard_map/ppermute | solution.py:14
  73.7 2.8 %collective-permute-done.2.refs_5_ = bf16[256,128]{1,0:T(8,128)(2,1)S(1)} collective-permute-done((bf16[256,128]{1,0:T(8,128)(2,1)S(1)}, bf16[256,128]{1,0:T(8,128)(2,1)S(1)}, u32[]{:S(2)}, u32[]{:S(2)}) %collective-permute-start.2) | collective-permute-done | bytes 65568 | tf_op jit(solution)/shard_map/ppermute | solution.py:14
  76.5 25.3 %collective-permute-done.12.refs_9_ = bf16[64,128,128]{2,1,0:T(8,128)(2,1)} collective-permute-done((bf16[64,128,128]{2,1,0:T(8,128)(2,1)}, bf16[64,128,128]{2,1,0:T(8,128)(2,1)}, u32[]{:S(2)}, u32[]{:S(2)}) %collective-permute-start.12) | collective-permute-done | bytes 2097184 | tf_op jit(solution)/shard_map/ppermute | solution.py:19
  101.7 3.2 %collective-permute-start.3 = (bf16[256,128]{1,0:T(8,128)(2,1)S(1)}, bf16[256,128]{1,0:T(8,128)(2,1)S(1)}, u32[]{:S(2)}, u32[]{:S(2)}) collective-permute-start(bf16[256,128]{1,0:T(8,128)(2,1)S(1)} %get-tuple-element.44), channel_id=1, source_target_pairs={{16,0},{20,4},{24,8},{28,12},{0,16},{4,20},{8,24},{12,28},{17,1},{... | collective-permute-start | bytes 196616 | tf_op jit(solution)/shard_map/ppermute | solution.py:14
  104.9 2.8 %slice_bitcast_fusion.3 = (bf16[16,128,128]{2,1,0:T(8,128)(2,1)S(1)}, bf16[16,128,128]{2,1,0:T(8,128)(2,1)}, bf16[16,128,128]{2,1,0:T(8,128)(2,1)}, bf16[16,128,128]{2,1,0:T(8,128)(2,1)S(1)}) fusion(bf16[4,64,128,128]{3,2,1,0:T(8,128)(2,1)} %param.6), kind=kLoop, calls=%fused_computation.3 | loop fusion | bytes 4194304 | tf_op jit(solution)/shard_map/squeeze | solution.py:111
  107.7 38.2 %collective-permute-done.19.refs_9_ = bf16[64,128,128]{2,1,0:T(8,128)(2,1)} collective-permute-done((bf16[64,128,128]{2,1,0:T(8,128)(2,1)S(1)}, bf16[64,128,128]{2,1,0:T(8,128)(2,1)}, u32[]{:S(2)}, u32[]{:S(2)}) %collective-permute-start.19) | collective-permute-done | bytes 2097184 | tf_op jit(solution)/shard_map/ppermute | solution.py:19
  150.6 1.6 copy-done.4
  152.2 11.3 %shard_map.55.refs_2_ = bf16[256,8192]{1,0:T(8,128)(2,1)S(1)} custom-call(s32[1024]{0:T(1024)S(1)} %reshape.38.refs_0_, s32[1]{0:T(128)} %bitcast.refs_1_, bf16[256,8192]{1,0:T(8,128)(2,1)} %refs_2_.1, bf16[256,128]{1,0:T(8,128)(2,1)S(1)} %collective-permute-done.refs_3_, bf16[256,128]{1,0:T(8,128)(2,1)S(1)} %collective-permute-done.1.refs_4_, ...), custom_call_target="tpu_custom_call" | custom-call | flops 2147483648 | bytes 16777216 | tf_op jit(solution)/shard_map/pallas_call | solution.py:77
  163.6 2.0 copy-done.1
  166.3 2.8 %collective-permute-start.10 = (bf16[256,128]{1,0:T(8,128)(2,1)S(1)}, bf16[256,128]{1,0:T(8,128)(2,1)S(1)}, u32[]{:S(2)}, u32[]{:S(2)}) collective-permute-start(bf16[256,128]{1,0:T(8,128)(2,1)S(1)} %get-tuple-element.40), channel_id=1, source_target_pairs={{16,0},{20,4},{24,8},{28,12},{0,16},{4,20},{8,24},{12,28},{17,1},{... | collective-permute-start | bytes 196616 | tf_op jit(solution)/shard_map/ppermute | solution.py:14
  173.7 3.9 %collective-permute-done.7.refs_3_ = bf16[256,128]{1,0:T(8,128)(2,1)S(1)} collective-permute-done((bf16[256,128]{1,0:T(8,128)(2,1)S(1)}, bf16[256,128]{1,0:T(8,128)(2,1)S(1)}, u32[]{:S(2)}, u32[]{:S(2)}) %collective-permute-start.7) | collective-permute-done | bytes 65568 | tf_op jit(solution)/shard_map/ppermute | solution.py:14
  178.9 2.9 %collective-permute-start.9 = (bf16[256,128]{1,0:T(8,128)(2,1)}, bf16[256,128]{1,0:T(8,128)(2,1)S(1)}, u32[]{:S(2)}, u32[]{:S(2)}) collective-permute-start(bf16[256,128]{1,0:T(8,128)(2,1)} %get-tuple-element.41), channel_id=1, source_target_pairs={{4,0},{8,4},{12,8},{16,12},{20,16},{24,20},{28,24},{0,28},{5,1},{9... | collective-permute-start | bytes 196616 | tf_op jit(solution)/shard_map/ppermute | solution.py:14
  184.3 11.7 %shard_map.56.refs_2_ = bf16[256,8192]{1,0:T(8,128)(2,1)S(1)} custom-call(s32[1024]{0:T(1024)S(1)} %reshape.38.refs_0_, s32[1]{0:T(128)} %bitcast.refs_1_, bf16[256,8192]{1,0:T(8,128)(2,1)} %copy-done.1, bf16[256,128]{1,0:T(8,128)(2,1)S(1)} %collective-permute-done.7.refs_3_, bf16[256,128]{1,0:T(8,128)(2,1)S(1)} %collective-permute-done.8.refs_4_, ...), custom_call_target="tpu_custom_call" | custom-call | flops 2147483648 | bytes 16777216 | tf_op jit(solution)/shard_map/pallas_call | solution.py:77
  196.0 2.0 copy-done
  198.1 1.8 collective-permute-start.14
  199.9 3.3 %collective-permute-start.16 = (bf16[256,128]{1,0:T(8,128)(2,1)S(1)}, bf16[256,128]{1,0:T(8,128)(2,1)S(1)}, u32[]{:S(2)}, u32[]{:S(2)}) collective-permute-start(bf16[256,128]{1,0:T(8,128)(2,1)S(1)} %get-tuple-element.37), channel_id=1, source_target_pairs={{4,0},{8,4},{12,8},{16,12},{20,16},{24,20},{28,24},{0,28},{5,1},{9... | collective-permute-start | bytes 196616 | tf_op jit(solution)/shard_map/ppermute | solution.py:14
  203.2 2.6 %collective-permute-done.14.refs_3_ = bf16[256,128]{1,0:T(8,128)(2,1)S(1)} collective-permute-done((bf16[256,128]{1,0:T(8,128)(2,1)S(1)}, bf16[256,128]{1,0:T(8,128)(2,1)S(1)}, u32[]{:S(2)}, u32[]{:S(2)}) %collective-permute-start.14) | collective-permute-done | bytes 65568 | tf_op jit(solution)/shard_map/ppermute | solution.py:14
  208.0 3.0 %collective-permute-done.17.refs_6_ = bf16[256,128]{1,0:T(8,128)(2,1)S(1)} collective-permute-done((bf16[256,128]{1,0:T(8,128)(2,1)S(1)}, bf16[256,128]{1,0:T(8,128)(2,1)S(1)}, u32[]{:S(2)}, u32[]{:S(2)}) %collective-permute-start.17) | collective-permute-done | bytes 65568 | tf_op jit(solution)/shard_map/ppermute | solution.py:14
  214.9 11.3 %shard_map.57.refs_2_ = bf16[256,8192]{1,0:T(8,128)(2,1)S(1)} custom-call(s32[1024]{0:T(1024)S(1)} %reshape.38.refs_0_, s32[1]{0:T(128)} %bitcast.refs_1_, bf16[256,8192]{1,0:T(8,128)(2,1)} %copy-done, bf16[256,128]{1,0:T(8,128)(2,1)S(1)} %collective-permute-done.14.refs_3_, bf16[256,128]{1,0:T(8,128)(2,1)S(1)} %collective-permute-done.15.refs_4_, ...), custom_call_target="tpu_custom_call" | custom-call | flops 2147483648 | bytes 16777216 | tf_op jit(solution)/shard_map/pallas_call | solution.py:77
  226.7 4.5 %collective-permute-start.23 = (bf16[256,128]{1,0:T(8,128)(2,1)S(1)}, bf16[256,128]{1,0:T(8,128)(2,1)S(1)}, u32[]{:S(2)}, u32[]{:S(2)}) collective-permute-start(bf16[256,128]{1,0:T(8,128)(2,1)S(1)} %get-tuple-element.33), channel_id=1, source_target_pairs={{4,0},{8,4},{12,8},{16,12},{20,16},{24,20},{28,24},{0,28},{5,1},{9... | collective-permute-start | bytes 196616 | tf_op jit(solution)/shard_map/ppermute | solution.py:14
  231.7 2.7 %collective-permute-start.24 = (bf16[256,128]{1,0:T(8,128)(2,1)S(1)}, bf16[256,128]{1,0:T(8,128)(2,1)S(1)}, u32[]{:S(2)}, u32[]{:S(2)}) collective-permute-start(bf16[256,128]{1,0:T(8,128)(2,1)S(1)} %get-tuple-element.32), channel_id=1, source_target_pairs={{16,0},{20,4},{24,8},{28,12},{0,16},{4,20},{8,24},{12,28},{17,1},{... | collective-permute-start | bytes 196616 | tf_op jit(solution)/shard_map/ppermute | solution.py:14
  235.0 2.6 %collective-permute-done.24.refs_6_ = bf16[256,128]{1,0:T(8,128)(2,1)S(1)} collective-permute-done((bf16[256,128]{1,0:T(8,128)(2,1)S(1)}, bf16[256,128]{1,0:T(8,128)(2,1)S(1)}, u32[]{:S(2)}, u32[]{:S(2)}) %collective-permute-start.24) | collective-permute-done | bytes 65568 | tf_op jit(solution)/shard_map/ppermute | solution.py:14
  237.7 4.5 %shard_map.58.refs_12_ = bf16[256,8192]{1,0:T(8,128)(2,1)} custom-call(s32[1024]{0:T(1024)S(1)} %reshape.38.refs_0_, s32[1]{0:T(128)} %bitcast.refs_1_, bf16[256,8192]{1,0:T(8,128)(2,1)S(1)} %shard_map.57.refs_2_, bf16[256,128]{1,0:T(8,128)(2,1)S(1)} %collective-permute-done.21.refs_3_, bf16[256,128]{1,0:T(8,128)(2,1)S(1)} %collective-permute-done.22.refs_4_, ...), custom_call_target="tpu_custom_call" | custom-call | flops 536870912 | bytes 7340032 | tf_op jit(solution)/shard_map/pallas_call | solution.py:77
  242.2 4.4 %shard_map.59.refs_12_ = bf16[256,8192]{1,0:T(8,128)(2,1)} custom-call(s32[1024]{0:T(1024)S(1)} %reshape.38.refs_0_, s32[1]{0:T(128)} %bitcast.refs_1_, bf16[256,8192]{1,0:T(8,128)(2,1)S(1)} %shard_map.57.refs_2_, bf16[256,128]{1,0:T(8,128)(2,1)S(1)} %collective-permute-done.21.refs_3_, ...), custom_call_target="tpu_custom_call", output_to_operand_aliasing={{}: (12, {})} | custom-call | flops 536870912 | bytes 7340032 | tf_op jit(solution)/shard_map/pallas_call | solution.py:77
  246.6 4.3 %shard_map.60.refs_12_ = bf16[256,8192]{1,0:T(8,128)(2,1)} custom-call(s32[1024]{0:T(1024)S(1)} %reshape.38.refs_0_, s32[1]{0:T(128)} %bitcast.refs_1_, bf16[256,8192]{1,0:T(8,128)(2,1)S(1)} %shard_map.57.refs_2_, bf16[256,128]{1,0:T(8,128)(2,1)S(1)} %collective-permute-done.21.refs_3_, ...), custom_call_target="tpu_custom_call", output_to_operand_aliasing={{}: (12, {})} | custom-call | flops 536870912 | bytes 7340032 | tf_op jit(solution)/shard_map/pallas_call | solution.py:77
  250.9 4.2 %shard_map.61 = bf16[256,8192]{1,0:T(8,128)(2,1)} custom-call(s32[1024]{0:T(1024)S(1)} %reshape.38.refs_0_, s32[1]{0:T(128)} %bitcast.refs_1_, bf16[256,8192]{1,0:T(8,128)(2,1)S(1)} %shard_map.57.refs_2_, bf16[256,128]{1,0:T(8,128)(2,1)S(1)} %collective-permute-done.21.refs_3_, ...), custom_call_target="tpu_custom_call", output_to_operand_aliasing={{}: (12, {})} | custom-call | flops 536870912 | bytes 7340032 | tf_op jit(solution)/shard_map/pallas_call | solution.py:77
  (72 shorter events, 19.1 us)
Async XLA Ops:
  7.1 49.6 %collective-permute-start.5 = (bf16[64,128,128]{2,1,0:T(8,128)(2,1)}, bf16[64,128,128]{2,1,0:T(8,128)(2,1)S(1)}, u32[]{:S(2)}, u32[]{:S(2)}) collective-permute-start(bf16[64,128,128]{2,1,0:T(8,128)(2,1)} %get-tuple-element.31.refs_7_), channel_id=1, source_target_pairs={{0,2},{1,3},{2,0},{3,1},{4,6},{5,7},{6,4},{7,5},{8,10},{9,11},{10,... | collective-permute-start | bytes 6291464 | tf_op jit(solution)/shard_map/ppermute | solution.py:19
  10.0 91.7 %collective-permute-start.12 = (bf16[64,128,128]{2,1,0:T(8,128)(2,1)}, bf16[64,128,128]{2,1,0:T(8,128)(2,1)}, u32[]{:S(2)}, u32[]{:S(2)}) collective-permute-start(bf16[64,128,128]{2,1,0:T(8,128)(2,1)} %get-tuple-element.29.refs_7_), channel_id=1, source_target_pairs={{0,2},{1,3},{2,0},{3,1},{4,6},{5,7},{6,4},{7,5},{8,10},{9,11},{10,... | collective-permute-start | bytes 6291464 | tf_op jit(solution)/shard_map/ppermute | solution.py:19
  58.1 87.7 %collective-permute-start.19 = (bf16[64,128,128]{2,1,0:T(8,128)(2,1)S(1)}, bf16[64,128,128]{2,1,0:T(8,128)(2,1)}, u32[]{:S(2)}, u32[]{:S(2)}) collective-permute-start(bf16[64,128,128]{2,1,0:T(8,128)(2,1)S(1)} %get-tuple-element.17.refs_7_), channel_id=1, source_target_pairs={{0,2},{1,3},{2,0},{3,1},{4,6},{5,7},{6,4},{7,5},{8,10},{9,11},{10,... | collective-permute-start | bytes 6291464 | tf_op jit(solution)/shard_map/ppermute | solution.py:19
  60.2 85.7 %collective-permute-start.4 = (bf16[64,128,128]{2,1,0:T(8,128)(2,1)}, bf16[64,128,128]{2,1,0:T(8,128)(2,1)}, u32[]{:S(2)}, u32[]{:S(2)}) collective-permute-start(bf16[64,128,128]{2,1,0:T(8,128)(2,1)} %get-tuple-element.31.refs_7_), channel_id=1, source_target_pairs={{0,1},{1,0},{2,3},{3,2},{4,5},{5,4},{6,7},{7,6},{8,9},{9,8},{10,11... | collective-permute-start | bytes 6291464 | tf_op jit(solution)/shard_map/ppermute | solution.py:19
  64.6 7.6 %collective-permute-start = (bf16[256,128]{1,0:T(8,128)(2,1)S(1)}, bf16[256,128]{1,0:T(8,128)(2,1)S(1)}, u32[]{:S(2)}, u32[]{:S(2)}) collective-permute-start(bf16[256,128]{1,0:T(8,128)(2,1)S(1)} %get-tuple-element.47), channel_id=1, source_target_pairs={{28,0},{0,4},{4,8},{8,12},{12,16},{16,20},{20,24},{24,28},{29,1},{... | collective-permute-start | bytes 196616 | tf_op jit(solution)/shard_map/ppermute | solution.py:14
  66.1 7.5 %collective-permute-start.1 = (bf16[256,128]{1,0:T(8,128)(2,1)S(1)}, bf16[256,128]{1,0:T(8,128)(2,1)S(1)}, u32[]{:S(2)}, u32[]{:S(2)}) collective-permute-start(bf16[256,128]{1,0:T(8,128)(2,1)S(1)} %get-tuple-element.46), channel_id=1, source_target_pairs={{24,0},{28,4},{0,8},{4,12},{8,16},{12,20},{16,24},{20,28},{25,1},{... | collective-permute-start | bytes 196616 | tf_op jit(solution)/shard_map/ppermute | solution.py:14
  73.7 76.9 %collective-permute-start.6 = (bf16[64,128,128]{2,1,0:T(8,128)(2,1)}, bf16[64,128,128]{2,1,0:T(8,128)(2,1)}, u32[]{:S(2)}, u32[]{:S(2)}) collective-permute-start(bf16[64,128,128]{2,1,0:T(8,128)(2,1)} %copy-done.3), channel_id=1, source_target_pairs={{0,1},{1,0},{2,3},{3,2},{4,5},{5,4},{6,7},{7,6},{8,9},{9,8},{10,11... | collective-permute-start | bytes 6291464 | tf_op jit(solution)/shard_map/ppermute | solution.py:19
  76.5 92.6 %collective-permute-start.11 = (bf16[64,128,128]{2,1,0:T(8,128)(2,1)}, bf16[64,128,128]{2,1,0:T(8,128)(2,1)}, u32[]{:S(2)}, u32[]{:S(2)}) collective-permute-start(bf16[64,128,128]{2,1,0:T(8,128)(2,1)} %get-tuple-element.29.refs_7_), channel_id=1, source_target_pairs={{0,1},{1,0},{2,3},{3,2},{4,5},{5,4},{6,7},{7,6},{8,9},{9,8},{10,11... | collective-permute-start | bytes 6291464 | tf_op jit(solution)/shard_map/ppermute | solution.py:19
  107.7 62.9 %collective-permute-start.13 = (bf16[64,128,128]{2,1,0:T(8,128)(2,1)}, bf16[64,128,128]{2,1,0:T(8,128)(2,1)}, u32[]{:S(2)}, u32[]{:S(2)}) collective-permute-start(bf16[64,128,128]{2,1,0:T(8,128)(2,1)} %collective-permute-done.12.refs_9_), channel_id=1, source_target_pairs={{0,1},{1,0},{2,3},{3,2},{4,5},{5,4},{6,7},{7,6},{8,9},{9,8},{10,11... | collective-permute-start | bytes 6291464 | tf_op jit(solution)/shard_map/ppermute | solution.py:19
  145.8 54.0 %collective-permute-start.18 = (bf16[64,128,128]{2,1,0:T(8,128)(2,1)S(1)}, bf16[64,128,128]{2,1,0:T(8,128)(2,1)}, u32[]{:S(2)}, u32[]{:S(2)}) collective-permute-start(bf16[64,128,128]{2,1,0:T(8,128)(2,1)S(1)} %get-tuple-element.17.refs_7_), channel_id=1, source_target_pairs={{0,1},{1,0},{2,3},{3,2},{4,5},{5,4},{6,7},{7,6},{8,9},{9,8},{10,11... | collective-permute-start | bytes 6291464 | tf_op jit(solution)/shard_map/ppermute | solution.py:19
  145.9 65.1 %collective-permute-start.20 = (bf16[64,128,128]{2,1,0:T(8,128)(2,1)}, bf16[64,128,128]{2,1,0:T(8,128)(2,1)}, u32[]{:S(2)}, u32[]{:S(2)}) collective-permute-start(bf16[64,128,128]{2,1,0:T(8,128)(2,1)} %collective-permute-done.19.refs_9_), channel_id=1, source_target_pairs={{0,1},{1,0},{2,3},{3,2},{4,5},{5,4},{6,7},{7,6},{8,9},{9,8},{10,11... | collective-permute-start | bytes 6291464 | tf_op jit(solution)/shard_map/ppermute | solution.py:19
  166.3 6.6 %collective-permute-start.10 = (bf16[256,128]{1,0:T(8,128)(2,1)S(1)}, bf16[256,128]{1,0:T(8,128)(2,1)S(1)}, u32[]{:S(2)}, u32[]{:S(2)}) collective-permute-start(bf16[256,128]{1,0:T(8,128)(2,1)S(1)} %get-tuple-element.40), channel_id=1, source_target_pairs={{16,0},{20,4},{24,8},{28,12},{0,16},{4,20},{8,24},{12,28},{17,1},{... | collective-permute-start | bytes 196616 | tf_op jit(solution)/shard_map/ppermute | solution.py:14
  169.1 30.8 %collective-permute-start.29 = (bf16[16,128,128]{2,1,0:T(8,128)(2,1)}, bf16[16,128,128]{2,1,0:T(8,128)(2,1)}, u32[]{:S(2)}, u32[]{:S(2)}) collective-permute-start(bf16[16,128,128]{2,1,0:T(8,128)(2,1)} %get-tuple-element.21.refs_7_), channel_id=1, source_target_pairs={{0,2},{1,3},{2,0},{3,1},{4,6},{5,7},{6,4},{7,5},{8,10},{9,11},{10,... | collective-permute-start | bytes 1572872 | tf_op jit(solution)/shard_map/ppermute | solution.py:19
  170.6 7.0 %collective-permute-start.7 = (bf16[256,128]{1,0:T(8,128)(2,1)S(1)}, bf16[256,128]{1,0:T(8,128)(2,1)S(1)}, u32[]{:S(2)}, u32[]{:S(2)}) collective-permute-start(bf16[256,128]{1,0:T(8,128)(2,1)S(1)} %get-tuple-element.43), channel_id=1, source_target_pairs={{28,0},{0,4},{4,8},{8,12},{12,16},{16,20},{20,24},{24,28},{29,1},{... | collective-permute-start | bytes 196616 | tf_op jit(solution)/shard_map/ppermute | solution.py:14
  172.8 6.1 %collective-permute-start.8 = (bf16[256,128]{1,0:T(8,128)(2,1)S(1)}, bf16[256,128]{1,0:T(8,128)(2,1)S(1)}, u32[]{:S(2)}, u32[]{:S(2)}) collective-permute-start(bf16[256,128]{1,0:T(8,128)(2,1)S(1)} %get-tuple-element.42), channel_id=1, source_target_pairs={{24,0},{28,4},{0,8},{4,12},{8,16},{12,20},{16,24},{20,28},{25,1},{... | collective-permute-start | bytes 196616 | tf_op jit(solution)/shard_map/ppermute | solution.py:14
  177.5 28.9 %collective-permute-start.25 = (bf16[16,128,128]{2,1,0:T(8,128)(2,1)}, bf16[16,128,128]{2,1,0:T(8,128)(2,1)}, u32[]{:S(2)}, u32[]{:S(2)}) collective-permute-start(bf16[16,128,128]{2,1,0:T(8,128)(2,1)} %get-tuple-element.19.refs_7_), channel_id=1, source_target_pairs={{0,2},{1,3},{2,0},{3,1},{4,6},{5,7},{6,4},{7,5},{8,10},{9,11},{10,... | collective-permute-start | bytes 1572872 | tf_op jit(solution)/shard_map/ppermute | solution.py:19
  198.1 7.7 %collective-permute-start.14 = (bf16[256,128]{1,0:T(8,128)(2,1)S(1)}, bf16[256,128]{1,0:T(8,128)(2,1)S(1)}, u32[]{:S(2)}, u32[]{:S(2)}) collective-permute-start(bf16[256,128]{1,0:T(8,128)(2,1)S(1)} %get-tuple-element.39), channel_id=1, source_target_pairs={{28,0},{0,4},{4,8},{8,12},{12,16},{16,20},{20,24},{24,28},{29,1},{... | collective-permute-start | bytes 196616 | tf_op jit(solution)/shard_map/ppermute | solution.py:14
  199.9 6.1 %collective-permute-start.15 = (bf16[256,128]{1,0:T(8,128)(2,1)S(1)}, bf16[256,128]{1,0:T(8,128)(2,1)S(1)}, u32[]{:S(2)}, u32[]{:S(2)}) collective-permute-start(bf16[256,128]{1,0:T(8,128)(2,1)S(1)} %get-tuple-element.38), channel_id=1, source_target_pairs={{24,0},{28,4},{0,8},{4,12},{8,16},{12,20},{16,24},{20,28},{25,1},{... | collective-permute-start | bytes 196616 | tf_op jit(solution)/shard_map/ppermute | solution.py:14
  199.9 6.1 %collective-permute-start.16 = (bf16[256,128]{1,0:T(8,128)(2,1)S(1)}, bf16[256,128]{1,0:T(8,128)(2,1)S(1)}, u32[]{:S(2)}, u32[]{:S(2)}) collective-permute-start(bf16[256,128]{1,0:T(8,128)(2,1)S(1)} %get-tuple-element.37), channel_id=1, source_target_pairs={{4,0},{8,4},{12,8},{16,12},{20,16},{24,20},{28,24},{0,28},{5,1},{9... | collective-permute-start | bytes 196616 | tf_op jit(solution)/shard_map/ppermute | solution.py:14
  206.0 20.3 %collective-permute-start.35 = (bf16[16,128,128]{2,1,0:T(8,128)(2,1)}, bf16[16,128,128]{2,1,0:T(8,128)(2,1)}, u32[]{:S(2)}, u32[]{:S(2)}) collective-permute-start(bf16[16,128,128]{2,1,0:T(8,128)(2,1)} %get-tuple-element.21.refs_7_), channel_id=1, source_target_pairs={{0,1},{1,0},{2,3},{3,2},{4,5},{5,4},{6,7},{7,6},{8,9},{9,8},{10,11... | collective-permute-start | bytes 1572872 | tf_op jit(solution)/shard_map/ppermute | solution.py:19
  206.0 20.4 %collective-permute-start.36 = (bf16[16,128,128]{2,1,0:T(8,128)(2,1)}, bf16[16,128,128]{2,1,0:T(8,128)(2,1)}, u32[]{:S(2)}, u32[]{:S(2)}) collective-permute-start(bf16[16,128,128]{2,1,0:T(8,128)(2,1)} %collective-permute-done.29.refs_9_), channel_id=1, source_target_pairs={{0,1},{1,0},{2,3},{3,2},{4,5},{5,4},{6,7},{7,6},{8,9},{9,8},{10,11... | collective-permute-start | bytes 1572872 | tf_op jit(solution)/shard_map/ppermute | solution.py:19
  206.5 20.0 %collective-permute-start.31 = (bf16[16,128,128]{2,1,0:T(8,128)(2,1)S(1)}, bf16[16,128,128]{2,1,0:T(8,128)(2,1)}, u32[]{:S(2)}, u32[]{:S(2)}) collective-permute-start(bf16[16,128,128]{2,1,0:T(8,128)(2,1)S(1)} %get-tuple-element.22.refs_7_), channel_id=1, source_target_pairs={{0,2},{1,3},{2,0},{3,1},{4,6},{5,7},{6,4},{7,5},{8,10},{9,11},{10,... | collective-permute-start | bytes 1572872 | tf_op jit(solution)/shard_map/ppermute | solution.py:19
  210.9 15.8 %collective-permute-start.33 = (bf16[16,128,128]{2,1,0:T(8,128)(2,1)}, bf16[16,128,128]{2,1,0:T(8,128)(2,1)}, u32[]{:S(2)}, u32[]{:S(2)}) collective-permute-start(bf16[16,128,128]{2,1,0:T(8,128)(2,1)} %get-tuple-element.19.refs_7_), channel_id=1, source_target_pairs={{0,1},{1,0},{2,3},{3,2},{4,5},{5,4},{6,7},{7,6},{8,9},{9,8},{10,11... | collective-permute-start | bytes 1572872 | tf_op jit(solution)/shard_map/ppermute | solution.py:19
  210.9 20.8 %collective-permute-start.27 = (bf16[16,128,128]{2,1,0:T(8,128)(2,1)S(1)}, bf16[16,128,128]{2,1,0:T(8,128)(2,1)}, u32[]{:S(2)}, u32[]{:S(2)}) collective-permute-start(bf16[16,128,128]{2,1,0:T(8,128)(2,1)S(1)} %get-tuple-element.20.refs_7_), channel_id=1, source_target_pairs={{0,2},{1,3},{2,0},{3,1},{4,6},{5,7},{6,4},{7,5},{8,10},{9,11},{10,... | collective-permute-start | bytes 1572872 | tf_op jit(solution)/shard_map/ppermute | solution.py:19
  226.3 8.2 %collective-permute-start.21 = (bf16[256,128]{1,0:T(8,128)(2,1)S(1)}, bf16[256,128]{1,0:T(8,128)(2,1)S(1)}, u32[]{:S(2)}, u32[]{:S(2)}) collective-permute-start(bf16[256,128]{1,0:T(8,128)(2,1)S(1)} %get-tuple-element.35), channel_id=1, source_target_pairs={{28,0},{0,4},{4,8},{8,12},{12,16},{16,20},{20,24},{24,28},{29,1},{... | collective-permute-start | bytes 196616 | tf_op jit(solution)/shard_map/ppermute | solution.py:14
  226.3 8.1 %collective-permute-start.22 = (bf16[256,128]{1,0:T(8,128)(2,1)S(1)}, bf16[256,128]{1,0:T(8,128)(2,1)S(1)}, u32[]{:S(2)}, u32[]{:S(2)}) collective-permute-start(bf16[256,128]{1,0:T(8,128)(2,1)S(1)} %get-tuple-element.34), channel_id=1, source_target_pairs={{24,0},{28,4},{0,8},{4,12},{8,16},{12,20},{16,24},{20,28},{25,1},{... | collective-permute-start | bytes 196616 | tf_op jit(solution)/shard_map/ppermute | solution.py:14
  226.5 15.6 %collective-permute-start.34 = (bf16[16,128,128]{2,1,0:T(8,128)(2,1)}, bf16[16,128,128]{2,1,0:T(8,128)(2,1)S(1)}, u32[]{:S(2)}, u32[]{:S(2)}) collective-permute-start(bf16[16,128,128]{2,1,0:T(8,128)(2,1)} %collective-permute-done.25.refs_9_), channel_id=1, source_target_pairs={{0,1},{1,0},{2,3},{3,2},{4,5},{5,4},{6,7},{7,6},{8,9},{9,8},{10,11... | collective-permute-start | bytes 1572872 | tf_op jit(solution)/shard_map/ppermute | solution.py:19
  226.7 8.3 %collective-permute-start.23 = (bf16[256,128]{1,0:T(8,128)(2,1)S(1)}, bf16[256,128]{1,0:T(8,128)(2,1)S(1)}, u32[]{:S(2)}, u32[]{:S(2)}) collective-permute-start(bf16[256,128]{1,0:T(8,128)(2,1)S(1)} %get-tuple-element.33), channel_id=1, source_target_pairs={{4,0},{8,4},{12,8},{16,12},{20,16},{24,20},{28,24},{0,28},{5,1},{9... | collective-permute-start | bytes 196616 | tf_op jit(solution)/shard_map/ppermute | solution.py:14
  234.5 12.1 %collective-permute-start.30 = (bf16[16,128,128]{2,1,0:T(8,128)(2,1)S(1)}, bf16[16,128,128]{2,1,0:T(8,128)(2,1)S(1)}, u32[]{:S(2)}, u32[]{:S(2)}) collective-permute-start(bf16[16,128,128]{2,1,0:T(8,128)(2,1)S(1)} %get-tuple-element.22.refs_7_), channel_id=1, source_target_pairs={{0,1},{1,0},{2,3},{3,2},{4,5},{5,4},{6,7},{7,6},{8,9},{9,8},{10,11... | collective-permute-start | bytes 1572872 | tf_op jit(solution)/shard_map/ppermute | solution.py:19
  234.5 12.1 %collective-permute-start.32 = (bf16[16,128,128]{2,1,0:T(8,128)(2,1)}, bf16[16,128,128]{2,1,0:T(8,128)(2,1)S(1)}, u32[]{:S(2)}, u32[]{:S(2)}) collective-permute-start(bf16[16,128,128]{2,1,0:T(8,128)(2,1)} %collective-permute-done.31.refs_9_), channel_id=1, source_target_pairs={{0,1},{1,0},{2,3},{3,2},{4,5},{5,4},{6,7},{7,6},{8,9},{9,8},{10,11... | collective-permute-start | bytes 1572872 | tf_op jit(solution)/shard_map/ppermute | solution.py:19
  235.0 15.9 %collective-permute-start.26 = (bf16[16,128,128]{2,1,0:T(8,128)(2,1)S(1)}, bf16[16,128,128]{2,1,0:T(8,128)(2,1)S(1)}, u32[]{:S(2)}, u32[]{:S(2)}) collective-permute-start(bf16[16,128,128]{2,1,0:T(8,128)(2,1)S(1)} %get-tuple-element.20.refs_7_), channel_id=1, source_target_pairs={{0,1},{1,0},{2,3},{3,2},{4,5},{5,4},{6,7},{7,6},{8,9},{9,8},{10,11... | collective-permute-start | bytes 1572872 | tf_op jit(solution)/shard_map/ppermute | solution.py:19
  237.7 13.2 %collective-permute-start.28 = (bf16[16,128,128]{2,1,0:T(8,128)(2,1)}, bf16[16,128,128]{2,1,0:T(8,128)(2,1)S(1)}, u32[]{:S(2)}, u32[]{:S(2)}) collective-permute-start(bf16[16,128,128]{2,1,0:T(8,128)(2,1)} %collective-permute-done.27.refs_9_), channel_id=1, source_target_pairs={{0,1},{1,0},{2,3},{3,2},{4,5},{5,4},{6,7},{7,6},{8,9},{9,8},{10,11... | collective-permute-start | bytes 1572872 | tf_op jit(solution)/shard_map/ppermute | solution.py:19
  (12 other events, 379.1 us)

commit v2 on v1

v2 whole, which is shorter than its diff:
```python
import functools
import math

import jax
import jax.numpy as jnp
from jax import lax
from jax.experimental import pallas as pl
from jax.experimental.pallas import tpu as pltpu
from jax.sharding import PartitionSpec as P


PIECES = 4
FREE = pl.CostEstimate(flops=0, bytes_accessed=0, transcendentals=0)


def shifted(block, axis, distance):
    devices = range(lax.axis_size(axis))
    route = [((i - distance) % len(devices), i) for i in devices]
    return lax.ppermute(block, axis, route)


def swapped(block, mask):
    route = [(i, i ^ mask) for i in range(lax.axis_size("batch"))]
    return lax.ppermute(block, "batch", route)


def cut(tile_weights, layer, first, count, after):
    part = (count, *tile_weights.shape[2:])
    anywhere, in_hbm = (pl.BlockSpec(memory_space=space) for space in (pl.ANY, pltpu.HBM))

    def kernel(tiles, *refs):
        target, semaphore = refs[len(after) :]
        copy = pltpu.make_async_copy(tiles.at[layer, pl.ds(first, count)], target, semaphore)
        copy.start()
        copy.wait()

    return pl.pallas_call(
        kernel,
        out_shape=jax.ShapeDtypeStruct(part, tile_weights.dtype),
        in_specs=[in_hbm] + [anywhere] * len(after),
        out_specs=in_hbm,
        scratch_shapes=[pltpu.SemaphoreType.DMA],
        compiler_params=pltpu.CompilerParams(vmem_limit_bytes=56 * 2**20),
        cost_estimate=FREE,
    )(tile_weights, *after)


def layer_kernel(layer, first, group, blocks, neigh, width, pieces, aliased, *refs):
    refs = list(refs)
    codes, own, current = (refs.pop(0) for _ in range(3))
    arrived = [refs.pop(0) for _ in range(neigh)]
    tiles = [[refs.pop(0) for _ in range(number)] for number in pieces]
    bias = refs.pop(0)
    if aliased:
        refs.pop(0)
    result, pool, semaphores = refs
    fan = len(pieces)
    step = pl.program_id(0)

    @pl.when(step == 0)
    def _():
        copies = [pltpu.make_async_copy(current, pool.at[:, : blocks * width], semaphores.at[neigh])]
        for slot in range(neigh):
            place = pl.ds((blocks + slot) * width, width)
            copies.append(pltpu.make_async_copy(arrived[slot], pool.at[:, place], semaphores.at[slot]))
        for copy in copies:
            copy.start()
        for copy in copies:
            copy.wait()

    def work(held):
        for g in range(group):
            base = (layer * blocks + first + step * group + g) * fan
            panel = []
            for m in range(fan):
                code = codes[base + (own[0] ^ m)]
                panel.append(pool[:, pl.ds(pl.multiple_of(code * width, width), width)])
            summed = jnp.dot(
                jnp.concatenate(panel, axis=1),
                jnp.concatenate([tile[g] for tile in held], axis=0),
                preferred_element_type=jnp.float32,
            )
            columns = slice(g * width, (g + 1) * width)
            summed = summed + bias[layer : layer + 1, columns]
            result[:, columns] = jnp.maximum(summed, 0.0).astype(result.dtype)

    most = max(pieces)
    span = pl.num_programs(0) // most
    for part in range(most):

        @pl.when(step // span == part)
        def _():
            work([held[part * len(held) // most] for held in tiles])


def run_blocks(layer, first, count, codes, own, current, arrived, tiles, biases, target):
    rows, neurons = current.shape
    neigh, width = len(arrived), tiles[0].shape[3]
    blocks = neurons // width
    group = math.gcd(8, count // max(len(source) for source in tiles if isinstance(source, list)))
    steps = count // group
    offset = first // group
    anywhere = pl.BlockSpec(memory_space=pl.ANY)
    in_specs = [anywhere] * (1 + neigh)
    pieces, held = [], []
    for source in tiles:
        if isinstance(source, list):
            pieces.append(len(source))
            share = steps // len(source)
            for part, array in enumerate(source):
                held.append(array)
                in_specs.append(
                    pl.BlockSpec(
                        (group, width, width),
                        lambda i, *_, start=part * share, share=share: (jnp.clip(i - start, 0, share - 1), 0, 0),
                    )
                )
        else:
            pieces.append(1)
            held.append(source)
            in_specs.append(pl.BlockSpec((None, group, width, width), lambda i, *_: (layer, offset + i, 0, 0)))
    in_specs += [pl.BlockSpec((biases.shape[0], group * width), lambda i, *_: (0, offset + i))]
    operands = [codes, own, current, *arrived, *held, biases]
    aliases = {}
    if target is not None:
        in_specs += [anywhere]
        aliases = {len(operands): 0}
        operands += [target]
    kernel = functools.partial(layer_kernel, layer, first, group, blocks, neigh, width, pieces, target is not None)
    return pl.pallas_call(
        kernel,
        out_shape=jax.ShapeDtypeStruct((rows, neurons), current.dtype),
        grid_spec=pltpu.PrefetchScalarGridSpec(
            num_scalar_prefetch=2,
            grid=(steps,),
            in_specs=in_specs,
            out_specs=pl.BlockSpec((rows, group * width), lambda i, *_: (0, offset + i)),
            scratch_shapes=[
                pltpu.VMEM((rows, neurons + neigh * width), current.dtype),
                pltpu.SemaphoreType.DMA((neigh + 1,)),
            ],
        ),
        input_output_aliases=aliases,
        compiler_params=pltpu.CompilerParams(vmem_limit_bytes=52 * 2**20),
        cost_estimate=FREE,
    )(*operands)


def body(activations, tile_weights, biases, source_codes, send_list):
    layer_count, block_count, part_rows, width = tile_weights.shape
    fan = source_codes.shape[2]
    part_count = lax.axis_size("dom")
    neighbor_offsets = (1, 2, -1, part_count // 2)
    sharers = width // part_rows
    own = (lax.axis_index("batch") // sharers).reshape(1).astype(jnp.int32)
    codes = source_codes.reshape(-1)
    far = fan // 2
    unit = block_count // 16

    if sharers > 1:
        members = range(lax.axis_size("batch") // sharers)
        groups = [[m * sharers + s for s in range(sharers)] for m in members]
        tile_weights = lax.all_gather(tile_weights, "batch", axis=2, tiled=True, axis_index_groups=groups)

    def spread(held, first):
        for bit in range(far.bit_length() - 1):
            for m in range(1 << bit):
                held[first + m + (1 << bit)] = jax.tree.map(
                    lambda array: swapped(array, (1 << bit) * sharers), held[first + m]
                )

    last = layer_count - 1
    chunks = [(layer, 0, 16, PIECES) for layer in range(last)]
    chunks += [(last, 0, 8, PIECES), (last, 8, 4, PIECES), (last, 12, 4, 1)]
    chunks = [(layer, first * unit, count * unit, math.gcd(pieces, count * unit)) for layer, first, count, pieces in chunks]

    mine, crossed = {}, {}

    def send(index, *after):
        mine[index] = cut(tile_weights, *chunks[index][:3], after)
        crossed[index] = swapped(mine[index], far * sharers)

    near = [tile_weights] + [None] * (fan - 1)
    spread(near, 0)

    def tiles_of(index, *after):
        held = list(near)
        count, pieces = chunks[index][2:]
        arrived = lax.optimization_barrier((crossed[index], *after))[0]
        held[far] = [arrived[i * count // pieces : (i + 1) * count // pieces] for i in range(pieces)]
        spread(held, far)
        held[far] = [arrived]
        return held

    for index in range(len(chunks)):
        send(index)
    current = activations
    target = None
    for index, (layer, first, count, _) in enumerate(chunks):
        if first == 0:
            arrived = []
            for slot, offset in enumerate(neighbor_offsets):
                start = send_list[layer, 0, slot] * width
                block = lax.dynamic_slice(current, (0, start), (current.shape[0], width))
                arrived.append(shifted(block, "dom", offset))
            source, target = current, None
        before = [current] if index else []
        current = target = run_blocks(
            layer, first, count, codes, own, source, arrived, tiles_of(index, *before), biases, target
        )
    return current


def solution(mesh):
    in_specs = (
        P("batch", "dom"),
        P(None, "dom", "batch", None),
        P(None, "dom"),
        P(None, "dom", None),
        P(None, "dom", None),
    )
    out_specs = P("batch", "dom")
    return jax.shard_map(body, mesh=mesh, in_specs=in_specs, out_specs=out_specs, check_vma=False)
```

time: 256 us -> 405 us (1.58)
  Pallas kernels: 51.7 us -> 321 us
  waiting for transfers between devices: 132 us -> 21.6 us
  local copies, waits for them, and re-layouts: 21.2 us -> 14.1 us
  starting transfers between devices: 40.3 us -> 36 us
    pallas_call x0 -> x6, Pallas kernels: none -> 261 us  [cut(): pl.pallas_call(kernel, out_shape=jax.ShapeDtypeStruct(part, tile_weights....]
    ppermute x21 -> x28, waiting for transfers between devices: 111 us -> 4.8 us  [swapped(): return lax.ppermute(block, 'batch', route)]
    squeeze x2 -> x0, local copies, waits for them, and re-layouts: 9.84 us -> none  [local(): lax.slice(tile_weights, (layer, first, 0, 0), (layer + 1, first + count,...]
    pallas_call x7 -> x6, Pallas kernels: 51.7 us -> 60.4 us  [run_blocks(): pl.pallas_call(kernel, out_shape=jax.ShapeDtypeStruct((rows, neurons), cu...]
    slice x0 -> x5, local copies, waits for them, and re-layouts: none -> 6.87 us  [tiles_of(): arrived[i * count // pieces:(i + 1) * count // pieces]]
    unnamed x15 -> x17, local copies, waits for them, and re-layouts: 7.81 us -> 2.48 us
    ppermute x16, starting transfers between devices: 28.4 us -> 23.9 us  [shifted(): return lax.ppermute(block, axis, route)]
    ppermute x16, waiting for transfers between devices: 21 us -> 16.8 us  [shifted(): return lax.ppermute(block, axis, route)]
  transfers between devices with their start and end apart: 37 -> 44, of which waited for: 13 -> 13; matrix products, arithmetic and copies ran while one was open for 3% -> 3% of each run, Pallas kernels for 19% -> 78%
where the time goes in v2:
time: 405 us; the launch traced here: 404 us
  Pallas kernels  321 us (79%)
  starting transfers between devices  36 us (9%)
  waiting for transfers between devices  21.6 us (5%)
  local copies, waits for them, and re-layouts  14.1 us (3%)
  between operations  10.8 us (3%)
    pallas_call x6, Pallas kernels, cut(): pl.pallas_call(kernel, out_shape=jax.ShapeDtypeStruct(part, tile_weights....  261 us
    pallas_call x6, Pallas kernels, run_blocks(): pl.pallas_call(kernel, out_shape=jax.ShapeDtypeStruct((rows, neurons), cu...  60.4 us
    ppermute x16, starting transfers between devices, shifted(): return lax.ppermute(block, axis, route)  23.9 us
    ppermute x16, waiting for transfers between devices, shifted(): return lax.ppermute(block, axis, route)  16.8 us
    ppermute x28, starting transfers between devices, swapped(): return lax.ppermute(block, 'batch', route)  12.1 us
  transfers between devices with their start and end apart: 44, of which 13 were waited for; matrix products, arithmetic and copies ran while one was open for 3% of the time, Pallas kernels for 78%

profile of v2, /device:TPU:0, one launch (start us, length us, event | category | flops | bytes accessed | tf_op | source)
XLA Modules:
  0.0 403.6 jit_solution(13207531750134388)
XLA Ops:
  0.5 64.6 %shard_map.55 = bf16[64,128,128]{2,1,0:T(8,128)(2,1)} custom-call(bf16[4,64,128,128]{3,2,1,0:T(8,128)(2,1)} %refs_7_.11), custom_call_target="tpu_custom_call" | custom-call | tf_op jit(solution)/shard_map/pallas_call | solution.py:37
  65.1 2.6 collective-permute-start.5
  67.7 64.6 %shard_map.57 = bf16[64,128,128]{2,1,0:T(8,128)(2,1)} custom-call(bf16[4,64,128,128]{3,2,1,0:T(8,128)(2,1)} %refs_7_.11), custom_call_target="tpu_custom_call" | custom-call | tf_op jit(solution)/shard_map/pallas_call | solution.py:37
  136.6 2.1 collective-permute-start
  138.7 1.6 collective-permute-start.1
  140.2 64.6 %shard_map.59 = bf16[64,128,128]{2,1,0:T(8,128)(2,1)} custom-call(bf16[4,64,128,128]{3,2,1,0:T(8,128)(2,1)} %refs_7_.11), custom_call_target="tpu_custom_call" | custom-call | tf_op jit(solution)/shard_map/pallas_call | solution.py:37
  204.9 3.3 collective-permute-start.2
  209.0 1.5 collective-permute-start.23
  211.6 2.1 collective-permute-done.3.refs_6_
  214.2 2.1 collective-permute-done.7.refs_11_
  220.1 12.8 %shard_map.56.refs_2_ = bf16[256,8192]{1,0:T(8,128)(2,1)} custom-call(s32[1024]{0:T(1024)S(1)} %reshape.38.refs_0_, s32[1]{0:T(128)} %bitcast.refs_1_, bf16[256,8192]{1,0:T(8,128)(2,1)} %refs_2_.1, bf16[256,128]{1,0:T(8,128)(2,1)S(1)} %collective-permute-done.refs_3_, bf16[256,128]{1,0:T(8,128)(2,1)S(1)} %collective-permute-done.1.refs_4_, ...), custom_call_target="tpu_custom_call" | custom-call | tf_op jit(solution)/shard_map/pallas_call | solution.py:130
  233.9 2.7 fusion.1
  238.0 3.5 collective-permute-start.12
  243.9 3.9 collective-permute-done.13.refs_6_
  247.8 32.9 %shard_map.63 = bf16[32,128,128]{2,1,0:T(8,128)(2,1)} custom-call(bf16[4,64,128,128]{3,2,1,0:T(8,128)(2,1)} %refs_7_.11), custom_call_target="tpu_custom_call" | custom-call | tf_op jit(solution)/shard_map/pallas_call | solution.py:37
  280.7 1.5 collective-permute-start.34
  285.6 12.9 %shard_map.58.refs_2_ = bf16[256,8192]{1,0:T(8,128)(2,1)} custom-call(s32[1024]{0:T(1024)S(1)} %reshape.38.refs_0_, s32[1]{0:T(128)} %bitcast.refs_1_, bf16[256,8192]{1,0:T(8,128)(2,1)} %shard_map.56.refs_2_, bf16[256,128]{1,0:T(8,128)(2,1)S(1)} %collective-permute-done.10.refs_3_, bf16[256,128]{1,0:T(8,128)(2,1)S(1)} %collective-permute-done.11.refs_4_, ...), custom_call_target="tpu_custom_call" | custom-call | tf_op jit(solution)/shard_map/pallas_call | solution.py:130
  299.6 4.6 %collective-permute-start.21 = (bf16[256,128]{1,0:T(8,128)(2,1)S(1)}, bf16[256,128]{1,0:T(8,128)(2,1)S(1)}, u32[]{:S(2)}, u32[]{:S(2)}) collective-permute-start(bf16[256,128]{1,0:T(8,128)(2,1)S(1)} %get-tuple-element.20), channel_id=1, source_target_pairs={{4,0},{8,4},{12,8},{16,12},{20,16},{24,20},{28,24},{0,28},{5,1},{9... | collective-permute-start | bytes 196616 | tf_op jit(solution)/shard_map/ppermute | solution.py:19
  304.3 1.5 collective-permute-start.22
  305.8 2.9 fusion
  309.3 1.5 collective-permute-done.22.refs_6_
  313.3 17.0 %shard_map.62 = bf16[16,128,128]{2,1,0:T(8,128)(2,1)} custom-call(bf16[4,64,128,128]{3,2,1,0:T(8,128)(2,1)} %refs_7_.11), custom_call_target="tpu_custom_call" | custom-call | tf_op jit(solution)/shard_map/pallas_call | solution.py:37
  331.7 12.9 %shard_map.60.refs_2_ = bf16[256,8192]{1,0:T(8,128)(2,1)} custom-call(s32[1024]{0:T(1024)S(1)} %reshape.38.refs_0_, s32[1]{0:T(128)} %bitcast.refs_1_, bf16[256,8192]{1,0:T(8,128)(2,1)} %shard_map.58.refs_2_, bf16[256,128]{1,0:T(8,128)(2,1)S(1)} %collective-permute-done.19.refs_3_, bf16[256,128]{1,0:T(8,128)(2,1)S(1)} %collective-permute-done.20.refs_4_, ...), custom_call_target="tpu_custom_call" | custom-call | tf_op jit(solution)/shard_map/pallas_call | solution.py:130
  347.9 2.9 collective-permute-start.30
  350.8 2.9 collective-permute-done.28.refs_3_
  354.3 4.6 %collective-permute-done.31.refs_6_ = bf16[256,128]{1,0:T(8,128)(2,1)S(1)} collective-permute-done((bf16[256,128]{1,0:T(8,128)(2,1)S(1)}, bf16[256,128]{1,0:T(8,128)(2,1)S(1)}, u32[]{:S(2)}, u32[]{:S(2)}) %collective-permute-start.31) | collective-permute-done | bytes 65568 | tf_op jit(solution)/shard_map/ppermute | solution.py:19
  358.9 17.0 %shard_map.61 = bf16[16,128,128]{2,1,0:T(8,128)(2,1)} custom-call(bf16[4,64,128,128]{3,2,1,0:T(8,128)(2,1)} %refs_7_.11), custom_call_target="tpu_custom_call" | custom-call | tf_op jit(solution)/shard_map/pallas_call | solution.py:37
  375.9 1.5 collective-permute-start.32
  377.4 8.5 %shard_map.64.refs_15_ = bf16[256,8192]{1,0:T(8,128)(2,1)} custom-call(s32[1024]{0:T(1024)S(1)} %reshape.38.refs_0_, s32[1]{0:T(128)} %bitcast.refs_1_, bf16[256,8192]{1,0:T(8,128)(2,1)} %shard_map.60.refs_2_, bf16[256,128]{1,0:T(8,128)(2,1)S(1)} %collective-permute-done.28.refs_3_, bf16[256,128]{1,0:T(8,128)(2,1)S(1)} %collective-permute-done.29.refs_4_, ...), custom_call_target="tpu_custom_call" | custom-call | tf_op jit(solution)/shard_map/pallas_call | solution.py:130
  388.1 7.2 %shard_map.65.refs_12_ = bf16[256,8192]{1,0:T(8,128)(2,1)} custom-call(s32[1024]{0:T(1024)S(1)} %reshape.38.refs_0_, s32[1]{0:T(128)} %bitcast.refs_1_, bf16[256,8192]{1,0:T(8,128)(2,1)} %shard_map.60.refs_2_, bf16[256,128]{1,0:T(8,128)(2,1)S(1)} %collective-permute-done.28.refs_3_, ...), custom_call_target="tpu_custom_call", output_to_operand_aliasing={{}: (15, {})} | custom-call | tf_op jit(solution)/shard_map/pallas_call | solution.py:130
  395.6 1.6 collective-permute-done.43.refs_10_
  397.2 6.2 %shard_map.66 = bf16[256,8192]{1,0:T(8,128)(2,1)} custom-call(s32[1024]{0:T(1024)S(1)} %reshape.38.refs_0_, s32[1]{0:T(128)} %bitcast.refs_1_, bf16[256,8192]{1,0:T(8,128)(2,1)} %shard_map.60.refs_2_, bf16[256,128]{1,0:T(8,128)(2,1)S(1)} %collective-permute-done.28.refs_3_, ...), custom_call_target="tpu_custom_call", output_to_operand_aliasing={{}: (12, {})} | custom-call | tf_op jit(solution)/shard_map/pallas_call | solution.py:130
  (96 shorter events, 20.8 us)
Async XLA Ops:
  0.0 219.3 %collective-permute-start.4 = (bf16[4,64,128,128]{3,2,1,0:T(8,128)(2,1)}, bf16[4,64,128,128]{3,2,1,0:T(8,128)(2,1)}, u32[]{:S(2)}, u32[]{:S(2)}) collective-permute-start(bf16[4,64,128,128]{3,2,1,0:T(8,128)(2,1)} %refs_7_.11), channel_id=1, source_target_pairs={{0,1},{1,0},{2,3},{3,2},{4,5},{5,4},{6,7},{7,6},{8,9},{9,8},{10,11... | collective-permute-start | bytes 25165832 | tf_op jit(solution)/shard_map/ppermute | solution.py:24
  65.1 139.8 %collective-permute-start.5 = (bf16[64,128,128]{2,1,0:T(8,128)(2,1)}, bf16[64,128,128]{2,1,0:T(8,128)(2,1)S(1)}, u32[]{:S(2)}, u32[]{:S(2)}) collective-permute-start(bf16[64,128,128]{2,1,0:T(8,128)(2,1)} %shard_map.55), channel_id=1, source_target_pairs={{0,2},{1,3},{2,0},{3,1},{4,6},{5,7},{6,4},{7,5},{8,10},{9,11},{10,... | collective-permute-start | bytes 6291464 | tf_op jit(solution)/shard_map/ppermute | solution.py:24
  132.3 100.6 %collective-permute-start.14 = (bf16[64,128,128]{2,1,0:T(8,128)(2,1)}, bf16[64,128,128]{2,1,0:T(8,128)(2,1)}, u32[]{:S(2)}, u32[]{:S(2)}) collective-permute-start(bf16[64,128,128]{2,1,0:T(8,128)(2,1)} %shard_map.57), channel_id=1, source_target_pairs={{0,2},{1,3},{2,0},{3,1},{4,6},{5,7},{6,4},{7,5},{8,10},{9,11},{10,... | collective-permute-start | bytes 6291464 | tf_op jit(solution)/shard_map/ppermute | solution.py:24
  136.6 71.6 %collective-permute-start = (bf16[256,128]{1,0:T(8,128)(2,1)S(1)}, bf16[256,128]{1,0:T(8,128)(2,1)S(1)}, u32[]{:S(2)}, u32[]{:S(2)}) collective-permute-start(bf16[256,128]{1,0:T(8,128)(2,1)S(1)} %get-tuple-element.30), channel_id=1, source_target_pairs={{28,0},{0,4},{4,8},{8,12},{12,16},{16,20},{20,24},{24,28},{29,1},{... | collective-permute-start | bytes 196616 | tf_op jit(solution)/shard_map/ppermute | solution.py:19
  138.7 70.3 %collective-permute-start.1 = (bf16[256,128]{1,0:T(8,128)(2,1)S(1)}, bf16[256,128]{1,0:T(8,128)(2,1)S(1)}, u32[]{:S(2)}, u32[]{:S(2)}) collective-permute-start(bf16[256,128]{1,0:T(8,128)(2,1)S(1)} %get-tuple-element.29), channel_id=1, source_target_pairs={{24,0},{28,4},{0,8},{4,12},{8,16},{12,20},{16,24},{20,28},{25,1},{... | collective-permute-start | bytes 196616 | tf_op jit(solution)/shard_map/ppermute | solution.py:19
  204.9 6.7 %collective-permute-start.2 = (bf16[256,128]{1,0:T(8,128)(2,1)S(1)}, bf16[256,128]{1,0:T(8,128)(2,1)S(1)}, u32[]{:S(2)}, u32[]{:S(2)}) collective-permute-start(bf16[256,128]{1,0:T(8,128)(2,1)S(1)} %get-tuple-element.28), channel_id=1, source_target_pairs={{4,0},{8,4},{12,8},{16,12},{20,16},{24,20},{28,24},{0,28},{5,1},{9... | collective-permute-start | bytes 196616 | tf_op jit(solution)/shard_map/ppermute | solution.py:19
  209.0 89.6 %collective-permute-start.23 = (bf16[64,128,128]{2,1,0:T(8,128)(2,1)}, bf16[64,128,128]{2,1,0:T(8,128)(2,1)}, u32[]{:S(2)}, u32[]{:S(2)}) collective-permute-start(bf16[64,128,128]{2,1,0:T(8,128)(2,1)} %shard_map.59), channel_id=1, source_target_pairs={{0,2},{1,3},{2,0},{3,1},{4,6},{5,7},{6,4},{7,5},{8,10},{9,11},{10,... | collective-permute-start | bytes 6291464 | tf_op jit(solution)/shard_map/ppermute | solution.py:24
  233.9 7.6 %collective-permute-start.10 = (bf16[256,128]{1,0:T(8,128)(2,1)S(1)}, bf16[256,128]{1,0:T(8,128)(2,1)S(1)}, u32[]{:S(2)}, u32[]{:S(2)}) collective-permute-start(bf16[256,128]{1,0:T(8,128)(2,1)S(1)} %get-tuple-element.26), channel_id=1, source_target_pairs={{28,0},{0,4},{4,8},{8,12},{12,16},{16,20},{20,24},{24,28},{29,1},{... | collective-permute-start | bytes 196616 | tf_op jit(solution)/shard_map/ppermute | solution.py:19
  236.6 44.0 %collective-permute-start.15 = (bf16[16,128,128]{2,1,0:T(8,128)(2,1)S(1)}, bf16[16,128,128]{2,1,0:T(8,128)(2,1)S(1)}, u32[]{:S(2)}, u32[]{:S(2)}) collective-permute-start(bf16[16,128,128]{2,1,0:T(8,128)(2,1)S(1)} %get-tuple-element.38), channel_id=1, source_target_pairs={{0,1},{1,0},{2,3},{3,2},{4,5},{5,4},{6,7},{7,6},{8,9},{9,8},{10,11... | collective-permute-start | bytes 1572872 | tf_op jit(solution)/shard_map/ppermute | solution.py:24
  237.0 6.1 %collective-permute-start.11 = (bf16[256,128]{1,0:T(8,128)(2,1)S(1)}, bf16[256,128]{1,0:T(8,128)(2,1)S(1)}, u32[]{:S(2)}, u32[]{:S(2)}) collective-permute-start(bf16[256,128]{1,0:T(8,128)(2,1)S(1)} %get-tuple-element.25), channel_id=1, source_target_pairs={{24,0},{28,4},{0,8},{4,12},{8,16},{12,20},{16,24},{20,28},{25,1},{... | collective-permute-start | bytes 196616 | tf_op jit(solution)/shard_map/ppermute | solution.py:19
  241.5 6.3 %collective-permute-start.13 = (bf16[256,128]{1,0:T(8,128)(2,1)S(1)}, bf16[256,128]{1,0:T(8,128)(2,1)S(1)}, u32[]{:S(2)}, u32[]{:S(2)}) collective-permute-start(bf16[256,128]{1,0:T(8,128)(2,1)S(1)} %get-tuple-element.23), channel_id=1, source_target_pairs={{16,0},{20,4},{24,8},{28,12},{0,16},{4,20},{8,24},{12,28},{17,1},{... | collective-permute-start | bytes 196616 | tf_op jit(solution)/shard_map/ppermute | solution.py:19
  243.1 41.7 %collective-permute-start.16 = (bf16[16,128,128]{2,1,0:T(8,128)(2,1)}, bf16[16,128,128]{2,1,0:T(8,128)(2,1)S(1)}, u32[]{:S(2)}, u32[]{:S(2)}) collective-permute-start(bf16[16,128,128]{2,1,0:T(8,128)(2,1)} %get-tuple-element.37), channel_id=1, source_target_pairs={{0,1},{1,0},{2,3},{3,2},{4,5},{5,4},{6,7},{7,6},{8,9},{9,8},{10,11... | collective-permute-start | bytes 1572872 | tf_op jit(solution)/shard_map/ppermute | solution.py:24
  243.9 41.0 %collective-permute-start.17 = (bf16[16,128,128]{2,1,0:T(8,128)(2,1)}, bf16[16,128,128]{2,1,0:T(8,128)(2,1)S(1)}, u32[]{:S(2)}, u32[]{:S(2)}) collective-permute-start(bf16[16,128,128]{2,1,0:T(8,128)(2,1)} %get-tuple-element.36), channel_id=1, source_target_pairs={{0,1},{1,0},{2,3},{3,2},{4,5},{5,4},{6,7},{7,6},{8,9},{9,8},{10,11... | collective-permute-start | bytes 1572872 | tf_op jit(solution)/shard_map/ppermute | solution.py:24
  247.8 37.1 %collective-permute-start.18 = (bf16[16,128,128]{2,1,0:T(8,128)(2,1)}, bf16[16,128,128]{2,1,0:T(8,128)(2,1)S(1)}, u32[]{:S(2)}, u32[]{:S(2)}) collective-permute-start(bf16[16,128,128]{2,1,0:T(8,128)(2,1)} %get-tuple-element.35), channel_id=1, source_target_pairs={{0,1},{1,0},{2,3},{3,2},{4,5},{5,4},{6,7},{7,6},{8,9},{9,8},{10,11... | collective-permute-start | bytes 1572872 | tf_op jit(solution)/shard_map/ppermute | solution.py:24
  280.7 64.0 %collective-permute-start.34 = (bf16[32,128,128]{2,1,0:T(8,128)(2,1)}, bf16[32,128,128]{2,1,0:T(8,128)(2,1)S(1)}, u32[]{:S(2)}, u32[]{:S(2)}) collective-permute-start(bf16[32,128,128]{2,1,0:T(8,128)(2,1)} %shard_map.63), channel_id=1, source_target_pairs={{0,2},{1,3},{2,0},{3,1},{4,6},{5,7},{6,4},{7,5},{8,10},{9,11},{10,... | collective-permute-start | bytes 3145736 | tf_op jit(solution)/shard_map/ppermute | solution.py:24
  299.5 9.1 %collective-permute-start.19 = (bf16[256,128]{1,0:T(8,128)(2,1)S(1)}, bf16[256,128]{1,0:T(8,128)(2,1)S(1)}, u32[]{:S(2)}, u32[]{:S(2)}) collective-permute-start(bf16[256,128]{1,0:T(8,128)(2,1)S(1)} %get-tuple-element.22), channel_id=1, source_target_pairs={{28,0},{0,4},{4,8},{8,12},{12,16},{16,20},{20,24},{24,28},{29,1},{... | collective-permute-start | bytes 196616 | tf_op jit(solution)/shard_map/ppermute | solution.py:19
  299.6 9.1 %collective-permute-start.20 = (bf16[256,128]{1,0:T(8,128)(2,1)S(1)}, bf16[256,128]{1,0:T(8,128)(2,1)S(1)}, u32[]{:S(2)}, u32[]{:S(2)}) collective-permute-start(bf16[256,128]{1,0:T(8,128)(2,1)S(1)} %get-tuple-element.21), channel_id=1, source_target_pairs={{24,0},{28,4},{0,8},{4,12},{8,16},{12,20},{16,24},{20,28},{25,1},{... | collective-permute-start | bytes 196616 | tf_op jit(solution)/shard_map/ppermute | solution.py:19
  299.6 9.5 %collective-permute-start.21 = (bf16[256,128]{1,0:T(8,128)(2,1)S(1)}, bf16[256,128]{1,0:T(8,128)(2,1)S(1)}, u32[]{:S(2)}, u32[]{:S(2)}) collective-permute-start(bf16[256,128]{1,0:T(8,128)(2,1)S(1)} %get-tuple-element.20), channel_id=1, source_target_pairs={{4,0},{8,4},{12,8},{16,12},{20,16},{24,20},{28,24},{0,28},{5,1},{9... | collective-permute-start | bytes 196616 | tf_op jit(solution)/shard_map/ppermute | solution.py:19
  304.3 6.5 %collective-permute-start.22 = (bf16[256,128]{1,0:T(8,128)(2,1)S(1)}, bf16[256,128]{1,0:T(8,128)(2,1)S(1)}, u32[]{:S(2)}, u32[]{:S(2)}) collective-permute-start(bf16[256,128]{1,0:T(8,128)(2,1)S(1)} %get-tuple-element.19), channel_id=1, source_target_pairs={{16,0},{20,4},{24,8},{28,12},{0,16},{4,20},{8,24},{12,28},{17,1},{... | collective-permute-start | bytes 196616 | tf_op jit(solution)/shard_map/ppermute | solution.py:19
  308.7 21.6 %collective-permute-start.24 = (bf16[16,128,128]{2,1,0:T(8,128)(2,1)}, bf16[16,128,128]{2,1,0:T(8,128)(2,1)S(1)}, u32[]{:S(2)}, u32[]{:S(2)}) collective-permute-start(bf16[16,128,128]{2,1,0:T(8,128)(2,1)} %get-tuple-element.34), channel_id=1, source_target_pairs={{0,1},{1,0},{2,3},{3,2},{4,5},{5,4},{6,7},{7,6},{8,9},{9,8},{10,11... | collective-permute-start | bytes 1572872 | tf_op jit(solution)/shard_map/ppermute | solution.py:24
  308.7 22.2 %collective-permute-start.25 = (bf16[16,128,128]{2,1,0:T(8,128)(2,1)}, bf16[16,128,128]{2,1,0:T(8,128)(2,1)S(1)}, u32[]{:S(2)}, u32[]{:S(2)}) collective-permute-start(bf16[16,128,128]{2,1,0:T(8,128)(2,1)} %get-tuple-element.33), channel_id=1, source_target_pairs={{0,1},{1,0},{2,3},{3,2},{4,5},{5,4},{6,7},{7,6},{8,9},{9,8},{10,11... | collective-permute-start | bytes 1572872 | tf_op jit(solution)/shard_map/ppermute | solution.py:24
  309.2 21.7 %collective-permute-start.26 = (bf16[16,128,128]{2,1,0:T(8,128)(2,1)}, bf16[16,128,128]{2,1,0:T(8,128)(2,1)S(1)}, u32[]{:S(2)}, u32[]{:S(2)}) collective-permute-start(bf16[16,128,128]{2,1,0:T(8,128)(2,1)} %get-tuple-element.32), channel_id=1, source_target_pairs={{0,1},{1,0},{2,3},{3,2},{4,5},{5,4},{6,7},{7,6},{8,9},{9,8},{10,11... | collective-permute-start | bytes 1572872 | tf_op jit(solution)/shard_map/ppermute | solution.py:24
  310.8 20.2 %collective-permute-start.27 = (bf16[16,128,128]{2,1,0:T(8,128)(2,1)}, bf16[16,128,128]{2,1,0:T(8,128)(2,1)S(1)}, u32[]{:S(2)}, u32[]{:S(2)}) collective-permute-start(bf16[16,128,128]{2,1,0:T(8,128)(2,1)} %get-tuple-element.31), channel_id=1, source_target_pairs={{0,1},{1,0},{2,3},{3,2},{4,5},{5,4},{6,7},{7,6},{8,9},{9,8},{10,11... | collective-permute-start | bytes 1572872 | tf_op jit(solution)/shard_map/ppermute | solution.py:24
  330.3 55.6 %collective-permute-start.33 = (bf16[16,128,128]{2,1,0:T(8,128)(2,1)}, bf16[16,128,128]{2,1,0:T(8,128)(2,1)S(1)}, u32[]{:S(2)}, u32[]{:S(2)}) collective-permute-start(bf16[16,128,128]{2,1,0:T(8,128)(2,1)} %shard_map.62), channel_id=1, source_target_pairs={{0,2},{1,3},{2,0},{3,1},{4,6},{5,7},{6,4},{7,5},{8,10},{9,11},{10,... | collective-permute-start | bytes 1572872 | tf_op jit(solution)/shard_map/ppermute | solution.py:24
  344.8 31.2 %collective-permute-start.35 = (bf16[8,128,128]{2,1,0:T(8,128)(2,1)S(1)}, bf16[8,128,128]{2,1,0:T(8,128)(2,1)S(1)}, u32[]{:S(2)}, u32[]{:S(2)}) collective-permute-start(bf16[8,128,128]{2,1,0:T(8,128)(2,1)S(1)} %get-tuple-element.46), channel_id=1, source_target_pairs={{0,1},{1,0},{2,3},{3,2},{4,5},{5,4},{6,7},{7,6},{8,9},{9,8},{10,11... | collective-permute-start | bytes 786440 | tf_op jit(solution)/shard_map/ppermute | solution.py:24
  346.0 7.7 %collective-permute-start.28 = (bf16[256,128]{1,0:T(8,128)(2,1)S(1)}, bf16[256,128]{1,0:T(8,128)(2,1)S(1)}, u32[]{:S(2)}, u32[]{:S(2)}) collective-permute-start(bf16[256,128]{1,0:T(8,128)(2,1)S(1)} %get-tuple-element.18), channel_id=1, source_target_pairs={{28,0},{0,4},{4,8},{8,12},{12,16},{16,20},{20,24},{24,28},{29,1},{... | collective-permute-start | bytes 196616 | tf_op jit(solution)/shard_map/ppermute | solution.py:19
  346.6 7.2 %collective-permute-start.29 = (bf16[256,128]{1,0:T(8,128)(2,1)S(1)}, bf16[256,128]{1,0:T(8,128)(2,1)S(1)}, u32[]{:S(2)}, u32[]{:S(2)}) collective-permute-start(bf16[256,128]{1,0:T(8,128)(2,1)S(1)} %get-tuple-element.17), channel_id=1, source_target_pairs={{24,0},{28,4},{0,8},{4,12},{8,16},{12,20},{16,24},{20,28},{25,1},{... | collective-permute-start | bytes 196616 | tf_op jit(solution)/shard_map/ppermute | solution.py:19
  347.9 5.9 %collective-permute-start.30 = (bf16[256,128]{1,0:T(8,128)(2,1)S(1)}, bf16[256,128]{1,0:T(8,128)(2,1)S(1)}, u32[]{:S(2)}, u32[]{:S(2)}) collective-permute-start(bf16[256,128]{1,0:T(8,128)(2,1)S(1)} %get-tuple-element.16), channel_id=1, source_target_pairs={{4,0},{8,4},{12,8},{16,12},{20,16},{24,20},{28,24},{0,28},{5,1},{9... | collective-permute-start | bytes 196616 | tf_op jit(solution)/shard_map/ppermute | solution.py:19
  353.7 23.7 %collective-permute-start.36 = (bf16[8,128,128]{2,1,0:T(8,128)(2,1)S(1)}, bf16[8,128,128]{2,1,0:T(8,128)(2,1)S(1)}, u32[]{:S(2)}, u32[]{:S(2)}) collective-permute-start(bf16[8,128,128]{2,1,0:T(8,128)(2,1)S(1)} %get-tuple-element.45), channel_id=1, source_target_pairs={{0,1},{1,0},{2,3},{3,2},{4,5},{5,4},{6,7},{7,6},{8,9},{9,8},{10,11... | collective-permute-start | bytes 786440 | tf_op jit(solution)/shard_map/ppermute | solution.py:24
  353.8 23.7 %collective-permute-start.37 = (bf16[8,128,128]{2,1,0:T(8,128)(2,1)S(1)}, bf16[8,128,128]{2,1,0:T(8,128)(2,1)S(1)}, u32[]{:S(2)}, u32[]{:S(2)}) collective-permute-start(bf16[8,128,128]{2,1,0:T(8,128)(2,1)S(1)} %get-tuple-element.44), channel_id=1, source_target_pairs={{0,1},{1,0},{2,3},{3,2},{4,5},{5,4},{6,7},{7,6},{8,9},{9,8},{10,11... | collective-permute-start | bytes 786440 | tf_op jit(solution)/shard_map/ppermute | solution.py:24
  358.9 18.5 %collective-permute-start.38 = (bf16[8,128,128]{2,1,0:T(8,128)(2,1)S(1)}, bf16[8,128,128]{2,1,0:T(8,128)(2,1)S(1)}, u32[]{:S(2)}, u32[]{:S(2)}) collective-permute-start(bf16[8,128,128]{2,1,0:T(8,128)(2,1)S(1)} %get-tuple-element.43), channel_id=1, source_target_pairs={{0,1},{1,0},{2,3},{3,2},{4,5},{5,4},{6,7},{7,6},{8,9},{9,8},{10,11... | collective-permute-start | bytes 786440 | tf_op jit(solution)/shard_map/ppermute | solution.py:24
  375.9 19.3 %collective-permute-start.32 = (bf16[16,128,128]{2,1,0:T(8,128)(2,1)}, bf16[16,128,128]{2,1,0:T(8,128)(2,1)S(1)}, u32[]{:S(2)}, u32[]{:S(2)}) collective-permute-start(bf16[16,128,128]{2,1,0:T(8,128)(2,1)} %shard_map.61), channel_id=1, source_target_pairs={{0,2},{1,3},{2,0},{3,1},{4,6},{5,7},{6,4},{7,5},{8,10},{9,11},{10,... | collective-permute-start | bytes 1572872 | tf_op jit(solution)/shard_map/ppermute | solution.py:24
  (20 other events, 174.1 us)

commit v3 on v2

--- a/solution.py
+++ b/solution.py
@@ -24,28 +24,26 @@
     return lax.ppermute(block, "batch", route)
 
 
-def cut(tile_weights, layer, first, count, after):
-    part = (count, *tile_weights.shape[2:])
-    anywhere, in_hbm = (pl.BlockSpec(memory_space=space) for space in (pl.ANY, pltpu.HBM))
-
-    def kernel(tiles, *refs):
-        target, semaphore = refs[len(after) :]
-        copy = pltpu.make_async_copy(tiles.at[layer, pl.ds(first, count)], target, semaphore)
-        copy.start()
-        copy.wait()
+def cut(tile_weights, layer, first, count):
+    height, width = tile_weights.shape[2:]
+    group = math.gcd(8, count)
+    offset = first // group
+
+    def kernel(tiles, target):
+        target[...] = tiles[...]
 
     return pl.pallas_call(
         kernel,
-        out_shape=jax.ShapeDtypeStruct(part, tile_weights.dtype),
-        in_specs=[in_hbm] + [anywhere] * len(after),
-        out_specs=in_hbm,
-        scratch_shapes=[pltpu.SemaphoreType.DMA],
-        compiler_params=pltpu.CompilerParams(vmem_limit_bytes=56 * 2**20),
+        out_shape=jax.ShapeDtypeStruct((count, height, width), tile_weights.dtype),
+        grid=(count // group,),
+        in_specs=[pl.BlockSpec((None, group, height, width), lambda i: (layer, offset + i, 0, 0))],
+        out_specs=pl.BlockSpec((group, height, width), lambda i: (i, 0, 0)),
+        compiler_params=pltpu.CompilerParams(vmem_limit_bytes=52 * 2**20),
         cost_estimate=FREE,
-    )(tile_weights, *after)
-
-
-def layer_kernel(layer, first, group, blocks, neigh, width, pieces, aliased, *refs):
+    )(tile_weights)
+
+
+def layer_kernel(layer, first, group, steps, blocks, neigh, width, pieces, aliased, *refs):
     refs = list(refs)
     codes, own, current = (refs.pop(0) for _ in range(3))
     arrived = [refs.pop(0) for _ in range(neigh)]
@@ -68,36 +66,43 @@
         for copy in copies:
             copy.wait()
 
-    def work(held):
-        for g in range(group):
-            base = (layer * blocks + first + step * group + g) * fan
-            panel = []
-            for m in range(fan):
-                code = codes[base + (own[0] ^ m)]
-                panel.append(pool[:, pl.ds(pl.multiple_of(code * width, width), width)])
-            summed = jnp.dot(
-                jnp.concatenate(panel, axis=1),
-                jnp.concatenate([tile[g] for tile in held], axis=0),
-                preferred_element_type=jnp.float32,
-            )
-            columns = slice(g * width, (g + 1) * width)
-            summed = summed + bias[layer : layer + 1, columns]
-            result[:, columns] = jnp.maximum(summed, 0.0).astype(result.dtype)
-
-    most = max(pieces)
-    span = pl.num_programs(0) // most
-    for part in range(most):
-
-        @pl.when(step // span == part)
+    def tile(held, part, g):
+        share = steps * group // len(held)
+        if share >= group:
+            return held[part * len(held) // parts][g]
+        place = part * group + g
+        return held[place // share][place % share]
+
+    parts = min(max(pieces), steps)
+    for part in range(parts):
+
+        @pl.when(step // (steps // parts) == part)
         def _():
-            work([held[part * len(held) // most] for held in tiles])
+            for g in range(group):
+                base = (layer * blocks + first + step * group + g) * fan
+                panel = []
+                for m in range(fan):
+                    code = codes[base + (own[0] ^ m)]
+                    panel.append(pool[:, pl.ds(pl.multiple_of(code * width, width), width)])
+                summed = jnp.dot(
+                    jnp.concatenate(panel, axis=1),
+                    jnp.concatenate([tile(held, part, g) for held in tiles], axis=0),
+                    preferred_element_type=jnp.float32,
+                )
+                columns = slice(g * width, (g + 1) * width)
+                summed = summed + bias[layer : layer + 1, columns]
+                result[:, columns] = jnp.maximum(summed, 0.0).astype(result.dtype)
+
+
+def tile_spec(group, start, steps, width):
+    return pl.BlockSpec((group, width, width), lambda i, *_: (jnp.clip(i - start, 0, steps - 1), 0, 0))
 
 
 def run_blocks(layer, first, count, codes, own, current, arrived, tiles, biases, target):
     rows, neurons = current.shape
     neigh, width = len(arrived), tiles[0].shape[3]
     blocks = neurons // width
-    group = math.gcd(8, count // max(len(source) for source in tiles if isinstance(source, list)))
+    group = math.gcd(8, count)
     steps = count // group
     offset = first // group
     anywhere = pl.BlockSpec(memory_space=pl.ANY)
@@ -106,15 +111,10 @@
     for source in tiles:
         if isinstance(source, list):
             pieces.append(len(source))
-            share = steps // len(source)
+            share = count // len(source)
             for part, array in enumerate(source):
                 held.append(array)
-                in_specs.append(
-                    pl.BlockSpec(
-                        (group, width, width),
-                        lambda i, *_, start=part * share, share=share: (jnp.clip(i - start, 0, share - 1), 0, 0),
-                    )
-                )
+                in_specs.append(tile_spec(min(group, share), part * share // group, max(1, share // group), width))
         else:
             pieces.append(1)
             held.append(source)
@@ -126,7 +126,7 @@
         in_specs += [anywhere]
         aliases = {len(operands): 0}
         operands += [target]
-    kernel = functools.partial(layer_kernel, layer, first, group, blocks, neigh, width, pieces, target is not None)
+    kernel = functools.partial(layer_kernel, layer, first, group, steps, blocks, neigh, width, pieces, target is not None)
     return pl.pallas_call(
         kernel,
         out_shape=jax.ShapeDtypeStruct((rows, neurons), current.dtype),
@@ -171,13 +171,13 @@
 
     last = layer_count - 1
     chunks = [(layer, 0, 16, PIECES) for layer in range(last)]
-    chunks += [(last, 0, 8, PIECES), (last, 8, 4, PIECES), (last, 12, 4, 1)]
+    chunks += [(last, 0, 8, PIECES), (last, 8, 4, PIECES), (last, 12, 2, PIECES), (last, 14, 2, 1)]
     chunks = [(layer, first * unit, count * unit, math.gcd(pieces, count * unit)) for layer, first, count, pieces in chunks]
 
     mine, crossed = {}, {}
 
-    def send(index, *after):
-        mine[index] = cut(tile_weights, *chunks[index][:3], after)
+    def send(index):
+        mine[index] = cut(tile_weights, *chunks[index][:3])
         crossed[index] = swapped(mine[index], far * sharers)
 
     near = [tile_weights] + [None] * (fan - 1)

time: 405 us -> 225 us (0.56)
  Pallas kernels: 321 us -> 86 us
  waiting for transfers between devices: 21.6 us -> 67.2 us
  starting transfers between devices: 36 us -> 44.2 us
    pallas_call x6 -> x7, Pallas kernels: 261 us -> 22 us  [cut(): pl.pallas_call(kernel, out_shape=jax.ShapeDtypeStruct((count, height, wid...]
    ppermute x28 -> x33, waiting for transfers between devices: 4.8 us -> 59.7 us  [swapped(): return lax.ppermute(block, 'batch', route)]
    ppermute x16, waiting for transfers between devices: 16.8 us -> 7.53 us  [shifted(): return lax.ppermute(block, axis, route)]
    ppermute x16, starting transfers between devices: 23.9 us -> 29.5 us  [shifted(): return lax.ppermute(block, axis, route)]
    pallas_call x6 -> x7, Pallas kernels: 60.4 us -> 64 us  [run_blocks(): pl.pallas_call(kernel, out_shape=jax.ShapeDtypeStruct((rows, neurons), cu...]
    ppermute x28 -> x33, starting transfers between devices: 12.1 us -> 14.8 us  [swapped(): return lax.ppermute(block, 'batch', route)]
    slice x5 -> x6, local copies, waits for them, and re-layouts: 6.87 us -> 8.15 us  [tiles_of(): arrived[i * count // pieces:(i + 1) * count // pieces]]
  transfers between devices with their start and end apart: 44 -> 49, of which waited for: 13 -> 14; matrix products, arithmetic and copies ran while one was open for 3% -> 6% of each run, Pallas kernels for 78% -> 36%
where the time goes in v3:
time: 225 us; the launch traced here: 223 us
  Pallas kernels  86 us (38%)
  waiting for transfers between devices  67.2 us (30%)
  starting transfers between devices  44.2 us (20%)
  local copies, waits for them, and re-layouts  14.5 us (6%)
  between operations  10.6 us (5%)
    pallas_call x7, Pallas kernels, run_blocks(): pl.pallas_call(kernel, out_shape=jax.ShapeDtypeStruct((rows, neurons), cu...  64 us
    ppermute x33, waiting for transfers between devices, swapped(): return lax.ppermute(block, 'batch', route)  59.7 us
    ppermute x16, starting transfers between devices, shifted(): return lax.ppermute(block, axis, route)  29.5 us
    pallas_call x7, Pallas kernels, cut(): pl.pallas_call(kernel, out_shape=jax.ShapeDtypeStruct((count, height, wid...  22 us
    ppermute x33, starting transfers between devices, swapped(): return lax.ppermute(block, 'batch', route)  14.8 us
    slice x6, local copies, waits for them, and re-layouts, tiles_of(): arrived[i * count // pieces:(i + 1) * count // pieces]  8.15 us
    ppermute x16, waiting for transfers between devices, shifted(): return lax.ppermute(block, axis, route)  7.53 us
  transfers between devices with their start and end apart: 49, of which 14 were waited for; matrix products, arithmetic and copies ran while one was open for 6% of the time, Pallas kernels for 36%

profile of v3, /device:TPU:0, one launch (start us, length us, event | category | flops | bytes accessed | tf_op | source)
XLA Modules:
  0.0 222.5 jit_solution(10767127230693543340)
XLA Ops:
  0.5 5.6 %shard_map.55 = bf16[64,128,128]{2,1,0:T(8,128)(2,1)} custom-call(bf16[4,64,128,128]{3,2,1,0:T(8,128)(2,1)} %refs_7_.13), custom_call_target="tpu_custom_call" | custom-call | tf_op jit(solution)/shard_map/pallas_call | solution.py:35
  6.1 2.5 %collective-permute-start.5 = (bf16[64,128,128]{2,1,0:T(8,128)(2,1)}, bf16[64,128,128]{2,1,0:T(8,128)(2,1)S(1)}, u32[]{:S(2)}, u32[]{:S(2)}) collective-permute-start(bf16[64,128,128]{2,1,0:T(8,128)(2,1)} %shard_map.55), channel_id=1, source_target_pairs={{0,2},{1,3},{2,0},{3,1},{4,6},{5,7},{6,4},{7,5},{8,10},{9,11},{10,... | collective-permute-start | bytes 6291464 | tf_op jit(solution)/shard_map/ppermute | solution.py:24
  8.6 5.6 %shard_map.57 = bf16[64,128,128]{2,1,0:T(8,128)(2,1)} custom-call(bf16[4,64,128,128]{3,2,1,0:T(8,128)(2,1)} %refs_7_.13), custom_call_target="tpu_custom_call" | custom-call | tf_op jit(solution)/shard_map/pallas_call | solution.py:35
  18.4 2.1 collective-permute-start
  20.5 1.6 collective-permute-start.1
  22.1 5.6 %shard_map.59 = bf16[64,128,128]{2,1,0:T(8,128)(2,1)} custom-call(bf16[4,64,128,128]{3,2,1,0:T(8,128)(2,1)} %refs_7_.13), custom_call_target="tpu_custom_call" | custom-call | tf_op jit(solution)/shard_map/pallas_call | solution.py:35
  27.7 27.5 %collective-permute-done.5.refs_9_ = bf16[64,128,128]{2,1,0:T(8,128)(2,1)S(1)} collective-permute-done((bf16[64,128,128]{2,1,0:T(8,128)(2,1)}, bf16[64,128,128]{2,1,0:T(8,128)(2,1)S(1)}, u32[]{:S(2)}, u32[]{:S(2)}) %collective-permute-start.5) | collective-permute-done | bytes 2097184 | tf_op jit(solution)/shard_map/ppermute | solution.py:24
  55.3 5.0 %collective-permute-start.2 = (bf16[256,128]{1,0:T(8,128)(2,1)S(1)}, bf16[256,128]{1,0:T(8,128)(2,1)S(1)}, u32[]{:S(2)}, u32[]{:S(2)}) collective-permute-start(bf16[256,128]{1,0:T(8,128)(2,1)S(1)} %get-tuple-element.30), channel_id=1, source_target_pairs={{4,0},{8,4},{12,8},{16,12},{20,16},{24,20},{28,24},{0,28},{5,1},{9... | collective-permute-start | bytes 196616 | tf_op jit(solution)/shard_map/ppermute | solution.py:19
  60.3 1.6 collective-permute-start.23
  62.9 2.6 %collective-permute-done.3.refs_6_ = bf16[256,128]{1,0:T(8,128)(2,1)S(1)} collective-permute-done((bf16[256,128]{1,0:T(8,128)(2,1)S(1)}, bf16[256,128]{1,0:T(8,128)(2,1)S(1)}, u32[]{:S(2)}, u32[]{:S(2)}) %collective-permute-start.3) | collective-permute-done | bytes 65568 | tf_op jit(solution)/shard_map/ppermute | solution.py:19
  66.0 2.1 collective-permute-done.7.refs_11_
  71.7 12.8 %shard_map.56.refs_2_ = bf16[256,8192]{1,0:T(8,128)(2,1)} custom-call(s32[1024]{0:T(1024)S(1)} %reshape.38.refs_0_, s32[1]{0:T(128)} %bitcast.refs_1_, bf16[256,8192]{1,0:T(8,128)(2,1)} %refs_2_.1, bf16[256,128]{1,0:T(8,128)(2,1)S(1)} %collective-permute-done.refs_3_, bf16[256,128]{1,0:T(8,128)(2,1)S(1)} %collective-permute-done.1.refs_4_, ...), custom_call_target="tpu_custom_call" | custom-call | tf_op jit(solution)/shard_map/pallas_call | solution.py:130
  84.5 15.8 %collective-permute-done.14.refs_9_ = bf16[64,128,128]{2,1,0:T(8,128)(2,1)} collective-permute-done((bf16[64,128,128]{2,1,0:T(8,128)(2,1)}, bf16[64,128,128]{2,1,0:T(8,128)(2,1)}, u32[]{:S(2)}, u32[]{:S(2)}) %collective-permute-start.14) | collective-permute-done | bytes 2097184 | tf_op jit(solution)/shard_map/ppermute | solution.py:24
  101.3 2.0 collective-permute-start.10
  103.3 1.6 collective-permute-start.11
  104.9 3.2 %collective-permute-start.12 = (bf16[256,128]{1,0:T(8,128)(2,1)S(1)}, bf16[256,128]{1,0:T(8,128)(2,1)S(1)}, u32[]{:S(2)}, u32[]{:S(2)}) collective-permute-start(bf16[256,128]{1,0:T(8,128)(2,1)S(1)} %get-tuple-element.26), channel_id=1, source_target_pairs={{4,0},{8,4},{12,8},{16,12},{20,16},{24,20},{28,24},{0,28},{5,1},{9... | collective-permute-start | bytes 196616 | tf_op jit(solution)/shard_map/ppermute | solution.py:19
  108.9 2.9 %fusion.1 = (bf16[16,128,128]{2,1,0:T(8,128)(2,1)}, bf16[16,128,128]{2,1,0:T(8,128)(2,1)}, bf16[16,128,128]{2,1,0:T(8,128)(2,1)}, bf16[16,128,128]{2,1,0:T(8,128)(2,1)}) fusion(bf16[64,128,128]{2,1,0:T(8,128)(2,1)} %collective-permute-done.14.refs_9_), kind=kLoop, calls=%fused_computation.17 | loop fusion | bytes 4194304 | tf_op jit(solution)/shard_map/slice | solution.py:190
  115.7 2.1 shard_map.64
  120.2 12.9 %shard_map.58.refs_2_ = bf16[256,8192]{1,0:T(8,128)(2,1)} custom-call(s32[1024]{0:T(1024)S(1)} %reshape.38.refs_0_, s32[1]{0:T(128)} %bitcast.refs_1_, bf16[256,8192]{1,0:T(8,128)(2,1)} %shard_map.56.refs_2_, bf16[256,128]{1,0:T(8,128)(2,1)S(1)} %collective-permute-done.10.refs_3_, bf16[256,128]{1,0:T(8,128)(2,1)S(1)} %collective-permute-done.11.refs_4_, ...), custom_call_target="tpu_custom_call" | custom-call | tf_op jit(solution)/shard_map/pallas_call | solution.py:130
  133.1 12.2 %collective-permute-done.23.refs_9_ = bf16[64,128,128]{2,1,0:T(8,128)(2,1)} collective-permute-done((bf16[64,128,128]{2,1,0:T(8,128)(2,1)}, bf16[64,128,128]{2,1,0:T(8,128)(2,1)}, u32[]{:S(2)}, u32[]{:S(2)}) %collective-permute-start.23) | collective-permute-done | bytes 2097184 | tf_op jit(solution)/shard_map/ppermute | solution.py:24
  146.2 2.0 collective-permute-start.19
  148.2 1.6 collective-permute-start.20
  149.8 3.2 %collective-permute-start.21 = (bf16[256,128]{1,0:T(8,128)(2,1)S(1)}, bf16[256,128]{1,0:T(8,128)(2,1)S(1)}, u32[]{:S(2)}, u32[]{:S(2)}) collective-permute-start(bf16[256,128]{1,0:T(8,128)(2,1)S(1)} %get-tuple-element.22), channel_id=1, source_target_pairs={{4,0},{8,4},{12,8},{16,12},{20,16},{24,20},{28,24},{0,28},{5,1},{9... | collective-permute-start | bytes 196616 | tf_op jit(solution)/shard_map/ppermute | solution.py:19
  153.8 2.9 %fusion = (bf16[16,128,128]{2,1,0:T(8,128)(2,1)}, bf16[16,128,128]{2,1,0:T(8,128)(2,1)}, bf16[16,128,128]{2,1,0:T(8,128)(2,1)}, bf16[16,128,128]{2,1,0:T(8,128)(2,1)}) fusion(bf16[64,128,128]{2,1,0:T(8,128)(2,1)} %collective-permute-done.23.refs_9_), kind=kLoop, calls=%fused_computation.16 | loop fusion | bytes 4194304 | tf_op jit(solution)/shard_map/slice | solution.py:190
  163.5 12.9 %shard_map.60.refs_2_ = bf16[256,8192]{1,0:T(8,128)(2,1)} custom-call(s32[1024]{0:T(1024)S(1)} %reshape.38.refs_0_, s32[1]{0:T(128)} %bitcast.refs_1_, bf16[256,8192]{1,0:T(8,128)(2,1)} %shard_map.58.refs_2_, bf16[256,128]{1,0:T(8,128)(2,1)S(1)} %collective-permute-done.19.refs_3_, bf16[256,128]{1,0:T(8,128)(2,1)S(1)} %collective-permute-done.20.refs_4_, ...), custom_call_target="tpu_custom_call" | custom-call | tf_op jit(solution)/shard_map/pallas_call | solution.py:130
  178.4 3.7 %collective-permute-start.30 = (bf16[256,128]{1,0:T(8,128)(2,1)S(1)}, bf16[256,128]{1,0:T(8,128)(2,1)S(1)}, u32[]{:S(2)}, u32[]{:S(2)}) collective-permute-start(bf16[256,128]{1,0:T(8,128)(2,1)S(1)} %get-tuple-element.18), channel_id=1, source_target_pairs={{4,0},{8,4},{12,8},{16,12},{20,16},{24,20},{28,24},{0,28},{5,1},{9... | collective-permute-start | bytes 196616 | tf_op jit(solution)/shard_map/ppermute | solution.py:19
  185.7 2.3 %collective-permute-done.31.refs_6_ = bf16[256,128]{1,0:T(8,128)(2,1)S(1)} collective-permute-done((bf16[256,128]{1,0:T(8,128)(2,1)S(1)}, bf16[256,128]{1,0:T(8,128)(2,1)S(1)}, u32[]{:S(2)}, u32[]{:S(2)}) %collective-permute-start.31) | collective-permute-done | bytes 65568 | tf_op jit(solution)/shard_map/ppermute | solution.py:19
  189.6 8.5 %shard_map.65.refs_15_ = bf16[256,8192]{1,0:T(8,128)(2,1)} custom-call(s32[1024]{0:T(1024)S(1)} %reshape.38.refs_0_, s32[1]{0:T(128)} %bitcast.refs_1_, bf16[256,8192]{1,0:T(8,128)(2,1)} %shard_map.60.refs_2_, bf16[256,128]{1,0:T(8,128)(2,1)S(1)} %collective-permute-done.28.refs_3_, bf16[256,128]{1,0:T(8,128)(2,1)S(1)} %collective-permute-done.29.refs_4_, ...), custom_call_target="tpu_custom_call" | custom-call | tf_op jit(solution)/shard_map/pallas_call | solution.py:130
  200.1 1.6 collective-permute-start.32
  201.7 6.2 %shard_map.66.refs_15_ = bf16[256,8192]{1,0:T(8,128)(2,1)} custom-call(s32[1024]{0:T(1024)S(1)} %reshape.38.refs_0_, s32[1]{0:T(128)} %bitcast.refs_1_, bf16[256,8192]{1,0:T(8,128)(2,1)} %shard_map.60.refs_2_, bf16[256,128]{1,0:T(8,128)(2,1)S(1)} %collective-permute-done.28.refs_3_, ...), custom_call_target="tpu_custom_call", output_to_operand_aliasing={{}: (15, {})} | custom-call | tf_op jit(solution)/shard_map/pallas_call | solution.py:130
  210.0 5.4 %shard_map.67.refs_12_ = bf16[256,8192]{1,0:T(8,128)(2,1)} custom-call(s32[1024]{0:T(1024)S(1)} %reshape.38.refs_0_, s32[1]{0:T(128)} %bitcast.refs_1_, bf16[256,8192]{1,0:T(8,128)(2,1)} %shard_map.60.refs_2_, bf16[256,128]{1,0:T(8,128)(2,1)S(1)} %collective-permute-done.28.refs_3_, ...), custom_call_target="tpu_custom_call", output_to_operand_aliasing={{}: (15, {})} | custom-call | tf_op jit(solution)/shard_map/pallas_call | solution.py:130
  217.0 5.4 %shard_map.68 = bf16[256,8192]{1,0:T(8,128)(2,1)} custom-call(s32[1024]{0:T(1024)S(1)} %reshape.38.refs_0_, s32[1]{0:T(128)} %bitcast.refs_1_, bf16[256,8192]{1,0:T(8,128)(2,1)} %shard_map.60.refs_2_, bf16[256,128]{1,0:T(8,128)(2,1)S(1)} %collective-permute-done.28.refs_3_, ...), custom_call_target="tpu_custom_call", output_to_operand_aliasing={{}: (12, {})} | custom-call | tf_op jit(solution)/shard_map/pallas_call | solution.py:130
  (105 shorter events, 29.2 us)
Async XLA Ops:
  0.0 70.9 %collective-permute-start.4 = (bf16[4,64,128,128]{3,2,1,0:T(8,128)(2,1)}, bf16[4,64,128,128]{3,2,1,0:T(8,128)(2,1)}, u32[]{:S(2)}, u32[]{:S(2)}) collective-permute-start(bf16[4,64,128,128]{3,2,1,0:T(8,128)(2,1)} %refs_7_.13), channel_id=1, source_target_pairs={{0,1},{1,0},{2,3},{3,2},{4,5},{5,4},{6,7},{7,6},{8,9},{9,8},{10,11... | collective-permute-start | bytes 25165832 | tf_op jit(solution)/shard_map/ppermute | solution.py:24
  6.1 49.2 %collective-permute-start.5 = (bf16[64,128,128]{2,1,0:T(8,128)(2,1)}, bf16[64,128,128]{2,1,0:T(8,128)(2,1)S(1)}, u32[]{:S(2)}, u32[]{:S(2)}) collective-permute-start(bf16[64,128,128]{2,1,0:T(8,128)(2,1)} %shard_map.55), channel_id=1, source_target_pairs={{0,2},{1,3},{2,0},{3,1},{4,6},{5,7},{6,4},{7,5},{8,10},{9,11},{10,... | collective-permute-start | bytes 6291464 | tf_op jit(solution)/shard_map/ppermute | solution.py:24
  14.2 86.1 %collective-permute-start.14 = (bf16[64,128,128]{2,1,0:T(8,128)(2,1)}, bf16[64,128,128]{2,1,0:T(8,128)(2,1)}, u32[]{:S(2)}, u32[]{:S(2)}) collective-permute-start(bf16[64,128,128]{2,1,0:T(8,128)(2,1)} %shard_map.57), channel_id=1, source_target_pairs={{0,2},{1,3},{2,0},{3,1},{4,6},{5,7},{6,4},{7,5},{8,10},{9,11},{10,... | collective-permute-start | bytes 6291464 | tf_op jit(solution)/shard_map/ppermute | solution.py:24
  18.4 41.9 %collective-permute-start = (bf16[256,128]{1,0:T(8,128)(2,1)S(1)}, bf16[256,128]{1,0:T(8,128)(2,1)S(1)}, u32[]{:S(2)}, u32[]{:S(2)}) collective-permute-start(bf16[256,128]{1,0:T(8,128)(2,1)S(1)} %get-tuple-element.32), channel_id=1, source_target_pairs={{28,0},{0,4},{4,8},{8,12},{12,16},{16,20},{20,24},{24,28},{29,1},{... | collective-permute-start | bytes 196616 | tf_op jit(solution)/shard_map/ppermute | solution.py:19
  20.5 39.8 %collective-permute-start.1 = (bf16[256,128]{1,0:T(8,128)(2,1)S(1)}, bf16[256,128]{1,0:T(8,128)(2,1)S(1)}, u32[]{:S(2)}, u32[]{:S(2)}) collective-permute-start(bf16[256,128]{1,0:T(8,128)(2,1)S(1)} %get-tuple-element.31), channel_id=1, source_target_pairs={{24,0},{28,4},{0,8},{4,12},{8,16},{12,20},{16,24},{20,28},{25,1},{... | collective-permute-start | bytes 196616 | tf_op jit(solution)/shard_map/ppermute | solution.py:19
  55.3 7.6 %collective-permute-start.2 = (bf16[256,128]{1,0:T(8,128)(2,1)S(1)}, bf16[256,128]{1,0:T(8,128)(2,1)S(1)}, u32[]{:S(2)}, u32[]{:S(2)}) collective-permute-start(bf16[256,128]{1,0:T(8,128)(2,1)S(1)} %get-tuple-element.30), channel_id=1, source_target_pairs={{4,0},{8,4},{12,8},{16,12},{20,16},{24,20},{28,24},{0,28},{5,1},{9... | collective-permute-start | bytes 196616 | tf_op jit(solution)/shard_map/ppermute | solution.py:19
  60.3 5.2 %collective-permute-start.3 = (bf16[256,128]{1,0:T(8,128)(2,1)S(1)}, bf16[256,128]{1,0:T(8,128)(2,1)S(1)}, u32[]{:S(2)}, u32[]{:S(2)}) collective-permute-start(bf16[256,128]{1,0:T(8,128)(2,1)S(1)} %get-tuple-element.29), channel_id=1, source_target_pairs={{16,0},{20,4},{24,8},{28,12},{0,16},{4,20},{8,24},{12,28},{17,1},{... | collective-permute-start | bytes 196616 | tf_op jit(solution)/shard_map/ppermute | solution.py:19
  60.3 85.0 %collective-permute-start.23 = (bf16[64,128,128]{2,1,0:T(8,128)(2,1)}, bf16[64,128,128]{2,1,0:T(8,128)(2,1)}, u32[]{:S(2)}, u32[]{:S(2)}) collective-permute-start(bf16[64,128,128]{2,1,0:T(8,128)(2,1)} %shard_map.59), channel_id=1, source_target_pairs={{0,2},{1,3},{2,0},{3,1},{4,6},{5,7},{6,4},{7,5},{8,10},{9,11},{10,... | collective-permute-start | bytes 6291464 | tf_op jit(solution)/shard_map/ppermute | solution.py:24
  65.5 5.4 %collective-permute-start.8 = (bf16[16,128,128]{2,1,0:T(8,128)(2,1)}, bf16[16,128,128]{2,1,0:T(8,128)(2,1)S(1)}, u32[]{:S(2)}, u32[]{:S(2)}) collective-permute-start(bf16[16,128,128]{2,1,0:T(8,128)(2,1)} %get-tuple-element.42), channel_id=1, source_target_pairs={{0,1},{1,0},{2,3},{3,2},{4,5},{5,4},{6,7},{7,6},{8,9},{9,8},{10,11... | collective-permute-start | bytes 1572872 | tf_op jit(solution)/shard_map/ppermute | solution.py:24
  101.3 10.5 %collective-permute-start.10 = (bf16[256,128]{1,0:T(8,128)(2,1)S(1)}, bf16[256,128]{1,0:T(8,128)(2,1)S(1)}, u32[]{:S(2)}, u32[]{:S(2)}) collective-permute-start(bf16[256,128]{1,0:T(8,128)(2,1)S(1)} %get-tuple-element.28), channel_id=1, source_target_pairs={{28,0},{0,4},{4,8},{8,12},{12,16},{16,20},{20,24},{24,28},{29,1},{... | collective-permute-start | bytes 196616 | tf_op jit(solution)/shard_map/ppermute | solution.py:19
  103.3 8.5 %collective-permute-start.11 = (bf16[256,128]{1,0:T(8,128)(2,1)S(1)}, bf16[256,128]{1,0:T(8,128)(2,1)S(1)}, u32[]{:S(2)}, u32[]{:S(2)}) collective-permute-start(bf16[256,128]{1,0:T(8,128)(2,1)S(1)} %get-tuple-element.27), channel_id=1, source_target_pairs={{24,0},{28,4},{0,8},{4,12},{8,16},{12,20},{16,24},{20,28},{25,1},{... | collective-permute-start | bytes 196616 | tf_op jit(solution)/shard_map/ppermute | solution.py:19
  104.9 7.4 %collective-permute-start.12 = (bf16[256,128]{1,0:T(8,128)(2,1)S(1)}, bf16[256,128]{1,0:T(8,128)(2,1)S(1)}, u32[]{:S(2)}, u32[]{:S(2)}) collective-permute-start(bf16[256,128]{1,0:T(8,128)(2,1)S(1)} %get-tuple-element.26), channel_id=1, source_target_pairs={{4,0},{8,4},{12,8},{16,12},{20,16},{24,20},{28,24},{0,28},{5,1},{9... | collective-permute-start | bytes 196616 | tf_op jit(solution)/shard_map/ppermute | solution.py:19
  108.1 5.2 %collective-permute-start.13 = (bf16[256,128]{1,0:T(8,128)(2,1)S(1)}, bf16[256,128]{1,0:T(8,128)(2,1)S(1)}, u32[]{:S(2)}, u32[]{:S(2)}) collective-permute-start(bf16[256,128]{1,0:T(8,128)(2,1)S(1)} %get-tuple-element.25), channel_id=1, source_target_pairs={{16,0},{20,4},{24,8},{28,12},{0,16},{4,20},{8,24},{12,28},{17,1},{... | collective-permute-start | bytes 196616 | tf_op jit(solution)/shard_map/ppermute | solution.py:19
  111.8 6.1 %collective-permute-start.15 = (bf16[16,128,128]{2,1,0:T(8,128)(2,1)}, bf16[16,128,128]{2,1,0:T(8,128)(2,1)S(1)}, u32[]{:S(2)}, u32[]{:S(2)}) collective-permute-start(bf16[16,128,128]{2,1,0:T(8,128)(2,1)} %get-tuple-element.40), channel_id=1, source_target_pairs={{0,1},{1,0},{2,3},{3,2},{4,5},{5,4},{6,7},{7,6},{8,9},{9,8},{10,11... | collective-permute-start | bytes 1572872 | tf_op jit(solution)/shard_map/ppermute | solution.py:24
  111.8 7.6 %collective-permute-start.16 = (bf16[16,128,128]{2,1,0:T(8,128)(2,1)}, bf16[16,128,128]{2,1,0:T(8,128)(2,1)S(1)}, u32[]{:S(2)}, u32[]{:S(2)}) collective-permute-start(bf16[16,128,128]{2,1,0:T(8,128)(2,1)} %get-tuple-element.39), channel_id=1, source_target_pairs={{0,1},{1,0},{2,3},{3,2},{4,5},{5,4},{6,7},{7,6},{8,9},{9,8},{10,11... | collective-permute-start | bytes 1572872 | tf_op jit(solution)/shard_map/ppermute | solution.py:24
  112.3 7.1 %collective-permute-start.17 = (bf16[16,128,128]{2,1,0:T(8,128)(2,1)}, bf16[16,128,128]{2,1,0:T(8,128)(2,1)S(1)}, u32[]{:S(2)}, u32[]{:S(2)}) collective-permute-start(bf16[16,128,128]{2,1,0:T(8,128)(2,1)} %get-tuple-element.38), channel_id=1, source_target_pairs={{0,1},{1,0},{2,3},{3,2},{4,5},{5,4},{6,7},{7,6},{8,9},{9,8},{10,11... | collective-permute-start | bytes 1572872 | tf_op jit(solution)/shard_map/ppermute | solution.py:24
  113.2 6.2 %collective-permute-start.18 = (bf16[16,128,128]{2,1,0:T(8,128)(2,1)}, bf16[16,128,128]{2,1,0:T(8,128)(2,1)S(1)}, u32[]{:S(2)}, u32[]{:S(2)}) collective-permute-start(bf16[16,128,128]{2,1,0:T(8,128)(2,1)} %get-tuple-element.37), channel_id=1, source_target_pairs={{0,1},{1,0},{2,3},{3,2},{4,5},{5,4},{6,7},{7,6},{8,9},{9,8},{10,11... | collective-permute-start | bytes 1572872 | tf_op jit(solution)/shard_map/ppermute | solution.py:24
  117.8 59.5 %collective-permute-start.35 = (bf16[32,128,128]{2,1,0:T(8,128)(2,1)S(1)}, bf16[32,128,128]{2,1,0:T(8,128)(2,1)}, u32[]{:S(2)}, u32[]{:S(2)}) collective-permute-start(bf16[32,128,128]{2,1,0:T(8,128)(2,1)S(1)} %shard_map.64), channel_id=1, source_target_pairs={{0,2},{1,3},{2,0},{3,1},{4,6},{5,7},{6,4},{7,5},{8,10},{9,11},{10,... | collective-permute-start | bytes 3145736 | tf_op jit(solution)/shard_map/ppermute | solution.py:24
  146.2 10.5 %collective-permute-start.19 = (bf16[256,128]{1,0:T(8,128)(2,1)S(1)}, bf16[256,128]{1,0:T(8,128)(2,1)S(1)}, u32[]{:S(2)}, u32[]{:S(2)}) collective-permute-start(bf16[256,128]{1,0:T(8,128)(2,1)S(1)} %get-tuple-element.24), channel_id=1, source_target_pairs={{28,0},{0,4},{4,8},{8,12},{12,16},{16,20},{20,24},{24,28},{29,1},{... | collective-permute-start | bytes 196616 | tf_op jit(solution)/shard_map/ppermute | solution.py:19
  148.2 8.5 %collective-permute-start.20 = (bf16[256,128]{1,0:T(8,128)(2,1)S(1)}, bf16[256,128]{1,0:T(8,128)(2,1)S(1)}, u32[]{:S(2)}, u32[]{:S(2)}) collective-permute-start(bf16[256,128]{1,0:T(8,128)(2,1)S(1)} %get-tuple-element.23), channel_id=1, source_target_pairs={{24,0},{28,4},{0,8},{4,12},{8,16},{12,20},{16,24},{20,28},{25,1},{... | collective-permute-start | bytes 196616 | tf_op jit(solution)/shard_map/ppermute | solution.py:19
  149.8 7.4 %collective-permute-start.21 = (bf16[256,128]{1,0:T(8,128)(2,1)S(1)}, bf16[256,128]{1,0:T(8,128)(2,1)S(1)}, u32[]{:S(2)}, u32[]{:S(2)}) collective-permute-start(bf16[256,128]{1,0:T(8,128)(2,1)S(1)} %get-tuple-element.22), channel_id=1, source_target_pairs={{4,0},{8,4},{12,8},{16,12},{20,16},{24,20},{28,24},{0,28},{5,1},{9... | collective-permute-start | bytes 196616 | tf_op jit(solution)/shard_map/ppermute | solution.py:19
  153.0 5.2 %collective-permute-start.22 = (bf16[256,128]{1,0:T(8,128)(2,1)S(1)}, bf16[256,128]{1,0:T(8,128)(2,1)S(1)}, u32[]{:S(2)}, u32[]{:S(2)}) collective-permute-start(bf16[256,128]{1,0:T(8,128)(2,1)S(1)} %get-tuple-element.21), channel_id=1, source_target_pairs={{16,0},{20,4},{24,8},{28,12},{0,16},{4,20},{8,24},{12,28},{17,1},{... | collective-permute-start | bytes 196616 | tf_op jit(solution)/shard_map/ppermute | solution.py:19
  156.7 6.7 %collective-permute-start.25 = (bf16[16,128,128]{2,1,0:T(8,128)(2,1)}, bf16[16,128,128]{2,1,0:T(8,128)(2,1)S(1)}, u32[]{:S(2)}, u32[]{:S(2)}) collective-permute-start(bf16[16,128,128]{2,1,0:T(8,128)(2,1)} %get-tuple-element.35), channel_id=1, source_target_pairs={{0,1},{1,0},{2,3},{3,2},{4,5},{5,4},{6,7},{7,6},{8,9},{9,8},{10,11... | collective-permute-start | bytes 1572872 | tf_op jit(solution)/shard_map/ppermute | solution.py:24
  157.2 6.2 %collective-permute-start.26 = (bf16[16,128,128]{2,1,0:T(8,128)(2,1)}, bf16[16,128,128]{2,1,0:T(8,128)(2,1)S(1)}, u32[]{:S(2)}, u32[]{:S(2)}) collective-permute-start(bf16[16,128,128]{2,1,0:T(8,128)(2,1)} %get-tuple-element.34), channel_id=1, source_target_pairs={{0,1},{1,0},{2,3},{3,2},{4,5},{5,4},{6,7},{7,6},{8,9},{9,8},{10,11... | collective-permute-start | bytes 1572872 | tf_op jit(solution)/shard_map/ppermute | solution.py:24
  158.2 5.3 %collective-permute-start.27 = (bf16[16,128,128]{2,1,0:T(8,128)(2,1)}, bf16[16,128,128]{2,1,0:T(8,128)(2,1)}, u32[]{:S(2)}, u32[]{:S(2)}) collective-permute-start(bf16[16,128,128]{2,1,0:T(8,128)(2,1)} %get-tuple-element.33), channel_id=1, source_target_pairs={{0,1},{1,0},{2,3},{3,2},{4,5},{5,4},{6,7},{7,6},{8,9},{9,8},{10,11... | collective-permute-start | bytes 1572872 | tf_op jit(solution)/shard_map/ppermute | solution.py:24
  161.9 36.1 %collective-permute-start.34 = (bf16[16,128,128]{2,1,0:T(8,128)(2,1)S(1)}, bf16[16,128,128]{2,1,0:T(8,128)(2,1)S(1)}, u32[]{:S(2)}, u32[]{:S(2)}) collective-permute-start(bf16[16,128,128]{2,1,0:T(8,128)(2,1)S(1)} %shard_map.63), channel_id=1, source_target_pairs={{0,2},{1,3},{2,0},{3,1},{4,6},{5,7},{6,4},{7,5},{8,10},{9,11},{10,... | collective-permute-start | bytes 1572872 | tf_op jit(solution)/shard_map/ppermute | solution.py:24
  177.3 7.8 %collective-permute-start.28 = (bf16[256,128]{1,0:T(8,128)(2,1)S(1)}, bf16[256,128]{1,0:T(8,128)(2,1)S(1)}, u32[]{:S(2)}, u32[]{:S(2)}) collective-permute-start(bf16[256,128]{1,0:T(8,128)(2,1)S(1)} %get-tuple-element.20), channel_id=1, source_target_pairs={{28,0},{0,4},{4,8},{8,12},{12,16},{16,20},{20,24},{24,28},{29,1},{... | collective-permute-start | bytes 196616 | tf_op jit(solution)/shard_map/ppermute | solution.py:19
  177.6 7.5 %collective-permute-start.29 = (bf16[256,128]{1,0:T(8,128)(2,1)S(1)}, bf16[256,128]{1,0:T(8,128)(2,1)S(1)}, u32[]{:S(2)}, u32[]{:S(2)}) collective-permute-start(bf16[256,128]{1,0:T(8,128)(2,1)S(1)} %get-tuple-element.19), channel_id=1, source_target_pairs={{24,0},{28,4},{0,8},{4,12},{8,16},{12,20},{16,24},{20,28},{25,1},{... | collective-permute-start | bytes 196616 | tf_op jit(solution)/shard_map/ppermute | solution.py:19
  178.4 7.2 %collective-permute-start.30 = (bf16[256,128]{1,0:T(8,128)(2,1)S(1)}, bf16[256,128]{1,0:T(8,128)(2,1)S(1)}, u32[]{:S(2)}, u32[]{:S(2)}) collective-permute-start(bf16[256,128]{1,0:T(8,128)(2,1)S(1)} %get-tuple-element.18), channel_id=1, source_target_pairs={{4,0},{8,4},{12,8},{16,12},{20,16},{24,20},{28,24},{0,28},{5,1},{9... | collective-permute-start | bytes 196616 | tf_op jit(solution)/shard_map/ppermute | solution.py:19
  182.1 5.8 %collective-permute-start.31 = (bf16[256,128]{1,0:T(8,128)(2,1)S(1)}, bf16[256,128]{1,0:T(8,128)(2,1)S(1)}, u32[]{:S(2)}, u32[]{:S(2)}) collective-permute-start(bf16[256,128]{1,0:T(8,128)(2,1)S(1)} %get-tuple-element.17), channel_id=1, source_target_pairs={{16,0},{20,4},{24,8},{28,12},{0,16},{4,20},{8,24},{12,28},{17,1},{... | collective-permute-start | bytes 196616 | tf_op jit(solution)/shard_map/ppermute | solution.py:19
  188.9 19.0 %collective-permute-start.33 = (bf16[8,128,128]{2,1,0:T(8,128)(2,1)S(1)}, bf16[8,128,128]{2,1,0:T(8,128)(2,1)S(1)}, u32[]{:S(2)}, u32[]{:S(2)}) collective-permute-start(bf16[8,128,128]{2,1,0:T(8,128)(2,1)S(1)} %shard_map.62), channel_id=1, source_target_pairs={{0,2},{1,3},{2,0},{3,1},{4,6},{5,7},{6,4},{7,5},{8,10},{9,11},{10,... | collective-permute-start | bytes 786440 | tf_op jit(solution)/shard_map/ppermute | solution.py:24
  200.1 15.2 %collective-permute-start.32 = (bf16[8,128,128]{2,1,0:T(8,128)(2,1)S(1)}, bf16[8,128,128]{2,1,0:T(8,128)(2,1)S(1)}, u32[]{:S(2)}, u32[]{:S(2)}) collective-permute-start(bf16[8,128,128]{2,1,0:T(8,128)(2,1)S(1)} %shard_map.61), channel_id=1, source_target_pairs={{0,2},{1,3},{2,0},{3,1},{4,6},{5,7},{6,4},{7,5},{8,10},{9,11},{10,... | collective-permute-start | bytes 786440 | tf_op jit(solution)/shard_map/ppermute | solution.py:24
  (23 other events, 149.4 us)

commit v4 on v0

v4 whole, which is shorter than its diff:
```python
import math

import jax
import jax.numpy as jnp
from jax import lax
from jax.experimental import pallas as pl
from jax.experimental.pallas import tpu as pltpu
from jax.sharding import PartitionSpec as P


PIECES = 4
VMEM_LIMIT = 52 * 2**20
FREE = pl.CostEstimate(flops=0, bytes_accessed=0, transcendentals=0)


def shifted(block, axis, distance):
    devices = range(lax.axis_size(axis))
    route = [((i - distance) % len(devices), i) for i in devices]
    return lax.ppermute(block, axis, route)


def swapped(block, mask):
    route = [(i, i ^ mask) for i in range(lax.axis_size("batch"))]
    return lax.ppermute(block, "batch", route)


def cut(tile_weights, chunks):
    height, width = tile_weights.shape[2:]
    moves = []
    for place, (layer, first, count) in enumerate(chunks):
        step = math.gcd(8, count)
        moves += [(place, layer, first, start, step) for start in range(0, count, step)]

    def kernel(tiles, *refs):
        targets, (room, arrive, leave) = refs[: len(chunks)], refs[len(chunks) :]
        inward, outward = [], []
        for index, (place, layer, first, start, step) in enumerate(moves):
            here = room.at[index, pl.ds(0, step)]
            source = tiles.at[layer, pl.ds(first + start, step)]
            inward.append(pltpu.make_async_copy(source, here, arrive.at[index]))
            outward.append(pltpu.make_async_copy(here, targets[place].at[pl.ds(start, step)], leave.at[index]))
        for copy in inward:
            copy.start()
        for before, after in zip(inward, outward):
            before.wait()
            after.start()
        for copy in outward:
            copy.wait()

    anywhere = pl.BlockSpec(memory_space=pl.ANY)
    return pl.pallas_call(
        kernel,
        out_shape=[jax.ShapeDtypeStruct((count, height, width), tile_weights.dtype) for _, _, count in chunks],
        in_specs=[anywhere],
        out_specs=[anywhere] * len(chunks),
        scratch_shapes=[
            pltpu.VMEM((len(moves), 8, height, width), tile_weights.dtype),
            pltpu.SemaphoreType.DMA((len(moves),)),
            pltpu.SemaphoreType.DMA((len(moves),)),
        ],
        compiler_params=pltpu.CompilerParams(vmem_limit_bytes=VMEM_LIMIT),
        cost_estimate=FREE,
    )(tile_weights)


def run_blocks(layer, first, count, codes, own, pool, arrived, tiles, biases, target, keep, final):
    fan, width = len(tiles), biases.shape[1] // (codes.shape[0] // (biases.shape[0] * len(tiles)))
    blocks = biases.shape[1] // width
    neigh = len(arrived) if arrived else pool.shape[0] - blocks
    rows = pool.shape[-2]
    gather = not arrived
    columns = pool.ndim == 2
    group = math.gcd(8, count)
    pieces = [len(source) if isinstance(source, list) else 1 for source in tiles]
    step = min(group, count // max(pieces))
    held = [source if isinstance(source, list) else [source] for source in tiles]

    def kernel(*refs):
        refs = list(refs)
        codes, own, pool_ref = (refs.pop(0) for _ in range(3))
        arrived_refs = [refs.pop(0) for _ in arrived]
        tile_refs = [[refs.pop(0) for _ in source] for source in held]
        bias = refs.pop(0)
        if target is not None:
            refs.pop(0)
        result = refs.pop(0)
        kept = refs.pop(0) if keep else None
        inputs, weights, outputs, in_sems, weight_sems, out_sems, keep_sem = refs

        def code_of(block, m):
            return codes[(layer * blocks + first + block) * fan + (own[0] ^ m)]

        def gathered(block, m):
            place = block * fan + m
            return pltpu.make_async_copy(pool_ref.at[code_of(block, m)], inputs.at[place], in_sems.at[place])

        def tile_copy(part, m):
            source = tile_refs[m]
            start = part * step
            if held[m][0].ndim == 4:
                piece = source[0].at[layer, pl.ds(first + start, step)]
            else:
                share = count // len(source)
                piece = source[start // share].at[pl.ds(start % share, step)]
            return pltpu.make_async_copy(piece, weights.at[m, pl.ds(start, step)], weight_sems.at[part, m])

        def out_copy(part):
            start = part * group
            if final:
                here = outputs.at[:, pl.ds(start * width, group * width)]
                there = result.at[:, pl.ds((first + start) * width, group * width)]
            else:
                here = outputs.at[pl.ds(start, group)]
                there = result.at[pl.ds(first + start, group)]
            return pltpu.make_async_copy(here, there, out_sems.at[part])

        loads = []
        if not gather:
            if columns:
                for block in range(blocks):
                    source = pool_ref.at[:, pl.ds(block * width, width)]
                    loads.append(pltpu.make_async_copy(source, inputs.at[block], in_sems.at[block]))
            else:
                half = blocks // 2
                for part in range(2):
                    source = pool_ref.at[pl.ds(part * half, half)]
                    loads.append(pltpu.make_async_copy(source, inputs.at[pl.ds(part * half, half)], in_sems.at[part]))
            for slot, source in enumerate(arrived_refs):
                loads.append(pltpu.make_async_copy(source, inputs.at[blocks + slot], in_sems.at[blocks + slot]))
            for copy in loads:
                copy.start()
        for part in range(count // step):
            if gather:
                for g in range(step):
                    for m in range(fan):
                        gathered(part * step + g, m).start()
            for m in range(fan):
                tile_copy(part, m).start()
        for copy in loads:
            copy.wait()
        if keep:
            filled = pl.ds(blocks, neigh)
            hand_on = pltpu.make_async_copy(inputs.at[filled], kept.at[filled], keep_sem)
            hand_on.start()

        def compute(block):
            panel = []
            for m in range(fan):
                panel.append(inputs[block * fan + m if gather else code_of(block, m)])
            summed = jnp.dot(
                jnp.concatenate(panel, axis=1),
                jnp.concatenate([weights[m, block] for m in range(fan)], axis=0),
                preferred_element_type=jnp.float32,
            )
            place = pl.multiple_of((first + block) * width, width)
            summed = jnp.maximum(summed + bias[layer : layer + 1, pl.ds(place, width)], 0.0).astype(result.dtype)
            if final:
                outputs[:, pl.ds(pl.multiple_of(block * width, width), width)] = summed
            else:
                outputs[block] = summed

        def work(part, _):
            for sub in range(group // step):
                for m in range(fan):
                    here = weights.at[m, pl.ds((part * (group // step) + sub) * step, step)]
                    sem = weight_sems.at[part * (group // step) + sub, m]
                    pltpu.make_async_copy(here, here, sem).wait()
            for g in range(group):
                block = part * group + g
                if gather:
                    for m in range(fan):
                        place = block * fan + m
                        pltpu.make_async_copy(inputs.at[place], inputs.at[place], in_sems.at[place]).wait()
                compute(block)
            out_copy(part).start()
            return _

        lax.fori_loop(0, count // group, work, None)
        for part in range(count // group):
            out_copy(part).wait()
        if keep:
            hand_on.wait()

    anywhere = pl.BlockSpec(memory_space=pl.ANY)
    operands = [codes, own, pool, *arrived, *(array for source in held for array in source), biases]
    in_specs = [anywhere] * (len(operands) - 3) + [pl.BlockSpec(memory_space=pltpu.VMEM)]
    aliases = {}
    if target is not None:
        aliases[len(operands)] = 0
        operands.append(target)
        in_specs.append(anywhere)
    shape = (rows, blocks * width) if final else (blocks + neigh, rows, width)
    out_shape = [jax.ShapeDtypeStruct(shape, pool.dtype)]
    if keep:
        aliases[2] = 1
        out_shape.append(jax.ShapeDtypeStruct(pool.shape, pool.dtype))
    number = count * fan if gather else blocks + neigh
    out = (rows, count * width) if final else (count, rows, width)
    results = pl.pallas_call(
        kernel,
        out_shape=out_shape,
        grid_spec=pltpu.PrefetchScalarGridSpec(
            num_scalar_prefetch=2,
            in_specs=in_specs,
            out_specs=[anywhere] * len(out_shape),
            scratch_shapes=[
                pltpu.VMEM((number, rows, width), pool.dtype),
                pltpu.VMEM((fan, count, width, width), tiles[0].dtype),
                pltpu.VMEM(out, pool.dtype),
                pltpu.SemaphoreType.DMA((number,)),
                pltpu.SemaphoreType.DMA((count // step, fan)),
                pltpu.SemaphoreType.DMA((count // group,)),
                pltpu.SemaphoreType.DMA,
            ],
        ),
        input_output_aliases=aliases,
        compiler_params=pltpu.CompilerParams(vmem_limit_bytes=VMEM_LIMIT),
        cost_estimate=FREE,
    )(*operands)
    return results if keep else (results[0], pool)


def body(activations, tile_weights, biases, source_codes, send_list):
    layer_count, block_count, part_rows, width = tile_weights.shape
    fan = source_codes.shape[2]
    part_count = lax.axis_size("dom")
    neighbor_offsets = (1, 2, -1, part_count // 2)
    sharers = width // part_rows
    own = (lax.axis_index("batch") // sharers).reshape(1).astype(jnp.int32)
    codes = source_codes.reshape(-1)
    far = fan // 2
    unit = block_count // 16

    if sharers > 1:
        members = range(lax.axis_size("batch") // sharers)
        groups = [[m * sharers + s for s in range(sharers)] for m in members]
        tile_weights = lax.all_gather(tile_weights, "batch", axis=2, tiled=True, axis_index_groups=groups)

    def spread(held, first):
        for bit in range(far.bit_length() - 1):
            for m in range(1 << bit):
                held[first + m + (1 << bit)] = jax.tree.map(
                    lambda array: swapped(array, (1 << bit) * sharers), held[first + m]
                )

    last = layer_count - 1
    chunks = [(layer, 0, 16, PIECES) for layer in range(last)]
    chunks += [(last, 0, 8, PIECES), (last, 8, 4, PIECES), (last, 12, 2, 2), (last, 14, 2, 1)]
    chunks = [(layer, first * unit, count * unit, math.gcd(pieces, count * unit)) for layer, first, count, pieces in chunks]

    crossed = []
    for layer in range(layer_count):
        for mine in cut(tile_weights, [chunk[:3] for chunk in chunks if chunk[0] == layer]):
            crossed.append(swapped(mine, far * sharers))

    near = [tile_weights] + [None] * (fan - 1)
    spread(near, 0)

    def tiles_of(index, *after):
        held = list(near)
        count, pieces = chunks[index][2:]
        arrived = lax.optimization_barrier((crossed[index], *after))[0]
        held[far] = [arrived[i * count // pieces : (i + 1) * count // pieces] for i in range(pieces)]
        spread(held, far)
        held[far] = [arrived]
        return held

    current = activations
    for index, (layer, first, count, _) in enumerate(chunks):
        if first == 0:
            arrived = []
            for slot, offset in enumerate(neighbor_offsets):
                start = send_list[layer, 0, slot]
                if layer == 0:
                    block = lax.dynamic_slice(current, (0, start * width), (current.shape[0], width))
                else:
                    block = lax.dynamic_index_in_dim(current, start, 0, keepdims=False)
                if slot > 1:
                    block = lax.optimization_barrier((block, arrived[slot - 2]))[0]
                arrived.append(shifted(block, "dom", offset))
            pool, target, after = current, None, arrived
        else:
            arrived, after = [], [current]
        keep = first == 0 and count < block_count
        current, pool = run_blocks(
            layer, first, count, codes, own, pool, arrived, tiles_of(index, *after), biases, target, keep, layer == last
        )
        target = current
    return current


def solution(mesh):
    in_specs = (
        P("batch", "dom"),
        P(None, "dom", "batch", None),
        P(None, "dom"),
        P(None, "dom", None),
        P(None, "dom", None),
    )
    out_specs = P("batch", "dom")
    return jax.shard_map(body, mesh=mesh, in_specs=in_specs, out_specs=out_specs, check_vma=False)
```

time: 364 us -> 216 us (0.59)
  local copies, waits for them, and re-layouts: 200 us -> 15.6 us
  Pallas kernels: 0 us -> 66.6 us
  waiting for transfers between devices: 9.67 us -> 68.9 us
  other arithmetic: 57.9 us -> 0 us
  matrix products: 52.9 us -> 0 us
  between operations: 13.4 us -> 25.2 us
  starting transfers between devices: 27.1 us -> 38.9 us
    select_n x4 -> x0, local copies, waits for them, and re-layouts: 88.7 us -> none  [body(): jnp.take(block_pool, source_codes[layer_index].reshape(-1), axis=1)]
    pallas_call x0 -> x11, Pallas kernels: none -> 66.6 us  [the longest x7 57.4 us: run_blocks(): pl.pallas_call(kernel, out_shape=out_shape, grid_spec=pltpu.PrefetchScala...]
    gather x8 -> x0, local copies, waits for them, and re-layouts: 60.5 us -> none  [the longest x4 49.1 us: body(): jnp.take(block_pool, source_codes[layer_index].reshape(-1), axis=1)]
    select_n x12 -> x0, other arithmetic: 57.8 us -> none  [the longest x8 57.4 us: body(): jnp.take(block_pool, source_codes[layer_index].reshape(-1), axis=1)]
    dot_general x4 -> x0, matrix products: 52.9 us -> none  [body(): jnp.einsum('rjc,jco->rjo', input_panel, lax.all_gather(tile_weights[layer...]
    ppermute x0 -> x31, waiting for transfers between devices: none -> 46.1 us  [swapped(): return lax.ppermute(block, 'batch', route)]
    unnamed x23 -> x15, local copies, waits for them, and re-layouts: 21.6 us -> 2.84 us
    ppermute x0 -> x31, starting transfers between devices: none -> 16.9 us  [swapped(): return lax.ppermute(block, 'batch', route)]
  transfers between devices with their start and end apart: 20 -> 47, of which waited for: 6 -> 20; matrix products, arithmetic and copies ran while one was open for 78% -> 6% of each run, Pallas kernels for 0% -> 29%
where the time goes in v4:
time: 216 us; the launch traced here: 215 us
  waiting for transfers between devices  68.9 us (32%)
  Pallas kernels  66.6 us (31%)
  starting transfers between devices  38.9 us (18%)
  between operations  25.2 us (12%)
  local copies, waits for them, and re-layouts  15.6 us (7%)
    pallas_call x7, Pallas kernels, run_blocks(): pl.pallas_call(kernel, out_shape=out_shape, grid_spec=pltpu.PrefetchScala...  57.4 us
    ppermute x31, waiting for transfers between devices, swapped(): return lax.ppermute(block, 'batch', route)  46.1 us
    ppermute x16, waiting for transfers between devices, shifted(): return lax.ppermute(block, axis, route)  22.9 us
    ppermute x16, starting transfers between devices, shifted(): return lax.ppermute(block, axis, route)  22 us
    ppermute x31, starting transfers between devices, swapped(): return lax.ppermute(block, 'batch', route)  16.9 us
    pallas_call x4, Pallas kernels, cut(): pl.pallas_call(kernel, out_shape=[jax.ShapeDtypeStruct((count, height, wi...  9.27 us
    slice x6, local copies, waits for them, and re-layouts, tiles_of(): arrived[i * count // pieces:(i + 1) * count // pieces]  8.04 us
  transfers between devices with their start and end apart: 47, of which 20 were waited for; matrix products, arithmetic and copies ran while one was open for 6% of the time, Pallas kernels for 29%

profile of v4, /device:TPU:0, one launch (start us, length us, event | category | flops | bytes accessed | tf_op | source)
XLA Modules:
  0.0 215.2 jit_solution(6775792959988218783)
XLA Ops:
  0.5 2.4 %shard_map.55 = bf16[64,128,128]{2,1,0:T(8,128)(2,1)} custom-call(bf16[4,64,128,128]{3,2,1,0:T(8,128)(2,1)} %refs_3_.5), custom_call_target="tpu_custom_call" | custom-call | tf_op jit(solution)/shard_map/pallas_call | solution.py:51
  2.9 2.6 %collective-permute-start.5 = (bf16[64,128,128]{2,1,0:T(8,128)(2,1)}, bf16[64,128,128]{2,1,0:T(8,128)(2,1)S(1)}, u32[]{:S(2)}, u32[]{:S(2)}) collective-permute-start(bf16[64,128,128]{2,1,0:T(8,128)(2,1)} %shard_map.55), channel_id=1, source_target_pairs={{0,2},{1,3},{2,0},{3,1},{4,6},{5,7},{6,4},{7,5},{8,10},{9,11},{10,... | collective-permute-start | bytes 6291464 | tf_op jit(solution)/shard_map/ppermute | solution.py:24
  5.4 2.4 %shard_map.57 = bf16[64,128,128]{2,1,0:T(8,128)(2,1)} custom-call(bf16[4,64,128,128]{3,2,1,0:T(8,128)(2,1)} %refs_3_.5), custom_call_target="tpu_custom_call" | custom-call | tf_op jit(solution)/shard_map/pallas_call | solution.py:51
  12.0 2.1 collective-permute-start.1
  15.7 2.8 %collective-permute-done.1.refs_4_ = bf16[256,128]{1,0:T(8,128)(2,1)S(1)} collective-permute-done((bf16[256,128]{1,0:T(8,128)(2,1)S(1)}, bf16[256,128]{1,0:T(8,128)(2,1)S(1)}, u32[]{:S(2)}, u32[]{:S(2)}) %collective-permute-start.1) | collective-permute-done | bytes 65568 | tf_op jit(solution)/shard_map/ppermute | solution.py:19
  19.4 1.7 collective-permute-done.refs_3_
  22.2 2.2 %collective-permute-done.3.refs_6_ = bf16[256,128]{1,0:T(8,128)(2,1)S(1)} collective-permute-done((bf16[256,128]{1,0:T(8,128)(2,1)S(1)}, bf16[256,128]{1,0:T(8,128)(2,1)S(1)}, u32[]{:S(2)}, u32[]{:S(2)}) %collective-permute-start.3) | collective-permute-done | bytes 65568 | tf_op jit(solution)/shard_map/ppermute | solution.py:19
  25.4 26.7 %collective-permute-done.5.refs_9_ = bf16[64,128,128]{2,1,0:T(8,128)(2,1)S(1)} collective-permute-done((bf16[64,128,128]{2,1,0:T(8,128)(2,1)}, bf16[64,128,128]{2,1,0:T(8,128)(2,1)S(1)}, u32[]{:S(2)}, u32[]{:S(2)}) %collective-permute-start.5) | collective-permute-done | bytes 2097184 | tf_op jit(solution)/shard_map/ppermute | solution.py:24
  54.1 2.4 %shard_map.59 = bf16[64,128,128]{2,1,0:T(8,128)(2,1)} custom-call(bf16[4,64,128,128]{3,2,1,0:T(8,128)(2,1)} %refs_3_.5), custom_call_target="tpu_custom_call" | custom-call | tf_op jit(solution)/shard_map/pallas_call | solution.py:51
  56.5 2.0 collective-permute-start.23
  67.5 10.7 %shard_map.56.refs_2_ = bf16[68,256,128]{2,1,0:T(8,128)(2,1)} custom-call(s32[1024]{0:T(1024)S(1)} %reshape.14.refs_0_, s32[1]{0:T(128)} %bitcast.refs_1_, bf16[256,8192]{1,0:T(8,128)(2,1)} %refs_2_.1, bf16[256,128]{1,0:T(8,128)(2,1)S(1)} %collective-permute-done.refs_3_, bf16[256,128]{1,0:T(8,128)(2,1)S(1)} %collective-permute-done.1.refs_4_, ...), custom_call_target="tpu_custom_call" | custom-call | tf_op jit(solution)/shard_map/pallas_call | solution.py:199
  79.2 1.6 collective-permute-start.11
  82.3 3.0 %collective-permute-done.11.refs_4_ = bf16[256,128]{1,0:T(8,128)(2,1)S(1)} collective-permute-done((bf16[256,128]{1,0:T(8,128)(2,1)S(1)}, bf16[256,128]{1,0:T(8,128)(2,1)S(1)}, u32[]{:S(2)}, u32[]{:S(2)}) %collective-permute-start.11) | collective-permute-done | bytes 65568 | tf_op jit(solution)/shard_map/ppermute | solution.py:19
  86.1 1.7 collective-permute-done.10.refs_3_
  88.8 8.4 %collective-permute-done.14.refs_9_ = bf16[64,128,128]{2,1,0:T(8,128)(2,1)} collective-permute-done((bf16[64,128,128]{2,1,0:T(8,128)(2,1)}, bf16[64,128,128]{2,1,0:T(8,128)(2,1)}, u32[]{:S(2)}, u32[]{:S(2)}) %collective-permute-start.14) | collective-permute-done | bytes 2097184 | tf_op jit(solution)/shard_map/ppermute | solution.py:24
  97.2 2.7 %fusion.1 = (bf16[16,128,128]{2,1,0:T(8,128)(2,1)S(1)}, bf16[16,128,128]{2,1,0:T(8,128)(2,1)S(1)}, bf16[16,128,128]{2,1,0:T(8,128)(2,1)}, bf16[16,128,128]{2,1,0:T(8,128)(2,1)}) fusion(bf16[64,128,128]{2,1,0:T(8,128)(2,1)} %collective-permute-done.14.refs_9_), kind=kLoop, calls=%fused_computation.17 | loop fusion | bytes 4194304 | tf_op jit(solution)/shard_map/slice | solution.py:263
  109.2 10.5 %shard_map.58.refs_2_ = bf16[68,256,128]{2,1,0:T(8,128)(2,1)} custom-call(s32[1024]{0:T(1024)S(1)} %reshape.14.refs_0_, s32[1]{0:T(128)} %bitcast.refs_1_, bf16[68,256,128]{2,1,0:T(8,128)(2,1)} %shard_map.56.refs_2_, bf16[256,128]{1,0:T(8,128)(2,1)S(1)} %collective-permute-done.10.refs_3_, bf16[256,128]{1,0:T(8,128)(2,1)S(1)} %collective-permute-done.11.refs_4_, ...), custom_call_target="tpu_custom_call" | custom-call | tf_op jit(solution)/shard_map/pallas_call | solution.py:199
  120.6 2.1 collective-permute-start.20
  124.3 2.8 %collective-permute-done.20.refs_4_ = bf16[256,128]{1,0:T(8,128)(2,1)S(1)} collective-permute-done((bf16[256,128]{1,0:T(8,128)(2,1)S(1)}, bf16[256,128]{1,0:T(8,128)(2,1)S(1)}, u32[]{:S(2)}, u32[]{:S(2)}) %collective-permute-start.20) | collective-permute-done | bytes 65568 | tf_op jit(solution)/shard_map/ppermute | solution.py:19
  128.0 1.7 collective-permute-done.19.refs_3_
  130.7 2.1 shard_map.61
  132.8 1.6 collective-permute-start.32
  134.4 7.7 %collective-permute-done.23.refs_9_ = bf16[64,128,128]{2,1,0:T(8,128)(2,1)} collective-permute-done((bf16[64,128,128]{2,1,0:T(8,128)(2,1)}, bf16[64,128,128]{2,1,0:T(8,128)(2,1)}, u32[]{:S(2)}, u32[]{:S(2)}) %collective-permute-start.23) | collective-permute-done | bytes 2097184 | tf_op jit(solution)/shard_map/ppermute | solution.py:24
  142.1 2.9 %fusion = (bf16[16,128,128]{2,1,0:T(8,128)(2,1)}, bf16[16,128,128]{2,1,0:T(8,128)(2,1)}, bf16[16,128,128]{2,1,0:T(8,128)(2,1)}, bf16[16,128,128]{2,1,0:T(8,128)(2,1)}) fusion(bf16[64,128,128]{2,1,0:T(8,128)(2,1)} %collective-permute-done.23.refs_9_), kind=kLoop, calls=%fused_computation.16 | loop fusion | bytes 4194304 | tf_op jit(solution)/shard_map/slice | solution.py:263
  154.3 10.5 %shard_map.60.refs_2_ = bf16[68,256,128]{2,1,0:T(8,128)(2,1)} custom-call(s32[1024]{0:T(1024)S(1)} %reshape.14.refs_0_, s32[1]{0:T(128)} %bitcast.refs_1_, bf16[68,256,128]{2,1,0:T(8,128)(2,1)} %shard_map.58.refs_2_, bf16[256,128]{1,0:T(8,128)(2,1)S(1)} %collective-permute-done.19.refs_3_, bf16[256,128]{1,0:T(8,128)(2,1)S(1)} %collective-permute-done.20.refs_4_, ...), custom_call_target="tpu_custom_call" | custom-call | tf_op jit(solution)/shard_map/pallas_call | solution.py:199
  165.8 2.1 collective-permute-start.29
  169.4 2.8 %collective-permute-done.29.refs_4_ = bf16[256,128]{1,0:T(8,128)(2,1)S(1)} collective-permute-done((bf16[256,128]{1,0:T(8,128)(2,1)S(1)}, bf16[256,128]{1,0:T(8,128)(2,1)S(1)}, u32[]{:S(2)}, u32[]{:S(2)}) %collective-permute-start.29) | collective-permute-done | bytes 65568 | tf_op jit(solution)/shard_map/ppermute | solution.py:19
  173.1 1.7 collective-permute-done.28.refs_3_
  183.5 7.5 %shard_map.62 = (bf16[256,8192]{1,0:T(8,128)(2,1)}, bf16[68,256,128]{2,1,0:T(8,128)(2,1)}) custom-call(s32[1024]{0:T(1024)S(1)} %reshape.14.refs_0_, s32[1]{0:T(128)} %bitcast.refs_1_, bf16[68,256,128]{2,1,0:T(8,128)(2,1)} %shard_map.60.refs_2_, bf16[256,128]{1,0:T(8,128)(2,1)S(1)} %collective-permute-done.28.refs_3_, ...), custom_call_target="tpu_custom_call", output_to_operand_aliasing={{1}: (2, {})} | custom-call | tf_op jit(solution)/shard_map/pallas_call | solution.py:199
  193.5 7.6 %shard_map.63.refs_9_ = bf16[256,8192]{1,0:T(8,128)(2,1)} custom-call(s32[1024]{0:T(1024)S(1)} %reshape.14.refs_0_, s32[1]{0:T(128)} %bitcast.refs_1_, bf16[68,256,128]{2,1,0:T(8,128)(2,1)} %get-tuple-element.39.refs_2_, bf16[4,64,128,128]{3,2,1,0:T(8,128)(2,1)} %refs_3_.5, ...), custom_call_target="tpu_custom_call", output_to_operand_aliasing={{}: (11, {})} | custom-call | tf_op jit(solution)/shard_map/pallas_call | solution.py:199
  202.7 5.4 %shard_map.64.refs_8_ = bf16[256,8192]{1,0:T(8,128)(2,1)} custom-call(s32[1024]{0:T(1024)S(1)} %reshape.14.refs_0_, s32[1]{0:T(128)} %bitcast.refs_1_, bf16[68,256,128]{2,1,0:T(8,128)(2,1)} %get-tuple-element.39.refs_2_, bf16[4,64,128,128]{3,2,1,0:T(8,128)(2,1)} %refs_3_.5, ...), custom_call_target="tpu_custom_call", output_to_operand_aliasing={{}: (9, {})} | custom-call | tf_op jit(solution)/shard_map/pallas_call | solution.py:199
  209.8 5.3 %shard_map.65 = bf16[256,8192]{1,0:T(8,128)(2,1)} custom-call(s32[1024]{0:T(1024)S(1)} %reshape.14.refs_0_, s32[1]{0:T(128)} %bitcast.refs_1_, bf16[68,256,128]{2,1,0:T(8,128)(2,1)} %get-tuple-element.39.refs_2_, bf16[4,64,128,128]{3,2,1,0:T(8,128)(2,1)} %refs_3_.5, ...), custom_call_target="tpu_custom_call", output_to_operand_aliasing={{}: (8, {})} | custom-call | tf_op jit(solution)/shard_map/pallas_call | solution.py:199
  (100 shorter events, 40.7 us)
Async XLA Ops:
  0.0 66.7 %collective-permute-start.4 = (bf16[4,64,128,128]{3,2,1,0:T(8,128)(2,1)}, bf16[4,64,128,128]{3,2,1,0:T(8,128)(2,1)}, u32[]{:S(2)}, u32[]{:S(2)}) collective-permute-start(bf16[4,64,128,128]{3,2,1,0:T(8,128)(2,1)} %refs_3_.5), channel_id=1, source_target_pairs={{0,1},{1,0},{2,3},{3,2},{4,5},{5,4},{6,7},{7,6},{8,9},{9,8},{10,11... | collective-permute-start | bytes 25165832 | tf_op jit(solution)/shard_map/ppermute | solution.py:24
  2.9 49.2 %collective-permute-start.5 = (bf16[64,128,128]{2,1,0:T(8,128)(2,1)}, bf16[64,128,128]{2,1,0:T(8,128)(2,1)S(1)}, u32[]{:S(2)}, u32[]{:S(2)}) collective-permute-start(bf16[64,128,128]{2,1,0:T(8,128)(2,1)} %shard_map.55), channel_id=1, source_target_pairs={{0,2},{1,3},{2,0},{3,1},{4,6},{5,7},{6,4},{7,5},{8,10},{9,11},{10,... | collective-permute-start | bytes 6291464 | tf_op jit(solution)/shard_map/ppermute | solution.py:24
  7.8 89.3 %collective-permute-start.14 = (bf16[64,128,128]{2,1,0:T(8,128)(2,1)}, bf16[64,128,128]{2,1,0:T(8,128)(2,1)}, u32[]{:S(2)}, u32[]{:S(2)}) collective-permute-start(bf16[64,128,128]{2,1,0:T(8,128)(2,1)} %shard_map.57), channel_id=1, source_target_pairs={{0,2},{1,3},{2,0},{3,1},{4,6},{5,7},{6,4},{7,5},{8,10},{9,11},{10,... | collective-permute-start | bytes 6291464 | tf_op jit(solution)/shard_map/ppermute | solution.py:24
  12.0 6.4 %collective-permute-start.1 = (bf16[256,128]{1,0:T(8,128)(2,1)S(1)}, bf16[256,128]{1,0:T(8,128)(2,1)S(1)}, u32[]{:S(2)}, u32[]{:S(2)}) collective-permute-start(bf16[256,128]{1,0:T(8,128)(2,1)S(1)} %get-tuple-element.61), channel_id=1, source_target_pairs={{24,0},{28,4},{0,8},{4,12},{8,16},{12,20},{16,24},{20,28},{25,1},{... | collective-permute-start | bytes 196616 | tf_op jit(solution)/shard_map/ppermute | solution.py:19
  14.1 7.0 %collective-permute-start = (bf16[256,128]{1,0:T(8,128)(2,1)S(1)}, bf16[256,128]{1,0:T(8,128)(2,1)S(1)}, u32[]{:S(2)}, u32[]{:S(2)}) collective-permute-start(bf16[256,128]{1,0:T(8,128)(2,1)S(1)} %get-tuple-element.62), channel_id=1, source_target_pairs={{28,0},{0,4},{4,8},{8,12},{12,16},{16,20},{20,24},{24,28},{29,1},{... | collective-permute-start | bytes 196616 | tf_op jit(solution)/shard_map/ppermute | solution.py:19
  18.4 6.0 %collective-permute-start.3 = (bf16[256,128]{1,0:T(8,128)(2,1)S(1)}, bf16[256,128]{1,0:T(8,128)(2,1)S(1)}, u32[]{:S(2)}, u32[]{:S(2)}) collective-permute-start(bf16[256,128]{1,0:T(8,128)(2,1)S(1)} %get-tuple-element.27), channel_id=1, source_target_pairs={{16,0},{20,4},{24,8},{28,12},{0,16},{4,20},{8,24},{12,28},{17,1},{... | collective-permute-start | bytes 196616 | tf_op jit(solution)/shard_map/ppermute | solution.py:19
  56.5 85.6 %collective-permute-start.23 = (bf16[64,128,128]{2,1,0:T(8,128)(2,1)}, bf16[64,128,128]{2,1,0:T(8,128)(2,1)}, u32[]{:S(2)}, u32[]{:S(2)}) collective-permute-start(bf16[64,128,128]{2,1,0:T(8,128)(2,1)} %shard_map.59), channel_id=1, source_target_pairs={{0,2},{1,3},{2,0},{3,1},{4,6},{5,7},{6,4},{7,5},{8,10},{9,11},{10,... | collective-permute-start | bytes 6291464 | tf_op jit(solution)/shard_map/ppermute | solution.py:24
  58.6 8.1 %collective-permute-start.8 = (bf16[16,128,128]{2,1,0:T(8,128)(2,1)}, bf16[16,128,128]{2,1,0:T(8,128)(2,1)S(1)}, u32[]{:S(2)}, u32[]{:S(2)}) collective-permute-start(bf16[16,128,128]{2,1,0:T(8,128)(2,1)} %get-tuple-element.72), channel_id=1, source_target_pairs={{0,1},{1,0},{2,3},{3,2},{4,5},{5,4},{6,7},{7,6},{8,9},{9,8},{10,11... | collective-permute-start | bytes 1572872 | tf_op jit(solution)/shard_map/ppermute | solution.py:24
  58.6 8.1 %collective-permute-start.9 = (bf16[16,128,128]{2,1,0:T(8,128)(2,1)S(1)}, bf16[16,128,128]{2,1,0:T(8,128)(2,1)S(1)}, u32[]{:S(2)}, u32[]{:S(2)}) collective-permute-start(bf16[16,128,128]{2,1,0:T(8,128)(2,1)S(1)} %get-tuple-element.71), channel_id=1, source_target_pairs={{0,1},{1,0},{2,3},{3,2},{4,5},{5,4},{6,7},{7,6},{8,9},{9,8},{10,11... | collective-permute-start | bytes 1572872 | tf_op jit(solution)/shard_map/ppermute | solution.py:24
  79.2 6.1 %collective-permute-start.11 = (bf16[256,128]{1,0:T(8,128)(2,1)S(1)}, bf16[256,128]{1,0:T(8,128)(2,1)S(1)}, u32[]{:S(2)}, u32[]{:S(2)}) collective-permute-start(bf16[256,128]{1,0:T(8,128)(2,1)S(1)} %get-tuple-element.57), channel_id=1, source_target_pairs={{24,0},{28,4},{0,8},{4,12},{8,16},{12,20},{16,24},{20,28},{25,1},{... | collective-permute-start | bytes 196616 | tf_op jit(solution)/shard_map/ppermute | solution.py:19
  80.8 7.0 %collective-permute-start.10 = (bf16[256,128]{1,0:T(8,128)(2,1)S(1)}, bf16[256,128]{1,0:T(8,128)(2,1)S(1)}, u32[]{:S(2)}, u32[]{:S(2)}) collective-permute-start(bf16[256,128]{1,0:T(8,128)(2,1)S(1)} %get-tuple-element.58), channel_id=1, source_target_pairs={{28,0},{0,4},{4,8},{8,12},{12,16},{16,20},{20,24},{24,28},{29,1},{... | collective-permute-start | bytes 196616 | tf_op jit(solution)/shard_map/ppermute | solution.py:19
  85.3 11.9 %collective-permute-start.13 = (bf16[256,128]{1,0:T(8,128)(2,1)S(1)}, bf16[256,128]{1,0:T(8,128)(2,1)S(1)}, u32[]{:S(2)}, u32[]{:S(2)}) collective-permute-start(bf16[256,128]{1,0:T(8,128)(2,1)S(1)} %get-tuple-element.30), channel_id=1, source_target_pairs={{16,0},{20,4},{24,8},{28,12},{0,16},{4,20},{8,24},{12,28},{17,1},{... | collective-permute-start | bytes 196616 | tf_op jit(solution)/shard_map/ppermute | solution.py:19
  87.8 9.4 %collective-permute-start.12 = (bf16[256,128]{1,0:T(8,128)(2,1)S(1)}, bf16[256,128]{1,0:T(8,128)(2,1)S(1)}, u32[]{:S(2)}, u32[]{:S(2)}) collective-permute-start(bf16[256,128]{1,0:T(8,128)(2,1)S(1)} %get-tuple-element.29), channel_id=1, source_target_pairs={{4,0},{8,4},{12,8},{16,12},{20,16},{24,20},{28,24},{0,28},{5,1},{9... | collective-permute-start | bytes 196616 | tf_op jit(solution)/shard_map/ppermute | solution.py:19
  99.8 8.5 %collective-permute-start.15 = (bf16[16,128,128]{2,1,0:T(8,128)(2,1)}, bf16[16,128,128]{2,1,0:T(8,128)(2,1)S(1)}, u32[]{:S(2)}, u32[]{:S(2)}) collective-permute-start(bf16[16,128,128]{2,1,0:T(8,128)(2,1)} %get-tuple-element.70), channel_id=1, source_target_pairs={{0,1},{1,0},{2,3},{3,2},{4,5},{5,4},{6,7},{7,6},{8,9},{9,8},{10,11... | collective-permute-start | bytes 1572872 | tf_op jit(solution)/shard_map/ppermute | solution.py:24
  99.8 8.5 %collective-permute-start.16 = (bf16[16,128,128]{2,1,0:T(8,128)(2,1)}, bf16[16,128,128]{2,1,0:T(8,128)(2,1)S(1)}, u32[]{:S(2)}, u32[]{:S(2)}) collective-permute-start(bf16[16,128,128]{2,1,0:T(8,128)(2,1)} %get-tuple-element.69), channel_id=1, source_target_pairs={{0,1},{1,0},{2,3},{3,2},{4,5},{5,4},{6,7},{7,6},{8,9},{9,8},{10,11... | collective-permute-start | bytes 1572872 | tf_op jit(solution)/shard_map/ppermute | solution.py:24
  100.4 8.0 %collective-permute-start.17 = (bf16[16,128,128]{2,1,0:T(8,128)(2,1)S(1)}, bf16[16,128,128]{2,1,0:T(8,128)(2,1)S(1)}, u32[]{:S(2)}, u32[]{:S(2)}) collective-permute-start(bf16[16,128,128]{2,1,0:T(8,128)(2,1)S(1)} %get-tuple-element.68), channel_id=1, source_target_pairs={{0,1},{1,0},{2,3},{3,2},{4,5},{5,4},{6,7},{7,6},{8,9},{9,8},{10,11... | collective-permute-start | bytes 1572872 | tf_op jit(solution)/shard_map/ppermute | solution.py:24
  100.4 8.0 %collective-permute-start.18 = (bf16[16,128,128]{2,1,0:T(8,128)(2,1)S(1)}, bf16[16,128,128]{2,1,0:T(8,128)(2,1)S(1)}, u32[]{:S(2)}, u32[]{:S(2)}) collective-permute-start(bf16[16,128,128]{2,1,0:T(8,128)(2,1)S(1)} %get-tuple-element.67), channel_id=1, source_target_pairs={{0,1},{1,0},{2,3},{3,2},{4,5},{5,4},{6,7},{7,6},{8,9},{9,8},{10,11... | collective-permute-start | bytes 1572872 | tf_op jit(solution)/shard_map/ppermute | solution.py:24
  120.6 6.4 %collective-permute-start.20 = (bf16[256,128]{1,0:T(8,128)(2,1)S(1)}, bf16[256,128]{1,0:T(8,128)(2,1)S(1)}, u32[]{:S(2)}, u32[]{:S(2)}) collective-permute-start(bf16[256,128]{1,0:T(8,128)(2,1)S(1)} %get-tuple-element.53), channel_id=1, source_target_pairs={{24,0},{28,4},{0,8},{4,12},{8,16},{12,20},{16,24},{20,28},{25,1},{... | collective-permute-start | bytes 196616 | tf_op jit(solution)/shard_map/ppermute | solution.py:19
  122.7 7.0 %collective-permute-start.19 = (bf16[256,128]{1,0:T(8,128)(2,1)S(1)}, bf16[256,128]{1,0:T(8,128)(2,1)S(1)}, u32[]{:S(2)}, u32[]{:S(2)}) collective-permute-start(bf16[256,128]{1,0:T(8,128)(2,1)S(1)} %get-tuple-element.54), channel_id=1, source_target_pairs={{28,0},{0,4},{4,8},{8,12},{12,16},{16,20},{20,24},{24,28},{29,1},{... | collective-permute-start | bytes 196616 | tf_op jit(solution)/shard_map/ppermute | solution.py:19
  127.0 15.1 %collective-permute-start.22 = (bf16[256,128]{1,0:T(8,128)(2,1)S(1)}, bf16[256,128]{1,0:T(8,128)(2,1)S(1)}, u32[]{:S(2)}, u32[]{:S(2)}) collective-permute-start(bf16[256,128]{1,0:T(8,128)(2,1)S(1)} %get-tuple-element.33), channel_id=1, source_target_pairs={{16,0},{20,4},{24,8},{28,12},{0,16},{4,20},{8,24},{12,28},{17,1},{... | collective-permute-start | bytes 196616 | tf_op jit(solution)/shard_map/ppermute | solution.py:19
  129.7 12.4 %collective-permute-start.21 = (bf16[256,128]{1,0:T(8,128)(2,1)S(1)}, bf16[256,128]{1,0:T(8,128)(2,1)S(1)}, u32[]{:S(2)}, u32[]{:S(2)}) collective-permute-start(bf16[256,128]{1,0:T(8,128)(2,1)S(1)} %get-tuple-element.32), channel_id=1, source_target_pairs={{4,0},{8,4},{12,8},{16,12},{20,16},{24,20},{28,24},{0,28},{5,1},{9... | collective-permute-start | bytes 196616 | tf_op jit(solution)/shard_map/ppermute | solution.py:19
  132.8 44.6 %collective-permute-start.32 = (bf16[32,128,128]{2,1,0:T(8,128)(2,1)}, bf16[32,128,128]{2,1,0:T(8,128)(2,1)}, u32[]{:S(2)}, u32[]{:S(2)}) collective-permute-start(bf16[32,128,128]{2,1,0:T(8,128)(2,1)} %get-tuple-element.37), channel_id=1, source_target_pairs={{0,2},{1,3},{2,0},{3,1},{4,6},{5,7},{6,4},{7,5},{8,10},{9,11},{10,... | collective-permute-start | bytes 3145736 | tf_op jit(solution)/shard_map/ppermute | solution.py:24
  145.0 8.5 %collective-permute-start.24 = (bf16[16,128,128]{2,1,0:T(8,128)(2,1)}, bf16[16,128,128]{2,1,0:T(8,128)(2,1)S(1)}, u32[]{:S(2)}, u32[]{:S(2)}) collective-permute-start(bf16[16,128,128]{2,1,0:T(8,128)(2,1)} %get-tuple-element.66), channel_id=1, source_target_pairs={{0,1},{1,0},{2,3},{3,2},{4,5},{5,4},{6,7},{7,6},{8,9},{9,8},{10,11... | collective-permute-start | bytes 1572872 | tf_op jit(solution)/shard_map/ppermute | solution.py:24
  145.0 8.5 %collective-permute-start.25 = (bf16[16,128,128]{2,1,0:T(8,128)(2,1)}, bf16[16,128,128]{2,1,0:T(8,128)(2,1)S(1)}, u32[]{:S(2)}, u32[]{:S(2)}) collective-permute-start(bf16[16,128,128]{2,1,0:T(8,128)(2,1)} %get-tuple-element.65), channel_id=1, source_target_pairs={{0,1},{1,0},{2,3},{3,2},{4,5},{5,4},{6,7},{7,6},{8,9},{9,8},{10,11... | collective-permute-start | bytes 1572872 | tf_op jit(solution)/shard_map/ppermute | solution.py:24
  145.5 8.0 %collective-permute-start.26 = (bf16[16,128,128]{2,1,0:T(8,128)(2,1)}, bf16[16,128,128]{2,1,0:T(8,128)(2,1)S(1)}, u32[]{:S(2)}, u32[]{:S(2)}) collective-permute-start(bf16[16,128,128]{2,1,0:T(8,128)(2,1)} %get-tuple-element.64), channel_id=1, source_target_pairs={{0,1},{1,0},{2,3},{3,2},{4,5},{5,4},{6,7},{7,6},{8,9},{9,8},{10,11... | collective-permute-start | bytes 1572872 | tf_op jit(solution)/shard_map/ppermute | solution.py:24
  145.5 8.0 %collective-permute-start.27 = (bf16[16,128,128]{2,1,0:T(8,128)(2,1)}, bf16[16,128,128]{2,1,0:T(8,128)(2,1)S(1)}, u32[]{:S(2)}, u32[]{:S(2)}) collective-permute-start(bf16[16,128,128]{2,1,0:T(8,128)(2,1)} %get-tuple-element.63), channel_id=1, source_target_pairs={{0,1},{1,0},{2,3},{3,2},{4,5},{5,4},{6,7},{7,6},{8,9},{9,8},{10,11... | collective-permute-start | bytes 1572872 | tf_op jit(solution)/shard_map/ppermute | solution.py:24
  165.8 6.4 %collective-permute-start.29 = (bf16[256,128]{1,0:T(8,128)(2,1)S(1)}, bf16[256,128]{1,0:T(8,128)(2,1)S(1)}, u32[]{:S(2)}, u32[]{:S(2)}) collective-permute-start(bf16[256,128]{1,0:T(8,128)(2,1)S(1)} %get-tuple-element.49), channel_id=1, source_target_pairs={{24,0},{28,4},{0,8},{4,12},{8,16},{12,20},{16,24},{20,28},{25,1},{... | collective-permute-start | bytes 196616 | tf_op jit(solution)/shard_map/ppermute | solution.py:19
  167.8 7.0 %collective-permute-start.28 = (bf16[256,128]{1,0:T(8,128)(2,1)S(1)}, bf16[256,128]{1,0:T(8,128)(2,1)S(1)}, u32[]{:S(2)}, u32[]{:S(2)}) collective-permute-start(bf16[256,128]{1,0:T(8,128)(2,1)S(1)} %get-tuple-element.50), channel_id=1, source_target_pairs={{28,0},{0,4},{4,8},{8,12},{12,16},{16,20},{20,24},{24,28},{29,1},{... | collective-permute-start | bytes 196616 | tf_op jit(solution)/shard_map/ppermute | solution.py:19
  172.1 6.1 %collective-permute-start.31 = (bf16[256,128]{1,0:T(8,128)(2,1)S(1)}, bf16[256,128]{1,0:T(8,128)(2,1)S(1)}, u32[]{:S(2)}, u32[]{:S(2)}) collective-permute-start(bf16[256,128]{1,0:T(8,128)(2,1)S(1)} %get-tuple-element.36), channel_id=1, source_target_pairs={{16,0},{20,4},{24,8},{28,12},{0,16},{4,20},{8,24},{12,28},{17,1},{... | collective-permute-start | bytes 196616 | tf_op jit(solution)/shard_map/ppermute | solution.py:19
  175.9 15.1 %collective-permute-start.39 = (bf16[16,128,128]{2,1,0:T(8,128)(2,1)S(1)}, bf16[16,128,128]{2,1,0:T(8,128)(2,1)S(1)}, u32[]{:S(2)}, u32[]{:S(2)}) collective-permute-start(bf16[16,128,128]{2,1,0:T(8,128)(2,1)S(1)} %get-tuple-element.42), channel_id=1, source_target_pairs={{0,2},{1,3},{2,0},{3,1},{4,6},{5,7},{6,4},{7,5},{8,10},{9,11},{10,... | collective-permute-start | bytes 1572872 | tf_op jit(solution)/shard_map/ppermute | solution.py:24
  182.0 19.1 %collective-permute-start.38 = (bf16[8,128,128]{2,1,0:T(8,128)(2,1)S(1)}, bf16[8,128,128]{2,1,0:T(8,128)(2,1)S(1)}, u32[]{:S(2)}, u32[]{:S(2)}) collective-permute-start(bf16[8,128,128]{2,1,0:T(8,128)(2,1)S(1)} %get-tuple-element.41), channel_id=1, source_target_pairs={{0,2},{1,3},{2,0},{3,1},{4,6},{5,7},{6,4},{7,5},{8,10},{9,11},{10,... | collective-permute-start | bytes 786440 | tf_op jit(solution)/shard_map/ppermute | solution.py:24
  192.4 15.7 %collective-permute-start.37 = (bf16[8,128,128]{2,1,0:T(8,128)(2,1)S(1)}, bf16[8,128,128]{2,1,0:T(8,128)(2,1)S(1)}, u32[]{:S(2)}, u32[]{:S(2)}) collective-permute-start(bf16[8,128,128]{2,1,0:T(8,128)(2,1)S(1)} %get-tuple-element.40), channel_id=1, source_target_pairs={{0,2},{1,3},{2,0},{3,1},{4,6},{5,7},{6,4},{7,5},{8,10},{9,11},{10,... | collective-permute-start | bytes 786440 | tf_op jit(solution)/shard_map/ppermute | solution.py:24
  (22 other events, 73.4 us)

commit v5 on v4

v5 whole, which is shorter than its diff:
```python
import math

import jax
import jax.numpy as jnp
from jax import lax
from jax.experimental import pallas as pl
from jax.experimental.pallas import tpu as pltpu
from jax.sharding import PartitionSpec as P


BOUNDARY = 3
VMEM_LIMIT = 52 * 2**20
FREE = pl.CostEstimate(flops=0, bytes_accessed=0, transcendentals=0)


def shifted(block, axis, distance):
    devices = range(lax.axis_size(axis))
    route = [((i - distance) % len(devices), i) for i in devices]
    return lax.ppermute(block, axis, route)


def swapped(block, mask):
    route = [(i, i ^ mask) for i in range(lax.axis_size("batch"))]
    return lax.ppermute(block, "batch", route)


def cut(tile_weights, chunks):
    height, width = tile_weights.shape[2:]
    moves = []
    for place, (layer, first, count) in enumerate(chunks):
        step = math.gcd(8, count)
        moves += [(place, layer, first, start, step) for start in range(0, count, step)]

    def kernel(tiles, *refs):
        targets, (room, arrive, leave) = refs[: len(chunks)], refs[len(chunks) :]
        inward, outward = [], []
        for index, (place, layer, first, start, step) in enumerate(moves):
            here = room.at[index, pl.ds(0, step)]
            source = tiles.at[layer, pl.ds(first + start, step)]
            inward.append(pltpu.make_async_copy(source, here, arrive.at[index]))
            outward.append(pltpu.make_async_copy(here, targets[place].at[pl.ds(start, step)], leave.at[index]))
        for copy in inward:
            copy.start()
        for before, after in zip(inward, outward):
            before.wait()
            after.start()
        for copy in outward:
            copy.wait()

    anywhere = pl.BlockSpec(memory_space=pl.ANY)
    return pl.pallas_call(
        kernel,
        out_shape=[jax.ShapeDtypeStruct((count, height, width), tile_weights.dtype) for _, _, count in chunks],
        in_specs=[anywhere],
        out_specs=[anywhere] * len(chunks),
        scratch_shapes=[
            pltpu.VMEM((len(moves), 8, height, width), tile_weights.dtype),
            pltpu.SemaphoreType.DMA((len(moves),)),
            pltpu.SemaphoreType.DMA((len(moves),)),
        ],
        compiler_params=pltpu.CompilerParams(vmem_limit_bytes=VMEM_LIMIT),
        cost_estimate=FREE,
    )(tile_weights)


def run_blocks(layer, first, count, codes, pool, arrived, tiles, biases, target, final):
    fan, neigh, width = len(tiles), len(arrived), arrived[0].shape[1]
    rows, blocks = pool.shape[-2], biases.shape[1] // width
    columns = pool.ndim == 2
    group = math.gcd(8, count)
    held = [source if isinstance(source, list) else [source] for source in tiles]
    step = group
    for source in held:
        for array in source:
            step = math.gcd(step, array.shape[-3])
    parts = count // step

    def kernel(*refs):
        refs = list(refs)
        codes, pool_ref = (refs.pop(0) for _ in range(2))
        arrived_refs = [refs.pop(0) for _ in arrived]
        tile_refs = [[refs.pop(0) for _ in source] for source in held]
        bias = refs.pop(0)
        if target is not None:
            refs.pop(0)
        result, inputs, weights, outputs, in_sems, weight_sems, out_sems = refs

        def tile_copy(part, m):
            start = part * step
            if held[m][0].ndim == 4:
                piece = tile_refs[m][0].at[layer, pl.ds(first + start, step)]
            else:
                place, inside = 0, start
                while inside >= held[m][place].shape[0]:
                    inside -= held[m][place].shape[0]
                    place += 1
                piece = tile_refs[m][place].at[pl.ds(inside, step)]
            return pltpu.make_async_copy(piece, weights.at[m, pl.ds(start, step)], weight_sems.at[part, m])

        def out_copy(part):
            start = part * group
            if final:
                here = outputs.at[:, pl.ds(start * width, group * width)]
                there = result.at[:, pl.ds((first + start) * width, group * width)]
            else:
                here = outputs.at[pl.ds(start, group)]
                there = result.at[pl.ds(first + start, group)]
            return pltpu.make_async_copy(here, there, out_sems.at[part])

        loads = []
        for slot, source in enumerate(arrived_refs):
            loads.append((source, inputs.at[blocks + slot]))
        if columns:
            for block in range(blocks):
                loads.append((pool_ref.at[:, pl.ds(block * width, width)], inputs.at[block]))
        else:
            share = blocks // 4
            for start in range(0, blocks, share):
                loads.append((pool_ref.at[pl.ds(start, share)], inputs.at[pl.ds(start, share)]))
        loads = [pltpu.make_async_copy(*load, in_sems.at[place]) for place, load in enumerate(loads)]
        for copy in loads:
            copy.start()
        early = min(parts, max(1, 8 // step))
        for part in range(early):
            for m in range(fan):
                tile_copy(part, m).start()
        for copy in loads:
            copy.wait()
        for part in range(early, parts):
            for m in range(fan):
                tile_copy(part, m).start()

        def work(part, _):
            for sub in range(group // step):
                for m in range(fan):
                    here = weights.at[m, pl.ds((part * (group // step) + sub) * step, step)]
                    sem = weight_sems.at[part * (group // step) + sub, m]
                    pltpu.make_async_copy(here, here, sem).wait()
            for g in range(group):
                block = part * group + g
                base = (layer * blocks + first + block) * fan
                summed = jnp.dot(
                    jnp.concatenate([inputs[codes[base + m]] for m in range(fan)], axis=1),
                    jnp.concatenate([weights[m, block] for m in range(fan)], axis=0),
                    preferred_element_type=jnp.float32,
                )
                place = pl.multiple_of((first + block) * width, width)
                summed = summed + bias[layer : layer + 1, pl.ds(place, width)]
                summed = jnp.maximum(summed, 0.0).astype(result.dtype)
                if final:
                    outputs[:, pl.ds(pl.multiple_of(block * width, width), width)] = summed
                else:
                    outputs[block] = summed
            out_copy(part).start()
            return _

        lax.fori_loop(0, count // group, work, None)
        for part in range(count // group):
            out_copy(part).wait()

    anywhere = pl.BlockSpec(memory_space=pl.ANY)
    operands = [codes, pool, *arrived, *(array for source in held for array in source), biases]
    in_specs = [anywhere] * (len(operands) - 2) + [pl.BlockSpec(memory_space=pltpu.VMEM)]
    aliases = {}
    if target is not None:
        aliases[len(operands)] = 0
        operands.append(target)
        in_specs.append(anywhere)
    shape = (rows, blocks * width) if final else (blocks, rows, width)
    out = (rows, count * width) if final else (count, rows, width)
    return pl.pallas_call(
        kernel,
        out_shape=jax.ShapeDtypeStruct(shape, pool.dtype),
        grid_spec=pltpu.PrefetchScalarGridSpec(
            num_scalar_prefetch=1,
            in_specs=in_specs,
            out_specs=anywhere,
            scratch_shapes=[
                pltpu.VMEM((blocks + neigh, rows, width), pool.dtype),
                pltpu.VMEM((fan, count, width, width), tiles[0].dtype),
                pltpu.VMEM(out, pool.dtype),
                pltpu.SemaphoreType.DMA((blocks + neigh,)),
                pltpu.SemaphoreType.DMA((parts, fan)),
                pltpu.SemaphoreType.DMA((count // group,)),
            ],
        ),
        input_output_aliases=aliases,
        compiler_params=pltpu.CompilerParams(vmem_limit_bytes=VMEM_LIMIT),
        cost_estimate=FREE,
    )(*operands)


def body(activations, tile_weights, biases, source_codes, send_list):
    layer_count, block_count, part_rows, width = tile_weights.shape
    fan = source_codes.shape[2]
    part_count = lax.axis_size("dom")
    neighbor_offsets = (1, 2, -1, part_count // 2)
    sharers = width // part_rows
    own = lax.axis_index("batch") // sharers
    codes = jnp.take(source_codes, own ^ jnp.arange(fan), axis=2).reshape(-1)
    far = fan // 2
    unit = block_count // 16

    if sharers > 1:
        members = range(lax.axis_size("batch") // sharers)
        groups = [[m * sharers + s for s in range(sharers)] for m in members]
        tile_weights = lax.all_gather(tile_weights, "batch", axis=2, tiled=True, axis_index_groups=groups)

    def spread(held, first):
        for bit in range(far.bit_length() - 1):
            for m in range(1 << bit):
                held[first + m + (1 << bit)] = jax.tree.map(
                    lambda array: swapped(array, (1 << bit) * sharers), held[first + m]
                )

    last = layer_count - 1
    shares = [(layer, (16,), (4,)) for layer in range(last - 1)]
    shares += [(last - 1, (12, 4), (3, 1))]
    shares += [(last, (8, 4), (2, 2)), (last, (4,), (1,))]

    moves = {layer: [] for layer in range(layer_count)}
    for layer, sizes, _ in shares:
        for size in sizes:
            start = sum(count for _, _, count in moves[layer])
            moves[layer].append((layer, start, size * unit))
    crossed = {}
    for layer in moves:
        crossed[layer] = [swapped(mine, far * sharers) for mine in cut(tile_weights, moves[layer])]

    near = [tile_weights] + [None] * (fan - 1)
    spread(near, 0)

    current = activations
    before = None
    for layer, sizes, pieces in shares:
        if layer != before:
            arrived = []
            for slot, offset in enumerate(neighbor_offsets):
                start = send_list[layer, 0, slot]
                if layer == 0:
                    block = lax.dynamic_slice(current, (0, start * width), (current.shape[0], width))
                else:
                    block = lax.dynamic_index_in_dim(current, start, 0, keepdims=False)
                if slot >= BOUNDARY:
                    block = lax.optimization_barrier((block, arrived[slot - BOUNDARY]))[0]
                arrived.append(shifted(block, "dom", offset))
            pool, target, first, after = current, None, 0, arrived
        before = layer
        tiles = list(near)
        tiles[far], passed = [], []
        for number in pieces:
            tile = lax.optimization_barrier((crossed[layer].pop(0), *after))[0]
            share = tile.shape[0] // math.gcd(number, tile.shape[0])
            tiles[far].append(tile)
            passed += [tile[start : start + share] for start in range(0, tile.shape[0], share)]
        whole, tiles[far] = tiles[far], passed
        spread(tiles, far)
        tiles[far] = whole
        count = sum(sizes) * unit
        target = run_blocks(layer, first, count, codes, pool, arrived, tiles, biases, target, layer == last)
        current, first, after = target, first + count, [target]
    return current


def solution(mesh):
    in_specs = (
        P("batch", "dom"),
        P(None, "dom", "batch", None),
        P(None, "dom"),
        P(None, "dom", None),
        P(None, "dom", None),
    )
    out_specs = P("batch", "dom")
    return jax.shard_map(body, mesh=mesh, in_specs=in_specs, out_specs=out_specs, check_vma=False)
```

time: 216 us -> 202 us (0.935)
  waiting for transfers between devices: 68.9 us -> 60.2 us
  Pallas kernels: 66.6 us -> 58.6 us
    pallas_call x7 -> x5, Pallas kernels: 57.4 us -> 49.5 us  [run_blocks(): pl.pallas_call(kernel, out_shape=jax.ShapeDtypeStruct(shape, pool.dtype),...]
    ppermute x31 -> x25, waiting for transfers between devices: 46.1 us -> 41 us  [swapped(): return lax.ppermute(block, 'batch', route)]
    ppermute x16, starting transfers between devices: 22 us -> 26.5 us  [shifted(): return lax.ppermute(block, axis, route)]
    ppermute x16, waiting for transfers between devices: 22.9 us -> 19.2 us  [shifted(): return lax.ppermute(block, axis, route)]
    ppermute x31 -> x25, starting transfers between devices: 16.9 us -> 14 us  [swapped(): return lax.ppermute(block, 'batch', route)]
    slice x6 -> x5, local copies, waits for them, and re-layouts: 8.04 us -> 7.91 us  [body(): tile[start:start + share]]
  transfers between devices with their start and end apart: 47 -> 41, of which waited for: 20 -> 16; matrix products, arithmetic and copies ran while one was open for 6% -> 7% of each run, Pallas kernels for 29% -> 26%
where the time goes in v5:
time: 202 us; the launch traced here: 201 us
  waiting for transfers between devices  60.2 us (30%)
  Pallas kernels  58.6 us (29%)
  starting transfers between devices  40.5 us (20%)
  between operations  25.2 us (12%)
  local copies, waits for them, and re-layouts  16.4 us (8%)
    pallas_call x5, Pallas kernels, run_blocks(): pl.pallas_call(kernel, out_shape=jax.ShapeDtypeStruct(shape, pool.dtype),...  49.5 us
    ppermute x25, waiting for transfers between devices, swapped(): return lax.ppermute(block, 'batch', route)  41 us
    ppermute x16, starting transfers between devices, shifted(): return lax.ppermute(block, axis, route)  26.5 us
    ppermute x16, waiting for transfers between devices, shifted(): return lax.ppermute(block, axis, route)  19.2 us
    ppermute x25, starting transfers between devices, swapped(): return lax.ppermute(block, 'batch', route)  14 us
    pallas_call x4, Pallas kernels, cut(): pl.pallas_call(kernel, out_shape=[jax.ShapeDtypeStruct((count, height, wi...  9.13 us
    slice x5, local copies, waits for them, and re-layouts, body(): tile[start:start + share]  7.91 us
  transfers between devices with their start and end apart: 41, of which 16 were waited for; matrix products, arithmetic and copies ran while one was open for 7% of the time, Pallas kernels for 26%

profile of v5, /device:TPU:0, one launch (start us, length us, event | category | flops | bytes accessed | tf_op | source)
XLA Modules:
  0.0 200.9 jit_solution(4414967884726218754)
XLA Ops:
  0.5 2.4 %shard_map.55 = bf16[64,128,128]{2,1,0:T(8,128)(2,1)} custom-call(bf16[4,64,128,128]{3,2,1,0:T(8,128)(2,1)} %refs_6_.9), custom_call_target="tpu_custom_call" | custom-call | tf_op jit(solution)/shard_map/pallas_call | solution.py:51
  2.9 2.6 %collective-permute-start.5 = (bf16[64,128,128]{2,1,0:T(8,128)(2,1)}, bf16[64,128,128]{2,1,0:T(8,128)(2,1)S(1)}, u32[]{:S(2)}, u32[]{:S(2)}) collective-permute-start(bf16[64,128,128]{2,1,0:T(8,128)(2,1)} %shard_map.55), channel_id=1, source_target_pairs={{0,2},{1,3},{2,0},{3,1},{4,6},{5,7},{6,4},{7,5},{8,10},{9,11},{10,... | collective-permute-start | bytes 6291464 | tf_op jit(solution)/shard_map/ppermute | solution.py:24
  5.4 2.4 %shard_map.57 = bf16[64,128,128]{2,1,0:T(8,128)(2,1)} custom-call(bf16[4,64,128,128]{3,2,1,0:T(8,128)(2,1)} %refs_6_.9), custom_call_target="tpu_custom_call" | custom-call | tf_op jit(solution)/shard_map/pallas_call | solution.py:51
  12.2 2.1 %collective-permute-start = (bf16[256,128]{1,0:T(8,128)(2,1)S(1)}, bf16[256,128]{1,0:T(8,128)(2,1)S(1)}, u32[]{:S(2)}, u32[]{:S(2)}) collective-permute-start(bf16[256,128]{1,0:T(8,128)(2,1)S(1)} %get-tuple-element.52), channel_id=1, source_target_pairs={{28,0},{0,4},{4,8},{8,12},{12,16},{16,20},{20,24},{24,28},{29,1},{... | collective-permute-start | bytes 196616 | tf_op jit(solution)/shard_map/ppermute | solution.py:19
  15.8 4.1 %collective-permute-done.refs_2_ = bf16[256,128]{1,0:T(8,128)(2,1)S(1)} collective-permute-done((bf16[256,128]{1,0:T(8,128)(2,1)S(1)}, bf16[256,128]{1,0:T(8,128)(2,1)S(1)}, u32[]{:S(2)}, u32[]{:S(2)}) %collective-permute-start) | collective-permute-done | bytes 65568 | tf_op jit(solution)/shard_map/ppermute | solution.py:19
  19.9 1.7 collective-permute-start.2
  21.6 2.6 %collective-permute-done.2.refs_4_ = bf16[256,128]{1,0:T(8,128)(2,1)S(1)} collective-permute-done((bf16[256,128]{1,0:T(8,128)(2,1)S(1)}, bf16[256,128]{1,0:T(8,128)(2,1)S(1)}, u32[]{:S(2)}, u32[]{:S(2)}) %collective-permute-start.2) | collective-permute-done | bytes 65568 | tf_op jit(solution)/shard_map/ppermute | solution.py:19
  24.2 2.6 %collective-permute-done.3.refs_5_ = bf16[256,128]{1,0:T(8,128)(2,1)S(1)} collective-permute-done((bf16[256,128]{1,0:T(8,128)(2,1)S(1)}, bf16[256,128]{1,0:T(8,128)(2,1)S(1)}, u32[]{:S(2)}, u32[]{:S(2)}) %collective-permute-start.3) | collective-permute-done | bytes 65568 | tf_op jit(solution)/shard_map/ppermute | solution.py:19
  26.7 25.4 %collective-permute-done.5.refs_8_ = bf16[64,128,128]{2,1,0:T(8,128)(2,1)S(1)} collective-permute-done((bf16[64,128,128]{2,1,0:T(8,128)(2,1)}, bf16[64,128,128]{2,1,0:T(8,128)(2,1)S(1)}, u32[]{:S(2)}, u32[]{:S(2)}) %collective-permute-start.5) | collective-permute-done | bytes 2097184 | tf_op jit(solution)/shard_map/ppermute | solution.py:24
  54.6 2.3 %shard_map.59 = (bf16[48,128,128]{2,1,0:T(8,128)(2,1)}, bf16[16,128,128]{2,1,0:T(8,128)(2,1)S(1)}) custom-call(bf16[4,64,128,128]{3,2,1,0:T(8,128)(2,1)} %refs_6_.9), custom_call_target="tpu_custom_call" | custom-call | tf_op jit(solution)/shard_map/pallas_call | solution.py:51
  57.5 2.0 collective-permute-start.23
  68.9 11.2 %shard_map.56.refs_1_ = bf16[64,256,128]{2,1,0:T(8,128)(2,1)} custom-call(s32[1024]{0:T(1024)S(1)} %select_n.79.refs_0_, bf16[256,8192]{1,0:T(8,128)(2,1)} %refs_1_.1, bf16[256,128]{1,0:T(8,128)(2,1)S(1)} %collective-permute-done.refs_2_, bf16[256,128]{1,0:T(8,128)(2,1)S(1)} %collective-permute-done.1.refs_3_, ...), custom_call_target="tpu_custom_call" | custom-call | tf_op jit(solution)/shard_map/pallas_call | solution.py:171
  82.6 1.6 collective-permute-start.11
  84.2 3.2 %collective-permute-start.12 = (bf16[256,128]{1,0:T(8,128)(2,1)S(1)}, bf16[256,128]{1,0:T(8,128)(2,1)S(1)}, u32[]{:S(2)}, u32[]{:S(2)}) collective-permute-start(bf16[256,128]{1,0:T(8,128)(2,1)S(1)} %get-tuple-element.46), channel_id=1, source_target_pairs={{4,0},{8,4},{12,8},{16,12},{20,16},{24,20},{28,24},{0,28},{5,1},{9... | collective-permute-start | bytes 196616 | tf_op jit(solution)/shard_map/ppermute | solution.py:19
  89.4 7.7 %collective-permute-done.14.refs_8_ = bf16[64,128,128]{2,1,0:T(8,128)(2,1)} collective-permute-done((bf16[64,128,128]{2,1,0:T(8,128)(2,1)}, bf16[64,128,128]{2,1,0:T(8,128)(2,1)}, u32[]{:S(2)}, u32[]{:S(2)}) %collective-permute-start.14) | collective-permute-done | bytes 2097184 | tf_op jit(solution)/shard_map/ppermute | solution.py:24
  97.2 2.7 %fusion.1 = (bf16[16,128,128]{2,1,0:T(8,128)(2,1)}, bf16[16,128,128]{2,1,0:T(8,128)(2,1)}, bf16[16,128,128]{2,1,0:T(8,128)(2,1)}, bf16[16,128,128]{2,1,0:T(8,128)(2,1)S(1)}) fusion(bf16[64,128,128]{2,1,0:T(8,128)(2,1)} %collective-permute-done.14.refs_8_), kind=kLoop, calls=%fused_computation.23 | loop fusion | bytes 4194304 | tf_op jit(solution)/shard_map/slice | solution.py:255
  108.4 2.0 collective-permute-start.24
  110.4 11.1 %shard_map.58.refs_1_ = bf16[64,256,128]{2,1,0:T(8,128)(2,1)} custom-call(s32[1024]{0:T(1024)S(1)} %select_n.79.refs_0_, bf16[64,256,128]{2,1,0:T(8,128)(2,1)} %shard_map.56.refs_1_, bf16[256,128]{1,0:T(8,128)(2,1)S(1)} %collective-permute-done.10.refs_2_, bf16[256,128]{1,0:T(8,128)(2,1)S(1)} %collective-permute-done.11.refs_3_, ...), custom_call_target="tpu_custom_call" | custom-call | tf_op jit(solution)/shard_map/pallas_call | solution.py:171
  124.1 1.6 collective-permute-start.20
  125.7 3.2 %collective-permute-start.21 = (bf16[256,128]{1,0:T(8,128)(2,1)S(1)}, bf16[256,128]{1,0:T(8,128)(2,1)S(1)}, u32[]{:S(2)}, u32[]{:S(2)}) collective-permute-start(bf16[256,128]{1,0:T(8,128)(2,1)S(1)} %get-tuple-element.42), channel_id=1, source_target_pairs={{4,0},{8,4},{12,8},{16,12},{20,16},{24,20},{28,24},{0,28},{5,1},{9... | collective-permute-start | bytes 196616 | tf_op jit(solution)/shard_map/ppermute | solution.py:19
  131.0 2.1 %shard_map.61 = (bf16[32,128,128]{2,1,0:T(8,128)(2,1)}, bf16[16,128,128]{2,1,0:T(8,128)(2,1)S(1)}, bf16[16,128,128]{2,1,0:T(8,128)(2,1)S(1)}) custom-call(bf16[4,64,128,128]{3,2,1,0:T(8,128)(2,1)} %refs_6_.9), custom_call_target="tpu_custom_call" | custom-call | tf_op jit(solution)/shard_map/pallas_call | solution.py:51
  133.7 1.7 collective-permute-done.22.refs_5_
  135.4 2.5 %fusion.3 = (bf16[16,128,128]{2,1,0:T(8,128)(2,1)}, bf16[16,128,128]{2,1,0:T(8,128)(2,1)}, bf16[16,128,128]{2,1,0:T(8,128)(2,1)}) fusion(bf16[48,128,128]{2,1,0:T(8,128)(2,1)} %collective-permute-done.23.refs_8_), kind=kLoop, calls=%fused_computation.25 | loop fusion | bytes 3145728 | tf_op jit(solution)/shard_map/slice | solution.py:255
  138.4 3.6 %collective-permute-done.24.refs_9_ = bf16[16,128,128]{2,1,0:T(8,128)(2,1)S(1)} collective-permute-done((bf16[16,128,128]{2,1,0:T(8,128)(2,1)S(1)}, bf16[16,128,128]{2,1,0:T(8,128)(2,1)S(1)}, u32[]{:S(2)}, u32[]{:S(2)}) %collective-permute-start.24) | collective-permute-done | bytes 524320 | tf_op jit(solution)/shard_map/ppermute | solution.py:24
  149.3 2.0 collective-permute-start.35
  152.1 11.1 %shard_map.60.refs_1_ = bf16[64,256,128]{2,1,0:T(8,128)(2,1)} custom-call(s32[1024]{0:T(1024)S(1)} %select_n.79.refs_0_, bf16[64,256,128]{2,1,0:T(8,128)(2,1)} %shard_map.58.refs_1_, bf16[256,128]{1,0:T(8,128)(2,1)S(1)} %collective-permute-done.19.refs_2_, bf16[256,128]{1,0:T(8,128)(2,1)S(1)} %collective-permute-done.20.refs_3_, ...), custom_call_target="tpu_custom_call" | custom-call | tf_op jit(solution)/shard_map/pallas_call | solution.py:171
  165.8 1.6 collective-permute-start.30
  167.4 3.2 %collective-permute-start.31 = (bf16[256,128]{1,0:T(8,128)(2,1)S(1)}, bf16[256,128]{1,0:T(8,128)(2,1)S(1)}, u32[]{:S(2)}, u32[]{:S(2)}) collective-permute-start(bf16[256,128]{1,0:T(8,128)(2,1)S(1)} %get-tuple-element.38), channel_id=1, source_target_pairs={{4,0},{8,4},{12,8},{16,12},{20,16},{24,20},{28,24},{0,28},{5,1},{9... | collective-permute-start | bytes 196616 | tf_op jit(solution)/shard_map/ppermute | solution.py:19
  172.7 4.2 %collective-permute-done.32.refs_5_ = bf16[256,128]{1,0:T(8,128)(2,1)S(1)} collective-permute-done((bf16[256,128]{1,0:T(8,128)(2,1)S(1)}, bf16[256,128]{1,0:T(8,128)(2,1)S(1)}, u32[]{:S(2)}, u32[]{:S(2)}) %collective-permute-start.32) | collective-permute-done | bytes 65568 | tf_op jit(solution)/shard_map/ppermute | solution.py:19
  182.4 9.6 %shard_map.62.refs_11_ = bf16[256,8192]{1,0:T(8,128)(2,1)} custom-call(s32[1024]{0:T(1024)S(1)} %select_n.79.refs_0_, bf16[64,256,128]{2,1,0:T(8,128)(2,1)} %shard_map.60.refs_1_, bf16[256,128]{1,0:T(8,128)(2,1)S(1)} %collective-permute-done.29.refs_2_, bf16[256,128]{1,0:T(8,128)(2,1)S(1)} %collective-permute-done.30.refs_3_, ...), custom_call_target="tpu_custom_call" | custom-call | tf_op jit(solution)/shard_map/pallas_call | solution.py:171
  192.6 1.9 collective-permute-done.40.refs_9_
  194.5 6.4 %shard_map.63 = bf16[256,8192]{1,0:T(8,128)(2,1)} custom-call(s32[1024]{0:T(1024)S(1)} %select_n.79.refs_0_, bf16[64,256,128]{2,1,0:T(8,128)(2,1)} %shard_map.60.refs_1_, bf16[256,128]{1,0:T(8,128)(2,1)S(1)} %collective-permute-done.29.refs_2_, bf16[256,128]{1,0:T(8,128)(2,1)S(1)} %collective-permute-done.30.refs_3_, ...), custom_call_target="tpu_custom_call", output_to_operand_aliasing={{}: (11, {})} | custom-call | tf_op jit(solution)/shard_map/pallas_call | solution.py:171
  (92 shorter events, 31.5 us)
Async XLA Ops:
  0.0 68.1 %collective-permute-start.4 = (bf16[4,64,128,128]{3,2,1,0:T(8,128)(2,1)}, bf16[4,64,128,128]{3,2,1,0:T(8,128)(2,1)}, u32[]{:S(2)}, u32[]{:S(2)}) collective-permute-start(bf16[4,64,128,128]{3,2,1,0:T(8,128)(2,1)} %refs_6_.9), channel_id=1, source_target_pairs={{0,1},{1,0},{2,3},{3,2},{4,5},{5,4},{6,7},{7,6},{8,9},{9,8},{10,11... | collective-permute-start | bytes 25165832 | tf_op jit(solution)/shard_map/ppermute | solution.py:24
  2.9 49.3 %collective-permute-start.5 = (bf16[64,128,128]{2,1,0:T(8,128)(2,1)}, bf16[64,128,128]{2,1,0:T(8,128)(2,1)S(1)}, u32[]{:S(2)}, u32[]{:S(2)}) collective-permute-start(bf16[64,128,128]{2,1,0:T(8,128)(2,1)} %shard_map.55), channel_id=1, source_target_pairs={{0,2},{1,3},{2,0},{3,1},{4,6},{5,7},{6,4},{7,5},{8,10},{9,11},{10,... | collective-permute-start | bytes 6291464 | tf_op jit(solution)/shard_map/ppermute | solution.py:24
  7.8 89.3 %collective-permute-start.14 = (bf16[64,128,128]{2,1,0:T(8,128)(2,1)}, bf16[64,128,128]{2,1,0:T(8,128)(2,1)}, u32[]{:S(2)}, u32[]{:S(2)}) collective-permute-start(bf16[64,128,128]{2,1,0:T(8,128)(2,1)} %shard_map.57), channel_id=1, source_target_pairs={{0,2},{1,3},{2,0},{3,1},{4,6},{5,7},{6,4},{7,5},{8,10},{9,11},{10,... | collective-permute-start | bytes 6291464 | tf_op jit(solution)/shard_map/ppermute | solution.py:24
  12.2 7.7 %collective-permute-start = (bf16[256,128]{1,0:T(8,128)(2,1)S(1)}, bf16[256,128]{1,0:T(8,128)(2,1)S(1)}, u32[]{:S(2)}, u32[]{:S(2)}) collective-permute-start(bf16[256,128]{1,0:T(8,128)(2,1)S(1)} %get-tuple-element.52), channel_id=1, source_target_pairs={{28,0},{0,4},{4,8},{8,12},{12,16},{16,20},{20,24},{24,28},{29,1},{... | collective-permute-start | bytes 196616 | tf_op jit(solution)/shard_map/ppermute | solution.py:19
  14.3 7.3 %collective-permute-start.1 = (bf16[256,128]{1,0:T(8,128)(2,1)S(1)}, bf16[256,128]{1,0:T(8,128)(2,1)S(1)}, u32[]{:S(2)}, u32[]{:S(2)}) collective-permute-start(bf16[256,128]{1,0:T(8,128)(2,1)S(1)} %get-tuple-element.51), channel_id=1, source_target_pairs={{24,0},{28,4},{0,8},{4,12},{8,16},{12,20},{16,24},{20,28},{25,1},{... | collective-permute-start | bytes 196616 | tf_op jit(solution)/shard_map/ppermute | solution.py:19
  21.6 5.2 %collective-permute-start.3 = (bf16[256,128]{1,0:T(8,128)(2,1)S(1)}, bf16[256,128]{1,0:T(8,128)(2,1)S(1)}, u32[]{:S(2)}, u32[]{:S(2)}) collective-permute-start(bf16[256,128]{1,0:T(8,128)(2,1)S(1)} %get-tuple-element.21), channel_id=1, source_target_pairs={{16,0},{20,4},{24,8},{28,12},{0,16},{4,20},{8,24},{12,28},{17,1},{... | collective-permute-start | bytes 196616 | tf_op jit(solution)/shard_map/ppermute | solution.py:19
  56.9 11.1 %collective-permute-start.8 = (bf16[16,128,128]{2,1,0:T(8,128)(2,1)}, bf16[16,128,128]{2,1,0:T(8,128)(2,1)S(1)}, u32[]{:S(2)}, u32[]{:S(2)}) collective-permute-start(bf16[16,128,128]{2,1,0:T(8,128)(2,1)} %get-tuple-element.58), channel_id=1, source_target_pairs={{0,1},{1,0},{2,3},{3,2},{4,5},{5,4},{6,7},{7,6},{8,9},{9,8},{10,11... | collective-permute-start | bytes 1572872 | tf_op jit(solution)/shard_map/ppermute | solution.py:24
  57.0 11.1 %collective-permute-start.9 = (bf16[16,128,128]{2,1,0:T(8,128)(2,1)}, bf16[16,128,128]{2,1,0:T(8,128)(2,1)S(1)}, u32[]{:S(2)}, u32[]{:S(2)}) collective-permute-start(bf16[16,128,128]{2,1,0:T(8,128)(2,1)} %get-tuple-element.57), channel_id=1, source_target_pairs={{0,1},{1,0},{2,3},{3,2},{4,5},{5,4},{6,7},{7,6},{8,9},{9,8},{10,11... | collective-permute-start | bytes 1572872 | tf_op jit(solution)/shard_map/ppermute | solution.py:24
  57.5 75.6 %collective-permute-start.23 = (bf16[48,128,128]{2,1,0:T(8,128)(2,1)}, bf16[48,128,128]{2,1,0:T(8,128)(2,1)}, u32[]{:S(2)}, u32[]{:S(2)}) collective-permute-start(bf16[48,128,128]{2,1,0:T(8,128)(2,1)} %get-tuple-element.26), channel_id=1, source_target_pairs={{0,2},{1,3},{2,0},{3,1},{4,6},{5,7},{6,4},{7,5},{8,10},{9,11},{10,... | collective-permute-start | bytes 4718600 | tf_op jit(solution)/shard_map/ppermute | solution.py:24
  81.1 7.6 %collective-permute-start.10 = (bf16[256,128]{1,0:T(8,128)(2,1)S(1)}, bf16[256,128]{1,0:T(8,128)(2,1)S(1)}, u32[]{:S(2)}, u32[]{:S(2)}) collective-permute-start(bf16[256,128]{1,0:T(8,128)(2,1)S(1)} %get-tuple-element.48), channel_id=1, source_target_pairs={{28,0},{0,4},{4,8},{8,12},{12,16},{16,20},{20,24},{24,28},{29,1},{... | collective-permute-start | bytes 196616 | tf_op jit(solution)/shard_map/ppermute | solution.py:19
  82.6 14.5 %collective-permute-start.11 = (bf16[256,128]{1,0:T(8,128)(2,1)S(1)}, bf16[256,128]{1,0:T(8,128)(2,1)S(1)}, u32[]{:S(2)}, u32[]{:S(2)}) collective-permute-start(bf16[256,128]{1,0:T(8,128)(2,1)S(1)} %get-tuple-element.47), channel_id=1, source_target_pairs={{24,0},{28,4},{0,8},{4,12},{8,16},{12,20},{16,24},{20,28},{25,1},{... | collective-permute-start | bytes 196616 | tf_op jit(solution)/shard_map/ppermute | solution.py:19
  84.2 13.0 %collective-permute-start.12 = (bf16[256,128]{1,0:T(8,128)(2,1)S(1)}, bf16[256,128]{1,0:T(8,128)(2,1)S(1)}, u32[]{:S(2)}, u32[]{:S(2)}) collective-permute-start(bf16[256,128]{1,0:T(8,128)(2,1)S(1)} %get-tuple-element.46), channel_id=1, source_target_pairs={{4,0},{8,4},{12,8},{16,12},{20,16},{24,20},{28,24},{0,28},{5,1},{9... | collective-permute-start | bytes 196616 | tf_op jit(solution)/shard_map/ppermute | solution.py:19
  88.7 8.5 %collective-permute-start.13 = (bf16[256,128]{1,0:T(8,128)(2,1)S(1)}, bf16[256,128]{1,0:T(8,128)(2,1)S(1)}, u32[]{:S(2)}, u32[]{:S(2)}) collective-permute-start(bf16[256,128]{1,0:T(8,128)(2,1)S(1)} %get-tuple-element.23), channel_id=1, source_target_pairs={{16,0},{20,4},{24,8},{28,12},{0,16},{4,20},{8,24},{12,28},{17,1},{... | collective-permute-start | bytes 196616 | tf_op jit(solution)/shard_map/ppermute | solution.py:19
  99.9 8.5 %collective-permute-start.15 = (bf16[16,128,128]{2,1,0:T(8,128)(2,1)S(1)}, bf16[16,128,128]{2,1,0:T(8,128)(2,1)S(1)}, u32[]{:S(2)}, u32[]{:S(2)}) collective-permute-start(bf16[16,128,128]{2,1,0:T(8,128)(2,1)S(1)} %get-tuple-element.56), channel_id=1, source_target_pairs={{0,1},{1,0},{2,3},{3,2},{4,5},{5,4},{6,7},{7,6},{8,9},{9,8},{10,11... | collective-permute-start | bytes 1572872 | tf_op jit(solution)/shard_map/ppermute | solution.py:24
  99.9 10.5 %collective-permute-start.16 = (bf16[16,128,128]{2,1,0:T(8,128)(2,1)}, bf16[16,128,128]{2,1,0:T(8,128)(2,1)S(1)}, u32[]{:S(2)}, u32[]{:S(2)}) collective-permute-start(bf16[16,128,128]{2,1,0:T(8,128)(2,1)} %get-tuple-element.55), channel_id=1, source_target_pairs={{0,1},{1,0},{2,3},{3,2},{4,5},{5,4},{6,7},{7,6},{8,9},{9,8},{10,11... | collective-permute-start | bytes 1572872 | tf_op jit(solution)/shard_map/ppermute | solution.py:24
  100.4 10.0 %collective-permute-start.17 = (bf16[16,128,128]{2,1,0:T(8,128)(2,1)}, bf16[16,128,128]{2,1,0:T(8,128)(2,1)S(1)}, u32[]{:S(2)}, u32[]{:S(2)}) collective-permute-start(bf16[16,128,128]{2,1,0:T(8,128)(2,1)} %get-tuple-element.54), channel_id=1, source_target_pairs={{0,1},{1,0},{2,3},{3,2},{4,5},{5,4},{6,7},{7,6},{8,9},{9,8},{10,11... | collective-permute-start | bytes 1572872 | tf_op jit(solution)/shard_map/ppermute | solution.py:24
  100.4 10.0 %collective-permute-start.18 = (bf16[16,128,128]{2,1,0:T(8,128)(2,1)}, bf16[16,128,128]{2,1,0:T(8,128)(2,1)}, u32[]{:S(2)}, u32[]{:S(2)}) collective-permute-start(bf16[16,128,128]{2,1,0:T(8,128)(2,1)} %get-tuple-element.53), channel_id=1, source_target_pairs={{0,1},{1,0},{2,3},{3,2},{4,5},{5,4},{6,7},{7,6},{8,9},{9,8},{10,11... | collective-permute-start | bytes 1572872 | tf_op jit(solution)/shard_map/ppermute | solution.py:24
  108.4 33.6 %collective-permute-start.24 = (bf16[16,128,128]{2,1,0:T(8,128)(2,1)S(1)}, bf16[16,128,128]{2,1,0:T(8,128)(2,1)S(1)}, u32[]{:S(2)}, u32[]{:S(2)}) collective-permute-start(bf16[16,128,128]{2,1,0:T(8,128)(2,1)S(1)} %get-tuple-element.28), channel_id=1, source_target_pairs={{0,2},{1,3},{2,0},{3,1},{4,6},{5,7},{6,4},{7,5},{8,10},{9,11},{10,... | collective-permute-start | bytes 1572872 | tf_op jit(solution)/shard_map/ppermute | solution.py:24
  122.5 7.7 %collective-permute-start.19 = (bf16[256,128]{1,0:T(8,128)(2,1)S(1)}, bf16[256,128]{1,0:T(8,128)(2,1)S(1)}, u32[]{:S(2)}, u32[]{:S(2)}) collective-permute-start(bf16[256,128]{1,0:T(8,128)(2,1)S(1)} %get-tuple-element.44), channel_id=1, source_target_pairs={{28,0},{0,4},{4,8},{8,12},{12,16},{16,20},{20,24},{24,28},{29,1},{... | collective-permute-start | bytes 196616 | tf_op jit(solution)/shard_map/ppermute | solution.py:19
  124.1 9.6 %collective-permute-start.20 = (bf16[256,128]{1,0:T(8,128)(2,1)S(1)}, bf16[256,128]{1,0:T(8,128)(2,1)S(1)}, u32[]{:S(2)}, u32[]{:S(2)}) collective-permute-start(bf16[256,128]{1,0:T(8,128)(2,1)S(1)} %get-tuple-element.43), channel_id=1, source_target_pairs={{24,0},{28,4},{0,8},{4,12},{8,16},{12,20},{16,24},{20,28},{25,1},{... | collective-permute-start | bytes 196616 | tf_op jit(solution)/shard_map/ppermute | solution.py:19
  125.7 8.0 %collective-permute-start.21 = (bf16[256,128]{1,0:T(8,128)(2,1)S(1)}, bf16[256,128]{1,0:T(8,128)(2,1)S(1)}, u32[]{:S(2)}, u32[]{:S(2)}) collective-permute-start(bf16[256,128]{1,0:T(8,128)(2,1)S(1)} %get-tuple-element.42), channel_id=1, source_target_pairs={{4,0},{8,4},{12,8},{16,12},{20,16},{24,20},{28,24},{0,28},{5,1},{9... | collective-permute-start | bytes 196616 | tf_op jit(solution)/shard_map/ppermute | solution.py:19
  133.1 39.1 %collective-permute-start.34 = (bf16[32,128,128]{2,1,0:T(8,128)(2,1)}, bf16[32,128,128]{2,1,0:T(8,128)(2,1)}, u32[]{:S(2)}, u32[]{:S(2)}) collective-permute-start(bf16[32,128,128]{2,1,0:T(8,128)(2,1)} %get-tuple-element.32), channel_id=1, source_target_pairs={{0,2},{1,3},{2,0},{3,1},{4,6},{5,7},{6,4},{7,5},{8,10},{9,11},{10,... | collective-permute-start | bytes 3145736 | tf_op jit(solution)/shard_map/ppermute | solution.py:24
  137.9 11.4 %collective-permute-start.25 = (bf16[16,128,128]{2,1,0:T(8,128)(2,1)}, bf16[16,128,128]{2,1,0:T(8,128)(2,1)S(1)}, u32[]{:S(2)}, u32[]{:S(2)}) collective-permute-start(bf16[16,128,128]{2,1,0:T(8,128)(2,1)} %get-tuple-element.63), channel_id=1, source_target_pairs={{0,1},{1,0},{2,3},{3,2},{4,5},{5,4},{6,7},{7,6},{8,9},{9,8},{10,11... | collective-permute-start | bytes 1572872 | tf_op jit(solution)/shard_map/ppermute | solution.py:24
  137.9 13.4 %collective-permute-start.26 = (bf16[16,128,128]{2,1,0:T(8,128)(2,1)}, bf16[16,128,128]{2,1,0:T(8,128)(2,1)S(1)}, u32[]{:S(2)}, u32[]{:S(2)}) collective-permute-start(bf16[16,128,128]{2,1,0:T(8,128)(2,1)} %get-tuple-element.62), channel_id=1, source_target_pairs={{0,1},{1,0},{2,3},{3,2},{4,5},{5,4},{6,7},{7,6},{8,9},{9,8},{10,11... | collective-permute-start | bytes 1572872 | tf_op jit(solution)/shard_map/ppermute | solution.py:24
  138.4 12.9 %collective-permute-start.27 = (bf16[16,128,128]{2,1,0:T(8,128)(2,1)}, bf16[16,128,128]{2,1,0:T(8,128)(2,1)}, u32[]{:S(2)}, u32[]{:S(2)}) collective-permute-start(bf16[16,128,128]{2,1,0:T(8,128)(2,1)} %get-tuple-element.61), channel_id=1, source_target_pairs={{0,1},{1,0},{2,3},{3,2},{4,5},{5,4},{6,7},{7,6},{8,9},{9,8},{10,11... | collective-permute-start | bytes 1572872 | tf_op jit(solution)/shard_map/ppermute | solution.py:24
  142.0 9.3 %collective-permute-start.28 = (bf16[16,128,128]{2,1,0:T(8,128)(2,1)S(1)}, bf16[16,128,128]{2,1,0:T(8,128)(2,1)S(1)}, u32[]{:S(2)}, u32[]{:S(2)}) collective-permute-start(bf16[16,128,128]{2,1,0:T(8,128)(2,1)S(1)} %collective-permute-done.24.refs_9_), channel_id=1, source_target_pairs={{0,1},{1,0},{2,3},{3,2},{4,5},{5,4},{6,7},{7,6},{8,9},{9,8},{10,11... | collective-permute-start | bytes 1572872 | tf_op jit(solution)/shard_map/ppermute | solution.py:24
  149.3 29.9 %collective-permute-start.35 = (bf16[16,128,128]{2,1,0:T(8,128)(2,1)S(1)}, bf16[16,128,128]{2,1,0:T(8,128)(2,1)S(1)}, u32[]{:S(2)}, u32[]{:S(2)}) collective-permute-start(bf16[16,128,128]{2,1,0:T(8,128)(2,1)S(1)} %get-tuple-element.34), channel_id=1, source_target_pairs={{0,2},{1,3},{2,0},{3,1},{4,6},{5,7},{6,4},{7,5},{8,10},{9,11},{10,... | collective-permute-start | bytes 1572872 | tf_op jit(solution)/shard_map/ppermute | solution.py:24
  164.2 7.4 %collective-permute-start.29 = (bf16[256,128]{1,0:T(8,128)(2,1)S(1)}, bf16[256,128]{1,0:T(8,128)(2,1)S(1)}, u32[]{:S(2)}, u32[]{:S(2)}) collective-permute-start(bf16[256,128]{1,0:T(8,128)(2,1)S(1)} %get-tuple-element.40), channel_id=1, source_target_pairs={{28,0},{0,4},{4,8},{8,12},{12,16},{16,20},{20,24},{24,28},{29,1},{... | collective-permute-start | bytes 196616 | tf_op jit(solution)/shard_map/ppermute | solution.py:19
  165.8 6.5 %collective-permute-start.30 = (bf16[256,128]{1,0:T(8,128)(2,1)S(1)}, bf16[256,128]{1,0:T(8,128)(2,1)S(1)}, u32[]{:S(2)}, u32[]{:S(2)}) collective-permute-start(bf16[256,128]{1,0:T(8,128)(2,1)S(1)} %get-tuple-element.39), channel_id=1, source_target_pairs={{24,0},{28,4},{0,8},{4,12},{8,16},{12,20},{16,24},{20,28},{25,1},{... | collective-permute-start | bytes 196616 | tf_op jit(solution)/shard_map/ppermute | solution.py:19
  167.4 5.3 %collective-permute-start.31 = (bf16[256,128]{1,0:T(8,128)(2,1)S(1)}, bf16[256,128]{1,0:T(8,128)(2,1)S(1)}, u32[]{:S(2)}, u32[]{:S(2)}) collective-permute-start(bf16[256,128]{1,0:T(8,128)(2,1)S(1)} %get-tuple-element.38), channel_id=1, source_target_pairs={{4,0},{8,4},{12,8},{16,12},{20,16},{24,20},{28,24},{0,28},{5,1},{9... | collective-permute-start | bytes 196616 | tf_op jit(solution)/shard_map/ppermute | solution.py:19
  171.6 5.2 %collective-permute-start.32 = (bf16[256,128]{1,0:T(8,128)(2,1)S(1)}, bf16[256,128]{1,0:T(8,128)(2,1)S(1)}, u32[]{:S(2)}, u32[]{:S(2)}) collective-permute-start(bf16[256,128]{1,0:T(8,128)(2,1)S(1)} %get-tuple-element.30), channel_id=1, source_target_pairs={{16,0},{20,4},{24,8},{28,12},{0,16},{4,20},{8,24},{12,28},{17,1},{... | collective-permute-start | bytes 196616 | tf_op jit(solution)/shard_map/ppermute | solution.py:19
  178.7 13.9 %collective-permute-start.33 = (bf16[16,128,128]{2,1,0:T(8,128)(2,1)S(1)}, bf16[16,128,128]{2,1,0:T(8,128)(2,1)S(1)}, u32[]{:S(2)}, u32[]{:S(2)}) collective-permute-start(bf16[16,128,128]{2,1,0:T(8,128)(2,1)S(1)} %get-tuple-element.31), channel_id=1, source_target_pairs={{0,2},{1,3},{2,0},{3,1},{4,6},{5,7},{6,4},{7,5},{8,10},{9,11},{10,... | collective-permute-start | bytes 1572872 | tf_op jit(solution)/shard_map/ppermute | solution.py:24
  (17 other events, 123.4 us)

commit v6 on v5

--- a/solution.py
+++ b/solution.py
@@ -8,8 +8,9 @@
 from jax.sharding import PartitionSpec as P
 
 
-BOUNDARY = 3
+TURNS = (3, 1, 0, 2)
 VMEM_LIMIT = 52 * 2**20
+LAYER_LIMIT = 48 * 2**20
 FREE = pl.CostEstimate(flops=0, bytes_accessed=0, transcendentals=0)
 
 
@@ -63,7 +64,35 @@
     )(tile_weights)
 
 
-def run_blocks(layer, first, count, codes, pool, arrived, tiles, biases, target, final):
+def pick(table, place, number, width, activations):
+    rows = activations.shape[0]
+
+    def kernel(table, source, *refs):
+        targets, semaphores = refs[:number], refs[number]
+        copies = []
+        for slot in range(number):
+            start = pl.multiple_of(table[place + slot] * width, width)
+            copies.append(pltpu.make_async_copy(source.at[:, pl.ds(start, width)], targets[slot], semaphores.at[slot]))
+        for copy in copies:
+            copy.start()
+        for copy in copies:
+            copy.wait()
+
+    return pl.pallas_call(
+        kernel,
+        out_shape=[jax.ShapeDtypeStruct((rows, width), activations.dtype)] * number,
+        grid_spec=pltpu.PrefetchScalarGridSpec(
+            num_scalar_prefetch=1,
+            in_specs=[pl.BlockSpec(memory_space=pl.ANY)],
+            out_specs=[pl.BlockSpec(memory_space=pltpu.VMEM)] * number,
+            scratch_shapes=[pltpu.SemaphoreType.DMA((number,))],
+        ),
+        compiler_params=pltpu.CompilerParams(vmem_limit_bytes=VMEM_LIMIT),
+        cost_estimate=FREE,
+    )(table, activations)
+
+
+def run_blocks(layer, first, count, table, sends, pool, arrived, tiles, biases, target, final):
     fan, neigh, width = len(tiles), len(arrived), arrived[0].shape[1]
     rows, blocks = pool.shape[-2], biases.shape[1] // width
     columns = pool.ndim == 2
@@ -77,13 +106,15 @@
 
     def kernel(*refs):
         refs = list(refs)
-        codes, pool_ref = (refs.pop(0) for _ in range(2))
+        table, pool_ref = (refs.pop(0) for _ in range(2))
         arrived_refs = [refs.pop(0) for _ in arrived]
         tile_refs = [[refs.pop(0) for _ in source] for source in held]
         bias = refs.pop(0)
         if target is not None:
             refs.pop(0)
-        result, inputs, weights, outputs, in_sems, weight_sems, out_sems = refs
+        result = refs.pop(0)
+        outgoing = [] if final else [refs.pop(0) for _ in arrived]
+        inputs, weights, outputs, in_sems, weight_sems, out_sems, send_sems = refs
 
         def tile_copy(part, m):
             start = part * step
@@ -140,7 +171,7 @@
                 block = part * group + g
                 base = (layer * blocks + first + block) * fan
                 summed = jnp.dot(
-                    jnp.concatenate([inputs[codes[base + m]] for m in range(fan)], axis=1),
+                    jnp.concatenate([inputs[table[base + m]] for m in range(fan)], axis=1),
                     jnp.concatenate([weights[m, block] for m in range(fan)], axis=0),
                     preferred_element_type=jnp.float32,
                 )
@@ -155,11 +186,17 @@
             return _
 
         lax.fori_loop(0, count // group, work, None)
+        handed = []
+        for slot, there in enumerate(outgoing):
+            handed.append(pltpu.make_async_copy(outputs.at[table[sends + slot]], there, send_sems.at[slot]))
+            handed[-1].start()
+        for copy in handed:
+            copy.wait()
         for part in range(count // group):
             out_copy(part).wait()
 
     anywhere = pl.BlockSpec(memory_space=pl.ANY)
-    operands = [codes, pool, *arrived, *(array for source in held for array in source), biases]
+    operands = [table, pool, *arrived, *(array for source in held for array in source), biases]
     in_specs = [anywhere] * (len(operands) - 2) + [pl.BlockSpec(memory_space=pltpu.VMEM)]
     aliases = {}
     if target is not None:
@@ -168,13 +205,16 @@
         in_specs.append(anywhere)
     shape = (rows, blocks * width) if final else (blocks, rows, width)
     out = (rows, count * width) if final else (count, rows, width)
-    return pl.pallas_call(
+    out_shape = [jax.ShapeDtypeStruct(shape, pool.dtype)]
+    if not final:
+        out_shape += [jax.ShapeDtypeStruct((rows, width), pool.dtype)] * neigh
+    result, *outgoing = pl.pallas_call(
         kernel,
-        out_shape=jax.ShapeDtypeStruct(shape, pool.dtype),
+        out_shape=out_shape,
         grid_spec=pltpu.PrefetchScalarGridSpec(
             num_scalar_prefetch=1,
             in_specs=in_specs,
-            out_specs=anywhere,
+            out_specs=[anywhere] * len(out_shape),
             scratch_shapes=[
                 pltpu.VMEM((blocks + neigh, rows, width), pool.dtype),
                 pltpu.VMEM((fan, count, width, width), tiles[0].dtype),
@@ -182,12 +222,14 @@
                 pltpu.SemaphoreType.DMA((blocks + neigh,)),
                 pltpu.SemaphoreType.DMA((parts, fan)),
                 pltpu.SemaphoreType.DMA((count // group,)),
+                pltpu.SemaphoreType.DMA((neigh,)),
             ],
         ),
         input_output_aliases=aliases,
-        compiler_params=pltpu.CompilerParams(vmem_limit_bytes=VMEM_LIMIT),
+        compiler_params=pltpu.CompilerParams(vmem_limit_bytes=LAYER_LIMIT),
         cost_estimate=FREE,
     )(*operands)
+    return result, outgoing
 
 
 def body(activations, tile_weights, biases, source_codes, send_list):
@@ -198,6 +240,7 @@
     sharers = width // part_rows
     own = lax.axis_index("batch") // sharers
     codes = jnp.take(source_codes, own ^ jnp.arange(fan), axis=2).reshape(-1)
+    table = jnp.concatenate([codes, send_list.reshape(-1)])
     far = fan // 2
     unit = block_count // 16
 
@@ -231,19 +274,17 @@
     spread(near, 0)
 
     current = activations
+    neigh = len(neighbor_offsets)
+    outgoing = pick(table, codes.size, neigh, width, activations)
     before = None
     for layer, sizes, pieces in shares:
         if layer != before:
-            arrived = []
-            for slot, offset in enumerate(neighbor_offsets):
-                start = send_list[layer, 0, slot]
-                if layer == 0:
-                    block = lax.dynamic_slice(current, (0, start * width), (current.shape[0], width))
-                else:
-                    block = lax.dynamic_index_in_dim(current, start, 0, keepdims=False)
-                if slot >= BOUNDARY:
-                    block = lax.optimization_barrier((block, arrived[slot - BOUNDARY]))[0]
-                arrived.append(shifted(block, "dom", offset))
+            arrived = [None] * neigh
+            for turn, slot in enumerate(TURNS):
+                block = outgoing[slot]
+                if turn == neigh - 1:
+                    block = lax.optimization_barrier((block, arrived[TURNS[1]]))[0]
+                arrived[slot] = shifted(block, "dom", neighbor_offsets[slot])
             pool, target, first, after = current, None, 0, arrived
         before = layer
         tiles = list(near)
@@ -257,7 +298,10 @@
         spread(tiles, far)
         tiles[far] = whole
         count = sum(sizes) * unit
-        target = run_blocks(layer, first, count, codes, pool, arrived, tiles, biases, target, layer == last)
+        sends = codes.size + (layer + 1) * neigh
+        target, outgoing = run_blocks(
+            layer, first, count, table, sends, pool, arrived, tiles, biases, target, layer == last
+        )
         current, first, after = target, first + count, [target]
     return current
 

time: 202 us -> 195 us (0.965)
  between operations: 25.2 us -> 0.28 us
  waiting for transfers between devices: 60.2 us -> 80.8 us
  local copies, waits for them, and re-layouts: 16.4 us -> 3.63 us
  starting transfers between devices: 40.5 us -> 50.2 us
    ppermute x25, waiting for transfers between devices: 41 us -> 70.4 us  [swapped(): return lax.ppermute(block, 'batch', route)]
    ppermute x16, waiting for transfers between devices: 19.2 us -> 10.5 us  [shifted(): return lax.ppermute(block, axis, route)]
    ppermute x16, starting transfers between devices: 26.5 us -> 33.9 us  [shifted(): return lax.ppermute(block, axis, route)]
    slice x5, local copies, waits for them, and re-layouts: 7.91 us -> 2.2 us  [body(): tile[start:start + share]]
    squeeze x3 -> x0, local copies, waits for them, and re-layouts: 2.9 us -> none  [body(): block = lax.dynamic_index_in_dim(current, start, 0, keepdims=False)]
    unnamed x16 -> x12, local copies, waits for them, and re-layouts: 3.06 us -> 0.53 us
    ppermute x25, starting transfers between devices: 14 us -> 16.3 us  [swapped(): return lax.ppermute(block, 'batch', route)]
    pallas_call x5 -> x6, Pallas kernels: 49.5 us -> 49.9 us  [the longest x5 48.3 us: run_blocks(): pl.pallas_call(kernel, out_shape=out_shape, grid_spec=pltpu.PrefetchScala...]
  transfers between devices with their start and end apart: 41 -> 41, of which waited for: 16 -> 20; matrix products, arithmetic and copies ran while one was open for 7% -> 2% of each run, Pallas kernels for 26% -> 28%
where the time goes in v6:
time: 195 us
  waiting for transfers between devices  80.8 us (41%)
  Pallas kernels  59.1 us (30%)
  starting transfers between devices  50.2 us (26%)
  local copies, waits for them, and re-layouts  3.63 us (2%)
    ppermute x25, waiting for transfers between devices, swapped(): return lax.ppermute(block, 'batch', route)  70.4 us
    pallas_call x5, Pallas kernels, run_blocks(): pl.pallas_call(kernel, out_shape=out_shape, grid_spec=pltpu.PrefetchScala...  48.3 us
    ppermute x16, starting transfers between devices, shifted(): return lax.ppermute(block, axis, route)  33.9 us
    ppermute x25, starting transfers between devices, swapped(): return lax.ppermute(block, 'batch', route)  16.3 us
    ppermute x16, waiting for transfers between devices, shifted(): return lax.ppermute(block, axis, route)  10.5 us
    pallas_call x4, Pallas kernels, cut(): pl.pallas_call(kernel, out_shape=[jax.ShapeDtypeStruct((count, height, wi...  9.19 us
  transfers between devices with their start and end apart: 41, of which 20 were waited for; matrix products, arithmetic and copies ran while one was open for 2% of the time, Pallas kernels for 28%

profile of v6, /device:TPU:0, one launch (start us, length us, event | category | flops | bytes accessed | tf_op | source)
XLA Modules:
  0.0 194.7 jit_solution(8066822269967967412)
XLA Ops:
  0.5 2.4 %shard_map.56 = bf16[64,128,128]{2,1,0:T(8,128)(2,1)} custom-call(bf16[4,64,128,128]{3,2,1,0:T(8,128)(2,1)} %refs_6_.9), custom_call_target="tpu_custom_call" | custom-call | tf_op jit(solution)/shard_map/pallas_call | solution.py:52
  2.9 2.6 %collective-permute-start.5 = (bf16[64,128,128]{2,1,0:T(8,128)(2,1)}, bf16[64,128,128]{2,1,0:T(8,128)(2,1)}, u32[]{:S(2)}, u32[]{:S(2)}) collective-permute-start(bf16[64,128,128]{2,1,0:T(8,128)(2,1)} %shard_map.56), channel_id=1, source_target_pairs={{0,2},{1,3},{2,0},{3,1},{4,6},{5,7},{6,4},{7,5},{8,10},{9,11},{10,... | collective-permute-start | bytes 6291464 | tf_op jit(solution)/shard_map/ppermute | solution.py:25
  5.4 2.5 %shard_map.58 = bf16[64,128,128]{2,1,0:T(8,128)(2,1)} custom-call(bf16[4,64,128,128]{3,2,1,0:T(8,128)(2,1)} %refs_6_.9), custom_call_target="tpu_custom_call" | custom-call | tf_op jit(solution)/shard_map/pallas_call | solution.py:52
  11.8 2.1 %collective-permute-start.1 = (bf16[256,128]{1,0:T(8,128)(2,1)S(1)}, bf16[256,128]{1,0:T(8,128)(2,1)S(1)}, u32[]{:S(2)}, u32[]{:S(2)}) collective-permute-start(bf16[256,128]{1,0:T(8,128)(2,1)S(1)} %get-tuple-element.41), channel_id=1, source_target_pairs={{24,0},{28,4},{0,8},{4,12},{8,16},{12,20},{16,24},{20,28},{25,1},{... | collective-permute-start | bytes 196616 | tf_op jit(solution)/shard_map/ppermute | solution.py:20
  15.4 2.8 %collective-permute-done.1.refs_3_ = bf16[256,128]{1,0:T(8,128)(2,1)S(1)} collective-permute-done((bf16[256,128]{1,0:T(8,128)(2,1)S(1)}, bf16[256,128]{1,0:T(8,128)(2,1)S(1)}, u32[]{:S(2)}, u32[]{:S(2)}) %collective-permute-start.1) | collective-permute-done | bytes 65568 | tf_op jit(solution)/shard_map/ppermute | solution.py:20
  22.0 2.2 %collective-permute-done.3.refs_5_ = bf16[256,128]{1,0:T(8,128)(2,1)S(1)} collective-permute-done((bf16[256,128]{1,0:T(8,128)(2,1)S(1)}, bf16[256,128]{1,0:T(8,128)(2,1)S(1)}, u32[]{:S(2)}, u32[]{:S(2)}) %collective-permute-start.3) | collective-permute-done | bytes 65568 | tf_op jit(solution)/shard_map/ppermute | solution.py:20
  25.1 27.1 %collective-permute-done.5.refs_8_ = bf16[64,128,128]{2,1,0:T(8,128)(2,1)} collective-permute-done((bf16[64,128,128]{2,1,0:T(8,128)(2,1)}, bf16[64,128,128]{2,1,0:T(8,128)(2,1)}, u32[]{:S(2)}, u32[]{:S(2)}) %collective-permute-start.5) | collective-permute-done | bytes 2097184 | tf_op jit(solution)/shard_map/ppermute | solution.py:25
  52.2 1.8 fusion.2
  56.1 2.2 %shard_map.60 = (bf16[48,128,128]{2,1,0:T(8,128)(2,1)}, bf16[16,128,128]{2,1,0:T(8,128)(2,1)S(1)}) custom-call(bf16[4,64,128,128]{3,2,1,0:T(8,128)(2,1)} %refs_6_.9), custom_call_target="tpu_custom_call" | custom-call | tf_op jit(solution)/shard_map/pallas_call | solution.py:52
  58.4 2.0 %collective-permute-start.23 = (bf16[48,128,128]{2,1,0:T(8,128)(2,1)}, bf16[48,128,128]{2,1,0:T(8,128)(2,1)S(1)}, u32[]{:S(2)}, u32[]{:S(2)}) collective-permute-start(bf16[48,128,128]{2,1,0:T(8,128)(2,1)} %get-tuple-element.59), channel_id=1, source_target_pairs={{0,2},{1,3},{2,0},{3,1},{4,6},{5,7},{6,4},{7,5},{8,10},{9,11},{10,... | collective-permute-start | bytes 4718600 | tf_op jit(solution)/shard_map/ppermute | solution.py:25
  60.4 11.3 %shard_map.57 = (bf16[64,256,128]{2,1,0:T(8,128)(2,1)}, bf16[256,128]{1,0:T(8,128)(2,1)S(1)}, bf16[256,128]{1,0:T(8,128)(2,1)S(1)}, bf16[256,128]{1,0:T(8,128)(2,1)S(1)}, bf16[256,128]{1,0:T(8,128)(2,1)S(1)}) custom-call(s32[1040]{0:T(1024)S(1)} %constant_dynamic-update-slice_fusion.table.refs_0_, bf16[256,8192]{1,0:T(8,128)(2,1)} %refs_1_.1, ...), custom_call_target="tpu_custom_call" | custom-call | tf_op jit(solution)/shard_map/pallas_call | solution.py:211
  74.8 2.6 %collective-permute-start.13 = (bf16[256,128]{1,0:T(8,128)(2,1)S(1)}, bf16[256,128]{1,0:T(8,128)(2,1)S(1)}, u32[]{:S(2)}, u32[]{:S(2)}) collective-permute-start(bf16[256,128]{1,0:T(8,128)(2,1)S(1)} %get-tuple-element.51), channel_id=1, source_target_pairs={{16,0},{20,4},{24,8},{28,12},{0,16},{4,20},{8,24},{12,28},{17,1},{... | collective-permute-start | bytes 196616 | tf_op jit(solution)/shard_map/ppermute | solution.py:20
  77.8 3.3 %collective-permute-start.12 = (bf16[256,128]{1,0:T(8,128)(2,1)S(1)}, bf16[256,128]{1,0:T(8,128)(2,1)S(1)}, u32[]{:S(2)}, u32[]{:S(2)}) collective-permute-start(bf16[256,128]{1,0:T(8,128)(2,1)S(1)} %get-tuple-element.50), channel_id=1, source_target_pairs={{4,0},{8,4},{12,8},{16,12},{20,16},{24,20},{28,24},{0,28},{5,1},{9... | collective-permute-start | bytes 196616 | tf_op jit(solution)/shard_map/ppermute | solution.py:20
  81.1 16.0 %collective-permute-done.14.refs_8_ = bf16[64,128,128]{2,1,0:T(8,128)(2,1)S(1)} collective-permute-done((bf16[64,128,128]{2,1,0:T(8,128)(2,1)}, bf16[64,128,128]{2,1,0:T(8,128)(2,1)S(1)}, u32[]{:S(2)}, u32[]{:S(2)}) %collective-permute-start.14) | collective-permute-done | bytes 2097184 | tf_op jit(solution)/shard_map/ppermute | solution.py:25
  99.2 1.9 collective-permute-start.24
  101.5 11.1 %shard_map.59 = (bf16[64,256,128]{2,1,0:T(8,128)(2,1)}, bf16[256,128]{1,0:T(8,128)(2,1)S(1)}, bf16[256,128]{1,0:T(8,128)(2,1)S(1)}, bf16[256,128]{1,0:T(8,128)(2,1)S(1)}, bf16[256,128]{1,0:T(8,128)(2,1)S(1)}) custom-call(s32[1040]{0:T(1024)S(1)} %constant_dynamic-update-slice_fusion.table.refs_0_, bf16[64,256,128]{2,1,0:T(8,128)(2,1)} %get-tuple-element.46.refs_1_, ...), custom_call_target="tpu_custom_call" | custom-call | tf_op jit(solution)/shard_map/pallas_call | solution.py:211
  112.5 2.1 %collective-permute-start.20 = (bf16[256,128]{1,0:T(8,128)(2,1)S(1)}, bf16[256,128]{1,0:T(8,128)(2,1)S(1)}, u32[]{:S(2)}, u32[]{:S(2)}) collective-permute-start(bf16[256,128]{1,0:T(8,128)(2,1)S(1)} %get-tuple-element.55), channel_id=1, source_target_pairs={{24,0},{28,4},{0,8},{4,12},{8,16},{12,20},{16,24},{20,28},{25,1},{... | collective-permute-start | bytes 196616 | tf_op jit(solution)/shard_map/ppermute | solution.py:20
  116.1 2.6 %collective-permute-start.22 = (bf16[256,128]{1,0:T(8,128)(2,1)S(1)}, bf16[256,128]{1,0:T(8,128)(2,1)S(1)}, u32[]{:S(2)}, u32[]{:S(2)}) collective-permute-start(bf16[256,128]{1,0:T(8,128)(2,1)S(1)} %get-tuple-element.58), channel_id=1, source_target_pairs={{16,0},{20,4},{24,8},{28,12},{0,16},{4,20},{8,24},{12,28},{17,1},{... | collective-permute-start | bytes 196616 | tf_op jit(solution)/shard_map/ppermute | solution.py:20
  119.0 3.4 %collective-permute-start.21 = (bf16[256,128]{1,0:T(8,128)(2,1)S(1)}, bf16[256,128]{1,0:T(8,128)(2,1)S(1)}, u32[]{:S(2)}, u32[]{:S(2)}) collective-permute-start(bf16[256,128]{1,0:T(8,128)(2,1)S(1)} %get-tuple-element.57), channel_id=1, source_target_pairs={{4,0},{8,4},{12,8},{16,12},{20,16},{24,20},{28,24},{0,28},{5,1},{9... | collective-permute-start | bytes 196616 | tf_op jit(solution)/shard_map/ppermute | solution.py:20
  122.4 2.1 %shard_map.62 = (bf16[32,128,128]{2,1,0:T(8,128)(2,1)}, bf16[16,128,128]{2,1,0:T(8,128)(2,1)S(1)}, bf16[16,128,128]{2,1,0:T(8,128)(2,1)S(1)}) custom-call(bf16[4,64,128,128]{3,2,1,0:T(8,128)(2,1)} %refs_6_.9), custom_call_target="tpu_custom_call" | custom-call | tf_op jit(solution)/shard_map/pallas_call | solution.py:52
  124.5 6.3 %collective-permute-done.23.refs_8_ = bf16[48,128,128]{2,1,0:T(8,128)(2,1)S(1)} collective-permute-done((bf16[48,128,128]{2,1,0:T(8,128)(2,1)}, bf16[48,128,128]{2,1,0:T(8,128)(2,1)S(1)}, u32[]{:S(2)}, u32[]{:S(2)}) %collective-permute-start.23) | collective-permute-done | bytes 1572896 | tf_op jit(solution)/shard_map/ppermute | solution.py:25
  130.8 1.9 collective-permute-start.34
  133.6 8.5 %collective-permute-done.24.refs_9_ = bf16[16,128,128]{2,1,0:T(8,128)(2,1)S(1)} collective-permute-done((bf16[16,128,128]{2,1,0:T(8,128)(2,1)S(1)}, bf16[16,128,128]{2,1,0:T(8,128)(2,1)S(1)}, u32[]{:S(2)}, u32[]{:S(2)}) %collective-permute-start.24) | collective-permute-done | bytes 524320 | tf_op jit(solution)/shard_map/ppermute | solution.py:25
  142.0 1.9 collective-permute-start.35
  144.0 11.0 %shard_map.61 = (bf16[64,256,128]{2,1,0:T(8,128)(2,1)}, bf16[256,128]{1,0:T(8,128)(2,1)S(1)}, bf16[256,128]{1,0:T(8,128)(2,1)S(1)}, bf16[256,128]{1,0:T(8,128)(2,1)S(1)}, bf16[256,128]{1,0:T(8,128)(2,1)S(1)}) custom-call(s32[1040]{0:T(1024)S(1)} %constant_dynamic-update-slice_fusion.table.refs_0_, bf16[64,256,128]{2,1,0:T(8,128)(2,1)} %get-tuple-element.53.refs_1_, ...), custom_call_target="tpu_custom_call" | custom-call | tf_op jit(solution)/shard_map/pallas_call | solution.py:211
  155.0 2.0 %collective-permute-start.30 = (bf16[256,128]{1,0:T(8,128)(2,1)S(1)}, bf16[256,128]{1,0:T(8,128)(2,1)S(1)}, u32[]{:S(2)}, u32[]{:S(2)}) collective-permute-start(bf16[256,128]{1,0:T(8,128)(2,1)S(1)} %get-tuple-element.65), channel_id=1, source_target_pairs={{24,0},{28,4},{0,8},{4,12},{8,16},{12,20},{16,24},{20,28},{25,1},{... | collective-permute-start | bytes 196616 | tf_op jit(solution)/shard_map/ppermute | solution.py:20
  158.6 2.6 %collective-permute-start.32 = (bf16[256,128]{1,0:T(8,128)(2,1)S(1)}, bf16[256,128]{1,0:T(8,128)(2,1)S(1)}, u32[]{:S(2)}, u32[]{:S(2)}) collective-permute-start(bf16[256,128]{1,0:T(8,128)(2,1)S(1)} %get-tuple-element.68), channel_id=1, source_target_pairs={{16,0},{20,4},{24,8},{28,12},{0,16},{4,20},{8,24},{12,28},{17,1},{... | collective-permute-start | bytes 196616 | tf_op jit(solution)/shard_map/ppermute | solution.py:20
  161.5 3.4 %collective-permute-start.31 = (bf16[256,128]{1,0:T(8,128)(2,1)S(1)}, bf16[256,128]{1,0:T(8,128)(2,1)S(1)}, u32[]{:S(2)}, u32[]{:S(2)}) collective-permute-start(bf16[256,128]{1,0:T(8,128)(2,1)S(1)} %get-tuple-element.67), channel_id=1, source_target_pairs={{4,0},{8,4},{12,8},{16,12},{20,16},{24,20},{28,24},{0,28},{5,1},{9... | collective-permute-start | bytes 196616 | tf_op jit(solution)/shard_map/ppermute | solution.py:20
  168.9 6.8 %collective-permute-done.35.refs_9_ = bf16[16,128,128]{2,1,0:T(8,128)(2,1)S(1)} collective-permute-done((bf16[16,128,128]{2,1,0:T(8,128)(2,1)S(1)}, bf16[16,128,128]{2,1,0:T(8,128)(2,1)S(1)}, u32[]{:S(2)}, u32[]{:S(2)}) %collective-permute-start.35) | collective-permute-done | bytes 524320 | tf_op jit(solution)/shard_map/ppermute | solution.py:25
  177.8 9.8 %shard_map.63.refs_11_ = bf16[256,8192]{1,0:T(8,128)(2,1)} custom-call(s32[1040]{0:T(1024)S(1)} %constant_dynamic-update-slice_fusion.table.refs_0_, bf16[64,256,128]{2,1,0:T(8,128)(2,1)} %get-tuple-element.63.refs_1_, bf16[256,128]{1,0:T(8,128)(2,1)S(1)} %collective-permute-done.29.refs_2_, bf16[256,128]{1,0:T(8,128)(2,1)S(1)} %collective-permute-done.30.refs_3_, ...), custom_call_target="tpu_custom_call" | custom-call | tf_op jit(solution)/shard_map/pallas_call | solution.py:211
  187.8 1.8 collective-permute-done.40.refs_9_
  189.5 5.2 %shard_map.64 = bf16[256,8192]{1,0:T(8,128)(2,1)} custom-call(s32[1040]{0:T(1024)S(1)} %constant_dynamic-update-slice_fusion.table.refs_0_, bf16[64,256,128]{2,1,0:T(8,128)(2,1)S(1)} %copy-done.2, bf16[256,128]{1,0:T(8,128)(2,1)S(1)} %collective-permute-done.29.refs_2_, ...), custom_call_target="tpu_custom_call", output_to_operand_aliasing={{}: (11, {})} | custom-call | tf_op jit(solution)/shard_map/pallas_call | solution.py:211
  (87 shorter events, 29.3 us)
Async XLA Ops:
  0.0 60.4 %collective-permute-start.4 = (bf16[4,64,128,128]{3,2,1,0:T(8,128)(2,1)}, bf16[4,64,128,128]{3,2,1,0:T(8,128)(2,1)}, u32[]{:S(2)}, u32[]{:S(2)}) collective-permute-start(bf16[4,64,128,128]{3,2,1,0:T(8,128)(2,1)} %refs_6_.9), channel_id=1, source_target_pairs={{0,1},{1,0},{2,3},{3,2},{4,5},{5,4},{6,7},{7,6},{8,9},{9,8},{10,11... | collective-permute-start | bytes 25165832 | tf_op jit(solution)/shard_map/ppermute | solution.py:25
  2.9 49.4 %collective-permute-start.5 = (bf16[64,128,128]{2,1,0:T(8,128)(2,1)}, bf16[64,128,128]{2,1,0:T(8,128)(2,1)}, u32[]{:S(2)}, u32[]{:S(2)}) collective-permute-start(bf16[64,128,128]{2,1,0:T(8,128)(2,1)} %shard_map.56), channel_id=1, source_target_pairs={{0,2},{1,3},{2,0},{3,1},{4,6},{5,7},{6,4},{7,5},{8,10},{9,11},{10,... | collective-permute-start | bytes 6291464 | tf_op jit(solution)/shard_map/ppermute | solution.py:25
  7.9 89.1 %collective-permute-start.14 = (bf16[64,128,128]{2,1,0:T(8,128)(2,1)}, bf16[64,128,128]{2,1,0:T(8,128)(2,1)S(1)}, u32[]{:S(2)}, u32[]{:S(2)}) collective-permute-start(bf16[64,128,128]{2,1,0:T(8,128)(2,1)} %shard_map.58), channel_id=1, source_target_pairs={{0,2},{1,3},{2,0},{3,1},{4,6},{5,7},{6,4},{7,5},{8,10},{9,11},{10,... | collective-permute-start | bytes 6291464 | tf_op jit(solution)/shard_map/ppermute | solution.py:25
  11.8 6.4 %collective-permute-start.1 = (bf16[256,128]{1,0:T(8,128)(2,1)S(1)}, bf16[256,128]{1,0:T(8,128)(2,1)S(1)}, u32[]{:S(2)}, u32[]{:S(2)}) collective-permute-start(bf16[256,128]{1,0:T(8,128)(2,1)S(1)} %get-tuple-element.41), channel_id=1, source_target_pairs={{24,0},{28,4},{0,8},{4,12},{8,16},{12,20},{16,24},{20,28},{25,1},{... | collective-permute-start | bytes 196616 | tf_op jit(solution)/shard_map/ppermute | solution.py:20
  13.9 7.0 %collective-permute-start = (bf16[256,128]{1,0:T(8,128)(2,1)S(1)}, bf16[256,128]{1,0:T(8,128)(2,1)S(1)}, u32[]{:S(2)}, u32[]{:S(2)}) collective-permute-start(bf16[256,128]{1,0:T(8,128)(2,1)S(1)} %get-tuple-element.40), channel_id=1, source_target_pairs={{28,0},{0,4},{4,8},{8,12},{12,16},{16,20},{20,24},{24,28},{29,1},{... | collective-permute-start | bytes 196616 | tf_op jit(solution)/shard_map/ppermute | solution.py:20
  18.2 6.0 %collective-permute-start.3 = (bf16[256,128]{1,0:T(8,128)(2,1)S(1)}, bf16[256,128]{1,0:T(8,128)(2,1)S(1)}, u32[]{:S(2)}, u32[]{:S(2)}) collective-permute-start(bf16[256,128]{1,0:T(8,128)(2,1)S(1)} %get-tuple-element.44), channel_id=1, source_target_pairs={{16,0},{20,4},{24,8},{28,12},{0,16},{4,20},{8,24},{12,28},{17,1},{... | collective-permute-start | bytes 196616 | tf_op jit(solution)/shard_map/ppermute | solution.py:20
  20.8 4.3 %collective-permute-start.2 = (bf16[256,128]{1,0:T(8,128)(2,1)S(1)}, bf16[256,128]{1,0:T(8,128)(2,1)S(1)}, u32[]{:S(2)}, u32[]{:S(2)}) collective-permute-start(bf16[256,128]{1,0:T(8,128)(2,1)S(1)} %get-tuple-element.43), channel_id=1, source_target_pairs={{4,0},{8,4},{12,8},{16,12},{20,16},{24,20},{28,24},{0,28},{5,1},{9... | collective-permute-start | bytes 196616 | tf_op jit(solution)/shard_map/ppermute | solution.py:20
  54.1 4.3 %collective-permute-start.7 = (bf16[16,128,128]{2,1,0:T(8,128)(2,1)S(1)}, bf16[16,128,128]{2,1,0:T(8,128)(2,1)S(1)}, u32[]{:S(2)}, u32[]{:S(2)}) collective-permute-start(bf16[16,128,128]{2,1,0:T(8,128)(2,1)S(1)} %get-tuple-element.81), channel_id=1, source_target_pairs={{0,1},{1,0},{2,3},{3,2},{4,5},{5,4},{6,7},{7,6},{8,9},{9,8},{10,11... | collective-permute-start | bytes 1572872 | tf_op jit(solution)/shard_map/ppermute | solution.py:25
  54.6 5.8 %collective-permute-start.8 = (bf16[16,128,128]{2,1,0:T(8,128)(2,1)S(1)}, bf16[16,128,128]{2,1,0:T(8,128)(2,1)S(1)}, u32[]{:S(2)}, u32[]{:S(2)}) collective-permute-start(bf16[16,128,128]{2,1,0:T(8,128)(2,1)S(1)} %get-tuple-element.80), channel_id=1, source_target_pairs={{0,1},{1,0},{2,3},{3,2},{4,5},{5,4},{6,7},{7,6},{8,9},{9,8},{10,11... | collective-permute-start | bytes 1572872 | tf_op jit(solution)/shard_map/ppermute | solution.py:25
  56.0 4.4 %collective-permute-start.9 = (bf16[16,128,128]{2,1,0:T(8,128)(2,1)S(1)}, bf16[16,128,128]{2,1,0:T(8,128)(2,1)S(1)}, u32[]{:S(2)}, u32[]{:S(2)}) collective-permute-start(bf16[16,128,128]{2,1,0:T(8,128)(2,1)S(1)} %get-tuple-element.79), channel_id=1, source_target_pairs={{0,1},{1,0},{2,3},{3,2},{4,5},{5,4},{6,7},{7,6},{8,9},{9,8},{10,11... | collective-permute-start | bytes 1572872 | tf_op jit(solution)/shard_map/ppermute | solution.py:25
  58.4 72.4 %collective-permute-start.23 = (bf16[48,128,128]{2,1,0:T(8,128)(2,1)}, bf16[48,128,128]{2,1,0:T(8,128)(2,1)S(1)}, u32[]{:S(2)}, u32[]{:S(2)}) collective-permute-start(bf16[48,128,128]{2,1,0:T(8,128)(2,1)} %get-tuple-element.59), channel_id=1, source_target_pairs={{0,2},{1,3},{2,0},{3,1},{4,6},{5,7},{6,4},{7,5},{8,10},{9,11},{10,... | collective-permute-start | bytes 4718600 | tf_op jit(solution)/shard_map/ppermute | solution.py:25
  71.7 6.1 %collective-permute-start.11 = (bf16[256,128]{1,0:T(8,128)(2,1)S(1)}, bf16[256,128]{1,0:T(8,128)(2,1)S(1)}, u32[]{:S(2)}, u32[]{:S(2)}) collective-permute-start(bf16[256,128]{1,0:T(8,128)(2,1)S(1)} %get-tuple-element.48), channel_id=1, source_target_pairs={{24,0},{28,4},{0,8},{4,12},{8,16},{12,20},{16,24},{20,28},{25,1},{... | collective-permute-start | bytes 196616 | tf_op jit(solution)/shard_map/ppermute | solution.py:20
  73.3 23.8 %collective-permute-start.10 = (bf16[256,128]{1,0:T(8,128)(2,1)S(1)}, bf16[256,128]{1,0:T(8,128)(2,1)S(1)}, u32[]{:S(2)}, u32[]{:S(2)}) collective-permute-start(bf16[256,128]{1,0:T(8,128)(2,1)S(1)} %get-tuple-element.47), channel_id=1, source_target_pairs={{28,0},{0,4},{4,8},{8,12},{12,16},{16,20},{20,24},{24,28},{29,1},{... | collective-permute-start | bytes 196616 | tf_op jit(solution)/shard_map/ppermute | solution.py:20
  74.8 22.2 %collective-permute-start.13 = (bf16[256,128]{1,0:T(8,128)(2,1)S(1)}, bf16[256,128]{1,0:T(8,128)(2,1)S(1)}, u32[]{:S(2)}, u32[]{:S(2)}) collective-permute-start(bf16[256,128]{1,0:T(8,128)(2,1)S(1)} %get-tuple-element.51), channel_id=1, source_target_pairs={{16,0},{20,4},{24,8},{28,12},{0,16},{4,20},{8,24},{12,28},{17,1},{... | collective-permute-start | bytes 196616 | tf_op jit(solution)/shard_map/ppermute | solution.py:20
  77.8 19.3 %collective-permute-start.12 = (bf16[256,128]{1,0:T(8,128)(2,1)S(1)}, bf16[256,128]{1,0:T(8,128)(2,1)S(1)}, u32[]{:S(2)}, u32[]{:S(2)}) collective-permute-start(bf16[256,128]{1,0:T(8,128)(2,1)S(1)} %get-tuple-element.50), channel_id=1, source_target_pairs={{4,0},{8,4},{12,8},{16,12},{20,16},{24,20},{28,24},{0,28},{5,1},{9... | collective-permute-start | bytes 196616 | tf_op jit(solution)/shard_map/ppermute | solution.py:20
  99.2 42.8 %collective-permute-start.24 = (bf16[16,128,128]{2,1,0:T(8,128)(2,1)S(1)}, bf16[16,128,128]{2,1,0:T(8,128)(2,1)S(1)}, u32[]{:S(2)}, u32[]{:S(2)}) collective-permute-start(bf16[16,128,128]{2,1,0:T(8,128)(2,1)S(1)} %get-tuple-element.61), channel_id=1, source_target_pairs={{0,2},{1,3},{2,0},{3,1},{4,6},{5,7},{6,4},{7,5},{8,10},{9,11},{10,... | collective-permute-start | bytes 1572872 | tf_op jit(solution)/shard_map/ppermute | solution.py:25
  112.5 6.5 %collective-permute-start.20 = (bf16[256,128]{1,0:T(8,128)(2,1)S(1)}, bf16[256,128]{1,0:T(8,128)(2,1)S(1)}, u32[]{:S(2)}, u32[]{:S(2)}) collective-permute-start(bf16[256,128]{1,0:T(8,128)(2,1)S(1)} %get-tuple-element.55), channel_id=1, source_target_pairs={{24,0},{28,4},{0,8},{4,12},{8,16},{12,20},{16,24},{20,28},{25,1},{... | collective-permute-start | bytes 196616 | tf_op jit(solution)/shard_map/ppermute | solution.py:20
  114.6 18.1 %collective-permute-start.19 = (bf16[256,128]{1,0:T(8,128)(2,1)S(1)}, bf16[256,128]{1,0:T(8,128)(2,1)S(1)}, u32[]{:S(2)}, u32[]{:S(2)}) collective-permute-start(bf16[256,128]{1,0:T(8,128)(2,1)S(1)} %get-tuple-element.54), channel_id=1, source_target_pairs={{28,0},{0,4},{4,8},{8,12},{12,16},{16,20},{20,24},{24,28},{29,1},{... | collective-permute-start | bytes 196616 | tf_op jit(solution)/shard_map/ppermute | solution.py:20
  116.1 16.6 %collective-permute-start.22 = (bf16[256,128]{1,0:T(8,128)(2,1)S(1)}, bf16[256,128]{1,0:T(8,128)(2,1)S(1)}, u32[]{:S(2)}, u32[]{:S(2)}) collective-permute-start(bf16[256,128]{1,0:T(8,128)(2,1)S(1)} %get-tuple-element.58), channel_id=1, source_target_pairs={{16,0},{20,4},{24,8},{28,12},{0,16},{4,20},{8,24},{12,28},{17,1},{... | collective-permute-start | bytes 196616 | tf_op jit(solution)/shard_map/ppermute | solution.py:20
  119.0 13.7 %collective-permute-start.21 = (bf16[256,128]{1,0:T(8,128)(2,1)S(1)}, bf16[256,128]{1,0:T(8,128)(2,1)S(1)}, u32[]{:S(2)}, u32[]{:S(2)}) collective-permute-start(bf16[256,128]{1,0:T(8,128)(2,1)S(1)} %get-tuple-element.57), channel_id=1, source_target_pairs={{4,0},{8,4},{12,8},{16,12},{20,16},{24,20},{28,24},{0,28},{5,1},{9... | collective-permute-start | bytes 196616 | tf_op jit(solution)/shard_map/ppermute | solution.py:20
  130.8 34.1 %collective-permute-start.34 = (bf16[32,128,128]{2,1,0:T(8,128)(2,1)}, bf16[32,128,128]{2,1,0:T(8,128)(2,1)S(1)}, u32[]{:S(2)}, u32[]{:S(2)}) collective-permute-start(bf16[32,128,128]{2,1,0:T(8,128)(2,1)} %get-tuple-element.70), channel_id=1, source_target_pairs={{0,2},{1,3},{2,0},{3,1},{4,6},{5,7},{6,4},{7,5},{8,10},{9,11},{10,... | collective-permute-start | bytes 3145736 | tf_op jit(solution)/shard_map/ppermute | solution.py:25
  132.9 9.1 %collective-permute-start.25 = (bf16[16,128,128]{2,1,0:T(8,128)(2,1)S(1)}, bf16[16,128,128]{2,1,0:T(8,128)(2,1)S(1)}, u32[]{:S(2)}, u32[]{:S(2)}) collective-permute-start(bf16[16,128,128]{2,1,0:T(8,128)(2,1)S(1)} %get-tuple-element.85), channel_id=1, source_target_pairs={{0,1},{1,0},{2,3},{3,2},{4,5},{5,4},{6,7},{7,6},{8,9},{9,8},{10,11... | collective-permute-start | bytes 1572872 | tf_op jit(solution)/shard_map/ppermute | solution.py:25
  133.0 11.0 %collective-permute-start.26 = (bf16[16,128,128]{2,1,0:T(8,128)(2,1)S(1)}, bf16[16,128,128]{2,1,0:T(8,128)(2,1)S(1)}, u32[]{:S(2)}, u32[]{:S(2)}) collective-permute-start(bf16[16,128,128]{2,1,0:T(8,128)(2,1)S(1)} %get-tuple-element.84), channel_id=1, source_target_pairs={{0,1},{1,0},{2,3},{3,2},{4,5},{5,4},{6,7},{7,6},{8,9},{9,8},{10,11... | collective-permute-start | bytes 1572872 | tf_op jit(solution)/shard_map/ppermute | solution.py:25
  133.5 10.5 %collective-permute-start.27 = (bf16[16,128,128]{2,1,0:T(8,128)(2,1)S(1)}, bf16[16,128,128]{2,1,0:T(8,128)(2,1)S(1)}, u32[]{:S(2)}, u32[]{:S(2)}) collective-permute-start(bf16[16,128,128]{2,1,0:T(8,128)(2,1)S(1)} %get-tuple-element.83), channel_id=1, source_target_pairs={{0,1},{1,0},{2,3},{3,2},{4,5},{5,4},{6,7},{7,6},{8,9},{9,8},{10,11... | collective-permute-start | bytes 1572872 | tf_op jit(solution)/shard_map/ppermute | solution.py:25
  142.0 33.7 %collective-permute-start.35 = (bf16[16,128,128]{2,1,0:T(8,128)(2,1)S(1)}, bf16[16,128,128]{2,1,0:T(8,128)(2,1)S(1)}, u32[]{:S(2)}, u32[]{:S(2)}) collective-permute-start(bf16[16,128,128]{2,1,0:T(8,128)(2,1)S(1)} %get-tuple-element.72), channel_id=1, source_target_pairs={{0,2},{1,3},{2,0},{3,1},{4,6},{5,7},{6,4},{7,5},{8,10},{9,11},{10,... | collective-permute-start | bytes 1572872 | tf_op jit(solution)/shard_map/ppermute | solution.py:25
  155.0 6.4 %collective-permute-start.30 = (bf16[256,128]{1,0:T(8,128)(2,1)S(1)}, bf16[256,128]{1,0:T(8,128)(2,1)S(1)}, u32[]{:S(2)}, u32[]{:S(2)}) collective-permute-start(bf16[256,128]{1,0:T(8,128)(2,1)S(1)} %get-tuple-element.65), channel_id=1, source_target_pairs={{24,0},{28,4},{0,8},{4,12},{8,16},{12,20},{16,24},{20,28},{25,1},{... | collective-permute-start | bytes 196616 | tf_op jit(solution)/shard_map/ppermute | solution.py:20
  157.0 7.8 %collective-permute-start.29 = (bf16[256,128]{1,0:T(8,128)(2,1)S(1)}, bf16[256,128]{1,0:T(8,128)(2,1)S(1)}, u32[]{:S(2)}, u32[]{:S(2)}) collective-permute-start(bf16[256,128]{1,0:T(8,128)(2,1)S(1)} %get-tuple-element.64), channel_id=1, source_target_pairs={{28,0},{0,4},{4,8},{8,12},{12,16},{16,20},{20,24},{24,28},{29,1},{... | collective-permute-start | bytes 196616 | tf_op jit(solution)/shard_map/ppermute | solution.py:20
  158.6 6.6 %collective-permute-start.32 = (bf16[256,128]{1,0:T(8,128)(2,1)S(1)}, bf16[256,128]{1,0:T(8,128)(2,1)S(1)}, u32[]{:S(2)}, u32[]{:S(2)}) collective-permute-start(bf16[256,128]{1,0:T(8,128)(2,1)S(1)} %get-tuple-element.68), channel_id=1, source_target_pairs={{16,0},{20,4},{24,8},{28,12},{0,16},{4,20},{8,24},{12,28},{17,1},{... | collective-permute-start | bytes 196616 | tf_op jit(solution)/shard_map/ppermute | solution.py:20
  161.5 5.3 %collective-permute-start.31 = (bf16[256,128]{1,0:T(8,128)(2,1)S(1)}, bf16[256,128]{1,0:T(8,128)(2,1)S(1)}, u32[]{:S(2)}, u32[]{:S(2)}) collective-permute-start(bf16[256,128]{1,0:T(8,128)(2,1)S(1)} %get-tuple-element.67), channel_id=1, source_target_pairs={{4,0},{8,4},{12,8},{16,12},{20,16},{24,20},{28,24},{0,28},{5,1},{9... | collective-permute-start | bytes 196616 | tf_op jit(solution)/shard_map/ppermute | solution.py:20
  166.9 10.9 %collective-permute-start.36 = (bf16[16,128,128]{2,1,0:T(8,128)(2,1)S(1)}, bf16[16,128,128]{2,1,0:T(8,128)(2,1)S(1)}, u32[]{:S(2)}, u32[]{:S(2)}) collective-permute-start(bf16[16,128,128]{2,1,0:T(8,128)(2,1)S(1)} %get-tuple-element.87), channel_id=1, source_target_pairs={{0,1},{1,0},{2,3},{3,2},{4,5},{5,4},{6,7},{7,6},{8,9},{9,8},{10,11... | collective-permute-start | bytes 1572872 | tf_op jit(solution)/shard_map/ppermute | solution.py:25
  166.9 10.8 %collective-permute-start.37 = (bf16[16,128,128]{2,1,0:T(8,128)(2,1)S(1)}, bf16[16,128,128]{2,1,0:T(8,128)(2,1)S(1)}, u32[]{:S(2)}, u32[]{:S(2)}) collective-permute-start(bf16[16,128,128]{2,1,0:T(8,128)(2,1)S(1)} %get-tuple-element.86), channel_id=1, source_target_pairs={{0,1},{1,0},{2,3},{3,2},{4,5},{5,4},{6,7},{7,6},{8,9},{9,8},{10,11... | collective-permute-start | bytes 1572872 | tf_op jit(solution)/shard_map/ppermute | solution.py:25
  167.4 20.1 %collective-permute-start.33 = (bf16[16,128,128]{2,1,0:T(8,128)(2,1)S(1)}, bf16[16,128,128]{2,1,0:T(8,128)(2,1)S(1)}, u32[]{:S(2)}, u32[]{:S(2)}) collective-permute-start(bf16[16,128,128]{2,1,0:T(8,128)(2,1)S(1)} %get-tuple-element.69), channel_id=1, source_target_pairs={{0,2},{1,3},{2,0},{3,1},{4,6},{5,7},{6,4},{7,5},{8,10},{9,11},{10,... | collective-permute-start | bytes 1572872 | tf_op jit(solution)/shard_map/ppermute | solution.py:25
  (14 other events, 58.3 us)

commit v7 on v6

--- a/solution.py
+++ b/solution.py
@@ -9,8 +9,9 @@
 
 
 TURNS = (3, 1, 0, 2)
-VMEM_LIMIT = 52 * 2**20
-LAYER_LIMIT = 48 * 2**20
+NEIGH = 4
+VMEM_LIMIT = 16 * 2**20
+LAYER_LIMIT = 20 * 2**20
 FREE = pl.CostEstimate(flops=0, bytes_accessed=0, transcendentals=0)
 
 
@@ -25,43 +26,40 @@
     return lax.ppermute(block, "batch", route)
 
 
+def in_hbm(array):
+    return pltpu.with_memory_space_constraint(array, pltpu.HBM)
+
+
+def in_vmem(array):
+    return pltpu.with_memory_space_constraint(array, pltpu.VMEM)
+
+
 def cut(tile_weights, chunks):
     height, width = tile_weights.shape[2:]
-    moves = []
-    for place, (layer, first, count) in enumerate(chunks):
-        step = math.gcd(8, count)
-        moves += [(place, layer, first, start, step) for start in range(0, count, step)]
 
     def kernel(tiles, *refs):
-        targets, (room, arrive, leave) = refs[: len(chunks)], refs[len(chunks) :]
-        inward, outward = [], []
-        for index, (place, layer, first, start, step) in enumerate(moves):
-            here = room.at[index, pl.ds(0, step)]
-            source = tiles.at[layer, pl.ds(first + start, step)]
-            inward.append(pltpu.make_async_copy(source, here, arrive.at[index]))
-            outward.append(pltpu.make_async_copy(here, targets[place].at[pl.ds(start, step)], leave.at[index]))
-        for copy in inward:
+        targets, semaphores = refs[: len(chunks)], refs[len(chunks)]
+        copies = []
+        for place, (layer, first, count) in enumerate(chunks):
+            step = count // math.gcd(4, count)
+            for part, start in enumerate(range(0, count, step)):
+                source = tiles.at[layer, pl.ds(first + start, step)]
+                there = targets[place].at[pl.ds(start, step)]
+                copies.append(pltpu.make_async_copy(source, there, semaphores.at[place, part]))
+        for copy in copies:
             copy.start()
-        for before, after in zip(inward, outward):
-            before.wait()
-            after.start()
-        for copy in outward:
+        for copy in copies:
             copy.wait()
 
-    anywhere = pl.BlockSpec(memory_space=pl.ANY)
     return pl.pallas_call(
         kernel,
-        out_shape=[jax.ShapeDtypeStruct((count, height, width), tile_weights.dtype) for _, _, count in chunks],
-        in_specs=[anywhere],
-        out_specs=[anywhere] * len(chunks),
-        scratch_shapes=[
-            pltpu.VMEM((len(moves), 8, height, width), tile_weights.dtype),
-            pltpu.SemaphoreType.DMA((len(moves),)),
-            pltpu.SemaphoreType.DMA((len(moves),)),
-        ],
+        out_shape=[pltpu.VMEM((count, height, width), tile_weights.dtype) for _, _, count in chunks],
+        in_specs=[pl.BlockSpec(memory_space=pltpu.HBM)],
+        out_specs=[pl.BlockSpec(memory_space=pltpu.VMEM)] * len(chunks),
+        scratch_shapes=[pltpu.SemaphoreType.DMA((len(chunks), 4))],
         compiler_params=pltpu.CompilerParams(vmem_limit_bytes=VMEM_LIMIT),
         cost_estimate=FREE,
-    )(tile_weights)
+    )(in_hbm(tile_weights))
 
 
 def pick(table, place, number, width, activations):
@@ -83,19 +81,20 @@
         out_shape=[jax.ShapeDtypeStruct((rows, width), activations.dtype)] * number,
         grid_spec=pltpu.PrefetchScalarGridSpec(
             num_scalar_prefetch=1,
-            in_specs=[pl.BlockSpec(memory_space=pl.ANY)],
+            in_specs=[pl.BlockSpec(memory_space=pltpu.HBM)],
             out_specs=[pl.BlockSpec(memory_space=pltpu.VMEM)] * number,
             scratch_shapes=[pltpu.SemaphoreType.DMA((number,))],
         ),
         compiler_params=pltpu.CompilerParams(vmem_limit_bytes=VMEM_LIMIT),
         cost_estimate=FREE,
-    )(table, activations)
+    )(table, in_hbm(activations))
 
 
 def run_blocks(layer, first, count, table, sends, pool, arrived, tiles, biases, target, final):
-    fan, neigh, width = len(tiles), len(arrived), arrived[0].shape[1]
+    fan, width = len(tiles), tiles[0].shape[3]
     rows, blocks = pool.shape[-2], biases.shape[1] // width
     columns = pool.ndim == 2
+    fill = bool(arrived) and not columns
     group = math.gcd(8, count)
     held = [source if isinstance(source, list) else [source] for source in tiles]
     step = group
@@ -113,8 +112,13 @@
         if target is not None:
             refs.pop(0)
         result = refs.pop(0)
-        outgoing = [] if final else [refs.pop(0) for _ in arrived]
-        inputs, weights, outputs, in_sems, weight_sems, out_sems, send_sems = refs
+        inputs = refs.pop(0) if fill else pool_ref
+        outgoing = [] if final else [refs.pop(0) for _ in range(neigh)]
+        weights, in_sems, weight_sems = (refs.pop(0) for _ in range(3))
+        if final:
+            outputs, out_sems = (refs.pop(0) for _ in range(2))
+        if columns:
+            inputs = refs.pop(0)
 
         def tile_copy(part, m):
             start = part * step
@@ -129,13 +133,8 @@
             return pltpu.make_async_copy(piece, weights.at[m, pl.ds(start, step)], weight_sems.at[part, m])
 
         def out_copy(part):
-            start = part * group
-            if final:
-                here = outputs.at[:, pl.ds(start * width, group * width)]
-                there = result.at[:, pl.ds((first + start) * width, group * width)]
-            else:
-                here = outputs.at[pl.ds(start, group)]
-                there = result.at[pl.ds(first + start, group)]
+            here = outputs.at[:, pl.ds(part * group * width, group * width)]
+            there = result.at[:, pl.ds((first + part * group) * width, group * width)]
             return pltpu.make_async_copy(here, there, out_sems.at[part])
 
         loads = []
@@ -144,22 +143,14 @@
         if columns:
             for block in range(blocks):
                 loads.append((pool_ref.at[:, pl.ds(block * width, width)], inputs.at[block]))
-        else:
-            share = blocks // 4
-            for start in range(0, blocks, share):
-                loads.append((pool_ref.at[pl.ds(start, share)], inputs.at[pl.ds(start, share)]))
         loads = [pltpu.make_async_copy(*load, in_sems.at[place]) for place, load in enumerate(loads)]
         for copy in loads:
             copy.start()
-        early = min(parts, max(1, 8 // step))
-        for part in range(early):
+        for part in range(parts):
             for m in range(fan):
                 tile_copy(part, m).start()
         for copy in loads:
             copy.wait()
-        for part in range(early, parts):
-            for m in range(fan):
-                tile_copy(part, m).start()
 
         def work(part, _):
             for sub in range(group // step):
@@ -181,55 +172,70 @@
                 if final:
                     outputs[:, pl.ds(pl.multiple_of(block * width, width), width)] = summed
                 else:
-                    outputs[block] = summed
-            out_copy(part).start()
+                    result[first + block] = summed
+            if final:
+                out_copy(part).start()
             return _
 
         lax.fori_loop(0, count // group, work, None)
-        handed = []
         for slot, there in enumerate(outgoing):
-            handed.append(pltpu.make_async_copy(outputs.at[table[sends + slot]], there, send_sems.at[slot]))
-            handed[-1].start()
-        for copy in handed:
-            copy.wait()
-        for part in range(count // group):
-            out_copy(part).wait()
+            there[...] = result[table[sends + slot]]
+        if final:
+            for part in range(count // group):
+                out_copy(part).wait()
 
     anywhere = pl.BlockSpec(memory_space=pl.ANY)
-    operands = [table, pool, *arrived, *(array for source in held for array in source), biases]
-    in_specs = [anywhere] * (len(operands) - 2) + [pl.BlockSpec(memory_space=pltpu.VMEM)]
+    vmem, hbm = (pl.BlockSpec(memory_space=space) for space in (pltpu.VMEM, pltpu.HBM))
+    neigh = NEIGH
+    operands = [table, in_hbm(pool) if columns else in_vmem(pool), *arrived]
+    in_specs = [hbm if columns else vmem] + [anywhere] * len(arrived)
+    for source in tiles:
+        if isinstance(source, list):
+            operands += source
+            in_specs += [anywhere] * len(source)
+        else:
+            operands.append(in_hbm(source))
+            in_specs.append(hbm)
+    operands.append(biases)
+    in_specs.append(vmem)
     aliases = {}
     if target is not None:
         aliases[len(operands)] = 0
         operands.append(target)
         in_specs.append(anywhere)
-    shape = (rows, blocks * width) if final else (blocks, rows, width)
-    out = (rows, count * width) if final else (count, rows, width)
-    out_shape = [jax.ShapeDtypeStruct(shape, pool.dtype)]
+    if final:
+        out_shape, out_specs = [jax.ShapeDtypeStruct((rows, blocks * width), pool.dtype)], [anywhere]
+    else:
+        out_shape, out_specs = [pltpu.VMEM((blocks + neigh, rows, width), pool.dtype)], [vmem]
+    if fill:
+        aliases[1] = 1
+        out_shape.append(pltpu.VMEM(pool.shape, pool.dtype))
+        out_specs.append(vmem)
     if not final:
         out_shape += [jax.ShapeDtypeStruct((rows, width), pool.dtype)] * neigh
-    result, *outgoing = pl.pallas_call(
-        kernel,
-        out_shape=out_shape,
-        grid_spec=pltpu.PrefetchScalarGridSpec(
-            num_scalar_prefetch=1,
-            in_specs=in_specs,
-            out_specs=[anywhere] * len(out_shape),
-            scratch_shapes=[
-                pltpu.VMEM((blocks + neigh, rows, width), pool.dtype),
-                pltpu.VMEM((fan, count, width, width), tiles[0].dtype),
-                pltpu.VMEM(out, pool.dtype),
-                pltpu.SemaphoreType.DMA((blocks + neigh,)),
-                pltpu.SemaphoreType.DMA((parts, fan)),
-                pltpu.SemaphoreType.DMA((count // group,)),
-                pltpu.SemaphoreType.DMA((neigh,)),
-            ],
-        ),
-        input_output_aliases=aliases,
-        compiler_params=pltpu.CompilerParams(vmem_limit_bytes=LAYER_LIMIT),
-        cost_estimate=FREE,
-    )(*operands)
-    return result, outgoing
+        out_specs += [vmem] * neigh
+    scratch = [
+        pltpu.VMEM((fan, count, width, width), tiles[0].dtype),
+        pltpu.SemaphoreType.DMA((blocks + neigh,)),
+        pltpu.SemaphoreType.DMA((parts, fan)),
+    ]
+    if final:
+        scratch += [pltpu.VMEM((rows, count * width), pool.dtype), pltpu.SemaphoreType.DMA((count // group,))]
+    if columns:
+        scratch.append(pltpu.VMEM((blocks + neigh, rows, width), pool.dtype))
+    results = list(
+        pl.pallas_call(
+            kernel,
+            out_shape=out_shape,
+            grid_spec=pltpu.PrefetchScalarGridSpec(
+                num_scalar_prefetch=1, in_specs=in_specs, out_specs=out_specs, scratch_shapes=scratch
+            ),
+            input_output_aliases=aliases,
+            compiler_params=pltpu.CompilerParams(vmem_limit_bytes=LAYER_LIMIT),
+            cost_estimate=FREE,
+        )(*operands)
+    )
+    return results.pop(0), results.pop(0) if fill else pool, results
 
 
 def body(activations, tile_weights, biases, source_codes, send_list):
@@ -274,15 +280,14 @@
     spread(near, 0)
 
     current = activations
-    neigh = len(neighbor_offsets)
-    outgoing = pick(table, codes.size, neigh, width, activations)
+    outgoing = pick(table, codes.size, NEIGH, width, activations)
     before = None
     for layer, sizes, pieces in shares:
         if layer != before:
-            arrived = [None] * neigh
+            arrived = [None] * NEIGH
             for turn, slot in enumerate(TURNS):
                 block = outgoing[slot]
-                if turn == neigh - 1:
+                if turn == NEIGH - 1:
                     block = lax.optimization_barrier((block, arrived[TURNS[1]]))[0]
                 arrived[slot] = shifted(block, "dom", neighbor_offsets[slot])
             pool, target, first, after = current, None, 0, arrived
@@ -298,10 +303,11 @@
         spread(tiles, far)
         tiles[far] = whole
         count = sum(sizes) * unit
-        sends = codes.size + (layer + 1) * neigh
-        target, outgoing = run_blocks(
+        sends = codes.size + (layer + 1) * NEIGH
+        target, pool, outgoing = run_blocks(
             layer, first, count, table, sends, pool, arrived, tiles, biases, target, layer == last
         )
+        arrived = []
         current, first, after = target, first + count, [target]
     return current
 

time: 195 us -> 194 us (level)
  Pallas kernels: 59.1 us -> 50.6 us
  waiting for transfers between devices: 80.8 us -> 88.2 us
    ppermute x25, waiting for transfers between devices: 70.4 us -> 79.6 us  [swapped(): return lax.ppermute(block, 'batch', route)]
    pallas_call x5, Pallas kernels: 48.3 us -> 40 us  [run_blocks(): pl.pallas_call(kernel, out_shape=out_shape, grid_spec=pltpu.PrefetchScala...]
  transfers between devices with their start and end apart: 41 -> 41, of which waited for: 20 -> 20; matrix products, arithmetic and copies ran while one was open for 2% -> 2% of each run, Pallas kernels for 28% -> 24%
where the time goes in v7:
time: 194 us
  waiting for transfers between devices  88.2 us (45%)
  Pallas kernels  50.6 us (26%)
  starting transfers between devices  50.4 us (26%)
  local copies, waits for them, and re-layouts  3.54 us (2%)
    ppermute x25, waiting for transfers between devices, swapped(): return lax.ppermute(block, 'batch', route)  79.6 us
    pallas_call x5, Pallas kernels, run_blocks(): pl.pallas_call(kernel, out_shape=out_shape, grid_spec=pltpu.PrefetchScala...  40 us
    ppermute x16, starting transfers between devices, shifted(): return lax.ppermute(block, axis, route)  33.9 us
    ppermute x25, starting transfers between devices, swapped(): return lax.ppermute(block, 'batch', route)  16.5 us
    pallas_call x4, Pallas kernels, cut(): pl.pallas_call(kernel, out_shape=[pltpu.VMEM((count, height, width), tile...  8.99 us
    ppermute x16, waiting for transfers between devices, shifted(): return lax.ppermute(block, axis, route)  8.61 us
  transfers between devices with their start and end apart: 41, of which 20 were waited for; matrix products, arithmetic and copies ran while one was open for 2% of the time, Pallas kernels for 24%

profile of v7, /device:TPU:0, one launch (start us, length us, event | category | flops | bytes accessed | tf_op | source)
XLA Modules:
  0.0 193.7 jit_solution(628068566712490964)
XLA Ops:
  0.5 2.9 %shard_map.56 = bf16[64,128,128]{2,1,0:T(8,128)(2,1)} custom-call(bf16[4,64,128,128]{3,2,1,0:T(8,128)(2,1)} %refs_2_.1), custom_call_target="tpu_custom_call" | custom-call | tf_op jit(solution)/shard_map/pallas_call | solution.py:54
  3.3 2.6 %collective-permute-start.5 = (bf16[64,128,128]{2,1,0:T(8,128)(2,1)}, bf16[64,128,128]{2,1,0:T(8,128)(2,1)}, u32[]{:S(2)}, u32[]{:S(2)}) collective-permute-start(bf16[64,128,128]{2,1,0:T(8,128)(2,1)} %shard_map.56), channel_id=1, source_target_pairs={{0,2},{1,3},{2,0},{3,1},{4,6},{5,7},{6,4},{7,5},{8,10},{9,11},{10,... | collective-permute-start | bytes 6291464 | tf_op jit(solution)/shard_map/ppermute | solution.py:26
  5.9 3.0 %shard_map.58 = bf16[64,128,128]{2,1,0:T(8,128)(2,1)} custom-call(bf16[4,64,128,128]{3,2,1,0:T(8,128)(2,1)} %refs_2_.1), custom_call_target="tpu_custom_call" | custom-call | tf_op jit(solution)/shard_map/pallas_call | solution.py:54
  12.7 2.1 %collective-permute-start.1 = (bf16[256,128]{1,0:T(8,128)(2,1)S(1)}, bf16[256,128]{1,0:T(8,128)(2,1)S(1)}, u32[]{:S(2)}, u32[]{:S(2)}) collective-permute-start(bf16[256,128]{1,0:T(8,128)(2,1)S(1)} %get-tuple-element.43), channel_id=1, source_target_pairs={{24,0},{28,4},{0,8},{4,12},{8,16},{12,20},{16,24},{20,28},{25,1},{... | collective-permute-start | bytes 196616 | tf_op jit(solution)/shard_map/ppermute | solution.py:21
  16.3 2.8 %collective-permute-done.1.refs_3_ = bf16[256,128]{1,0:T(8,128)(2,1)S(1)} collective-permute-done((bf16[256,128]{1,0:T(8,128)(2,1)S(1)}, bf16[256,128]{1,0:T(8,128)(2,1)S(1)}, u32[]{:S(2)}, u32[]{:S(2)}) %collective-permute-start.1) | collective-permute-done | bytes 65568 | tf_op jit(solution)/shard_map/ppermute | solution.py:21
  20.1 1.7 collective-permute-done.refs_2_
  22.9 2.2 %collective-permute-done.3.refs_5_ = bf16[256,128]{1,0:T(8,128)(2,1)S(1)} collective-permute-done((bf16[256,128]{1,0:T(8,128)(2,1)S(1)}, bf16[256,128]{1,0:T(8,128)(2,1)S(1)}, u32[]{:S(2)}, u32[]{:S(2)}) %collective-permute-start.3) | collective-permute-done | bytes 65568 | tf_op jit(solution)/shard_map/ppermute | solution.py:21
  26.0 26.7 %collective-permute-done.5.refs_8_ = bf16[64,128,128]{2,1,0:T(8,128)(2,1)} collective-permute-done((bf16[64,128,128]{2,1,0:T(8,128)(2,1)}, bf16[64,128,128]{2,1,0:T(8,128)(2,1)}, u32[]{:S(2)}, u32[]{:S(2)}) %collective-permute-start.5) | collective-permute-done | bytes 2097184 | tf_op jit(solution)/shard_map/ppermute | solution.py:26
  58.1 2.0 %collective-permute-start.23 = (bf16[48,128,128]{2,1,0:T(8,128)(2,1)S(1)}, bf16[48,128,128]{2,1,0:T(8,128)(2,1)S(1)}, u32[]{:S(2)}, u32[]{:S(2)}) collective-permute-start(bf16[48,128,128]{2,1,0:T(8,128)(2,1)S(1)} %get-tuple-element.61), channel_id=1, source_target_pairs={{0,2},{1,3},{2,0},{3,1},{4,6},{5,7},{6,4},{7,5},{8,10},{9,11},{10,... | collective-permute-start | bytes 4718600 | tf_op jit(solution)/shard_map/ppermute | solution.py:26
  60.1 10.1 %shard_map.57 = (bf16[68,256,128]{2,1,0:T(8,128)(2,1)S(1)}, bf16[256,128]{1,0:T(8,128)(2,1)S(1)}, bf16[256,128]{1,0:T(8,128)(2,1)S(1)}, bf16[256,128]{1,0:T(8,128)(2,1)S(1)}, bf16[256,128]{1,0:T(8,128)(2,1)S(1)}) custom-call(s32[1040]{0:T(1024)S(1)} %constant_dynamic-update-slice_fusion.table.refs_0_, bf16[256,8192]{1,0:T(8,128)(2,1)} %refs_1_.1, ...), custom_call_target="tpu_custom_call" | custom-call | tf_op jit(solution)/shard_map/pallas_call | solution.py:227
  73.4 2.6 %collective-permute-start.13 = (bf16[256,128]{1,0:T(8,128)(2,1)S(1)}, bf16[256,128]{1,0:T(8,128)(2,1)S(1)}, u32[]{:S(2)}, u32[]{:S(2)}) collective-permute-start(bf16[256,128]{1,0:T(8,128)(2,1)S(1)} %get-tuple-element.53), channel_id=1, source_target_pairs={{16,0},{20,4},{24,8},{28,12},{0,16},{4,20},{8,24},{12,28},{17,1},{... | collective-permute-start | bytes 196616 | tf_op jit(solution)/shard_map/ppermute | solution.py:21
  76.4 3.3 %collective-permute-start.12 = (bf16[256,128]{1,0:T(8,128)(2,1)S(1)}, bf16[256,128]{1,0:T(8,128)(2,1)S(1)}, u32[]{:S(2)}, u32[]{:S(2)}) collective-permute-start(bf16[256,128]{1,0:T(8,128)(2,1)S(1)} %get-tuple-element.52), channel_id=1, source_target_pairs={{4,0},{8,4},{12,8},{16,12},{20,16},{24,20},{28,24},{0,28},{5,1},{9... | collective-permute-start | bytes 196616 | tf_op jit(solution)/shard_map/ppermute | solution.py:21
  79.6 17.9 %collective-permute-done.14.refs_8_ = bf16[64,128,128]{2,1,0:T(8,128)(2,1)S(1)} collective-permute-done((bf16[64,128,128]{2,1,0:T(8,128)(2,1)}, bf16[64,128,128]{2,1,0:T(8,128)(2,1)S(1)}, u32[]{:S(2)}, u32[]{:S(2)}) %collective-permute-start.14) | collective-permute-done | bytes 2097184 | tf_op jit(solution)/shard_map/ppermute | solution.py:26
  99.7 1.9 %collective-permute-start.24 = (bf16[16,128,128]{2,1,0:T(8,128)(2,1)S(1)}, bf16[16,128,128]{2,1,0:T(8,128)(2,1)S(1)}, u32[]{:S(2)}, u32[]{:S(2)}) collective-permute-start(bf16[16,128,128]{2,1,0:T(8,128)(2,1)S(1)} %get-tuple-element.63), channel_id=1, source_target_pairs={{0,2},{1,3},{2,0},{3,1},{4,6},{5,7},{6,4},{7,5},{8,10},{9,11},{10,... | collective-permute-start | bytes 1572872 | tf_op jit(solution)/shard_map/ppermute | solution.py:26
  101.9 8.7 %shard_map.59 = (bf16[68,256,128]{2,1,0:T(8,128)(2,1)S(1)}, bf16[68,256,128]{2,1,0:T(8,128)(2,1)S(1)}, bf16[256,128]{1,0:T(8,128)(2,1)S(1)}, bf16[256,128]{1,0:T...) custom-call(s32[1040]{0:T(1024)S(1)} %constant_dynamic-update-slice_, ...), custom_call_target="tpu_custom_call", output_to_operand_aliasing={{1}: (1, {})} | custom-call | tf_op jit(solution)/shard_map/pallas_call | solution.py:227
  110.6 2.1 %collective-permute-start.20 = (bf16[256,128]{1,0:T(8,128)(2,1)S(1)}, bf16[256,128]{1,0:T(8,128)(2,1)S(1)}, u32[]{:S(2)}, u32[]{:S(2)}) collective-permute-start(bf16[256,128]{1,0:T(8,128)(2,1)S(1)} %get-tuple-element.57), channel_id=1, source_target_pairs={{24,0},{28,4},{0,8},{4,12},{8,16},{12,20},{16,24},{20,28},{25,1},{... | collective-permute-start | bytes 196616 | tf_op jit(solution)/shard_map/ppermute | solution.py:21
  114.2 2.6 %collective-permute-start.22 = (bf16[256,128]{1,0:T(8,128)(2,1)S(1)}, bf16[256,128]{1,0:T(8,128)(2,1)S(1)}, u32[]{:S(2)}, u32[]{:S(2)}) collective-permute-start(bf16[256,128]{1,0:T(8,128)(2,1)S(1)} %get-tuple-element.60), channel_id=1, source_target_pairs={{16,0},{20,4},{24,8},{28,12},{0,16},{4,20},{8,24},{12,28},{17,1},{... | collective-permute-start | bytes 196616 | tf_op jit(solution)/shard_map/ppermute | solution.py:21
  117.1 3.4 %collective-permute-start.21 = (bf16[256,128]{1,0:T(8,128)(2,1)S(1)}, bf16[256,128]{1,0:T(8,128)(2,1)S(1)}, u32[]{:S(2)}, u32[]{:S(2)}) collective-permute-start(bf16[256,128]{1,0:T(8,128)(2,1)S(1)} %get-tuple-element.59), channel_id=1, source_target_pairs={{4,0},{8,4},{12,8},{16,12},{20,16},{24,20},{28,24},{0,28},{5,1},{9... | collective-permute-start | bytes 196616 | tf_op jit(solution)/shard_map/ppermute | solution.py:21
  122.1 9.1 %collective-permute-done.23.refs_8_ = bf16[48,128,128]{2,1,0:T(8,128)(2,1)S(1)} collective-permute-done((bf16[48,128,128]{2,1,0:T(8,128)(2,1)S(1)}, bf16[48,128,128]{2,1,0:T(8,128)(2,1)S(1)}, u32[]{:S(2)}, u32[]{:S(2)}) %collective-permute-start.23) | collective-permute-done | bytes 1572896 | tf_op jit(solution)/shard_map/ppermute | solution.py:26
  131.3 1.9 %collective-permute-start.33 = (bf16[32,128,128]{2,1,0:T(8,128)(2,1)S(1)}, bf16[32,128,128]{2,1,0:T(8,128)(2,1)S(1)}, u32[]{:S(2)}, u32[]{:S(2)}) collective-permute-start(bf16[32,128,128]{2,1,0:T(8,128)(2,1)S(1)} %get-tuple-element.71), channel_id=1, source_target_pairs={{0,2},{1,3},{2,0},{3,1},{4,6},{5,7},{6,4},{7,5},{8,10},{9,11},{10,... | collective-permute-start | bytes 3145736 | tf_op jit(solution)/shard_map/ppermute | solution.py:26
  134.0 8.5 %collective-permute-done.24.refs_9_ = bf16[16,128,128]{2,1,0:T(8,128)(2,1)S(1)} collective-permute-done((bf16[16,128,128]{2,1,0:T(8,128)(2,1)S(1)}, bf16[16,128,128]{2,1,0:T(8,128)(2,1)S(1)}, u32[]{:S(2)}, u32[]{:S(2)}) %collective-permute-start.24) | collective-permute-done | bytes 524320 | tf_op jit(solution)/shard_map/ppermute | solution.py:26
  142.5 1.9 %collective-permute-start.34 = (bf16[16,128,128]{2,1,0:T(8,128)(2,1)S(1)}, bf16[16,128,128]{2,1,0:T(8,128)(2,1)S(1)}, u32[]{:S(2)}, u32[]{:S(2)}) collective-permute-start(bf16[16,128,128]{2,1,0:T(8,128)(2,1)S(1)} %get-tuple-element.73), channel_id=1, source_target_pairs={{0,2},{1,3},{2,0},{3,1},{4,6},{5,7},{6,4},{7,5},{8,10},{9,11},{10,... | collective-permute-start | bytes 1572872 | tf_op jit(solution)/shard_map/ppermute | solution.py:26
  144.4 8.7 %shard_map.61 = (bf16[68,256,128]{2,1,0:T(8,128)(2,1)S(1)}, bf16[68,256,128]{2,1,0:T(8,128)(2,1)S(1)}, bf16[256,128]{1,0:T(8,128)(2,1)S(1)}, bf16[256,128]{1,0:T...) custom-call(s32[1040]{0:T(1024)S(1)} %constant_dynamic-update-slice_, ...), custom_call_target="tpu_custom_call", output_to_operand_aliasing={{1}: (1, {})} | custom-call | tf_op jit(solution)/shard_map/pallas_call | solution.py:227
  153.2 2.0 %collective-permute-start.30 = (bf16[256,128]{1,0:T(8,128)(2,1)S(1)}, bf16[256,128]{1,0:T(8,128)(2,1)S(1)}, u32[]{:S(2)}, u32[]{:S(2)}) collective-permute-start(bf16[256,128]{1,0:T(8,128)(2,1)S(1)} %get-tuple-element.67), channel_id=1, source_target_pairs={{24,0},{28,4},{0,8},{4,12},{8,16},{12,20},{16,24},{20,28},{25,1},{... | collective-permute-start | bytes 196616 | tf_op jit(solution)/shard_map/ppermute | solution.py:21
  156.7 2.6 %collective-permute-start.32 = (bf16[256,128]{1,0:T(8,128)(2,1)S(1)}, bf16[256,128]{1,0:T(8,128)(2,1)S(1)}, u32[]{:S(2)}, u32[]{:S(2)}) collective-permute-start(bf16[256,128]{1,0:T(8,128)(2,1)S(1)} %get-tuple-element.70), channel_id=1, source_target_pairs={{16,0},{20,4},{24,8},{28,12},{0,16},{4,20},{8,24},{12,28},{17,1},{... | collective-permute-start | bytes 196616 | tf_op jit(solution)/shard_map/ppermute | solution.py:21
  159.6 3.4 %collective-permute-start.31 = (bf16[256,128]{1,0:T(8,128)(2,1)S(1)}, bf16[256,128]{1,0:T(8,128)(2,1)S(1)}, u32[]{:S(2)}, u32[]{:S(2)}) collective-permute-start(bf16[256,128]{1,0:T(8,128)(2,1)S(1)} %get-tuple-element.69), channel_id=1, source_target_pairs={{4,0},{8,4},{12,8},{16,12},{20,16},{24,20},{28,24},{0,28},{5,1},{9... | collective-permute-start | bytes 196616 | tf_op jit(solution)/shard_map/ppermute | solution.py:21
  163.0 1.9 %collective-permute-done.33.refs_8_ = bf16[32,128,128]{2,1,0:T(8,128)(2,1)S(1)} collective-permute-done((bf16[32,128,128]{2,1,0:T(8,128)(2,1)S(1)}, bf16[32,128,128]{2,1,0:T(8,128)(2,1)S(1)}, u32[]{:S(2)}, u32[]{:S(2)}) %collective-permute-start.33) | collective-permute-done | bytes 1048608 | tf_op jit(solution)/shard_map/ppermute | solution.py:26
  165.7 1.9 %collective-permute-start.39 = (bf16[16,128,128]{2,1,0:T(8,128)(2,1)S(1)}, bf16[16,128,128]{2,1,0:T(8,128)(2,1)S(1)}, u32[]{:S(2)}, u32[]{:S(2)}) collective-permute-start(bf16[16,128,128]{2,1,0:T(8,128)(2,1)S(1)} %get-tuple-element.76), channel_id=1, source_target_pairs={{0,2},{1,3},{2,0},{3,1},{4,6},{5,7},{6,4},{7,5},{8,10},{9,11},{10,... | collective-permute-start | bytes 1572872 | tf_op jit(solution)/shard_map/ppermute | solution.py:26
  167.6 8.6 %collective-permute-done.34.refs_9_ = bf16[16,128,128]{2,1,0:T(8,128)(2,1)S(1)} collective-permute-done((bf16[16,128,128]{2,1,0:T(8,128)(2,1)S(1)}, bf16[16,128,128]{2,1,0:T(8,128)(2,1)S(1)}, u32[]{:S(2)}, u32[]{:S(2)}) %collective-permute-start.34) | collective-permute-done | bytes 524320 | tf_op jit(solution)/shard_map/ppermute | solution.py:26
  178.2 8.0 %shard_map.63 = (bf16[256,8192]{1,0:T(8,128)(2,1)}, bf16[68,256,128]{2,1,0:T(8,128)(2,1)S(1)}) custom-call(s32[1040]{0:T(1024)S(1)} %constant_dynamic-update-slice_fusion.table.refs_0_, bf16[68,256,128]{2,1,0:T(8,128)(2,1)S(1)} %get-tuple-element.65.refs_1_, bf16[256,128]{1,0:T(8,128)(2,1)S(1)} %collective-permute-done.29.refs_2_, ...), custom_call_target="tpu_custom_call", output_to_operand_aliasing={{1}: (1, {})} | custom-call | tf_op jit(solution)/shard_map/pallas_call | solution.py:227
  187.2 1.9 collective-permute-done.40.refs_5_
  189.1 4.6 %shard_map.64 = bf16[256,8192]{1,0:T(8,128)(2,1)} custom-call(s32[1040]{0:T(1024)S(1)} %constant_dynamic-update-slice_fusion.table.refs_0_, bf16[68,256,128]{2,1,0:T(8,128)(2,1)S(1)} %get-tuple-element.75.refs_1_, bf16[4,64,128,128]{3,2,1,0:T(8,128)(2,1)} %refs_2_.1, ...), custom_call_target="tpu_custom_call", output_to_operand_aliasing={{}: (7, {})} | custom-call | tf_op jit(solution)/shard_map/pallas_call | solution.py:227
  (85 shorter events, 29.9 us)
Async XLA Ops:
  0.0 60.1 %collective-permute-start.4 = (bf16[4,64,128,128]{3,2,1,0:T(8,128)(2,1)}, bf16[4,64,128,128]{3,2,1,0:T(8,128)(2,1)}, u32[]{:S(2)}, u32[]{:S(2)}) collective-permute-start(bf16[4,64,128,128]{3,2,1,0:T(8,128)(2,1)} %refs_2_.1), channel_id=1, source_target_pairs={{0,1},{1,0},{2,3},{3,2},{4,5},{5,4},{6,7},{7,6},{8,9},{9,8},{10,11... | collective-permute-start | bytes 25165832 | tf_op jit(solution)/shard_map/ppermute | solution.py:26
  3.3 49.4 %collective-permute-start.5 = (bf16[64,128,128]{2,1,0:T(8,128)(2,1)}, bf16[64,128,128]{2,1,0:T(8,128)(2,1)}, u32[]{:S(2)}, u32[]{:S(2)}) collective-permute-start(bf16[64,128,128]{2,1,0:T(8,128)(2,1)} %shard_map.56), channel_id=1, source_target_pairs={{0,2},{1,3},{2,0},{3,1},{4,6},{5,7},{6,4},{7,5},{8,10},{9,11},{10,... | collective-permute-start | bytes 6291464 | tf_op jit(solution)/shard_map/ppermute | solution.py:26
  8.9 88.7 %collective-permute-start.14 = (bf16[64,128,128]{2,1,0:T(8,128)(2,1)}, bf16[64,128,128]{2,1,0:T(8,128)(2,1)S(1)}, u32[]{:S(2)}, u32[]{:S(2)}) collective-permute-start(bf16[64,128,128]{2,1,0:T(8,128)(2,1)} %shard_map.58), channel_id=1, source_target_pairs={{0,2},{1,3},{2,0},{3,1},{4,6},{5,7},{6,4},{7,5},{8,10},{9,11},{10,... | collective-permute-start | bytes 6291464 | tf_op jit(solution)/shard_map/ppermute | solution.py:26
  12.7 6.4 %collective-permute-start.1 = (bf16[256,128]{1,0:T(8,128)(2,1)S(1)}, bf16[256,128]{1,0:T(8,128)(2,1)S(1)}, u32[]{:S(2)}, u32[]{:S(2)}) collective-permute-start(bf16[256,128]{1,0:T(8,128)(2,1)S(1)} %get-tuple-element.43), channel_id=1, source_target_pairs={{24,0},{28,4},{0,8},{4,12},{8,16},{12,20},{16,24},{20,28},{25,1},{... | collective-permute-start | bytes 196616 | tf_op jit(solution)/shard_map/ppermute | solution.py:21
  14.8 7.0 %collective-permute-start = (bf16[256,128]{1,0:T(8,128)(2,1)S(1)}, bf16[256,128]{1,0:T(8,128)(2,1)S(1)}, u32[]{:S(2)}, u32[]{:S(2)}) collective-permute-start(bf16[256,128]{1,0:T(8,128)(2,1)S(1)} %get-tuple-element.42), channel_id=1, source_target_pairs={{28,0},{0,4},{4,8},{8,12},{12,16},{16,20},{20,24},{24,28},{29,1},{... | collective-permute-start | bytes 196616 | tf_op jit(solution)/shard_map/ppermute | solution.py:21
  19.1 6.0 %collective-permute-start.3 = (bf16[256,128]{1,0:T(8,128)(2,1)S(1)}, bf16[256,128]{1,0:T(8,128)(2,1)S(1)}, u32[]{:S(2)}, u32[]{:S(2)}) collective-permute-start(bf16[256,128]{1,0:T(8,128)(2,1)S(1)} %get-tuple-element.46), channel_id=1, source_target_pairs={{16,0},{20,4},{24,8},{28,12},{0,16},{4,20},{8,24},{12,28},{17,1},{... | collective-permute-start | bytes 196616 | tf_op jit(solution)/shard_map/ppermute | solution.py:21
  21.8 4.3 %collective-permute-start.2 = (bf16[256,128]{1,0:T(8,128)(2,1)S(1)}, bf16[256,128]{1,0:T(8,128)(2,1)S(1)}, u32[]{:S(2)}, u32[]{:S(2)}) collective-permute-start(bf16[256,128]{1,0:T(8,128)(2,1)S(1)} %get-tuple-element.45), channel_id=1, source_target_pairs={{4,0},{8,4},{12,8},{16,12},{20,16},{24,20},{28,24},{0,28},{5,1},{9... | collective-permute-start | bytes 196616 | tf_op jit(solution)/shard_map/ppermute | solution.py:21
  55.0 5.1 %collective-permute-start.8 = (bf16[16,128,128]{2,1,0:T(8,128)(2,1)S(1)}, bf16[16,128,128]{2,1,0:T(8,128)(2,1)S(1)}, u32[]{:S(2)}, u32[]{:S(2)}) collective-permute-start(bf16[16,128,128]{2,1,0:T(8,128)(2,1)S(1)} %get-tuple-element.84), channel_id=1, source_target_pairs={{0,1},{1,0},{2,3},{3,2},{4,5},{5,4},{6,7},{7,6},{8,9},{9,8},{10,11... | collective-permute-start | bytes 1572872 | tf_op jit(solution)/shard_map/ppermute | solution.py:26
  56.4 3.7 %collective-permute-start.9 = (bf16[16,128,128]{2,1,0:T(8,128)(2,1)S(1)}, bf16[16,128,128]{2,1,0:T(8,128)(2,1)S(1)}, u32[]{:S(2)}, u32[]{:S(2)}) collective-permute-start(bf16[16,128,128]{2,1,0:T(8,128)(2,1)S(1)} %get-tuple-element.83), channel_id=1, source_target_pairs={{0,1},{1,0},{2,3},{3,2},{4,5},{5,4},{6,7},{7,6},{8,9},{9,8},{10,11... | collective-permute-start | bytes 1572872 | tf_op jit(solution)/shard_map/ppermute | solution.py:26
  58.1 73.2 %collective-permute-start.23 = (bf16[48,128,128]{2,1,0:T(8,128)(2,1)S(1)}, bf16[48,128,128]{2,1,0:T(8,128)(2,1)S(1)}, u32[]{:S(2)}, u32[]{:S(2)}) collective-permute-start(bf16[48,128,128]{2,1,0:T(8,128)(2,1)S(1)} %get-tuple-element.61), channel_id=1, source_target_pairs={{0,2},{1,3},{2,0},{3,1},{4,6},{5,7},{6,4},{7,5},{8,10},{9,11},{10,... | collective-permute-start | bytes 4718600 | tf_op jit(solution)/shard_map/ppermute | solution.py:26
  70.2 6.1 %collective-permute-start.11 = (bf16[256,128]{1,0:T(8,128)(2,1)S(1)}, bf16[256,128]{1,0:T(8,128)(2,1)S(1)}, u32[]{:S(2)}, u32[]{:S(2)}) collective-permute-start(bf16[256,128]{1,0:T(8,128)(2,1)S(1)} %get-tuple-element.50), channel_id=1, source_target_pairs={{24,0},{28,4},{0,8},{4,12},{8,16},{12,20},{16,24},{20,28},{25,1},{... | collective-permute-start | bytes 196616 | tf_op jit(solution)/shard_map/ppermute | solution.py:21
  71.9 25.7 %collective-permute-start.10 = (bf16[256,128]{1,0:T(8,128)(2,1)S(1)}, bf16[256,128]{1,0:T(8,128)(2,1)S(1)}, u32[]{:S(2)}, u32[]{:S(2)}) collective-permute-start(bf16[256,128]{1,0:T(8,128)(2,1)S(1)} %get-tuple-element.49), channel_id=1, source_target_pairs={{28,0},{0,4},{4,8},{8,12},{12,16},{16,20},{20,24},{24,28},{29,1},{... | collective-permute-start | bytes 196616 | tf_op jit(solution)/shard_map/ppermute | solution.py:21
  73.4 24.2 %collective-permute-start.13 = (bf16[256,128]{1,0:T(8,128)(2,1)S(1)}, bf16[256,128]{1,0:T(8,128)(2,1)S(1)}, u32[]{:S(2)}, u32[]{:S(2)}) collective-permute-start(bf16[256,128]{1,0:T(8,128)(2,1)S(1)} %get-tuple-element.53), channel_id=1, source_target_pairs={{16,0},{20,4},{24,8},{28,12},{0,16},{4,20},{8,24},{12,28},{17,1},{... | collective-permute-start | bytes 196616 | tf_op jit(solution)/shard_map/ppermute | solution.py:21
  76.4 21.2 %collective-permute-start.12 = (bf16[256,128]{1,0:T(8,128)(2,1)S(1)}, bf16[256,128]{1,0:T(8,128)(2,1)S(1)}, u32[]{:S(2)}, u32[]{:S(2)}) collective-permute-start(bf16[256,128]{1,0:T(8,128)(2,1)S(1)} %get-tuple-element.52), channel_id=1, source_target_pairs={{4,0},{8,4},{12,8},{16,12},{20,16},{24,20},{28,24},{0,28},{5,1},{9... | collective-permute-start | bytes 196616 | tf_op jit(solution)/shard_map/ppermute | solution.py:21
  97.8 3.8 %collective-permute-start.16 = (bf16[16,128,128]{2,1,0:T(8,128)(2,1)S(1)}, bf16[16,128,128]{2,1,0:T(8,128)(2,1)S(1)}, u32[]{:S(2)}, u32[]{:S(2)}) collective-permute-start(bf16[16,128,128]{2,1,0:T(8,128)(2,1)S(1)} %get-tuple-element.81), channel_id=1, source_target_pairs={{0,1},{1,0},{2,3},{3,2},{4,5},{5,4},{6,7},{7,6},{8,9},{9,8},{10,11... | collective-permute-start | bytes 1572872 | tf_op jit(solution)/shard_map/ppermute | solution.py:26
  99.7 42.8 %collective-permute-start.24 = (bf16[16,128,128]{2,1,0:T(8,128)(2,1)S(1)}, bf16[16,128,128]{2,1,0:T(8,128)(2,1)S(1)}, u32[]{:S(2)}, u32[]{:S(2)}) collective-permute-start(bf16[16,128,128]{2,1,0:T(8,128)(2,1)S(1)} %get-tuple-element.63), channel_id=1, source_target_pairs={{0,2},{1,3},{2,0},{3,1},{4,6},{5,7},{6,4},{7,5},{8,10},{9,11},{10,... | collective-permute-start | bytes 1572872 | tf_op jit(solution)/shard_map/ppermute | solution.py:26
  110.6 6.5 %collective-permute-start.20 = (bf16[256,128]{1,0:T(8,128)(2,1)S(1)}, bf16[256,128]{1,0:T(8,128)(2,1)S(1)}, u32[]{:S(2)}, u32[]{:S(2)}) collective-permute-start(bf16[256,128]{1,0:T(8,128)(2,1)S(1)} %get-tuple-element.57), channel_id=1, source_target_pairs={{24,0},{28,4},{0,8},{4,12},{8,16},{12,20},{16,24},{20,28},{25,1},{... | collective-permute-start | bytes 196616 | tf_op jit(solution)/shard_map/ppermute | solution.py:21
  112.7 20.5 %collective-permute-start.19 = (bf16[256,128]{1,0:T(8,128)(2,1)S(1)}, bf16[256,128]{1,0:T(8,128)(2,1)S(1)}, u32[]{:S(2)}, u32[]{:S(2)}) collective-permute-start(bf16[256,128]{1,0:T(8,128)(2,1)S(1)} %get-tuple-element.56), channel_id=1, source_target_pairs={{28,0},{0,4},{4,8},{8,12},{12,16},{16,20},{20,24},{24,28},{29,1},{... | collective-permute-start | bytes 196616 | tf_op jit(solution)/shard_map/ppermute | solution.py:21
  114.2 19.0 %collective-permute-start.22 = (bf16[256,128]{1,0:T(8,128)(2,1)S(1)}, bf16[256,128]{1,0:T(8,128)(2,1)S(1)}, u32[]{:S(2)}, u32[]{:S(2)}) collective-permute-start(bf16[256,128]{1,0:T(8,128)(2,1)S(1)} %get-tuple-element.60), channel_id=1, source_target_pairs={{16,0},{20,4},{24,8},{28,12},{0,16},{4,20},{8,24},{12,28},{17,1},{... | collective-permute-start | bytes 196616 | tf_op jit(solution)/shard_map/ppermute | solution.py:21
  117.1 16.1 %collective-permute-start.21 = (bf16[256,128]{1,0:T(8,128)(2,1)S(1)}, bf16[256,128]{1,0:T(8,128)(2,1)S(1)}, u32[]{:S(2)}, u32[]{:S(2)}) collective-permute-start(bf16[256,128]{1,0:T(8,128)(2,1)S(1)} %get-tuple-element.59), channel_id=1, source_target_pairs={{4,0},{8,4},{12,8},{16,12},{20,16},{24,20},{28,24},{0,28},{5,1},{9... | collective-permute-start | bytes 196616 | tf_op jit(solution)/shard_map/ppermute | solution.py:21
  131.3 33.7 %collective-permute-start.33 = (bf16[32,128,128]{2,1,0:T(8,128)(2,1)S(1)}, bf16[32,128,128]{2,1,0:T(8,128)(2,1)S(1)}, u32[]{:S(2)}, u32[]{:S(2)}) collective-permute-start(bf16[32,128,128]{2,1,0:T(8,128)(2,1)S(1)} %get-tuple-element.71), channel_id=1, source_target_pairs={{0,2},{1,3},{2,0},{3,1},{4,6},{5,7},{6,4},{7,5},{8,10},{9,11},{10,... | collective-permute-start | bytes 3145736 | tf_op jit(solution)/shard_map/ppermute | solution.py:26
  133.4 9.1 %collective-permute-start.25 = (bf16[16,128,128]{2,1,0:T(8,128)(2,1)S(1)}, bf16[16,128,128]{2,1,0:T(8,128)(2,1)S(1)}, u32[]{:S(2)}, u32[]{:S(2)}) collective-permute-start(bf16[16,128,128]{2,1,0:T(8,128)(2,1)S(1)} %get-tuple-element.89), channel_id=1, source_target_pairs={{0,1},{1,0},{2,3},{3,2},{4,5},{5,4},{6,7},{7,6},{8,9},{9,8},{10,11... | collective-permute-start | bytes 1572872 | tf_op jit(solution)/shard_map/ppermute | solution.py:26
  133.5 11.0 %collective-permute-start.26 = (bf16[16,128,128]{2,1,0:T(8,128)(2,1)S(1)}, bf16[16,128,128]{2,1,0:T(8,128)(2,1)S(1)}, u32[]{:S(2)}, u32[]{:S(2)}) collective-permute-start(bf16[16,128,128]{2,1,0:T(8,128)(2,1)S(1)} %get-tuple-element.88), channel_id=1, source_target_pairs={{0,1},{1,0},{2,3},{3,2},{4,5},{5,4},{6,7},{7,6},{8,9},{9,8},{10,11... | collective-permute-start | bytes 1572872 | tf_op jit(solution)/shard_map/ppermute | solution.py:26
  134.0 10.5 %collective-permute-start.27 = (bf16[16,128,128]{2,1,0:T(8,128)(2,1)S(1)}, bf16[16,128,128]{2,1,0:T(8,128)(2,1)S(1)}, u32[]{:S(2)}, u32[]{:S(2)}) collective-permute-start(bf16[16,128,128]{2,1,0:T(8,128)(2,1)S(1)} %get-tuple-element.87), channel_id=1, source_target_pairs={{0,1},{1,0},{2,3},{3,2},{4,5},{5,4},{6,7},{7,6},{8,9},{9,8},{10,11... | collective-permute-start | bytes 1572872 | tf_op jit(solution)/shard_map/ppermute | solution.py:26
  142.5 33.7 %collective-permute-start.34 = (bf16[16,128,128]{2,1,0:T(8,128)(2,1)S(1)}, bf16[16,128,128]{2,1,0:T(8,128)(2,1)S(1)}, u32[]{:S(2)}, u32[]{:S(2)}) collective-permute-start(bf16[16,128,128]{2,1,0:T(8,128)(2,1)S(1)} %get-tuple-element.73), channel_id=1, source_target_pairs={{0,2},{1,3},{2,0},{3,1},{4,6},{5,7},{6,4},{7,5},{8,10},{9,11},{10,... | collective-permute-start | bytes 1572872 | tf_op jit(solution)/shard_map/ppermute | solution.py:26
  153.2 6.4 %collective-permute-start.30 = (bf16[256,128]{1,0:T(8,128)(2,1)S(1)}, bf16[256,128]{1,0:T(8,128)(2,1)S(1)}, u32[]{:S(2)}, u32[]{:S(2)}) collective-permute-start(bf16[256,128]{1,0:T(8,128)(2,1)S(1)} %get-tuple-element.67), channel_id=1, source_target_pairs={{24,0},{28,4},{0,8},{4,12},{8,16},{12,20},{16,24},{20,28},{25,1},{... | collective-permute-start | bytes 196616 | tf_op jit(solution)/shard_map/ppermute | solution.py:21
  155.2 9.8 %collective-permute-start.29 = (bf16[256,128]{1,0:T(8,128)(2,1)S(1)}, bf16[256,128]{1,0:T(8,128)(2,1)S(1)}, u32[]{:S(2)}, u32[]{:S(2)}) collective-permute-start(bf16[256,128]{1,0:T(8,128)(2,1)S(1)} %get-tuple-element.66), channel_id=1, source_target_pairs={{28,0},{0,4},{4,8},{8,12},{12,16},{16,20},{20,24},{24,28},{29,1},{... | collective-permute-start | bytes 196616 | tf_op jit(solution)/shard_map/ppermute | solution.py:21
  156.7 8.3 %collective-permute-start.32 = (bf16[256,128]{1,0:T(8,128)(2,1)S(1)}, bf16[256,128]{1,0:T(8,128)(2,1)S(1)}, u32[]{:S(2)}, u32[]{:S(2)}) collective-permute-start(bf16[256,128]{1,0:T(8,128)(2,1)S(1)} %get-tuple-element.70), channel_id=1, source_target_pairs={{16,0},{20,4},{24,8},{28,12},{0,16},{4,20},{8,24},{12,28},{17,1},{... | collective-permute-start | bytes 196616 | tf_op jit(solution)/shard_map/ppermute | solution.py:21
  159.6 5.4 %collective-permute-start.31 = (bf16[256,128]{1,0:T(8,128)(2,1)S(1)}, bf16[256,128]{1,0:T(8,128)(2,1)S(1)}, u32[]{:S(2)}, u32[]{:S(2)}) collective-permute-start(bf16[256,128]{1,0:T(8,128)(2,1)S(1)} %get-tuple-element.69), channel_id=1, source_target_pairs={{4,0},{8,4},{12,8},{16,12},{20,16},{24,20},{28,24},{0,28},{5,1},{9... | collective-permute-start | bytes 196616 | tf_op jit(solution)/shard_map/ppermute | solution.py:21
  165.1 13.1 %collective-permute-start.35 = (bf16[16,128,128]{2,1,0:T(8,128)(2,1)S(1)}, bf16[16,128,128]{2,1,0:T(8,128)(2,1)S(1)}, u32[]{:S(2)}, u32[]{:S(2)}) collective-permute-start(bf16[16,128,128]{2,1,0:T(8,128)(2,1)S(1)} %get-tuple-element.91), channel_id=1, source_target_pairs={{0,1},{1,0},{2,3},{3,2},{4,5},{5,4},{6,7},{7,6},{8,9},{9,8},{10,11... | collective-permute-start | bytes 1572872 | tf_op jit(solution)/shard_map/ppermute | solution.py:26
  165.2 13.1 %collective-permute-start.36 = (bf16[16,128,128]{2,1,0:T(8,128)(2,1)S(1)}, bf16[16,128,128]{2,1,0:T(8,128)(2,1)S(1)}, u32[]{:S(2)}, u32[]{:S(2)}) collective-permute-start(bf16[16,128,128]{2,1,0:T(8,128)(2,1)S(1)} %get-tuple-element.90), channel_id=1, source_target_pairs={{0,1},{1,0},{2,3},{3,2},{4,5},{5,4},{6,7},{7,6},{8,9},{9,8},{10,11... | collective-permute-start | bytes 1572872 | tf_op jit(solution)/shard_map/ppermute | solution.py:26
  165.7 21.6 %collective-permute-start.39 = (bf16[16,128,128]{2,1,0:T(8,128)(2,1)S(1)}, bf16[16,128,128]{2,1,0:T(8,128)(2,1)S(1)}, u32[]{:S(2)}, u32[]{:S(2)}) collective-permute-start(bf16[16,128,128]{2,1,0:T(8,128)(2,1)S(1)} %get-tuple-element.76), channel_id=1, source_target_pairs={{0,2},{1,3},{2,0},{3,1},{4,6},{5,7},{6,4},{7,5},{8,10},{9,11},{10,... | collective-permute-start | bytes 1572872 | tf_op jit(solution)/shard_map/ppermute | solution.py:26
  (13 other events, 46.3 us)

commit v8 on v7

--- a/solution.py
+++ b/solution.py
@@ -1,3 +1,4 @@
+import functools
 import math
 
 import jax
@@ -7,8 +8,9 @@
 from jax.experimental.pallas import tpu as pltpu
 from jax.sharding import PartitionSpec as P
 
-
 TURNS = (3, 1, 0, 2)
+BOUNDARY = 2
+CUTS = 16
 NEIGH = 4
 VMEM_LIMIT = 16 * 2**20
 LAYER_LIMIT = 20 * 2**20
@@ -41,7 +43,7 @@
         targets, semaphores = refs[: len(chunks)], refs[len(chunks)]
         copies = []
         for place, (layer, first, count) in enumerate(chunks):
-            step = count // math.gcd(4, count)
+            step = count // math.gcd(CUTS, count)
             for part, start in enumerate(range(0, count, step)):
                 source = tiles.at[layer, pl.ds(first + start, step)]
                 there = targets[place].at[pl.ds(start, step)]
@@ -51,15 +53,16 @@
         for copy in copies:
             copy.wait()
 
-    return pl.pallas_call(
+    parts = pl.pallas_call(
         kernel,
         out_shape=[pltpu.VMEM((count, height, width), tile_weights.dtype) for _, _, count in chunks],
         in_specs=[pl.BlockSpec(memory_space=pltpu.HBM)],
         out_specs=[pl.BlockSpec(memory_space=pltpu.VMEM)] * len(chunks),
-        scratch_shapes=[pltpu.SemaphoreType.DMA((len(chunks), 4))],
+        scratch_shapes=[pltpu.SemaphoreType.DMA((len(chunks), CUTS))],
         compiler_params=pltpu.CompilerParams(vmem_limit_bytes=VMEM_LIMIT),
         cost_estimate=FREE,
     )(in_hbm(tile_weights))
+    return list(parts)
 
 
 def pick(table, place, number, width, activations):
@@ -91,46 +94,32 @@
 
 
 def run_blocks(layer, first, count, table, sends, pool, arrived, tiles, biases, target, final):
-    fan, width = len(tiles), tiles[0].shape[3]
+    fan, width = len(tiles), tiles[0][0].shape[2]
     rows, blocks = pool.shape[-2], biases.shape[1] // width
     columns = pool.ndim == 2
     fill = bool(arrived) and not columns
-    group = math.gcd(8, count)
-    held = [source if isinstance(source, list) else [source] for source in tiles]
-    step = group
-    for source in held:
-        for array in source:
-            step = math.gcd(step, array.shape[-3])
-    parts = count // step
+    places = {}
+    for m in range(fan):
+        places[m] = [(part, inside) for part, array in enumerate(tiles[m]) for inside in range(array.shape[0])]
+    cuts = [block for block in range(count) if any(places[m][block][1] == 0 for m in range(fan))] + [count]
+    group = math.gcd(8, *cuts)
 
     def kernel(*refs):
         refs = list(refs)
         table, pool_ref = (refs.pop(0) for _ in range(2))
         arrived_refs = [refs.pop(0) for _ in arrived]
-        tile_refs = [[refs.pop(0) for _ in source] for source in held]
+        tile_refs = [[refs.pop(0) for _ in source] for source in tiles]
         bias = refs.pop(0)
         if target is not None:
             refs.pop(0)
         result = refs.pop(0)
         inputs = refs.pop(0) if fill else pool_ref
         outgoing = [] if final else [refs.pop(0) for _ in range(neigh)]
-        weights, in_sems, weight_sems = (refs.pop(0) for _ in range(3))
+        in_sems = refs.pop(0)
         if final:
             outputs, out_sems = (refs.pop(0) for _ in range(2))
         if columns:
             inputs = refs.pop(0)
-
-        def tile_copy(part, m):
-            start = part * step
-            if held[m][0].ndim == 4:
-                piece = tile_refs[m][0].at[layer, pl.ds(first + start, step)]
-            else:
-                place, inside = 0, start
-                while inside >= held[m][place].shape[0]:
-                    inside -= held[m][place].shape[0]
-                    place += 1
-                piece = tile_refs[m][place].at[pl.ds(inside, step)]
-            return pltpu.make_async_copy(piece, weights.at[m, pl.ds(start, step)], weight_sems.at[part, m])
 
         def out_copy(part):
             here = outputs.at[:, pl.ds(part * group * width, group * width)]
@@ -146,24 +135,20 @@
         loads = [pltpu.make_async_copy(*load, in_sems.at[place]) for place, load in enumerate(loads)]
         for copy in loads:
             copy.start()
-        for part in range(parts):
-            for m in range(fan):
-                tile_copy(part, m).start()
         for copy in loads:
             copy.wait()
 
-        def work(part, _):
-            for sub in range(group // step):
-                for m in range(fan):
-                    here = weights.at[m, pl.ds((part * (group // step) + sub) * step, step)]
-                    sem = weight_sems.at[part * (group // step) + sub, m]
-                    pltpu.make_async_copy(here, here, sem).wait()
+        def work(start, part, _):
             for g in range(group):
                 block = part * group + g
                 base = (layer * blocks + first + block) * fan
+                weights = []
+                for m in range(fan):
+                    place, inside = places[m][start]
+                    weights.append(tile_refs[m][place][block - start + inside])
                 summed = jnp.dot(
                     jnp.concatenate([inputs[table[base + m]] for m in range(fan)], axis=1),
-                    jnp.concatenate([weights[m, block] for m in range(fan)], axis=0),
+                    jnp.concatenate(weights, axis=0),
                     preferred_element_type=jnp.float32,
                 )
                 place = pl.multiple_of((first + block) * width, width)
@@ -177,7 +162,8 @@
                 out_copy(part).start()
             return _
 
-        lax.fori_loop(0, count // group, work, None)
+        for start, end in zip(cuts, cuts[1:]):
+            lax.fori_loop(start // group, end // group, functools.partial(work, start), None)
         for slot, there in enumerate(outgoing):
             there[...] = result[table[sends + slot]]
         if final:
@@ -190,12 +176,8 @@
     operands = [table, in_hbm(pool) if columns else in_vmem(pool), *arrived]
     in_specs = [hbm if columns else vmem] + [anywhere] * len(arrived)
     for source in tiles:
-        if isinstance(source, list):
-            operands += source
-            in_specs += [anywhere] * len(source)
-        else:
-            operands.append(in_hbm(source))
-            in_specs.append(hbm)
+        operands += [in_vmem(array) for array in source]
+        in_specs += [vmem] * len(source)
     operands.append(biases)
     in_specs.append(vmem)
     aliases = {}
@@ -214,11 +196,7 @@
     if not final:
         out_shape += [jax.ShapeDtypeStruct((rows, width), pool.dtype)] * neigh
         out_specs += [vmem] * neigh
-    scratch = [
-        pltpu.VMEM((fan, count, width, width), tiles[0].dtype),
-        pltpu.SemaphoreType.DMA((blocks + neigh,)),
-        pltpu.SemaphoreType.DMA((parts, fan)),
-    ]
+    scratch = [pltpu.SemaphoreType.DMA((blocks + neigh,))]
     if final:
         scratch += [pltpu.VMEM((rows, count * width), pool.dtype), pltpu.SemaphoreType.DMA((count // group,))]
     if columns:
@@ -272,12 +250,12 @@
         for size in sizes:
             start = sum(count for _, _, count in moves[layer])
             moves[layer].append((layer, start, size * unit))
-    crossed = {}
-    for layer in moves:
-        crossed[layer] = [swapped(mine, far * sharers) for mine in cut(tile_weights, moves[layer])]
-
-    near = [tile_weights] + [None] * (fan - 1)
-    spread(near, 0)
+    mine = {layer: cut(tile_weights, moves[layer]) for layer in moves}
+    crossed = {layer: [swapped(tile, far * sharers) for tile in mine[layer]] for layer in moves}
+
+    whole = [tile_weights] + [None] * (fan - 1)
+    spread(whole, 0)
+    near = {layer: [cut(array, moves[layer]) for array in whole[1:far]] for layer in moves}
 
     current = activations
     outgoing = pick(table, codes.size, NEIGH, width, activations)
@@ -287,21 +265,24 @@
             arrived = [None] * NEIGH
             for turn, slot in enumerate(TURNS):
                 block = outgoing[slot]
-                if turn == NEIGH - 1:
-                    block = lax.optimization_barrier((block, arrived[TURNS[1]]))[0]
+                if turn >= BOUNDARY:
+                    block = lax.optimization_barrier((block, arrived[TURNS[turn - BOUNDARY]]))[0]
                 arrived[slot] = shifted(block, "dom", neighbor_offsets[slot])
             pool, target, first, after = current, None, 0, arrived
         before = layer
-        tiles = list(near)
-        tiles[far], passed = [], []
-        for number in pieces:
-            tile = lax.optimization_barrier((crossed[layer].pop(0), *after))[0]
+        after = [*after, *(tile for source in near[layer] for tile in source)]
+        tiles = [None] * fan
+        for m, source in enumerate([mine[layer], *near[layer], crossed[layer]]):
+            tiles[m] = [source.pop(0) for _ in sizes]
+        passed = []
+        for number, tile in zip(pieces, tiles[far]):
+            tile = lax.optimization_barrier((tile, *after))[0]
+            after = [*after, tile]
             share = tile.shape[0] // math.gcd(number, tile.shape[0])
-            tiles[far].append(tile)
             passed += [tile[start : start + share] for start in range(0, tile.shape[0], share)]
-        whole, tiles[far] = tiles[far], passed
+        held, tiles[far] = tiles[far], passed
         spread(tiles, far)
-        tiles[far] = whole
+        tiles[far] = held
         count = sum(sizes) * unit
         sends = codes.size + (layer + 1) * NEIGH
         target, pool, outgoing = run_blocks(

time: 194 us -> 194 us (level)
  waiting for transfers between devices: 88.2 us -> 82.7 us
  Pallas kernels: 50.6 us -> 54.8 us
    ppermute x25, waiting for transfers between devices: 79.6 us -> 67.6 us  [swapped(): return lax.ppermute(block, 'batch', route)]
    pallas_call x4 -> x8, Pallas kernels: 8.99 us -> 15.5 us  [cut(): pl.pallas_call(kernel, out_shape=[pltpu.VMEM((count, height, width), tile...]
    ppermute x16, waiting for transfers between devices: 8.61 us -> 15.1 us  [shifted(): return lax.ppermute(block, axis, route)]
    pallas_call x5, Pallas kernels: 40 us -> 37.7 us  [run_blocks(): pl.pallas_call(kernel, out_shape=out_shape, grid_spec=pltpu.PrefetchScala...]
  transfers between devices with their start and end apart: 41 -> 41, of which waited for: 20 -> 18; matrix products, arithmetic and copies ran while one was open for 2% -> 3% of each run, Pallas kernels for 24% -> 27%
where the time goes in v8:
time: 194 us; the launch traced here: 193 us
  waiting for transfers between devices  82.7 us (43%)
  Pallas kernels  54.8 us (28%)
  starting transfers between devices  49.2 us (25%)
  local copies, waits for them, and re-layouts  5.05 us (3%)
    ppermute x25, waiting for transfers between devices, swapped(): return lax.ppermute(block, 'batch', route)  67.6 us
    pallas_call x5, Pallas kernels, run_blocks(): pl.pallas_call(kernel, out_shape=out_shape, grid_spec=pltpu.PrefetchScala...  37.7 us
    ppermute x16, starting transfers between devices, shifted(): return lax.ppermute(block, axis, route)  32.8 us
    ppermute x25, starting transfers between devices, swapped(): return lax.ppermute(block, 'batch', route)  16.4 us
    pallas_call x8, Pallas kernels, cut(): pl.pallas_call(kernel, out_shape=[pltpu.VMEM((count, height, width), tile...  15.5 us
    ppermute x16, waiting for transfers between devices, shifted(): return lax.ppermute(block, axis, route)  15.1 us
  transfers between devices with their start and end apart: 41, of which 18 were waited for; matrix products, arithmetic and copies ran while one was open for 3% of the time, Pallas kernels for 27%

profile of v8, /device:TPU:0, one launch (start us, length us, event | category | flops | bytes accessed | tf_op | source)
XLA Modules:
  0.0 193.0 jit_solution(16883617726478393431)
XLA Ops:
  0.5 3.1 %shard_map.56.refs_6_ = bf16[64,128,128]{2,1,0:T(8,128)(2,1)} custom-call(bf16[4,64,128,128]{3,2,1,0:T(8,128)(2,1)} %tiles.7), custom_call_target="tpu_custom_call" | custom-call | tf_op jit(solution)/shard_map/pallas_call | solution.py:56
  3.5 2.6 %collective-permute-start.5 = (bf16[64,128,128]{2,1,0:T(8,128)(2,1)}, bf16[64,128,128]{2,1,0:T(8,128)(2,1)}, u32[]{:S(2)}, u32[]{:S(2)}) collective-permute-start(bf16[64,128,128]{2,1,0:T(8,128)(2,1)} %shard_map.56.refs_6_), channel_id=1, source_target_pairs={{0,2},{1,3},{2,0},{3,1},{4,6},{5,7},{6,4},{7,5},{8,10},{9,11},{10,... | collective-permute-start | bytes 6291464 | tf_op jit(solution)/shard_map/ppermute | solution.py:28
  11.7 2.1 %collective-permute-start.2 = (bf16[256,128]{1,0:T(8,128)(2,1)S(1)}, bf16[256,128]{1,0:T(8,128)(2,1)S(1)}, u32[]{:S(2)}, u32[]{:S(2)}) collective-permute-start(bf16[256,128]{1,0:T(8,128)(2,1)S(1)} %get-tuple-element.54), channel_id=1, source_target_pairs={{24,0},{28,4},{0,8},{4,12},{8,16},{12,20},{16,24},{20,28},{25,1},{... | collective-permute-start | bytes 196616 | tf_op jit(solution)/shard_map/ppermute | solution.py:23
  13.8 2.6 %collective-permute-start = (bf16[256,128]{1,0:T(8,128)(2,1)S(1)}, bf16[256,128]{1,0:T(8,128)(2,1)S(1)}, u32[]{:S(2)}, u32[]{:S(2)}) collective-permute-start(bf16[256,128]{1,0:T(8,128)(2,1)S(1)} %get-tuple-element.52), channel_id=1, source_target_pairs={{16,0},{20,4},{24,8},{28,12},{0,16},{4,20},{8,24},{12,28},{17,1},{... | collective-permute-start | bytes 196616 | tf_op jit(solution)/shard_map/ppermute | solution.py:23
  18.3 3.3 %collective-permute-start.3 = (bf16[256,128]{1,0:T(8,128)(2,1)S(1)}, bf16[256,128]{1,0:T(8,128)(2,1)S(1)}, u32[]{:S(2)}, u32[]{:S(2)}) collective-permute-start(bf16[256,128]{1,0:T(8,128)(2,1)S(1)} %get-tuple-element.56), channel_id=1, source_target_pairs={{4,0},{8,4},{12,8},{16,12},{20,16},{24,20},{28,24},{0,28},{5,1},{9... | collective-permute-start | bytes 196616 | tf_op jit(solution)/shard_map/ppermute | solution.py:23
  24.1 4.5 %collective-permute-done.1.refs_2_ = bf16[256,128]{1,0:T(8,128)(2,1)S(1)} collective-permute-done((bf16[256,128]{1,0:T(8,128)(2,1)S(1)}, bf16[256,128]{1,0:T(8,128)(2,1)S(1)}, u32[]{:S(2)}, u32[]{:S(2)}) %collective-permute-start.1) | collective-permute-done | bytes 65568 | tf_op jit(solution)/shard_map/ppermute | solution.py:23
  28.6 24.3 %collective-permute-done.5.refs_8_ = bf16[64,128,128]{2,1,0:T(8,128)(2,1)} collective-permute-done((bf16[64,128,128]{2,1,0:T(8,128)(2,1)}, bf16[64,128,128]{2,1,0:T(8,128)(2,1)}, u32[]{:S(2)}, u32[]{:S(2)}) %collective-permute-start.5) | collective-permute-done | bytes 2097184 | tf_op jit(solution)/shard_map/ppermute | solution.py:28
  57.4 2.0 %collective-permute-start.23 = (bf16[48,128,128]{2,1,0:T(8,128)(2,1)S(1)}, bf16[48,128,128]{2,1,0:T(8,128)(2,1)S(1)}, u32[]{:S(2)}, u32[]{:S(2)}) collective-permute-start(bf16[48,128,128]{2,1,0:T(8,128)(2,1)S(1)} %get-tuple-element.73.refs_6_), channel_id=1, source_target_pairs={{0,2},{1,3},{2,0},{3,1},{4,6},{5,7},{6,4},{7,5},{8,10},{9,11},{10,... | collective-permute-start | bytes 4718600 | tf_op jit(solution)/shard_map/ppermute | solution.py:28
  59.4 11.7 %shard_map.58 = (bf16[68,256,128]{2,1,0:T(8,128)(2,1)S(1)}, bf16[256,128]{1,0:T(8,128)(2,1)S(1)}, bf16[256,128]{1,0:T(8,128)(2,1)S(1)}, bf16[256,128]{1,0:T(8,128)(2,1)S(1)}, bf16[256,128]{1,0:T(8,128)(2,1)S(1)}) custom-call(s32[1040]{0:T(1024)S(1)} %constant_dynamic-update-slice_fusion.table.refs_0_, bf16[256,8192]{1,0:T(8,128)(2,1)} %refs_1_.1, ...), custom_call_target="tpu_custom_call" | custom-call | tf_op jit(solution)/shard_map/pallas_call | solution.py:205
  72.8 2.6 %collective-permute-start.10 = (bf16[256,128]{1,0:T(8,128)(2,1)S(1)}, bf16[256,128]{1,0:T(8,128)(2,1)S(1)}, u32[]{:S(2)}, u32[]{:S(2)}) collective-permute-start(bf16[256,128]{1,0:T(8,128)(2,1)S(1)} %get-tuple-element.60), channel_id=1, source_target_pairs={{16,0},{20,4},{24,8},{28,12},{0,16},{4,20},{8,24},{12,28},{17,1},{... | collective-permute-start | bytes 196616 | tf_op jit(solution)/shard_map/ppermute | solution.py:23
  75.4 2.3 %collective-permute-done.12.refs_3_ = bf16[256,128]{1,0:T(8,128)(2,1)S(1)} collective-permute-done((bf16[256,128]{1,0:T(8,128)(2,1)S(1)}, bf16[256,128]{1,0:T(8,128)(2,1)S(1)}, u32[]{:S(2)}, u32[]{:S(2)}) %collective-permute-start.12) | collective-permute-done | bytes 65568 | tf_op jit(solution)/shard_map/ppermute | solution.py:23
  77.8 2.9 %collective-permute-start.13 = (bf16[256,128]{1,0:T(8,128)(2,1)S(1)}, bf16[256,128]{1,0:T(8,128)(2,1)S(1)}, u32[]{:S(2)}, u32[]{:S(2)}) collective-permute-start(bf16[256,128]{1,0:T(8,128)(2,1)S(1)} %get-tuple-element.64), channel_id=1, source_target_pairs={{4,0},{8,4},{12,8},{16,12},{20,16},{24,20},{28,24},{0,28},{5,1},{9... | collective-permute-start | bytes 196616 | tf_op jit(solution)/shard_map/ppermute | solution.py:23
  83.1 14.7 %collective-permute-done.14.refs_8_ = bf16[64,128,128]{2,1,0:T(8,128)(2,1)} collective-permute-done((bf16[64,128,128]{2,1,0:T(8,128)(2,1)S(1)}, bf16[64,128,128]{2,1,0:T(8,128)(2,1)}, u32[]{:S(2)}, u32[]{:S(2)}) %collective-permute-start.14) | collective-permute-done | bytes 2097184 | tf_op jit(solution)/shard_map/ppermute | solution.py:28
  101.5 1.9 %collective-permute-start.24 = (bf16[16,128,128]{2,1,0:T(8,128)(2,1)S(1)}, bf16[16,128,128]{2,1,0:T(8,128)(2,1)S(1)}, u32[]{:S(2)}, u32[]{:S(2)}) collective-permute-start(bf16[16,128,128]{2,1,0:T(8,128)(2,1)S(1)} %get-tuple-element.74.refs_7_), channel_id=1, source_target_pairs={{0,2},{1,3},{2,0},{3,1},{4,6},{5,7},{6,4},{7,5},{8,10},{9,11},{10,... | collective-permute-start | bytes 1572872 | tf_op jit(solution)/shard_map/ppermute | solution.py:28
  103.7 8.8 %shard_map.61 = (bf16[68,256,128]{2,1,0:T(8,128)(2,1)S(1)}, bf16[68,256,128]{2,1,0:T(8,128)(2,1)S(1)}, bf16[256,128]{1,0:T(8,128)(2,1)S(1)}, bf16[256,128]{1,0:T...) custom-call(s32[1040]{0:T(1024)S(1)} %constant_dynamic-update-slice_, ...), custom_call_target="tpu_custom_call", output_to_operand_aliasing={{1}: (1, {})} | custom-call | tf_op jit(solution)/shard_map/pallas_call | solution.py:205
  112.5 2.1 %collective-permute-start.21 = (bf16[256,128]{1,0:T(8,128)(2,1)S(1)}, bf16[256,128]{1,0:T(8,128)(2,1)S(1)}, u32[]{:S(2)}, u32[]{:S(2)}) collective-permute-start(bf16[256,128]{1,0:T(8,128)(2,1)S(1)} %get-tuple-element.70), channel_id=1, source_target_pairs={{24,0},{28,4},{0,8},{4,12},{8,16},{12,20},{16,24},{20,28},{25,1},{... | collective-permute-start | bytes 196616 | tf_op jit(solution)/shard_map/ppermute | solution.py:23
  114.6 2.6 %collective-permute-start.19 = (bf16[256,128]{1,0:T(8,128)(2,1)S(1)}, bf16[256,128]{1,0:T(8,128)(2,1)S(1)}, u32[]{:S(2)}, u32[]{:S(2)}) collective-permute-start(bf16[256,128]{1,0:T(8,128)(2,1)S(1)} %get-tuple-element.68), channel_id=1, source_target_pairs={{16,0},{20,4},{24,8},{28,12},{0,16},{4,20},{8,24},{12,28},{17,1},{... | collective-permute-start | bytes 196616 | tf_op jit(solution)/shard_map/ppermute | solution.py:23
  120.6 2.3 %collective-permute-start.22 = (bf16[256,128]{1,0:T(8,128)(2,1)S(1)}, bf16[256,128]{1,0:T(8,128)(2,1)S(1)}, u32[]{:S(2)}, u32[]{:S(2)}) collective-permute-start(bf16[256,128]{1,0:T(8,128)(2,1)S(1)} %get-tuple-element.72), channel_id=1, source_target_pairs={{4,0},{8,4},{12,8},{16,12},{20,16},{24,20},{28,24},{0,28},{5,1},{9... | collective-permute-start | bytes 196616 | tf_op jit(solution)/shard_map/ppermute | solution.py:23
  125.1 6.3 %collective-permute-done.23.refs_10_ = bf16[48,128,128]{2,1,0:T(8,128)(2,1)S(1)} collective-permute-done((bf16[48,128,128]{2,1,0:T(8,128)(2,1)S(1)}, bf16[48,128,128]{2,1,0:T(8,128)(2,1)S(1)}, u32[]{:S(2)}, u32[]{:S(2)}) %collective-permute-start.23) | collective-permute-done | bytes 1572896 | tf_op jit(solution)/shard_map/ppermute | solution.py:28
  131.4 11.2 %collective-permute-done.24.refs_11_ = bf16[16,128,128]{2,1,0:T(8,128)(2,1)S(1)} collective-permute-done((bf16[16,128,128]{2,1,0:T(8,128)(2,1)S(1)}, bf16[16,128,128]{2,1,0:T(8,128)(2,1)S(1)}, u32[]{:S(2)}, u32[]{:S(2)}) %collective-permute-start.24) | collective-permute-done | bytes 524320 | tf_op jit(solution)/shard_map/ppermute | solution.py:28
  144.6 1.9 %collective-permute-start.34 = (bf16[16,128,128]{2,1,0:T(8,128)(2,1)S(1)}, bf16[16,128,128]{2,1,0:T(8,128)(2,1)S(1)}, u32[]{:S(2)}, u32[]{:S(2)}) collective-permute-start(bf16[16,128,128]{2,1,0:T(8,128)(2,1)S(1)} %get-tuple-element.87.refs_7_), channel_id=1, source_target_pairs={{0,2},{1,3},{2,0},{3,1},{4,6},{5,7},{6,4},{7,5},{8,10},{9,11},{10,... | collective-permute-start | bytes 1572872 | tf_op jit(solution)/shard_map/ppermute | solution.py:28
  146.8 7.2 %shard_map.64 = (bf16[68,256,128]{2,1,0:T(8,128)(2,1)S(1)}, bf16[68,256,128]{2,1,0:T(8,128)(2,1)S(1)}, bf16[256,128]{1,0:T(8,128)(2,1)S(1)}, bf16[256,128]{1,0:T...) custom-call(s32[1040]{0:T(1024)S(1)} %constant_dynamic-update-slice_, ...), custom_call_target="tpu_custom_call", output_to_operand_aliasing={{1}: (1, {})} | custom-call | tf_op jit(solution)/shard_map/pallas_call | solution.py:205
  154.1 2.1 %collective-permute-start.31 = (bf16[256,128]{1,0:T(8,128)(2,1)S(1)}, bf16[256,128]{1,0:T(8,128)(2,1)S(1)}, u32[]{:S(2)}, u32[]{:S(2)}) collective-permute-start(bf16[256,128]{1,0:T(8,128)(2,1)S(1)} %get-tuple-element.83), channel_id=1, source_target_pairs={{24,0},{28,4},{0,8},{4,12},{8,16},{12,20},{16,24},{20,28},{25,1},{... | collective-permute-start | bytes 196616 | tf_op jit(solution)/shard_map/ppermute | solution.py:23
  156.2 2.6 %collective-permute-start.29 = (bf16[256,128]{1,0:T(8,128)(2,1)S(1)}, bf16[256,128]{1,0:T(8,128)(2,1)S(1)}, u32[]{:S(2)}, u32[]{:S(2)}) collective-permute-start(bf16[256,128]{1,0:T(8,128)(2,1)S(1)} %get-tuple-element.81), channel_id=1, source_target_pairs={{16,0},{20,4},{24,8},{28,12},{0,16},{4,20},{8,24},{12,28},{17,1},{... | collective-permute-start | bytes 196616 | tf_op jit(solution)/shard_map/ppermute | solution.py:23
  158.8 2.0 %collective-permute-done.31.refs_3_ = bf16[256,128]{1,0:T(8,128)(2,1)S(1)} collective-permute-done((bf16[256,128]{1,0:T(8,128)(2,1)S(1)}, bf16[256,128]{1,0:T(8,128)(2,1)S(1)}, u32[]{:S(2)}, u32[]{:S(2)}) %collective-permute-start.31) | collective-permute-done | bytes 65568 | tf_op jit(solution)/shard_map/ppermute | solution.py:23
  160.8 3.4 %collective-permute-start.32 = (bf16[256,128]{1,0:T(8,128)(2,1)S(1)}, bf16[256,128]{1,0:T(8,128)(2,1)S(1)}, u32[]{:S(2)}, u32[]{:S(2)}) collective-permute-start(bf16[256,128]{1,0:T(8,128)(2,1)S(1)} %get-tuple-element.85), channel_id=1, source_target_pairs={{4,0},{8,4},{12,8},{16,12},{20,16},{24,20},{28,24},{0,28},{5,1},{9... | collective-permute-start | bytes 196616 | tf_op jit(solution)/shard_map/ppermute | solution.py:23
  166.8 4.3 %collective-permute-done.30.refs_2_ = bf16[256,128]{1,0:T(8,128)(2,1)S(1)} collective-permute-done((bf16[256,128]{1,0:T(8,128)(2,1)S(1)}, bf16[256,128]{1,0:T(8,128)(2,1)S(1)}, u32[]{:S(2)}, u32[]{:S(2)}) %collective-permute-start.30) | collective-permute-done | bytes 65568 | tf_op jit(solution)/shard_map/ppermute | solution.py:23
  173.3 3.1 %collective-permute-done.34.refs_11_ = bf16[16,128,128]{2,1,0:T(8,128)(2,1)S(1)} collective-permute-done((bf16[16,128,128]{2,1,0:T(8,128)(2,1)S(1)}, bf16[16,128,128]{2,1,0:T(8,128)(2,1)S(1)}, u32[]{:S(2)}, u32[]{:S(2)}) %collective-permute-start.34) | collective-permute-done | bytes 524320 | tf_op jit(solution)/shard_map/ppermute | solution.py:28
  178.4 6.5 %shard_map.67 = (bf16[256,8192]{1,0:T(8,128)(2,1)}, bf16[68,256,128]{2,1,0:T(8,128)(2,1)S(1)}) custom-call(s32[1040]{0:T(1024)S(1)} %constant_dynamic-update-slice_fusion.table.refs_0_, bf16[68,256,128]{2,1,0:T(8,128)(2,1)S(1)} %get-tuple-element.79.refs_1_, bf16[256,128]{1,0:T(8,128)(2,1)S(1)} %collective-permute-done.30.refs_2_, ...), custom_call_target="tpu_custom_call", output_to_operand_aliasing={{1}: (1, {})} | custom-call | tf_op jit(solution)/shard_map/pallas_call | solution.py:205
  184.9 2.5 %collective-permute-done.39.refs_4_ = bf16[16,128,128]{2,1,0:T(8,128)(2,1)S(1)} collective-permute-done((bf16[16,128,128]{2,1,0:T(8,128)(2,1)S(1)}, bf16[16,128,128]{2,1,0:T(8,128)(2,1)S(1)}, u32[]{:S(2)}, u32[]{:S(2)}) %collective-permute-start.39) | collective-permute-done | bytes 524320 | tf_op jit(solution)/shard_map/ppermute | solution.py:28
  187.4 1.9 collective-permute-done.40.refs_5_
  189.3 3.5 %shard_map.68 = bf16[256,8192]{1,0:T(8,128)(2,1)} custom-call(s32[1040]{0:T(1024)S(1)} %constant_dynamic-update-slice_fusion.table.refs_0_, bf16[68,256,128]{2,1,0:T(8,128)(2,1)S(1)} %get-tuple-element.93.refs_1_, bf16[16,128,128]{2,1,0:T(8,128)(2,1)S(1)} %get-tuple-element.94.refs_2_, ...), custom_call_target="tpu_custom_call", output_to_operand_aliasing={{}: (7, {})} | custom-call | tf_op jit(solution)/shard_map/pallas_call | solution.py:205
  (89 shorter events, 37.5 us)
Async XLA Ops:
  0.0 22.3 %collective-permute-start.4 = (bf16[4,64,128,128]{3,2,1,0:T(8,128)(2,1)}, bf16[4,64,128,128]{3,2,1,0:T(8,128)(2,1)}, u32[]{:S(2)}, u32[]{:S(2)}) collective-permute-start(bf16[4,64,128,128]{3,2,1,0:T(8,128)(2,1)} %tiles.7), channel_id=1, source_target_pairs={{0,1},{1,0},{2,3},{3,2},{4,5},{5,4},{6,7},{7,6},{8,9},{9,8},{10,11... | collective-permute-start | bytes 25165832 | tf_op jit(solution)/shard_map/ppermute | solution.py:28
  3.5 49.4 %collective-permute-start.5 = (bf16[64,128,128]{2,1,0:T(8,128)(2,1)}, bf16[64,128,128]{2,1,0:T(8,128)(2,1)}, u32[]{:S(2)}, u32[]{:S(2)}) collective-permute-start(bf16[64,128,128]{2,1,0:T(8,128)(2,1)} %shard_map.56.refs_6_), channel_id=1, source_target_pairs={{0,2},{1,3},{2,0},{3,1},{4,6},{5,7},{6,4},{7,5},{8,10},{9,11},{10,... | collective-permute-start | bytes 6291464 | tf_op jit(solution)/shard_map/ppermute | solution.py:28
  7.8 90.0 %collective-permute-start.14 = (bf16[64,128,128]{2,1,0:T(8,128)(2,1)S(1)}, bf16[64,128,128]{2,1,0:T(8,128)(2,1)}, u32[]{:S(2)}, u32[]{:S(2)}) collective-permute-start(bf16[64,128,128]{2,1,0:T(8,128)(2,1)S(1)} %shard_map.59.refs_6_), channel_id=1, source_target_pairs={{0,2},{1,3},{2,0},{3,1},{4,6},{5,7},{6,4},{7,5},{8,10},{9,11},{10,... | collective-permute-start | bytes 6291464 | tf_op jit(solution)/shard_map/ppermute | solution.py:28
  11.7 6.6 %collective-permute-start.2 = (bf16[256,128]{1,0:T(8,128)(2,1)S(1)}, bf16[256,128]{1,0:T(8,128)(2,1)S(1)}, u32[]{:S(2)}, u32[]{:S(2)}) collective-permute-start(bf16[256,128]{1,0:T(8,128)(2,1)S(1)} %get-tuple-element.54), channel_id=1, source_target_pairs={{24,0},{28,4},{0,8},{4,12},{8,16},{12,20},{16,24},{20,28},{25,1},{... | collective-permute-start | bytes 196616 | tf_op jit(solution)/shard_map/ppermute | solution.py:23
  13.8 7.8 %collective-permute-start = (bf16[256,128]{1,0:T(8,128)(2,1)S(1)}, bf16[256,128]{1,0:T(8,128)(2,1)S(1)}, u32[]{:S(2)}, u32[]{:S(2)}) collective-permute-start(bf16[256,128]{1,0:T(8,128)(2,1)S(1)} %get-tuple-element.52), channel_id=1, source_target_pairs={{16,0},{20,4},{24,8},{28,12},{0,16},{4,20},{8,24},{12,28},{17,1},{... | collective-permute-start | bytes 196616 | tf_op jit(solution)/shard_map/ppermute | solution.py:23
  18.3 5.8 %collective-permute-start.3 = (bf16[256,128]{1,0:T(8,128)(2,1)S(1)}, bf16[256,128]{1,0:T(8,128)(2,1)S(1)}, u32[]{:S(2)}, u32[]{:S(2)}) collective-permute-start(bf16[256,128]{1,0:T(8,128)(2,1)S(1)} %get-tuple-element.56), channel_id=1, source_target_pairs={{4,0},{8,4},{12,8},{16,12},{20,16},{24,20},{28,24},{0,28},{5,1},{9... | collective-permute-start | bytes 196616 | tf_op jit(solution)/shard_map/ppermute | solution.py:23
  21.6 7.0 %collective-permute-start.1 = (bf16[256,128]{1,0:T(8,128)(2,1)S(1)}, bf16[256,128]{1,0:T(8,128)(2,1)S(1)}, u32[]{:S(2)}, u32[]{:S(2)}) collective-permute-start(bf16[256,128]{1,0:T(8,128)(2,1)S(1)} %get-tuple-element.53), channel_id=1, source_target_pairs={{28,0},{0,4},{4,8},{8,12},{12,16},{16,20},{20,24},{24,28},{29,1},{... | collective-permute-start | bytes 196616 | tf_op jit(solution)/shard_map/ppermute | solution.py:23
  54.6 4.8 %collective-permute-start.7 = (bf16[16,128,128]{2,1,0:T(8,128)(2,1)S(1)}, bf16[16,128,128]{2,1,0:T(8,128)(2,1)S(1)}, u32[]{:S(2)}, u32[]{:S(2)}) collective-permute-start(bf16[16,128,128]{2,1,0:T(8,128)(2,1)S(1)} %get-tuple-element.103), channel_id=1, source_target_pairs={{0,1},{1,0},{2,3},{3,2},{4,5},{5,4},{6,7},{7,6},{8,9},{9,8},{10,11... | collective-permute-start | bytes 1572872 | tf_op jit(solution)/shard_map/ppermute | solution.py:28
  55.1 4.3 %collective-permute-start.8 = (bf16[16,128,128]{2,1,0:T(8,128)(2,1)S(1)}, bf16[16,128,128]{2,1,0:T(8,128)(2,1)S(1)}, u32[]{:S(2)}, u32[]{:S(2)}) collective-permute-start(bf16[16,128,128]{2,1,0:T(8,128)(2,1)S(1)} %get-tuple-element.102), channel_id=1, source_target_pairs={{0,1},{1,0},{2,3},{3,2},{4,5},{5,4},{6,7},{7,6},{8,9},{9,8},{10,11... | collective-permute-start | bytes 1572872 | tf_op jit(solution)/shard_map/ppermute | solution.py:28
  55.2 4.2 %collective-permute-start.9 = (bf16[16,128,128]{2,1,0:T(8,128)(2,1)S(1)}, bf16[16,128,128]{2,1,0:T(8,128)(2,1)S(1)}, u32[]{:S(2)}, u32[]{:S(2)}) collective-permute-start(bf16[16,128,128]{2,1,0:T(8,128)(2,1)S(1)} %get-tuple-element.101), channel_id=1, source_target_pairs={{0,1},{1,0},{2,3},{3,2},{4,5},{5,4},{6,7},{7,6},{8,9},{9,8},{10,11... | collective-permute-start | bytes 1572872 | tf_op jit(solution)/shard_map/ppermute | solution.py:28
  57.4 74.0 %collective-permute-start.23 = (bf16[48,128,128]{2,1,0:T(8,128)(2,1)S(1)}, bf16[48,128,128]{2,1,0:T(8,128)(2,1)S(1)}, u32[]{:S(2)}, u32[]{:S(2)}) collective-permute-start(bf16[48,128,128]{2,1,0:T(8,128)(2,1)S(1)} %get-tuple-element.73.refs_6_), channel_id=1, source_target_pairs={{0,2},{1,3},{2,0},{3,1},{4,6},{5,7},{6,4},{7,5},{8,10},{9,11},{10,... | collective-permute-start | bytes 4718600 | tf_op jit(solution)/shard_map/ppermute | solution.py:28
  71.2 6.6 %collective-permute-start.12 = (bf16[256,128]{1,0:T(8,128)(2,1)S(1)}, bf16[256,128]{1,0:T(8,128)(2,1)S(1)}, u32[]{:S(2)}, u32[]{:S(2)}) collective-permute-start(bf16[256,128]{1,0:T(8,128)(2,1)S(1)} %get-tuple-element.62), channel_id=1, source_target_pairs={{24,0},{28,4},{0,8},{4,12},{8,16},{12,20},{16,24},{20,28},{25,1},{... | collective-permute-start | bytes 196616 | tf_op jit(solution)/shard_map/ppermute | solution.py:23
  72.8 7.8 %collective-permute-start.10 = (bf16[256,128]{1,0:T(8,128)(2,1)S(1)}, bf16[256,128]{1,0:T(8,128)(2,1)S(1)}, u32[]{:S(2)}, u32[]{:S(2)}) collective-permute-start(bf16[256,128]{1,0:T(8,128)(2,1)S(1)} %get-tuple-element.60), channel_id=1, source_target_pairs={{16,0},{20,4},{24,8},{28,12},{0,16},{4,20},{8,24},{12,28},{17,1},{... | collective-permute-start | bytes 196616 | tf_op jit(solution)/shard_map/ppermute | solution.py:23
  77.8 20.1 %collective-permute-start.13 = (bf16[256,128]{1,0:T(8,128)(2,1)S(1)}, bf16[256,128]{1,0:T(8,128)(2,1)S(1)}, u32[]{:S(2)}, u32[]{:S(2)}) collective-permute-start(bf16[256,128]{1,0:T(8,128)(2,1)S(1)} %get-tuple-element.64), channel_id=1, source_target_pairs={{4,0},{8,4},{12,8},{16,12},{20,16},{24,20},{28,24},{0,28},{5,1},{9... | collective-permute-start | bytes 196616 | tf_op jit(solution)/shard_map/ppermute | solution.py:23
  80.6 17.2 %collective-permute-start.11 = (bf16[256,128]{1,0:T(8,128)(2,1)S(1)}, bf16[256,128]{1,0:T(8,128)(2,1)S(1)}, u32[]{:S(2)}, u32[]{:S(2)}) collective-permute-start(bf16[256,128]{1,0:T(8,128)(2,1)S(1)} %get-tuple-element.61), channel_id=1, source_target_pairs={{28,0},{0,4},{4,8},{8,12},{12,16},{16,20},{20,24},{24,28},{29,1},{... | collective-permute-start | bytes 196616 | tf_op jit(solution)/shard_map/ppermute | solution.py:23
  99.6 3.8 %collective-permute-start.16 = (bf16[16,128,128]{2,1,0:T(8,128)(2,1)S(1)}, bf16[16,128,128]{2,1,0:T(8,128)(2,1)S(1)}, u32[]{:S(2)}, u32[]{:S(2)}) collective-permute-start(bf16[16,128,128]{2,1,0:T(8,128)(2,1)S(1)} %get-tuple-element.99), channel_id=1, source_target_pairs={{0,1},{1,0},{2,3},{3,2},{4,5},{5,4},{6,7},{7,6},{8,9},{9,8},{10,11... | collective-permute-start | bytes 1572872 | tf_op jit(solution)/shard_map/ppermute | solution.py:28
  100.2 3.6 %collective-permute-start.18 = (bf16[16,128,128]{2,1,0:T(8,128)(2,1)S(1)}, bf16[16,128,128]{2,1,0:T(8,128)(2,1)S(1)}, u32[]{:S(2)}, u32[]{:S(2)}) collective-permute-start(bf16[16,128,128]{2,1,0:T(8,128)(2,1)S(1)} %get-tuple-element.97), channel_id=1, source_target_pairs={{0,1},{1,0},{2,3},{3,2},{4,5},{5,4},{6,7},{7,6},{8,9},{9,8},{10,11... | collective-permute-start | bytes 1572872 | tf_op jit(solution)/shard_map/ppermute | solution.py:28
  101.5 41.2 %collective-permute-start.24 = (bf16[16,128,128]{2,1,0:T(8,128)(2,1)S(1)}, bf16[16,128,128]{2,1,0:T(8,128)(2,1)S(1)}, u32[]{:S(2)}, u32[]{:S(2)}) collective-permute-start(bf16[16,128,128]{2,1,0:T(8,128)(2,1)S(1)} %get-tuple-element.74.refs_7_), channel_id=1, source_target_pairs={{0,2},{1,3},{2,0},{3,1},{4,6},{5,7},{6,4},{7,5},{8,10},{9,11},{10,... | collective-permute-start | bytes 1572872 | tf_op jit(solution)/shard_map/ppermute | solution.py:28
  112.5 8.1 %collective-permute-start.21 = (bf16[256,128]{1,0:T(8,128)(2,1)S(1)}, bf16[256,128]{1,0:T(8,128)(2,1)S(1)}, u32[]{:S(2)}, u32[]{:S(2)}) collective-permute-start(bf16[256,128]{1,0:T(8,128)(2,1)S(1)} %get-tuple-element.70), channel_id=1, source_target_pairs={{24,0},{28,4},{0,8},{4,12},{8,16},{12,20},{16,24},{20,28},{25,1},{... | collective-permute-start | bytes 196616 | tf_op jit(solution)/shard_map/ppermute | solution.py:23
  114.6 8.3 %collective-permute-start.19 = (bf16[256,128]{1,0:T(8,128)(2,1)S(1)}, bf16[256,128]{1,0:T(8,128)(2,1)S(1)}, u32[]{:S(2)}, u32[]{:S(2)}) collective-permute-start(bf16[256,128]{1,0:T(8,128)(2,1)S(1)} %get-tuple-element.68), channel_id=1, source_target_pairs={{16,0},{20,4},{24,8},{28,12},{0,16},{4,20},{8,24},{12,28},{17,1},{... | collective-permute-start | bytes 196616 | tf_op jit(solution)/shard_map/ppermute | solution.py:23
  119.1 47.7 %collective-permute-start.33 = (bf16[32,128,128]{2,1,0:T(8,128)(2,1)S(1)}, bf16[32,128,128]{2,1,0:T(8,128)(2,1)S(1)}, u32[]{:S(2)}, u32[]{:S(2)}) collective-permute-start(bf16[32,128,128]{2,1,0:T(8,128)(2,1)S(1)} %get-tuple-element.86.refs_6_), channel_id=1, source_target_pairs={{0,2},{1,3},{2,0},{3,1},{4,6},{5,7},{6,4},{7,5},{8,10},{9,11},{10,... | collective-permute-start | bytes 3145736 | tf_op jit(solution)/shard_map/ppermute | solution.py:28
  120.6 10.8 %collective-permute-start.22 = (bf16[256,128]{1,0:T(8,128)(2,1)S(1)}, bf16[256,128]{1,0:T(8,128)(2,1)S(1)}, u32[]{:S(2)}, u32[]{:S(2)}) collective-permute-start(bf16[256,128]{1,0:T(8,128)(2,1)S(1)} %get-tuple-element.72), channel_id=1, source_target_pairs={{4,0},{8,4},{12,8},{16,12},{20,16},{24,20},{28,24},{0,28},{5,1},{9... | collective-permute-start | bytes 196616 | tf_op jit(solution)/shard_map/ppermute | solution.py:23
  122.9 8.5 %collective-permute-start.20 = (bf16[256,128]{1,0:T(8,128)(2,1)S(1)}, bf16[256,128]{1,0:T(8,128)(2,1)S(1)}, u32[]{:S(2)}, u32[]{:S(2)}) collective-permute-start(bf16[256,128]{1,0:T(8,128)(2,1)S(1)} %get-tuple-element.69), channel_id=1, source_target_pairs={{28,0},{0,4},{4,8},{8,12},{12,16},{16,20},{20,24},{24,28},{29,1},{... | collective-permute-start | bytes 196616 | tf_op jit(solution)/shard_map/ppermute | solution.py:23
  142.8 3.7 %collective-permute-start.25 = (bf16[16,128,128]{2,1,0:T(8,128)(2,1)S(1)}, bf16[16,128,128]{2,1,0:T(8,128)(2,1)S(1)}, u32[]{:S(2)}, u32[]{:S(2)}) collective-permute-start(bf16[16,128,128]{2,1,0:T(8,128)(2,1)S(1)} %get-tuple-element.107), channel_id=1, source_target_pairs={{0,1},{1,0},{2,3},{3,2},{4,5},{5,4},{6,7},{7,6},{8,9},{9,8},{10,11... | collective-permute-start | bytes 1572872 | tf_op jit(solution)/shard_map/ppermute | solution.py:28
  144.6 31.8 %collective-permute-start.34 = (bf16[16,128,128]{2,1,0:T(8,128)(2,1)S(1)}, bf16[16,128,128]{2,1,0:T(8,128)(2,1)S(1)}, u32[]{:S(2)}, u32[]{:S(2)}) collective-permute-start(bf16[16,128,128]{2,1,0:T(8,128)(2,1)S(1)} %get-tuple-element.87.refs_7_), channel_id=1, source_target_pairs={{0,2},{1,3},{2,0},{3,1},{4,6},{5,7},{6,4},{7,5},{8,10},{9,11},{10,... | collective-permute-start | bytes 1572872 | tf_op jit(solution)/shard_map/ppermute | solution.py:28
  154.1 6.7 %collective-permute-start.31 = (bf16[256,128]{1,0:T(8,128)(2,1)S(1)}, bf16[256,128]{1,0:T(8,128)(2,1)S(1)}, u32[]{:S(2)}, u32[]{:S(2)}) collective-permute-start(bf16[256,128]{1,0:T(8,128)(2,1)S(1)} %get-tuple-element.83), channel_id=1, source_target_pairs={{24,0},{28,4},{0,8},{4,12},{8,16},{12,20},{16,24},{20,28},{25,1},{... | collective-permute-start | bytes 196616 | tf_op jit(solution)/shard_map/ppermute | solution.py:23
  156.2 8.0 %collective-permute-start.29 = (bf16[256,128]{1,0:T(8,128)(2,1)S(1)}, bf16[256,128]{1,0:T(8,128)(2,1)S(1)}, u32[]{:S(2)}, u32[]{:S(2)}) collective-permute-start(bf16[256,128]{1,0:T(8,128)(2,1)S(1)} %get-tuple-element.81), channel_id=1, source_target_pairs={{16,0},{20,4},{24,8},{28,12},{0,16},{4,20},{8,24},{12,28},{17,1},{... | collective-permute-start | bytes 196616 | tf_op jit(solution)/shard_map/ppermute | solution.py:23
  160.8 6.0 %collective-permute-start.32 = (bf16[256,128]{1,0:T(8,128)(2,1)S(1)}, bf16[256,128]{1,0:T(8,128)(2,1)S(1)}, u32[]{:S(2)}, u32[]{:S(2)}) collective-permute-start(bf16[256,128]{1,0:T(8,128)(2,1)S(1)} %get-tuple-element.85), channel_id=1, source_target_pairs={{4,0},{8,4},{12,8},{16,12},{20,16},{24,20},{28,24},{0,28},{5,1},{9... | collective-permute-start | bytes 196616 | tf_op jit(solution)/shard_map/ppermute | solution.py:23
  164.2 7.0 %collective-permute-start.30 = (bf16[256,128]{1,0:T(8,128)(2,1)S(1)}, bf16[256,128]{1,0:T(8,128)(2,1)S(1)}, u32[]{:S(2)}, u32[]{:S(2)}) collective-permute-start(bf16[256,128]{1,0:T(8,128)(2,1)S(1)} %get-tuple-element.82), channel_id=1, source_target_pairs={{28,0},{0,4},{4,8},{8,12},{12,16},{16,20},{20,24},{24,28},{29,1},{... | collective-permute-start | bytes 196616 | tf_op jit(solution)/shard_map/ppermute | solution.py:23
  171.2 7.2 %collective-permute-start.35 = (bf16[16,128,128]{2,1,0:T(8,128)(2,1)S(1)}, bf16[16,128,128]{2,1,0:T(8,128)(2,1)S(1)}, u32[]{:S(2)}, u32[]{:S(2)}) collective-permute-start(bf16[16,128,128]{2,1,0:T(8,128)(2,1)S(1)} %get-tuple-element.109), channel_id=1, source_target_pairs={{0,1},{1,0},{2,3},{3,2},{4,5},{5,4},{6,7},{7,6},{8,9},{9,8},{10,11... | collective-permute-start | bytes 1572872 | tf_op jit(solution)/shard_map/ppermute | solution.py:28
  171.3 7.1 %collective-permute-start.36 = (bf16[16,128,128]{2,1,0:T(8,128)(2,1)S(1)}, bf16[16,128,128]{2,1,0:T(8,128)(2,1)S(1)}, u32[]{:S(2)}, u32[]{:S(2)}) collective-permute-start(bf16[16,128,128]{2,1,0:T(8,128)(2,1)S(1)} %get-tuple-element.108), channel_id=1, source_target_pairs={{0,1},{1,0},{2,3},{3,2},{4,5},{5,4},{6,7},{7,6},{8,9},{9,8},{10,11... | collective-permute-start | bytes 1572872 | tf_op jit(solution)/shard_map/ppermute | solution.py:28
  171.8 15.6 %collective-permute-start.39 = (bf16[16,128,128]{2,1,0:T(8,128)(2,1)S(1)}, bf16[16,128,128]{2,1,0:T(8,128)(2,1)S(1)}, u32[]{:S(2)}, u32[]{:S(2)}) collective-permute-start(bf16[16,128,128]{2,1,0:T(8,128)(2,1)S(1)} %get-tuple-element.94.refs_2_), channel_id=1, source_target_pairs={{0,2},{1,3},{2,0},{3,1},{4,6},{5,7},{6,4},{7,5},{8,10},{9,11},{10,... | collective-permute-start | bytes 1572872 | tf_op jit(solution)/shard_map/ppermute | solution.py:28
  (13 other events, 43.5 us)

commit v9 on v8

--- a/solution.py
+++ b/solution.py
@@ -241,16 +241,17 @@
                 )
 
     last = layer_count - 1
-    shares = [(layer, (16,), (4,)) for layer in range(last - 1)]
+    shares = [(0, (8, 8), (2, 2))] + [(layer, (16,), (4,)) for layer in range(1, last - 1)]
     shares += [(last - 1, (12, 4), (3, 1))]
-    shares += [(last, (8, 4), (2, 2)), (last, (4,), (1,))]
+    shares += [(last, (8, 4), (2, 2)), (last, (3, 1), (3, 1))]
 
     moves = {layer: [] for layer in range(layer_count)}
     for layer, sizes, _ in shares:
         for size in sizes:
             start = sum(count for _, _, count in moves[layer])
             moves[layer].append((layer, start, size * unit))
-    mine = {layer: cut(tile_weights, moves[layer]) for layer in moves}
+    mine = {layer: cut(tile_weights, moves[layer]) for layer in moves if layer}
+    mine[0] = [cut(tile_weights, [move])[0] for move in moves[0]]
     crossed = {layer: [swapped(tile, far * sharers) for tile in mine[layer]] for layer in moves}
 
     whole = [tile_weights] + [None] * (fan - 1)
@@ -274,15 +275,15 @@
         tiles = [None] * fan
         for m, source in enumerate([mine[layer], *near[layer], crossed[layer]]):
             tiles[m] = [source.pop(0) for _ in sizes]
-        passed = []
         for number, tile in zip(pieces, tiles[far]):
             tile = lax.optimization_barrier((tile, *after))[0]
-            after = [*after, tile]
             share = tile.shape[0] // math.gcd(number, tile.shape[0])
-            passed += [tile[start : start + share] for start in range(0, tile.shape[0], share)]
-        held, tiles[far] = tiles[far], passed
-        spread(tiles, far)
-        tiles[far] = held
+            passed = [None] * fan
+            passed[far] = [tile[start : start + share] for start in range(0, tile.shape[0], share)]
+            spread(passed, far)
+            for m in range(far + 1, fan):
+                tiles[m] = [*(tiles[m] or []), *passed[m]]
+                after = [*after, *passed[m]]
         count = sum(sizes) * unit
         sends = codes.size + (layer + 1) * NEIGH
         target, pool, outgoing = run_blocks(

time: 194 us -> 192 us (0.990)
  waiting for transfers between devices: 82.7 us -> 77.2 us
  starting transfers between devices: 49.2 us -> 51.2 us
    ppermute x25 -> x30, waiting for transfers between devices: 67.6 us -> 54.2 us  [swapped(): return lax.ppermute(block, 'batch', route)]
    ppermute x16, waiting for transfers between devices: 15.1 us -> 22.9 us  [shifted(): return lax.ppermute(block, axis, route)]
    ppermute x25 -> x30, starting transfers between devices: 16.4 us -> 20.1 us  [swapped(): return lax.ppermute(block, 'batch', route)]
    pallas_call x8 -> x9, Pallas kernels: 15.5 us -> 16.8 us  [cut(): pl.pallas_call(kernel, out_shape=[pltpu.VMEM((count, height, width), tile...]
    slice x5 -> x7, local copies, waits for them, and re-layouts: 3.61 us -> 4.53 us  [body(): tile[start:start + share]]
  transfers between devices with their start and end apart: 41 -> 46, of which waited for: 18 -> 23; matrix products, arithmetic and copies ran while one was open for 3% -> 3% of each run, Pallas kernels for 27% -> 27%
where the time goes in v9:
time: 192 us; the launch traced here: 191 us
  waiting for transfers between devices  77.2 us (40%)
  Pallas kernels  55.6 us (29%)
  starting transfers between devices  51.2 us (27%)
  local copies, waits for them, and re-layouts  5.94 us (3%)
    ppermute x30, waiting for transfers between devices, swapped(): return lax.ppermute(block, 'batch', route)  54.2 us
    pallas_call x5, Pallas kernels, run_blocks(): pl.pallas_call(kernel, out_shape=out_shape, grid_spec=pltpu.PrefetchScala...  37.2 us
    ppermute x16, starting transfers between devices, shifted(): return lax.ppermute(block, axis, route)  31.1 us
    ppermute x16, waiting for transfers between devices, shifted(): return lax.ppermute(block, axis, route)  22.9 us
    ppermute x30, starting transfers between devices, swapped(): return lax.ppermute(block, 'batch', route)  20.1 us
    pallas_call x9, Pallas kernels, cut(): pl.pallas_call(kernel, out_shape=[pltpu.VMEM((count, height, width), tile...  16.8 us
    slice x7, local copies, waits for them, and re-layouts, body(): tile[start:start + share]  4.53 us
  transfers between devices with their start and end apart: 46, of which 23 were waited for; matrix products, arithmetic and copies ran while one was open for 3% of the time, Pallas kernels for 27%

profile of v9, /device:TPU:0, one launch (start us, length us, event | category | flops | bytes accessed | tf_op | source)
XLA Modules:
  0.0 191.0 jit_solution(5160281873199661642)
XLA Ops:
  1.8 2.6 %collective-permute-start.5 = (bf16[32,128,128]{2,1,0:T(8,128)(2,1)S(1)}, bf16[32,128,128]{2,1,0:T(8,128)(2,1)}, u32[]{:S(2)}, u32[]{:S(2)}) collective-permute-start(bf16[32,128,128]{2,1,0:T(8,128)(2,1)S(1)} %shard_map.56.refs_6_), channel_id=1, source_target_pairs={{0,2},{1,3},{2,0},{3,1},{4,6},{5,7},{6,4},{7,5},{8,10},{9,11},{10,... | collective-permute-start | bytes 3145736 | tf_op jit(solution)/shard_map/ppermute | solution.py:28
  4.4 2.3 %shard_map.57.refs_7_ = bf16[32,128,128]{2,1,0:T(8,128)(2,1)} custom-call(bf16[4,64,128,128]{3,2,1,0:T(8,128)(2,1)} %tiles.9), custom_call_target="tpu_custom_call" | custom-call | tf_op jit(solution)/shard_map/pallas_call | solution.py:56
  8.6 2.1 %collective-permute-start.15 = (bf16[64,128,128]{2,1,0:T(8,128)(2,1)S(1)}, bf16[64,128,128]{2,1,0:T(8,128)(2,1)}, u32[]{:S(2)}, u32[]{:S(2)}) collective-permute-start(bf16[64,128,128]{2,1,0:T(8,128)(2,1)S(1)} %shard_map.60.refs_6_), channel_id=1, source_target_pairs={{0,2},{1,3},{2,0},{3,1},{4,6},{5,7},{6,4},{7,5},{8,10},{9,11},{10,... | collective-permute-start | bytes 6291464 | tf_op jit(solution)/shard_map/ppermute | solution.py:28
  16.0 4.5 %collective-permute-done.2.refs_3_ = bf16[256,128]{1,0:T(8,128)(2,1)S(1)} collective-permute-done((bf16[256,128]{1,0:T(8,128)(2,1)S(1)}, bf16[256,128]{1,0:T(8,128)(2,1)S(1)}, u32[]{:S(2)}, u32[]{:S(2)}) %collective-permute-start.2) | collective-permute-done | bytes 65568 | tf_op jit(solution)/shard_map/ppermute | solution.py:23
  21.3 4.4 %collective-permute-done.refs_5_ = bf16[256,128]{1,0:T(8,128)(2,1)S(1)} collective-permute-done((bf16[256,128]{1,0:T(8,128)(2,1)S(1)}, bf16[256,128]{1,0:T(8,128)(2,1)S(1)}, u32[]{:S(2)}, u32[]{:S(2)}) %collective-permute-start) | collective-permute-done | bytes 65568 | tf_op jit(solution)/shard_map/ppermute | solution.py:23
  25.6 3.3 %collective-permute-start.3 = (bf16[256,128]{1,0:T(8,128)(2,1)S(1)}, bf16[256,128]{1,0:T(8,128)(2,1)S(1)}, u32[]{:S(2)}, u32[]{:S(2)}) collective-permute-start(bf16[256,128]{1,0:T(8,128)(2,1)S(1)} %get-tuple-element.62), channel_id=1, source_target_pairs={{4,0},{8,4},{12,8},{16,12},{20,16},{24,20},{28,24},{0,28},{5,1},{9... | collective-permute-start | bytes 196616 | tf_op jit(solution)/shard_map/ppermute | solution.py:23
  30.9 5.1 %collective-permute-done.1.refs_2_ = bf16[256,128]{1,0:T(8,128)(2,1)S(1)} collective-permute-done((bf16[256,128]{1,0:T(8,128)(2,1)S(1)}, bf16[256,128]{1,0:T(8,128)(2,1)S(1)}, u32[]{:S(2)}, u32[]{:S(2)}) %collective-permute-start.1) | collective-permute-done | bytes 65568 | tf_op jit(solution)/shard_map/ppermute | solution.py:23
  37.8 13.2 %collective-permute-done.6.refs_11_ = bf16[32,128,128]{2,1,0:T(8,128)(2,1)} collective-permute-done((bf16[32,128,128]{2,1,0:T(8,128)(2,1)}, bf16[32,128,128]{2,1,0:T(8,128)(2,1)}, u32[]{:S(2)}, u32[]{:S(2)}) %collective-permute-start.6) | collective-permute-done | bytes 1048608 | tf_op jit(solution)/shard_map/ppermute | solution.py:28
  54.6 2.0 %collective-permute-start.24 = (bf16[48,128,128]{2,1,0:T(8,128)(2,1)S(1)}, bf16[48,128,128]{2,1,0:T(8,128)(2,1)S(1)}, u32[]{:S(2)}, u32[]{:S(2)}) collective-permute-start(bf16[48,128,128]{2,1,0:T(8,128)(2,1)S(1)} %get-tuple-element.82.refs_6_), channel_id=1, source_target_pairs={{0,2},{1,3},{2,0},{3,1},{4,6},{5,7},{6,4},{7,5},{8,10},{9,11},{10,... | collective-permute-start | bytes 4718600 | tf_op jit(solution)/shard_map/ppermute | solution.py:28
  56.6 11.4 %shard_map.59 = (bf16[68,256,128]{2,1,0:T(8,128)(2,1)S(1)}, bf16[256,128]{1,0:T(8,128)(2,1)S(1)}, bf16[256,128]{1,0:T(8,128)(2,1)S(1)}, bf16[256,128]{1,0:T(8,128)(2,1)S(1)}, bf16[256,128]{1,0:T(8,128)(2,1)S(1)}) custom-call(s32[1040]{0:T(1024)S(1)} %constant_dynamic-update-slice_fusion.table.refs_0_, bf16[256,8192]{1,0:T(8,128)(2,1)} %refs_1_.1, ...), custom_call_target="tpu_custom_call" | custom-call | tf_op jit(solution)/shard_map/pallas_call | solution.py:205
  69.7 2.6 %collective-permute-start.11 = (bf16[256,128]{1,0:T(8,128)(2,1)S(1)}, bf16[256,128]{1,0:T(8,128)(2,1)S(1)}, u32[]{:S(2)}, u32[]{:S(2)}) collective-permute-start(bf16[256,128]{1,0:T(8,128)(2,1)S(1)} %get-tuple-element.69), channel_id=1, source_target_pairs={{16,0},{20,4},{24,8},{28,12},{0,16},{4,20},{8,24},{12,28},{17,1},{... | collective-permute-start | bytes 196616 | tf_op jit(solution)/shard_map/ppermute | solution.py:23
  72.3 2.3 %collective-permute-done.13.refs_3_ = bf16[256,128]{1,0:T(8,128)(2,1)S(1)} collective-permute-done((bf16[256,128]{1,0:T(8,128)(2,1)S(1)}, bf16[256,128]{1,0:T(8,128)(2,1)S(1)}, u32[]{:S(2)}, u32[]{:S(2)}) %collective-permute-start.13) | collective-permute-done | bytes 65568 | tf_op jit(solution)/shard_map/ppermute | solution.py:23
  74.7 2.8 %collective-permute-start.14 = (bf16[256,128]{1,0:T(8,128)(2,1)S(1)}, bf16[256,128]{1,0:T(8,128)(2,1)S(1)}, u32[]{:S(2)}, u32[]{:S(2)}) collective-permute-start(bf16[256,128]{1,0:T(8,128)(2,1)S(1)} %get-tuple-element.73), channel_id=1, source_target_pairs={{4,0},{8,4},{12,8},{16,12},{20,16},{24,20},{28,24},{0,28},{5,1},{9... | collective-permute-start | bytes 196616 | tf_op jit(solution)/shard_map/ppermute | solution.py:23
  79.9 16.0 %collective-permute-done.15.refs_8_ = bf16[64,128,128]{2,1,0:T(8,128)(2,1)} collective-permute-done((bf16[64,128,128]{2,1,0:T(8,128)(2,1)S(1)}, bf16[64,128,128]{2,1,0:T(8,128)(2,1)}, u32[]{:S(2)}, u32[]{:S(2)}) %collective-permute-start.15) | collective-permute-done | bytes 2097184 | tf_op jit(solution)/shard_map/ppermute | solution.py:28
  101.8 8.8 %shard_map.62 = (bf16[68,256,128]{2,1,0:T(8,128)(2,1)S(1)}, bf16[68,256,128]{2,1,0:T(8,128)(2,1)S(1)}, bf16[256,128]{1,0:T(8,128)(2,1)S(1)}, bf16[256,128]{1,0:T...) custom-call(s32[1040]{0:T(1024)S(1)} %constant_dynamic-update-slice_, ...), custom_call_target="tpu_custom_call", output_to_operand_aliasing={{1}: (1, {})} | custom-call | tf_op jit(solution)/shard_map/pallas_call | solution.py:205
  110.6 2.1 %collective-permute-start.22 = (bf16[256,128]{1,0:T(8,128)(2,1)S(1)}, bf16[256,128]{1,0:T(8,128)(2,1)S(1)}, u32[]{:S(2)}, u32[]{:S(2)}) collective-permute-start(bf16[256,128]{1,0:T(8,128)(2,1)S(1)} %get-tuple-element.79), channel_id=1, source_target_pairs={{24,0},{28,4},{0,8},{4,12},{8,16},{12,20},{16,24},{20,28},{25,1},{... | collective-permute-start | bytes 196616 | tf_op jit(solution)/shard_map/ppermute | solution.py:23
  112.7 2.6 %collective-permute-start.20 = (bf16[256,128]{1,0:T(8,128)(2,1)S(1)}, bf16[256,128]{1,0:T(8,128)(2,1)S(1)}, u32[]{:S(2)}, u32[]{:S(2)}) collective-permute-start(bf16[256,128]{1,0:T(8,128)(2,1)S(1)} %get-tuple-element.77), channel_id=1, source_target_pairs={{16,0},{20,4},{24,8},{28,12},{0,16},{4,20},{8,24},{12,28},{17,1},{... | collective-permute-start | bytes 196616 | tf_op jit(solution)/shard_map/ppermute | solution.py:23
  115.3 2.0 %collective-permute-done.22.refs_3_ = bf16[256,128]{1,0:T(8,128)(2,1)S(1)} collective-permute-done((bf16[256,128]{1,0:T(8,128)(2,1)S(1)}, bf16[256,128]{1,0:T(8,128)(2,1)S(1)}, u32[]{:S(2)}, u32[]{:S(2)}) %collective-permute-start.22) | collective-permute-done | bytes 65568 | tf_op jit(solution)/shard_map/ppermute | solution.py:23
  117.3 3.4 %collective-permute-start.23 = (bf16[256,128]{1,0:T(8,128)(2,1)S(1)}, bf16[256,128]{1,0:T(8,128)(2,1)S(1)}, u32[]{:S(2)}, u32[]{:S(2)}) collective-permute-start(bf16[256,128]{1,0:T(8,128)(2,1)S(1)} %get-tuple-element.81), channel_id=1, source_target_pairs={{4,0},{8,4},{12,8},{16,12},{20,16},{24,20},{28,24},{0,28},{5,1},{9... | collective-permute-start | bytes 196616 | tf_op jit(solution)/shard_map/ppermute | solution.py:23
  124.7 4.8 %collective-permute-done.24.refs_10_ = bf16[48,128,128]{2,1,0:T(8,128)(2,1)S(1)} collective-permute-done((bf16[48,128,128]{2,1,0:T(8,128)(2,1)S(1)}, bf16[48,128,128]{2,1,0:T(8,128)(2,1)S(1)}, u32[]{:S(2)}, u32[]{:S(2)}) %collective-permute-start.24) | collective-permute-done | bytes 1572896 | tf_op jit(solution)/shard_map/ppermute | solution.py:28
  130.4 2.1 %shard_map.66 = (bf16[32,128,128]{2,1,0:T(8,128)(2,1)S(1)}, bf16[16,128,128]{2,1,0:T(8,128)(2,1)S(1)}, bf16[12,128,128]{2,1,0:T(8,128)(2,1)S(1)}, bf16[4,128,128]{2,1,0:T(8,128)(2,1)S(1)}) custom-call(bf16[4,64,128,128]{3,2,1,0:T(8,128)(2,1)} %tiles.9), custom_call_target="tpu_custom_call" | custom-call | tf_op jit(solution)/shard_map/pallas_call | solution.py:56
  134.5 6.2 %collective-permute-done.25.refs_11_ = bf16[16,128,128]{2,1,0:T(8,128)(2,1)S(1)} collective-permute-done((bf16[16,128,128]{2,1,0:T(8,128)(2,1)S(1)}, bf16[16,128,128]{2,1,0:T(8,128)(2,1)S(1)}, u32[]{:S(2)}, u32[]{:S(2)}) %collective-permute-start.25) | collective-permute-done | bytes 524320 | tf_op jit(solution)/shard_map/ppermute | solution.py:28
  142.8 7.2 %shard_map.65 = (bf16[68,256,128]{2,1,0:T(8,128)(2,1)S(1)}, bf16[68,256,128]{2,1,0:T(8,128)(2,1)S(1)}, bf16[256,128]{1,0:T(8,128)(2,1)S(1)}, bf16[256,128]{1,0:T...) custom-call(s32[1040]{0:T(1024)S(1)} %constant_dynamic-update-slice_, ...), custom_call_target="tpu_custom_call", output_to_operand_aliasing={{1}: (1, {})} | custom-call | tf_op jit(solution)/shard_map/pallas_call | solution.py:205
  150.0 2.1 %collective-permute-start.32 = (bf16[256,128]{1,0:T(8,128)(2,1)S(1)}, bf16[256,128]{1,0:T(8,128)(2,1)S(1)}, u32[]{:S(2)}, u32[]{:S(2)}) collective-permute-start(bf16[256,128]{1,0:T(8,128)(2,1)S(1)} %get-tuple-element.92), channel_id=1, source_target_pairs={{24,0},{28,4},{0,8},{4,12},{8,16},{12,20},{16,24},{20,28},{25,1},{... | collective-permute-start | bytes 196616 | tf_op jit(solution)/shard_map/ppermute | solution.py:23
  152.1 2.6 %collective-permute-start.30 = (bf16[256,128]{1,0:T(8,128)(2,1)S(1)}, bf16[256,128]{1,0:T(8,128)(2,1)S(1)}, u32[]{:S(2)}, u32[]{:S(2)}) collective-permute-start(bf16[256,128]{1,0:T(8,128)(2,1)S(1)} %get-tuple-element.90), channel_id=1, source_target_pairs={{16,0},{20,4},{24,8},{28,12},{0,16},{4,20},{8,24},{12,28},{17,1},{... | collective-permute-start | bytes 196616 | tf_op jit(solution)/shard_map/ppermute | solution.py:23
  154.7 2.0 %collective-permute-done.32.refs_3_ = bf16[256,128]{1,0:T(8,128)(2,1)S(1)} collective-permute-done((bf16[256,128]{1,0:T(8,128)(2,1)S(1)}, bf16[256,128]{1,0:T(8,128)(2,1)S(1)}, u32[]{:S(2)}, u32[]{:S(2)}) %collective-permute-start.32) | collective-permute-done | bytes 65568 | tf_op jit(solution)/shard_map/ppermute | solution.py:23
  156.7 3.4 %collective-permute-start.33 = (bf16[256,128]{1,0:T(8,128)(2,1)S(1)}, bf16[256,128]{1,0:T(8,128)(2,1)S(1)}, u32[]{:S(2)}, u32[]{:S(2)}) collective-permute-start(bf16[256,128]{1,0:T(8,128)(2,1)S(1)} %get-tuple-element.94), channel_id=1, source_target_pairs={{4,0},{8,4},{12,8},{16,12},{20,16},{24,20},{28,24},{0,28},{5,1},{9... | collective-permute-start | bytes 196616 | tf_op jit(solution)/shard_map/ppermute | solution.py:23
  162.3 2.1 %shard_map.67 = (bf16[32,128,128]{2,1,0:T(8,128)(2,1)S(1)}, bf16[16,128,128]{2,1,0:T(8,128)(2,1)S(1)}, bf16[12,128,128]{2,1,0:T(8,128)(2,1)S(1)}, bf16[4,128,128]{2,1,0:T(8,128)(2,1)S(1)}) custom-call(bf16[4,64,128,128]{3,2,1,0:T(8,128)(2,1)} %collective-permute-done.4.tiles), custom_call_target="tpu_custom_call" | custom-call | tf_op jit(solution)/shard_map/pallas_call | solution.py:56
  164.5 2.6 %collective-permute-done.31.refs_2_ = bf16[256,128]{1,0:T(8,128)(2,1)S(1)} collective-permute-done((bf16[256,128]{1,0:T(8,128)(2,1)S(1)}, bf16[256,128]{1,0:T(8,128)(2,1)S(1)}, u32[]{:S(2)}, u32[]{:S(2)}) %collective-permute-start.31) | collective-permute-done | bytes 65568 | tf_op jit(solution)/shard_map/ppermute | solution.py:23
  169.2 6.4 %collective-permute-done.35.refs_11_ = bf16[16,128,128]{2,1,0:T(8,128)(2,1)S(1)} collective-permute-done((bf16[16,128,128]{2,1,0:T(8,128)(2,1)S(1)}, bf16[16,128,128]{2,1,0:T(8,128)(2,1)S(1)}, u32[]{:S(2)}, u32[]{:S(2)}) %collective-permute-start.35) | collective-permute-done | bytes 524320 | tf_op jit(solution)/shard_map/ppermute | solution.py:28
  177.8 6.5 %shard_map.68 = (bf16[256,8192]{1,0:T(8,128)(2,1)}, bf16[68,256,128]{2,1,0:T(8,128)(2,1)S(1)}) custom-call(s32[1040]{0:T(1024)S(1)} %constant_dynamic-update-slice_fusion.table.refs_0_, bf16[68,256,128]{2,1,0:T(8,128)(2,1)S(1)} %get-tuple-element.88.refs_1_, bf16[256,128]{1,0:T(8,128)(2,1)S(1)} %collective-permute-done.31.refs_2_, ...), custom_call_target="tpu_custom_call", output_to_operand_aliasing={{1}: (1, {})} | custom-call | tf_op jit(solution)/shard_map/pallas_call | solution.py:205
  187.7 3.2 %shard_map.69 = bf16[256,8192]{1,0:T(8,128)(2,1)} custom-call(s32[1040]{0:T(1024)S(1)} %constant_dynamic-update-slice_fusion.table.refs_0_, bf16[68,256,128]{2,1,0:T(8,128)(2,1)S(1)} %get-tuple-element.103.refs_1_, bf16[12,128,128]{2,1,0:T(8,128)(2,1)S(1)} %get-tuple-element.104.refs_2_, ...), custom_call_target="tpu_custom_call", output_to_operand_aliasing={{}: (13, {})} | custom-call | tf_op jit(solution)/shard_map/pallas_call | solution.py:205
  (102 shorter events, 45.6 us)
Async XLA Ops:
  0.0 29.0 %collective-permute-start.4 = (bf16[4,64,128,128]{3,2,1,0:T(8,128)(2,1)}, bf16[4,64,128,128]{3,2,1,0:T(8,128)(2,1)}, u32[]{:S(2)}, u32[]{:S(2)}) collective-permute-start(bf16[4,64,128,128]{3,2,1,0:T(8,128)(2,1)} %tiles.9), channel_id=1, source_target_pairs={{0,1},{1,0},{2,3},{3,2},{4,5},{5,4},{6,7},{7,6},{8,9},{9,8},{10,11... | collective-permute-start | bytes 25165832 | tf_op jit(solution)/shard_map/ppermute | solution.py:28
  1.8 34.1 %collective-permute-start.5 = (bf16[32,128,128]{2,1,0:T(8,128)(2,1)S(1)}, bf16[32,128,128]{2,1,0:T(8,128)(2,1)}, u32[]{:S(2)}, u32[]{:S(2)}) collective-permute-start(bf16[32,128,128]{2,1,0:T(8,128)(2,1)S(1)} %shard_map.56.refs_6_), channel_id=1, source_target_pairs={{0,2},{1,3},{2,0},{3,1},{4,6},{5,7},{6,4},{7,5},{8,10},{9,11},{10,... | collective-permute-start | bytes 3145736 | tf_op jit(solution)/shard_map/ppermute | solution.py:28
  6.8 44.2 %collective-permute-start.6 = (bf16[32,128,128]{2,1,0:T(8,128)(2,1)}, bf16[32,128,128]{2,1,0:T(8,128)(2,1)}, u32[]{:S(2)}, u32[]{:S(2)}) collective-permute-start(bf16[32,128,128]{2,1,0:T(8,128)(2,1)} %shard_map.57.refs_7_), channel_id=1, source_target_pairs={{0,2},{1,3},{2,0},{3,1},{4,6},{5,7},{6,4},{7,5},{8,10},{9,11},{10,... | collective-permute-start | bytes 3145736 | tf_op jit(solution)/shard_map/ppermute | solution.py:28
  8.6 87.3 %collective-permute-start.15 = (bf16[64,128,128]{2,1,0:T(8,128)(2,1)S(1)}, bf16[64,128,128]{2,1,0:T(8,128)(2,1)}, u32[]{:S(2)}, u32[]{:S(2)}) collective-permute-start(bf16[64,128,128]{2,1,0:T(8,128)(2,1)S(1)} %shard_map.60.refs_6_), channel_id=1, source_target_pairs={{0,2},{1,3},{2,0},{3,1},{4,6},{5,7},{6,4},{7,5},{8,10},{9,11},{10,... | collective-permute-start | bytes 6291464 | tf_op jit(solution)/shard_map/ppermute | solution.py:28
  14.4 6.1 %collective-permute-start.2 = (bf16[256,128]{1,0:T(8,128)(2,1)S(1)}, bf16[256,128]{1,0:T(8,128)(2,1)S(1)}, u32[]{:S(2)}, u32[]{:S(2)}) collective-permute-start(bf16[256,128]{1,0:T(8,128)(2,1)S(1)} %get-tuple-element.60), channel_id=1, source_target_pairs={{24,0},{28,4},{0,8},{4,12},{8,16},{12,20},{16,24},{20,28},{25,1},{... | collective-permute-start | bytes 196616 | tf_op jit(solution)/shard_map/ppermute | solution.py:23
  25.6 5.3 %collective-permute-start.3 = (bf16[256,128]{1,0:T(8,128)(2,1)S(1)}, bf16[256,128]{1,0:T(8,128)(2,1)S(1)}, u32[]{:S(2)}, u32[]{:S(2)}) collective-permute-start(bf16[256,128]{1,0:T(8,128)(2,1)S(1)} %get-tuple-element.62), channel_id=1, source_target_pairs={{4,0},{8,4},{12,8},{16,12},{20,16},{24,20},{28,24},{0,28},{5,1},{9... | collective-permute-start | bytes 196616 | tf_op jit(solution)/shard_map/ppermute | solution.py:23
  29.0 7.0 %collective-permute-start.1 = (bf16[256,128]{1,0:T(8,128)(2,1)S(1)}, bf16[256,128]{1,0:T(8,128)(2,1)S(1)}, u32[]{:S(2)}, u32[]{:S(2)}) collective-permute-start(bf16[256,128]{1,0:T(8,128)(2,1)S(1)} %get-tuple-element.59), channel_id=1, source_target_pairs={{28,0},{0,4},{4,8},{8,12},{12,16},{16,20},{20,24},{24,28},{29,1},{... | collective-permute-start | bytes 196616 | tf_op jit(solution)/shard_map/ppermute | solution.py:23
  37.2 13.8 %collective-permute-start.7 = (bf16[16,128,128]{2,1,0:T(8,128)(2,1)S(1)}, bf16[16,128,128]{2,1,0:T(8,128)(2,1)S(1)}, u32[]{:S(2)}, u32[]{:S(2)}) collective-permute-start(bf16[16,128,128]{2,1,0:T(8,128)(2,1)S(1)} %get-tuple-element.121), channel_id=1, source_target_pairs={{0,1},{1,0},{2,3},{3,2},{4,5},{5,4},{6,7},{7,6},{8,9},{9,8},{10,11... | collective-permute-start | bytes 1572872 | tf_op jit(solution)/shard_map/ppermute | solution.py:28
  37.3 13.7 %collective-permute-start.8 = (bf16[16,128,128]{2,1,0:T(8,128)(2,1)S(1)}, bf16[16,128,128]{2,1,0:T(8,128)(2,1)S(1)}, u32[]{:S(2)}, u32[]{:S(2)}) collective-permute-start(bf16[16,128,128]{2,1,0:T(8,128)(2,1)S(1)} %get-tuple-element.120), channel_id=1, source_target_pairs={{0,1},{1,0},{2,3},{3,2},{4,5},{5,4},{6,7},{7,6},{8,9},{9,8},{10,11... | collective-permute-start | bytes 1572872 | tf_op jit(solution)/shard_map/ppermute | solution.py:28
  54.6 74.9 %collective-permute-start.24 = (bf16[48,128,128]{2,1,0:T(8,128)(2,1)S(1)}, bf16[48,128,128]{2,1,0:T(8,128)(2,1)S(1)}, u32[]{:S(2)}, u32[]{:S(2)}) collective-permute-start(bf16[48,128,128]{2,1,0:T(8,128)(2,1)S(1)} %get-tuple-element.82.refs_6_), channel_id=1, source_target_pairs={{0,2},{1,3},{2,0},{3,1},{4,6},{5,7},{6,4},{7,5},{8,10},{9,11},{10,... | collective-permute-start | bytes 4718600 | tf_op jit(solution)/shard_map/ppermute | solution.py:28
  68.1 6.6 %collective-permute-start.13 = (bf16[256,128]{1,0:T(8,128)(2,1)S(1)}, bf16[256,128]{1,0:T(8,128)(2,1)S(1)}, u32[]{:S(2)}, u32[]{:S(2)}) collective-permute-start(bf16[256,128]{1,0:T(8,128)(2,1)S(1)} %get-tuple-element.71), channel_id=1, source_target_pairs={{24,0},{28,4},{0,8},{4,12},{8,16},{12,20},{16,24},{20,28},{25,1},{... | collective-permute-start | bytes 196616 | tf_op jit(solution)/shard_map/ppermute | solution.py:23
  69.7 7.8 %collective-permute-start.11 = (bf16[256,128]{1,0:T(8,128)(2,1)S(1)}, bf16[256,128]{1,0:T(8,128)(2,1)S(1)}, u32[]{:S(2)}, u32[]{:S(2)}) collective-permute-start(bf16[256,128]{1,0:T(8,128)(2,1)S(1)} %get-tuple-element.69), channel_id=1, source_target_pairs={{16,0},{20,4},{24,8},{28,12},{0,16},{4,20},{8,24},{12,28},{17,1},{... | collective-permute-start | bytes 196616 | tf_op jit(solution)/shard_map/ppermute | solution.py:23
  74.7 21.3 %collective-permute-start.14 = (bf16[256,128]{1,0:T(8,128)(2,1)S(1)}, bf16[256,128]{1,0:T(8,128)(2,1)S(1)}, u32[]{:S(2)}, u32[]{:S(2)}) collective-permute-start(bf16[256,128]{1,0:T(8,128)(2,1)S(1)} %get-tuple-element.73), channel_id=1, source_target_pairs={{4,0},{8,4},{12,8},{16,12},{20,16},{24,20},{28,24},{0,28},{5,1},{9... | collective-permute-start | bytes 196616 | tf_op jit(solution)/shard_map/ppermute | solution.py:23
  77.5 18.4 %collective-permute-start.12 = (bf16[256,128]{1,0:T(8,128)(2,1)S(1)}, bf16[256,128]{1,0:T(8,128)(2,1)S(1)}, u32[]{:S(2)}, u32[]{:S(2)}) collective-permute-start(bf16[256,128]{1,0:T(8,128)(2,1)S(1)} %get-tuple-element.70), channel_id=1, source_target_pairs={{28,0},{0,4},{4,8},{8,12},{12,16},{16,20},{20,24},{24,28},{29,1},{... | collective-permute-start | bytes 196616 | tf_op jit(solution)/shard_map/ppermute | solution.py:23
  110.6 6.7 %collective-permute-start.22 = (bf16[256,128]{1,0:T(8,128)(2,1)S(1)}, bf16[256,128]{1,0:T(8,128)(2,1)S(1)}, u32[]{:S(2)}, u32[]{:S(2)}) collective-permute-start(bf16[256,128]{1,0:T(8,128)(2,1)S(1)} %get-tuple-element.79), channel_id=1, source_target_pairs={{24,0},{28,4},{0,8},{4,12},{8,16},{12,20},{16,24},{20,28},{25,1},{... | collective-permute-start | bytes 196616 | tf_op jit(solution)/shard_map/ppermute | solution.py:23
  112.7 8.0 %collective-permute-start.20 = (bf16[256,128]{1,0:T(8,128)(2,1)S(1)}, bf16[256,128]{1,0:T(8,128)(2,1)S(1)}, u32[]{:S(2)}, u32[]{:S(2)}) collective-permute-start(bf16[256,128]{1,0:T(8,128)(2,1)S(1)} %get-tuple-element.77), channel_id=1, source_target_pairs={{16,0},{20,4},{24,8},{28,12},{0,16},{4,20},{8,24},{12,28},{17,1},{... | collective-permute-start | bytes 196616 | tf_op jit(solution)/shard_map/ppermute | solution.py:23
  117.3 12.3 %collective-permute-start.23 = (bf16[256,128]{1,0:T(8,128)(2,1)S(1)}, bf16[256,128]{1,0:T(8,128)(2,1)S(1)}, u32[]{:S(2)}, u32[]{:S(2)}) collective-permute-start(bf16[256,128]{1,0:T(8,128)(2,1)S(1)} %get-tuple-element.81), channel_id=1, source_target_pairs={{4,0},{8,4},{12,8},{16,12},{20,16},{24,20},{28,24},{0,28},{5,1},{9... | collective-permute-start | bytes 196616 | tf_op jit(solution)/shard_map/ppermute | solution.py:23
  120.7 8.8 %collective-permute-start.21 = (bf16[256,128]{1,0:T(8,128)(2,1)S(1)}, bf16[256,128]{1,0:T(8,128)(2,1)S(1)}, u32[]{:S(2)}, u32[]{:S(2)}) collective-permute-start(bf16[256,128]{1,0:T(8,128)(2,1)S(1)} %get-tuple-element.78), channel_id=1, source_target_pairs={{28,0},{0,4},{4,8},{8,12},{12,16},{16,20},{20,24},{24,28},{29,1},{... | collective-permute-start | bytes 196616 | tf_op jit(solution)/shard_map/ppermute | solution.py:23
  121.4 19.3 %collective-permute-start.25 = (bf16[16,128,128]{2,1,0:T(8,128)(2,1)S(1)}, bf16[16,128,128]{2,1,0:T(8,128)(2,1)S(1)}, u32[]{:S(2)}, u32[]{:S(2)}) collective-permute-start(bf16[16,128,128]{2,1,0:T(8,128)(2,1)S(1)} %get-tuple-element.83.refs_7_), channel_id=1, source_target_pairs={{0,2},{1,3},{2,0},{3,1},{4,6},{5,7},{6,4},{7,5},{8,10},{9,11},{10,... | collective-permute-start | bytes 1572872 | tf_op jit(solution)/shard_map/ppermute | solution.py:28
  129.7 11.1 %collective-permute-start.26 = (bf16[16,128,128]{2,1,0:T(8,128)(2,1)S(1)}, bf16[16,128,128]{2,1,0:T(8,128)(2,1)S(1)}, u32[]{:S(2)}, u32[]{:S(2)}) collective-permute-start(bf16[16,128,128]{2,1,0:T(8,128)(2,1)S(1)} %get-tuple-element.115), channel_id=1, source_target_pairs={{0,1},{1,0},{2,3},{3,2},{4,5},{5,4},{6,7},{7,6},{8,9},{9,8},{10,11... | collective-permute-start | bytes 1572872 | tf_op jit(solution)/shard_map/ppermute | solution.py:28
  129.8 11.0 %collective-permute-start.27 = (bf16[16,128,128]{2,1,0:T(8,128)(2,1)S(1)}, bf16[16,128,128]{2,1,0:T(8,128)(2,1)S(1)}, u32[]{:S(2)}, u32[]{:S(2)}) collective-permute-start(bf16[16,128,128]{2,1,0:T(8,128)(2,1)S(1)} %get-tuple-element.114), channel_id=1, source_target_pairs={{0,1},{1,0},{2,3},{3,2},{4,5},{5,4},{6,7},{7,6},{8,9},{9,8},{10,11... | collective-permute-start | bytes 1572872 | tf_op jit(solution)/shard_map/ppermute | solution.py:28
  130.3 10.5 %collective-permute-start.28 = (bf16[16,128,128]{2,1,0:T(8,128)(2,1)S(1)}, bf16[16,128,128]{2,1,0:T(8,128)(2,1)S(1)}, u32[]{:S(2)}, u32[]{:S(2)}) collective-permute-start(bf16[16,128,128]{2,1,0:T(8,128)(2,1)S(1)} %get-tuple-element.113), channel_id=1, source_target_pairs={{0,1},{1,0},{2,3},{3,2},{4,5},{5,4},{6,7},{7,6},{8,9},{9,8},{10,11... | collective-permute-start | bytes 1572872 | tf_op jit(solution)/shard_map/ppermute | solution.py:28
  132.5 32.0 %collective-permute-start.34 = (bf16[32,128,128]{2,1,0:T(8,128)(2,1)S(1)}, bf16[32,128,128]{2,1,0:T(8,128)(2,1)S(1)}, u32[]{:S(2)}, u32[]{:S(2)}) collective-permute-start(bf16[32,128,128]{2,1,0:T(8,128)(2,1)S(1)} %get-tuple-element.95.refs_6_), channel_id=1, source_target_pairs={{0,2},{1,3},{2,0},{3,1},{4,6},{5,7},{6,4},{7,5},{8,10},{9,11},{10,... | collective-permute-start | bytes 3145736 | tf_op jit(solution)/shard_map/ppermute | solution.py:28
  150.0 6.7 %collective-permute-start.32 = (bf16[256,128]{1,0:T(8,128)(2,1)S(1)}, bf16[256,128]{1,0:T(8,128)(2,1)S(1)}, u32[]{:S(2)}, u32[]{:S(2)}) collective-permute-start(bf16[256,128]{1,0:T(8,128)(2,1)S(1)} %get-tuple-element.92), channel_id=1, source_target_pairs={{24,0},{28,4},{0,8},{4,12},{8,16},{12,20},{16,24},{20,28},{25,1},{... | collective-permute-start | bytes 196616 | tf_op jit(solution)/shard_map/ppermute | solution.py:23
  152.1 8.0 %collective-permute-start.30 = (bf16[256,128]{1,0:T(8,128)(2,1)S(1)}, bf16[256,128]{1,0:T(8,128)(2,1)S(1)}, u32[]{:S(2)}, u32[]{:S(2)}) collective-permute-start(bf16[256,128]{1,0:T(8,128)(2,1)S(1)} %get-tuple-element.90), channel_id=1, source_target_pairs={{16,0},{20,4},{24,8},{28,12},{0,16},{4,20},{8,24},{12,28},{17,1},{... | collective-permute-start | bytes 196616 | tf_op jit(solution)/shard_map/ppermute | solution.py:23
  156.7 7.8 %collective-permute-start.33 = (bf16[256,128]{1,0:T(8,128)(2,1)S(1)}, bf16[256,128]{1,0:T(8,128)(2,1)S(1)}, u32[]{:S(2)}, u32[]{:S(2)}) collective-permute-start(bf16[256,128]{1,0:T(8,128)(2,1)S(1)} %get-tuple-element.94), channel_id=1, source_target_pairs={{4,0},{8,4},{12,8},{16,12},{20,16},{24,20},{28,24},{0,28},{5,1},{9... | collective-permute-start | bytes 196616 | tf_op jit(solution)/shard_map/ppermute | solution.py:23
  160.1 7.0 %collective-permute-start.31 = (bf16[256,128]{1,0:T(8,128)(2,1)S(1)}, bf16[256,128]{1,0:T(8,128)(2,1)S(1)}, u32[]{:S(2)}, u32[]{:S(2)}) collective-permute-start(bf16[256,128]{1,0:T(8,128)(2,1)S(1)} %get-tuple-element.91), channel_id=1, source_target_pairs={{28,0},{0,4},{4,8},{8,12},{12,16},{16,20},{20,24},{24,28},{29,1},{... | collective-permute-start | bytes 196616 | tf_op jit(solution)/shard_map/ppermute | solution.py:23
  160.8 14.8 %collective-permute-start.35 = (bf16[16,128,128]{2,1,0:T(8,128)(2,1)S(1)}, bf16[16,128,128]{2,1,0:T(8,128)(2,1)S(1)}, u32[]{:S(2)}, u32[]{:S(2)}) collective-permute-start(bf16[16,128,128]{2,1,0:T(8,128)(2,1)S(1)} %get-tuple-element.96.refs_7_), channel_id=1, source_target_pairs={{0,2},{1,3},{2,0},{3,1},{4,6},{5,7},{6,4},{7,5},{8,10},{9,11},{10,... | collective-permute-start | bytes 1572872 | tf_op jit(solution)/shard_map/ppermute | solution.py:28
  167.2 8.5 %collective-permute-start.36 = (bf16[16,128,128]{2,1,0:T(8,128)(2,1)S(1)}, bf16[16,128,128]{2,1,0:T(8,128)(2,1)S(1)}, u32[]{:S(2)}, u32[]{:S(2)}) collective-permute-start(bf16[16,128,128]{2,1,0:T(8,128)(2,1)S(1)} %get-tuple-element.117), channel_id=1, source_target_pairs={{0,1},{1,0},{2,3},{3,2},{4,5},{5,4},{6,7},{7,6},{8,9},{9,8},{10,11... | collective-permute-start | bytes 1572872 | tf_op jit(solution)/shard_map/ppermute | solution.py:28
  167.2 8.4 %collective-permute-start.37 = (bf16[16,128,128]{2,1,0:T(8,128)(2,1)S(1)}, bf16[16,128,128]{2,1,0:T(8,128)(2,1)S(1)}, u32[]{:S(2)}, u32[]{:S(2)}) collective-permute-start(bf16[16,128,128]{2,1,0:T(8,128)(2,1)S(1)} %get-tuple-element.116), channel_id=1, source_target_pairs={{0,1},{1,0},{2,3},{3,2},{4,5},{5,4},{6,7},{7,6},{8,9},{9,8},{10,11... | collective-permute-start | bytes 1572872 | tf_op jit(solution)/shard_map/ppermute | solution.py:28
  167.7 16.6 %collective-permute-start.40 = (bf16[12,128,128]{2,1,0:T(8,128)(2,1)S(1)}, bf16[12,128,128]{2,1,0:T(8,128)(2,1)S(1)}, u32[]{:S(2)}, u32[]{:S(2)}) collective-permute-start(bf16[12,128,128]{2,1,0:T(8,128)(2,1)S(1)} %get-tuple-element.104.refs_2_), channel_id=1, source_target_pairs={{0,2},{1,3},{2,0},{3,1},{4,6},{5,7},{6,4},{7,5},{8,10},{9,11},{10,... | collective-permute-start | bytes 1179656 | tf_op jit(solution)/shard_map/ppermute | solution.py:28
  176.3 9.3 %collective-permute-start.41 = (bf16[4,128,128]{2,1,0:T(8,128)(2,1)S(1)}, bf16[4,128,128]{2,1,0:T(8,128)(2,1)S(1)}, u32[]{:S(2)}, u32[]{:S(2)}) collective-permute-start(bf16[4,128,128]{2,1,0:T(8,128)(2,1)S(1)} %get-tuple-element.105.refs_3_), channel_id=1, source_target_pairs={{0,2},{1,3},{2,0},{3,1},{4,6},{5,7},{6,4},{7,5},{8,10},{9,11},{10,... | collective-permute-start | bytes 393224 | tf_op jit(solution)/shard_map/ppermute | solution.py:28
  (18 other events, 60.1 us)

commit v10 on v9

--- a/solution.py
+++ b/solution.py
@@ -241,9 +241,10 @@
                 )
 
     last = layer_count - 1
-    shares = [(0, (8, 8), (2, 2))] + [(layer, (16,), (4,)) for layer in range(1, last - 1)]
-    shares += [(last - 1, (12, 4), (3, 1))]
-    shares += [(last, (8, 4), (2, 2)), (last, (3, 1), (3, 1))]
+    shares = [(0, (8, 8), ((4, 4), (4, 4)))]
+    shares += [(layer, (16,), ((4, 4, 4, 4),)) for layer in range(1, last - 1)]
+    shares += [(last - 1, (12, 4), ((4, 4, 4), (4,)))]
+    shares += [(last, (8,), ((4, 4),)), (last, (5,), ((2, 2, 1),)), (last, (3,), ((2, 1),))]
 
     moves = {layer: [] for layer in range(layer_count)}
     for layer, sizes, _ in shares:
@@ -275,11 +276,11 @@
         tiles = [None] * fan
         for m, source in enumerate([mine[layer], *near[layer], crossed[layer]]):
             tiles[m] = [source.pop(0) for _ in sizes]
-        for number, tile in zip(pieces, tiles[far]):
+        for parts, tile in zip(pieces, tiles[far]):
             tile = lax.optimization_barrier((tile, *after))[0]
-            share = tile.shape[0] // math.gcd(number, tile.shape[0])
             passed = [None] * fan
-            passed[far] = [tile[start : start + share] for start in range(0, tile.shape[0], share)]
+            starts = [sum(parts[:place]) * unit for place in range(len(parts) + 1)]
+            passed[far] = [tile[start:end] for start, end in zip(starts, starts[1:])]
             spread(passed, far)
             for m in range(far + 1, fan):
                 tiles[m] = [*(tiles[m] or []), *passed[m]]

time: 192 us -> 192 us (level)
  Pallas kernels: 55.6 us -> 58.2 us
    pallas_call x5 -> x6, Pallas kernels: 37.2 us -> 40 us  [run_blocks(): pl.pallas_call(kernel, out_shape=out_shape, grid_spec=pltpu.PrefetchScala...]
    ppermute x30 -> x28, starting transfers between devices: 20.1 us -> 18.5 us  [swapped(): return lax.ppermute(block, 'batch', route)]
    ppermute x30 -> x28, waiting for transfers between devices: 54.2 us -> 52.8 us  [swapped(): return lax.ppermute(block, 'batch', route)]
    slice x7 -> x9, local copies, waits for them, and re-layouts: 4.53 us -> 4.53 us  [body(): passed[far] = [tile[start:end] for start, end in zip(starts, starts[1:])]]
  transfers between devices with their start and end apart: 46 -> 44, of which waited for: 23 -> 22; matrix products, arithmetic and copies ran while one was open for 3% -> 4% of each run, Pallas kernels for 27% -> 29%
where the time goes in v10:
time: 192 us; the launch traced here: 191 us
  waiting for transfers between devices  75.8 us (39%)
  Pallas kernels  58.2 us (30%)
  starting transfers between devices  49.6 us (26%)
  local copies, waits for them, and re-layouts  5.99 us (3%)
    ppermute x28, waiting for transfers between devices, swapped(): return lax.ppermute(block, 'batch', route)  52.8 us
    pallas_call x6, Pallas kernels, run_blocks(): pl.pallas_call(kernel, out_shape=out_shape, grid_spec=pltpu.PrefetchScala...  40 us
    ppermute x16, starting transfers between devices, shifted(): return lax.ppermute(block, axis, route)  31.1 us
    ppermute x16, waiting for transfers between devices, shifted(): return lax.ppermute(block, axis, route)  23 us
    ppermute x28, starting transfers between devices, swapped(): return lax.ppermute(block, 'batch', route)  18.5 us
    pallas_call x9, Pallas kernels, cut(): pl.pallas_call(kernel, out_shape=[pltpu.VMEM((count, height, width), tile...  16.6 us
    slice x9, local copies, waits for them, and re-layouts, body(): passed[far] = [tile[start:end] for start, end in zip(starts, starts[1:])]  4.53 us
  transfers between devices with their start and end apart: 44, of which 22 were waited for; matrix products, arithmetic and copies ran while one was open for 4% of the time, Pallas kernels for 29%

profile of v10, /device:TPU:0, one launch (start us, length us, event | category | flops | bytes accessed | tf_op | source)
XLA Modules:
  0.0 190.9 jit_solution(2400315886713353308)
XLA Ops:
  1.8 2.6 %collective-permute-start.5 = (bf16[32,128,128]{2,1,0:T(8,128)(2,1)S(1)}, bf16[32,128,128]{2,1,0:T(8,128)(2,1)}, u32[]{:S(2)}, u32[]{:S(2)}) collective-permute-start(bf16[32,128,128]{2,1,0:T(8,128)(2,1)S(1)} %shard_map.56.refs_6_), channel_id=1, source_target_pairs={{0,2},{1,3},{2,0},{3,1},{4,6},{5,7},{6,4},{7,5},{8,10},{9,11},{10,... | collective-permute-start | bytes 3145736 | tf_op jit(solution)/shard_map/ppermute | solution.py:28
  4.4 2.3 %shard_map.57.refs_7_ = bf16[32,128,128]{2,1,0:T(8,128)(2,1)} custom-call(bf16[4,64,128,128]{3,2,1,0:T(8,128)(2,1)} %tiles.9), custom_call_target="tpu_custom_call" | custom-call | tf_op jit(solution)/shard_map/pallas_call | solution.py:56
  8.6 2.1 %collective-permute-start.15 = (bf16[64,128,128]{2,1,0:T(8,128)(2,1)S(1)}, bf16[64,128,128]{2,1,0:T(8,128)(2,1)}, u32[]{:S(2)}, u32[]{:S(2)}) collective-permute-start(bf16[64,128,128]{2,1,0:T(8,128)(2,1)S(1)} %shard_map.60.refs_6_), channel_id=1, source_target_pairs={{0,2},{1,3},{2,0},{3,1},{4,6},{5,7},{6,4},{7,5},{8,10},{9,11},{10,... | collective-permute-start | bytes 6291464 | tf_op jit(solution)/shard_map/ppermute | solution.py:28
  16.1 4.5 %collective-permute-done.2.refs_3_ = bf16[256,128]{1,0:T(8,128)(2,1)S(1)} collective-permute-done((bf16[256,128]{1,0:T(8,128)(2,1)S(1)}, bf16[256,128]{1,0:T(8,128)(2,1)S(1)}, u32[]{:S(2)}, u32[]{:S(2)}) %collective-permute-start.2) | collective-permute-done | bytes 65568 | tf_op jit(solution)/shard_map/ppermute | solution.py:23
  21.4 4.4 %collective-permute-done.refs_5_ = bf16[256,128]{1,0:T(8,128)(2,1)S(1)} collective-permute-done((bf16[256,128]{1,0:T(8,128)(2,1)S(1)}, bf16[256,128]{1,0:T(8,128)(2,1)S(1)}, u32[]{:S(2)}, u32[]{:S(2)}) %collective-permute-start) | collective-permute-done | bytes 65568 | tf_op jit(solution)/shard_map/ppermute | solution.py:23
  25.7 3.3 %collective-permute-start.3 = (bf16[256,128]{1,0:T(8,128)(2,1)S(1)}, bf16[256,128]{1,0:T(8,128)(2,1)S(1)}, u32[]{:S(2)}, u32[]{:S(2)}) collective-permute-start(bf16[256,128]{1,0:T(8,128)(2,1)S(1)} %get-tuple-element.59), channel_id=1, source_target_pairs={{4,0},{8,4},{12,8},{16,12},{20,16},{24,20},{28,24},{0,28},{5,1},{9... | collective-permute-start | bytes 196616 | tf_op jit(solution)/shard_map/ppermute | solution.py:23
  31.0 5.1 %collective-permute-done.1.refs_2_ = bf16[256,128]{1,0:T(8,128)(2,1)S(1)} collective-permute-done((bf16[256,128]{1,0:T(8,128)(2,1)S(1)}, bf16[256,128]{1,0:T(8,128)(2,1)S(1)}, u32[]{:S(2)}, u32[]{:S(2)}) %collective-permute-start.1) | collective-permute-done | bytes 65568 | tf_op jit(solution)/shard_map/ppermute | solution.py:23
  37.9 13.1 %collective-permute-done.6.refs_11_ = bf16[32,128,128]{2,1,0:T(8,128)(2,1)} collective-permute-done((bf16[32,128,128]{2,1,0:T(8,128)(2,1)}, bf16[32,128,128]{2,1,0:T(8,128)(2,1)}, u32[]{:S(2)}, u32[]{:S(2)}) %collective-permute-start.6) | collective-permute-done | bytes 1048608 | tf_op jit(solution)/shard_map/ppermute | solution.py:28
  56.6 11.4 %shard_map.59 = (bf16[68,256,128]{2,1,0:T(8,128)(2,1)S(1)}, bf16[256,128]{1,0:T(8,128)(2,1)S(1)}, bf16[256,128]{1,0:T(8,128)(2,1)S(1)}, bf16[256,128]{1,0:T(8,128)(2,1)S(1)}, bf16[256,128]{1,0:T(8,128)(2,1)S(1)}) custom-call(s32[1040]{0:T(1024)S(1)} %constant_dynamic-update-slice_fusion.table.refs_0_, bf16[256,8192]{1,0:T(8,128)(2,1)} %refs_1_.1, ...), custom_call_target="tpu_custom_call" | custom-call | tf_op jit(solution)/shard_map/pallas_call | solution.py:205
  69.7 2.6 %collective-permute-start.11 = (bf16[256,128]{1,0:T(8,128)(2,1)S(1)}, bf16[256,128]{1,0:T(8,128)(2,1)S(1)}, u32[]{:S(2)}, u32[]{:S(2)}) collective-permute-start(bf16[256,128]{1,0:T(8,128)(2,1)S(1)} %get-tuple-element.66), channel_id=1, source_target_pairs={{16,0},{20,4},{24,8},{28,12},{0,16},{4,20},{8,24},{12,28},{17,1},{... | collective-permute-start | bytes 196616 | tf_op jit(solution)/shard_map/ppermute | solution.py:23
  72.3 2.3 %collective-permute-done.13.refs_3_ = bf16[256,128]{1,0:T(8,128)(2,1)S(1)} collective-permute-done((bf16[256,128]{1,0:T(8,128)(2,1)S(1)}, bf16[256,128]{1,0:T(8,128)(2,1)S(1)}, u32[]{:S(2)}, u32[]{:S(2)}) %collective-permute-start.13) | collective-permute-done | bytes 65568 | tf_op jit(solution)/shard_map/ppermute | solution.py:23
  74.7 2.8 %collective-permute-start.14 = (bf16[256,128]{1,0:T(8,128)(2,1)S(1)}, bf16[256,128]{1,0:T(8,128)(2,1)S(1)}, u32[]{:S(2)}, u32[]{:S(2)}) collective-permute-start(bf16[256,128]{1,0:T(8,128)(2,1)S(1)} %get-tuple-element.70), channel_id=1, source_target_pairs={{4,0},{8,4},{12,8},{16,12},{20,16},{24,20},{28,24},{0,28},{5,1},{9... | collective-permute-start | bytes 196616 | tf_op jit(solution)/shard_map/ppermute | solution.py:23
  79.9 16.0 %collective-permute-done.15.refs_8_ = bf16[64,128,128]{2,1,0:T(8,128)(2,1)} collective-permute-done((bf16[64,128,128]{2,1,0:T(8,128)(2,1)S(1)}, bf16[64,128,128]{2,1,0:T(8,128)(2,1)}, u32[]{:S(2)}, u32[]{:S(2)}) %collective-permute-start.15) | collective-permute-done | bytes 2097184 | tf_op jit(solution)/shard_map/ppermute | solution.py:28
  101.8 8.8 %shard_map.62 = (bf16[68,256,128]{2,1,0:T(8,128)(2,1)S(1)}, bf16[68,256,128]{2,1,0:T(8,128)(2,1)S(1)}, bf16[256,128]{1,0:T(8,128)(2,1)S(1)}, bf16[256,128]{1,0:T...) custom-call(s32[1040]{0:T(1024)S(1)} %constant_dynamic-update-slice_, ...), custom_call_target="tpu_custom_call", output_to_operand_aliasing={{1}: (1, {})} | custom-call | tf_op jit(solution)/shard_map/pallas_call | solution.py:205
  110.6 2.1 %collective-permute-start.22 = (bf16[256,128]{1,0:T(8,128)(2,1)S(1)}, bf16[256,128]{1,0:T(8,128)(2,1)S(1)}, u32[]{:S(2)}, u32[]{:S(2)}) collective-permute-start(bf16[256,128]{1,0:T(8,128)(2,1)S(1)} %get-tuple-element.76), channel_id=1, source_target_pairs={{24,0},{28,4},{0,8},{4,12},{8,16},{12,20},{16,24},{20,28},{25,1},{... | collective-permute-start | bytes 196616 | tf_op jit(solution)/shard_map/ppermute | solution.py:23
  112.7 2.6 %collective-permute-start.20 = (bf16[256,128]{1,0:T(8,128)(2,1)S(1)}, bf16[256,128]{1,0:T(8,128)(2,1)S(1)}, u32[]{:S(2)}, u32[]{:S(2)}) collective-permute-start(bf16[256,128]{1,0:T(8,128)(2,1)S(1)} %get-tuple-element.74), channel_id=1, source_target_pairs={{16,0},{20,4},{24,8},{28,12},{0,16},{4,20},{8,24},{12,28},{17,1},{... | collective-permute-start | bytes 196616 | tf_op jit(solution)/shard_map/ppermute | solution.py:23
  115.3 2.0 %collective-permute-done.22.refs_3_ = bf16[256,128]{1,0:T(8,128)(2,1)S(1)} collective-permute-done((bf16[256,128]{1,0:T(8,128)(2,1)S(1)}, bf16[256,128]{1,0:T(8,128)(2,1)S(1)}, u32[]{:S(2)}, u32[]{:S(2)}) %collective-permute-start.22) | collective-permute-done | bytes 65568 | tf_op jit(solution)/shard_map/ppermute | solution.py:23
  117.3 3.4 %collective-permute-start.23 = (bf16[256,128]{1,0:T(8,128)(2,1)S(1)}, bf16[256,128]{1,0:T(8,128)(2,1)S(1)}, u32[]{:S(2)}, u32[]{:S(2)}) collective-permute-start(bf16[256,128]{1,0:T(8,128)(2,1)S(1)} %get-tuple-element.78), channel_id=1, source_target_pairs={{4,0},{8,4},{12,8},{16,12},{20,16},{24,20},{28,24},{0,28},{5,1},{9... | collective-permute-start | bytes 196616 | tf_op jit(solution)/shard_map/ppermute | solution.py:23
  124.7 4.8 %collective-permute-done.24.refs_10_ = bf16[48,128,128]{2,1,0:T(8,128)(2,1)S(1)} collective-permute-done((bf16[48,128,128]{2,1,0:T(8,128)(2,1)S(1)}, bf16[48,128,128]{2,1,0:T(8,128)(2,1)S(1)}, u32[]{:S(2)}, u32[]{:S(2)}) %collective-permute-start.24) | collective-permute-done | bytes 1572896 | tf_op jit(solution)/shard_map/ppermute | solution.py:28
  130.4 2.0 %shard_map.66 = (bf16[32,128,128]{2,1,0:T(8,128)(2,1)S(1)}, bf16[20,128,128]{2,1,0:T(8,128)(2,1)S(1)}, bf16[12,128,128]{2,1,0:T(8,128)(2,1)S(1)}) custom-call(bf16[4,64,128,128]{3,2,1,0:T(8,128)(2,1)} %tiles.9), custom_call_target="tpu_custom_call" | custom-call | tf_op jit(solution)/shard_map/pallas_call | solution.py:56
  134.4 6.4 %collective-permute-done.25.refs_11_ = bf16[16,128,128]{2,1,0:T(8,128)(2,1)S(1)} collective-permute-done((bf16[16,128,128]{2,1,0:T(8,128)(2,1)S(1)}, bf16[16,128,128]{2,1,0:T(8,128)(2,1)S(1)}, u32[]{:S(2)}, u32[]{:S(2)}) %collective-permute-start.25) | collective-permute-done | bytes 524320 | tf_op jit(solution)/shard_map/ppermute | solution.py:28
  142.8 7.2 %shard_map.65 = (bf16[68,256,128]{2,1,0:T(8,128)(2,1)S(1)}, bf16[68,256,128]{2,1,0:T(8,128)(2,1)S(1)}, bf16[256,128]{1,0:T(8,128)(2,1)S(1)}, bf16[256,128]{1,0:T...) custom-call(s32[1040]{0:T(1024)S(1)} %constant_dynamic-update-slice_, ...), custom_call_target="tpu_custom_call", output_to_operand_aliasing={{1}: (1, {})} | custom-call | tf_op jit(solution)/shard_map/pallas_call | solution.py:205
  150.0 2.1 %collective-permute-start.32 = (bf16[256,128]{1,0:T(8,128)(2,1)S(1)}, bf16[256,128]{1,0:T(8,128)(2,1)S(1)}, u32[]{:S(2)}, u32[]{:S(2)}) collective-permute-start(bf16[256,128]{1,0:T(8,128)(2,1)S(1)} %get-tuple-element.89), channel_id=1, source_target_pairs={{24,0},{28,4},{0,8},{4,12},{8,16},{12,20},{16,24},{20,28},{25,1},{... | collective-permute-start | bytes 196616 | tf_op jit(solution)/shard_map/ppermute | solution.py:23
  152.1 2.6 %collective-permute-start.30 = (bf16[256,128]{1,0:T(8,128)(2,1)S(1)}, bf16[256,128]{1,0:T(8,128)(2,1)S(1)}, u32[]{:S(2)}, u32[]{:S(2)}) collective-permute-start(bf16[256,128]{1,0:T(8,128)(2,1)S(1)} %get-tuple-element.87), channel_id=1, source_target_pairs={{16,0},{20,4},{24,8},{28,12},{0,16},{4,20},{8,24},{12,28},{17,1},{... | collective-permute-start | bytes 196616 | tf_op jit(solution)/shard_map/ppermute | solution.py:23
  154.7 2.0 %collective-permute-done.32.refs_3_ = bf16[256,128]{1,0:T(8,128)(2,1)S(1)} collective-permute-done((bf16[256,128]{1,0:T(8,128)(2,1)S(1)}, bf16[256,128]{1,0:T(8,128)(2,1)S(1)}, u32[]{:S(2)}, u32[]{:S(2)}) %collective-permute-start.32) | collective-permute-done | bytes 65568 | tf_op jit(solution)/shard_map/ppermute | solution.py:23
  156.7 3.4 %collective-permute-start.33 = (bf16[256,128]{1,0:T(8,128)(2,1)S(1)}, bf16[256,128]{1,0:T(8,128)(2,1)S(1)}, u32[]{:S(2)}, u32[]{:S(2)}) collective-permute-start(bf16[256,128]{1,0:T(8,128)(2,1)S(1)} %get-tuple-element.91), channel_id=1, source_target_pairs={{4,0},{8,4},{12,8},{16,12},{20,16},{24,20},{28,24},{0,28},{5,1},{9... | collective-permute-start | bytes 196616 | tf_op jit(solution)/shard_map/ppermute | solution.py:23
  162.3 2.0 %shard_map.67 = (bf16[32,128,128]{2,1,0:T(8,128)(2,1)S(1)}, bf16[20,128,128]{2,1,0:T(8,128)(2,1)S(1)}, bf16[12,128,128]{2,1,0:T(8,128)(2,1)S(1)}) custom-call(bf16[4,64,128,128]{3,2,1,0:T(8,128)(2,1)} %collective-permute-done.4.tiles), custom_call_target="tpu_custom_call" | custom-call | tf_op jit(solution)/shard_map/pallas_call | solution.py:56
  164.4 2.7 %collective-permute-done.31.refs_2_ = bf16[256,128]{1,0:T(8,128)(2,1)S(1)} collective-permute-done((bf16[256,128]{1,0:T(8,128)(2,1)S(1)}, bf16[256,128]{1,0:T(8,128)(2,1)S(1)}, u32[]{:S(2)}, u32[]{:S(2)}) %collective-permute-start.31) | collective-permute-done | bytes 65568 | tf_op jit(solution)/shard_map/ppermute | solution.py:23
  169.9 5.2 %shard_map.68 = (bf16[256,8192]{1,0:T(8,128)(2,1)}, bf16[68,256,128]{2,1,0:T(8,128)(2,1)S(1)}) custom-call(s32[1040]{0:T(1024)S(1)} %constant_dynamic-update-slice_fusion.table.refs_0_, bf16[68,256,128]{2,1,0:T(8,128)(2,1)S(1)} %get-tuple-element.85.refs_1_, bf16[256,128]{1,0:T(8,128)(2,1)S(1)} %collective-permute-done.31.refs_2_, ...), custom_call_target="tpu_custom_call", output_to_operand_aliasing={{1}: (1, {})} | custom-call | tf_op jit(solution)/shard_map/pallas_call | solution.py:205
  175.1 3.3 %collective-permute-done.38.refs_4_ = bf16[20,128,128]{2,1,0:T(8,128)(2,1)S(1)} collective-permute-done((bf16[20,128,128]{2,1,0:T(8,128)(2,1)S(1)}, bf16[20,128,128]{2,1,0:T(8,128)(2,1)S(1)}, u32[]{:S(2)}, u32[]{:S(2)}) %collective-permute-start.38) | collective-permute-done | bytes 655392 | tf_op jit(solution)/shard_map/ppermute | solution.py:28
  180.7 4.1 %shard_map.69.refs_8_ = bf16[256,8192]{1,0:T(8,128)(2,1)} custom-call(s32[1040]{0:T(1024)S(1)} %constant_dynamic-update-slice_fusion.table.refs_0_, bf16[68,256,128]{2,1,0:T(8,128)(2,1)S(1)} %get-tuple-element.97.refs_1_, bf16[20,128,128]{2,1,0:T(8,128)(2,1)S(1)} %get-tuple-element.99.refs_2_, ...), custom_call_target="tpu_custom_call", output_to_operand_aliasing={{}: (9, {})} | custom-call | tf_op jit(solution)/shard_map/pallas_call | solution.py:205
  187.4 3.2 %shard_map.70 = bf16[256,8192]{1,0:T(8,128)(2,1)} custom-call(s32[1040]{0:T(1024)S(1)} %constant_dynamic-update-slice_fusion.table.refs_0_, bf16[68,256,128]{2,1,0:T(8,128)(2,1)S(1)} %get-tuple-element.97.refs_1_, bf16[12,128,128]{2,1,0:T(8,128)(2,1)S(1)} %get-tuple-element.98.refs_2_, ...), custom_call_target="tpu_custom_call", output_to_operand_aliasing={{}: (8, {})} | custom-call | tf_op jit(solution)/shard_map/pallas_call | solution.py:205
  (101 shorter events, 47.8 us)
Async XLA Ops:
  0.0 29.1 %collective-permute-start.4 = (bf16[4,64,128,128]{3,2,1,0:T(8,128)(2,1)}, bf16[4,64,128,128]{3,2,1,0:T(8,128)(2,1)}, u32[]{:S(2)}, u32[]{:S(2)}) collective-permute-start(bf16[4,64,128,128]{3,2,1,0:T(8,128)(2,1)} %tiles.9), channel_id=1, source_target_pairs={{0,1},{1,0},{2,3},{3,2},{4,5},{5,4},{6,7},{7,6},{8,9},{9,8},{10,11... | collective-permute-start | bytes 25165832 | tf_op jit(solution)/shard_map/ppermute | solution.py:28
  1.8 34.2 %collective-permute-start.5 = (bf16[32,128,128]{2,1,0:T(8,128)(2,1)S(1)}, bf16[32,128,128]{2,1,0:T(8,128)(2,1)}, u32[]{:S(2)}, u32[]{:S(2)}) collective-permute-start(bf16[32,128,128]{2,1,0:T(8,128)(2,1)S(1)} %shard_map.56.refs_6_), channel_id=1, source_target_pairs={{0,2},{1,3},{2,0},{3,1},{4,6},{5,7},{6,4},{7,5},{8,10},{9,11},{10,... | collective-permute-start | bytes 3145736 | tf_op jit(solution)/shard_map/ppermute | solution.py:28
  6.8 44.2 %collective-permute-start.6 = (bf16[32,128,128]{2,1,0:T(8,128)(2,1)}, bf16[32,128,128]{2,1,0:T(8,128)(2,1)}, u32[]{:S(2)}, u32[]{:S(2)}) collective-permute-start(bf16[32,128,128]{2,1,0:T(8,128)(2,1)} %shard_map.57.refs_7_), channel_id=1, source_target_pairs={{0,2},{1,3},{2,0},{3,1},{4,6},{5,7},{6,4},{7,5},{8,10},{9,11},{10,... | collective-permute-start | bytes 3145736 | tf_op jit(solution)/shard_map/ppermute | solution.py:28
  8.6 87.3 %collective-permute-start.15 = (bf16[64,128,128]{2,1,0:T(8,128)(2,1)S(1)}, bf16[64,128,128]{2,1,0:T(8,128)(2,1)}, u32[]{:S(2)}, u32[]{:S(2)}) collective-permute-start(bf16[64,128,128]{2,1,0:T(8,128)(2,1)S(1)} %shard_map.60.refs_6_), channel_id=1, source_target_pairs={{0,2},{1,3},{2,0},{3,1},{4,6},{5,7},{6,4},{7,5},{8,10},{9,11},{10,... | collective-permute-start | bytes 6291464 | tf_op jit(solution)/shard_map/ppermute | solution.py:28
  14.4 6.1 %collective-permute-start.2 = (bf16[256,128]{1,0:T(8,128)(2,1)S(1)}, bf16[256,128]{1,0:T(8,128)(2,1)S(1)}, u32[]{:S(2)}, u32[]{:S(2)}) collective-permute-start(bf16[256,128]{1,0:T(8,128)(2,1)S(1)} %get-tuple-element.57), channel_id=1, source_target_pairs={{24,0},{28,4},{0,8},{4,12},{8,16},{12,20},{16,24},{20,28},{25,1},{... | collective-permute-start | bytes 196616 | tf_op jit(solution)/shard_map/ppermute | solution.py:23
  20.6 5.2 %collective-permute-start = (bf16[256,128]{1,0:T(8,128)(2,1)S(1)}, bf16[256,128]{1,0:T(8,128)(2,1)S(1)}, u32[]{:S(2)}, u32[]{:S(2)}) collective-permute-start(bf16[256,128]{1,0:T(8,128)(2,1)S(1)} %get-tuple-element.55), channel_id=1, source_target_pairs={{16,0},{20,4},{24,8},{28,12},{0,16},{4,20},{8,24},{12,28},{17,1},{... | collective-permute-start | bytes 196616 | tf_op jit(solution)/shard_map/ppermute | solution.py:23
  25.7 5.3 %collective-permute-start.3 = (bf16[256,128]{1,0:T(8,128)(2,1)S(1)}, bf16[256,128]{1,0:T(8,128)(2,1)S(1)}, u32[]{:S(2)}, u32[]{:S(2)}) collective-permute-start(bf16[256,128]{1,0:T(8,128)(2,1)S(1)} %get-tuple-element.59), channel_id=1, source_target_pairs={{4,0},{8,4},{12,8},{16,12},{20,16},{24,20},{28,24},{0,28},{5,1},{9... | collective-permute-start | bytes 196616 | tf_op jit(solution)/shard_map/ppermute | solution.py:23
  29.1 7.0 %collective-permute-start.1 = (bf16[256,128]{1,0:T(8,128)(2,1)S(1)}, bf16[256,128]{1,0:T(8,128)(2,1)S(1)}, u32[]{:S(2)}, u32[]{:S(2)}) collective-permute-start(bf16[256,128]{1,0:T(8,128)(2,1)S(1)} %get-tuple-element.56), channel_id=1, source_target_pairs={{28,0},{0,4},{4,8},{8,12},{12,16},{16,20},{20,24},{24,28},{29,1},{... | collective-permute-start | bytes 196616 | tf_op jit(solution)/shard_map/ppermute | solution.py:23
  37.3 13.7 %collective-permute-start.7 = (bf16[16,128,128]{2,1,0:T(8,128)(2,1)S(1)}, bf16[16,128,128]{2,1,0:T(8,128)(2,1)S(1)}, u32[]{:S(2)}, u32[]{:S(2)}) collective-permute-start(bf16[16,128,128]{2,1,0:T(8,128)(2,1)S(1)} %get-tuple-element.115), channel_id=1, source_target_pairs={{0,1},{1,0},{2,3},{3,2},{4,5},{5,4},{6,7},{7,6},{8,9},{9,8},{10,11... | collective-permute-start | bytes 1572872 | tf_op jit(solution)/shard_map/ppermute | solution.py:28
  37.4 13.6 %collective-permute-start.8 = (bf16[16,128,128]{2,1,0:T(8,128)(2,1)S(1)}, bf16[16,128,128]{2,1,0:T(8,128)(2,1)S(1)}, u32[]{:S(2)}, u32[]{:S(2)}) collective-permute-start(bf16[16,128,128]{2,1,0:T(8,128)(2,1)S(1)} %get-tuple-element.114), channel_id=1, source_target_pairs={{0,1},{1,0},{2,3},{3,2},{4,5},{5,4},{6,7},{7,6},{8,9},{9,8},{10,11... | collective-permute-start | bytes 1572872 | tf_op jit(solution)/shard_map/ppermute | solution.py:28
  52.3 4.4 %collective-permute-start.10 = (bf16[16,128,128]{2,1,0:T(8,128)(2,1)S(1)}, bf16[16,128,128]{2,1,0:T(8,128)(2,1)S(1)}, u32[]{:S(2)}, u32[]{:S(2)}) collective-permute-start(bf16[16,128,128]{2,1,0:T(8,128)(2,1)S(1)} %get-tuple-element.112), channel_id=1, source_target_pairs={{0,1},{1,0},{2,3},{3,2},{4,5},{5,4},{6,7},{7,6},{8,9},{9,8},{10,11... | collective-permute-start | bytes 1572872 | tf_op jit(solution)/shard_map/ppermute | solution.py:28
  52.4 4.3 %collective-permute-start.9 = (bf16[16,128,128]{2,1,0:T(8,128)(2,1)S(1)}, bf16[16,128,128]{2,1,0:T(8,128)(2,1)S(1)}, u32[]{:S(2)}, u32[]{:S(2)}) collective-permute-start(bf16[16,128,128]{2,1,0:T(8,128)(2,1)S(1)} %get-tuple-element.113), channel_id=1, source_target_pairs={{0,1},{1,0},{2,3},{3,2},{4,5},{5,4},{6,7},{7,6},{8,9},{9,8},{10,11... | collective-permute-start | bytes 1572872 | tf_op jit(solution)/shard_map/ppermute | solution.py:28
  54.6 74.9 %collective-permute-start.24 = (bf16[48,128,128]{2,1,0:T(8,128)(2,1)S(1)}, bf16[48,128,128]{2,1,0:T(8,128)(2,1)S(1)}, u32[]{:S(2)}, u32[]{:S(2)}) collective-permute-start(bf16[48,128,128]{2,1,0:T(8,128)(2,1)S(1)} %get-tuple-element.79.refs_6_), channel_id=1, source_target_pairs={{0,2},{1,3},{2,0},{3,1},{4,6},{5,7},{6,4},{7,5},{8,10},{9,11},{10,... | collective-permute-start | bytes 4718600 | tf_op jit(solution)/shard_map/ppermute | solution.py:28
  68.1 6.6 %collective-permute-start.13 = (bf16[256,128]{1,0:T(8,128)(2,1)S(1)}, bf16[256,128]{1,0:T(8,128)(2,1)S(1)}, u32[]{:S(2)}, u32[]{:S(2)}) collective-permute-start(bf16[256,128]{1,0:T(8,128)(2,1)S(1)} %get-tuple-element.68), channel_id=1, source_target_pairs={{24,0},{28,4},{0,8},{4,12},{8,16},{12,20},{16,24},{20,28},{25,1},{... | collective-permute-start | bytes 196616 | tf_op jit(solution)/shard_map/ppermute | solution.py:23
  69.7 7.8 %collective-permute-start.11 = (bf16[256,128]{1,0:T(8,128)(2,1)S(1)}, bf16[256,128]{1,0:T(8,128)(2,1)S(1)}, u32[]{:S(2)}, u32[]{:S(2)}) collective-permute-start(bf16[256,128]{1,0:T(8,128)(2,1)S(1)} %get-tuple-element.66), channel_id=1, source_target_pairs={{16,0},{20,4},{24,8},{28,12},{0,16},{4,20},{8,24},{12,28},{17,1},{... | collective-permute-start | bytes 196616 | tf_op jit(solution)/shard_map/ppermute | solution.py:23
  74.7 21.3 %collective-permute-start.14 = (bf16[256,128]{1,0:T(8,128)(2,1)S(1)}, bf16[256,128]{1,0:T(8,128)(2,1)S(1)}, u32[]{:S(2)}, u32[]{:S(2)}) collective-permute-start(bf16[256,128]{1,0:T(8,128)(2,1)S(1)} %get-tuple-element.70), channel_id=1, source_target_pairs={{4,0},{8,4},{12,8},{16,12},{20,16},{24,20},{28,24},{0,28},{5,1},{9... | collective-permute-start | bytes 196616 | tf_op jit(solution)/shard_map/ppermute | solution.py:23
  77.5 18.4 %collective-permute-start.12 = (bf16[256,128]{1,0:T(8,128)(2,1)S(1)}, bf16[256,128]{1,0:T(8,128)(2,1)S(1)}, u32[]{:S(2)}, u32[]{:S(2)}) collective-permute-start(bf16[256,128]{1,0:T(8,128)(2,1)S(1)} %get-tuple-element.67), channel_id=1, source_target_pairs={{28,0},{0,4},{4,8},{8,12},{12,16},{16,20},{20,24},{24,28},{29,1},{... | collective-permute-start | bytes 196616 | tf_op jit(solution)/shard_map/ppermute | solution.py:23
  110.6 6.7 %collective-permute-start.22 = (bf16[256,128]{1,0:T(8,128)(2,1)S(1)}, bf16[256,128]{1,0:T(8,128)(2,1)S(1)}, u32[]{:S(2)}, u32[]{:S(2)}) collective-permute-start(bf16[256,128]{1,0:T(8,128)(2,1)S(1)} %get-tuple-element.76), channel_id=1, source_target_pairs={{24,0},{28,4},{0,8},{4,12},{8,16},{12,20},{16,24},{20,28},{25,1},{... | collective-permute-start | bytes 196616 | tf_op jit(solution)/shard_map/ppermute | solution.py:23
  112.7 8.0 %collective-permute-start.20 = (bf16[256,128]{1,0:T(8,128)(2,1)S(1)}, bf16[256,128]{1,0:T(8,128)(2,1)S(1)}, u32[]{:S(2)}, u32[]{:S(2)}) collective-permute-start(bf16[256,128]{1,0:T(8,128)(2,1)S(1)} %get-tuple-element.74), channel_id=1, source_target_pairs={{16,0},{20,4},{24,8},{28,12},{0,16},{4,20},{8,24},{12,28},{17,1},{... | collective-permute-start | bytes 196616 | tf_op jit(solution)/shard_map/ppermute | solution.py:23
  117.3 12.3 %collective-permute-start.23 = (bf16[256,128]{1,0:T(8,128)(2,1)S(1)}, bf16[256,128]{1,0:T(8,128)(2,1)S(1)}, u32[]{:S(2)}, u32[]{:S(2)}) collective-permute-start(bf16[256,128]{1,0:T(8,128)(2,1)S(1)} %get-tuple-element.78), channel_id=1, source_target_pairs={{4,0},{8,4},{12,8},{16,12},{20,16},{24,20},{28,24},{0,28},{5,1},{9... | collective-permute-start | bytes 196616 | tf_op jit(solution)/shard_map/ppermute | solution.py:23
  120.7 8.8 %collective-permute-start.21 = (bf16[256,128]{1,0:T(8,128)(2,1)S(1)}, bf16[256,128]{1,0:T(8,128)(2,1)S(1)}, u32[]{:S(2)}, u32[]{:S(2)}) collective-permute-start(bf16[256,128]{1,0:T(8,128)(2,1)S(1)} %get-tuple-element.75), channel_id=1, source_target_pairs={{28,0},{0,4},{4,8},{8,12},{12,16},{16,20},{20,24},{24,28},{29,1},{... | collective-permute-start | bytes 196616 | tf_op jit(solution)/shard_map/ppermute | solution.py:23
  121.4 19.3 %collective-permute-start.25 = (bf16[16,128,128]{2,1,0:T(8,128)(2,1)S(1)}, bf16[16,128,128]{2,1,0:T(8,128)(2,1)S(1)}, u32[]{:S(2)}, u32[]{:S(2)}) collective-permute-start(bf16[16,128,128]{2,1,0:T(8,128)(2,1)S(1)} %get-tuple-element.80.refs_7_), channel_id=1, source_target_pairs={{0,2},{1,3},{2,0},{3,1},{4,6},{5,7},{6,4},{7,5},{8,10},{9,11},{10,... | collective-permute-start | bytes 1572872 | tf_op jit(solution)/shard_map/ppermute | solution.py:28
  129.7 11.1 %collective-permute-start.26 = (bf16[16,128,128]{2,1,0:T(8,128)(2,1)S(1)}, bf16[16,128,128]{2,1,0:T(8,128)(2,1)S(1)}, u32[]{:S(2)}, u32[]{:S(2)}) collective-permute-start(bf16[16,128,128]{2,1,0:T(8,128)(2,1)S(1)} %get-tuple-element.109), channel_id=1, source_target_pairs={{0,1},{1,0},{2,3},{3,2},{4,5},{5,4},{6,7},{7,6},{8,9},{9,8},{10,11... | collective-permute-start | bytes 1572872 | tf_op jit(solution)/shard_map/ppermute | solution.py:28
  129.8 11.0 %collective-permute-start.27 = (bf16[16,128,128]{2,1,0:T(8,128)(2,1)S(1)}, bf16[16,128,128]{2,1,0:T(8,128)(2,1)S(1)}, u32[]{:S(2)}, u32[]{:S(2)}) collective-permute-start(bf16[16,128,128]{2,1,0:T(8,128)(2,1)S(1)} %get-tuple-element.108), channel_id=1, source_target_pairs={{0,1},{1,0},{2,3},{3,2},{4,5},{5,4},{6,7},{7,6},{8,9},{9,8},{10,11... | collective-permute-start | bytes 1572872 | tf_op jit(solution)/shard_map/ppermute | solution.py:28
  130.3 10.5 %collective-permute-start.28 = (bf16[16,128,128]{2,1,0:T(8,128)(2,1)S(1)}, bf16[16,128,128]{2,1,0:T(8,128)(2,1)S(1)}, u32[]{:S(2)}, u32[]{:S(2)}) collective-permute-start(bf16[16,128,128]{2,1,0:T(8,128)(2,1)S(1)} %get-tuple-element.107), channel_id=1, source_target_pairs={{0,1},{1,0},{2,3},{3,2},{4,5},{5,4},{6,7},{7,6},{8,9},{9,8},{10,11... | collective-permute-start | bytes 1572872 | tf_op jit(solution)/shard_map/ppermute | solution.py:28
  132.4 32.0 %collective-permute-start.34 = (bf16[32,128,128]{2,1,0:T(8,128)(2,1)S(1)}, bf16[32,128,128]{2,1,0:T(8,128)(2,1)S(1)}, u32[]{:S(2)}, u32[]{:S(2)}) collective-permute-start(bf16[32,128,128]{2,1,0:T(8,128)(2,1)S(1)} %get-tuple-element.92.refs_6_), channel_id=1, source_target_pairs={{0,2},{1,3},{2,0},{3,1},{4,6},{5,7},{6,4},{7,5},{8,10},{9,11},{10,... | collective-permute-start | bytes 3145736 | tf_op jit(solution)/shard_map/ppermute | solution.py:28
  150.0 6.7 %collective-permute-start.32 = (bf16[256,128]{1,0:T(8,128)(2,1)S(1)}, bf16[256,128]{1,0:T(8,128)(2,1)S(1)}, u32[]{:S(2)}, u32[]{:S(2)}) collective-permute-start(bf16[256,128]{1,0:T(8,128)(2,1)S(1)} %get-tuple-element.89), channel_id=1, source_target_pairs={{24,0},{28,4},{0,8},{4,12},{8,16},{12,20},{16,24},{20,28},{25,1},{... | collective-permute-start | bytes 196616 | tf_op jit(solution)/shard_map/ppermute | solution.py:23
  152.1 8.0 %collective-permute-start.30 = (bf16[256,128]{1,0:T(8,128)(2,1)S(1)}, bf16[256,128]{1,0:T(8,128)(2,1)S(1)}, u32[]{:S(2)}, u32[]{:S(2)}) collective-permute-start(bf16[256,128]{1,0:T(8,128)(2,1)S(1)} %get-tuple-element.87), channel_id=1, source_target_pairs={{16,0},{20,4},{24,8},{28,12},{0,16},{4,20},{8,24},{12,28},{17,1},{... | collective-permute-start | bytes 196616 | tf_op jit(solution)/shard_map/ppermute | solution.py:23
  156.7 7.7 %collective-permute-start.33 = (bf16[256,128]{1,0:T(8,128)(2,1)S(1)}, bf16[256,128]{1,0:T(8,128)(2,1)S(1)}, u32[]{:S(2)}, u32[]{:S(2)}) collective-permute-start(bf16[256,128]{1,0:T(8,128)(2,1)S(1)} %get-tuple-element.91), channel_id=1, source_target_pairs={{4,0},{8,4},{12,8},{16,12},{20,16},{24,20},{28,24},{0,28},{5,1},{9... | collective-permute-start | bytes 196616 | tf_op jit(solution)/shard_map/ppermute | solution.py:23
  160.1 7.0 %collective-permute-start.31 = (bf16[256,128]{1,0:T(8,128)(2,1)S(1)}, bf16[256,128]{1,0:T(8,128)(2,1)S(1)}, u32[]{:S(2)}, u32[]{:S(2)}) collective-permute-start(bf16[256,128]{1,0:T(8,128)(2,1)S(1)} %get-tuple-element.88), channel_id=1, source_target_pairs={{28,0},{0,4},{4,8},{8,12},{12,16},{16,20},{20,24},{24,28},{29,1},{... | collective-permute-start | bytes 196616 | tf_op jit(solution)/shard_map/ppermute | solution.py:23
  160.8 17.6 %collective-permute-start.38 = (bf16[20,128,128]{2,1,0:T(8,128)(2,1)S(1)}, bf16[20,128,128]{2,1,0:T(8,128)(2,1)S(1)}, u32[]{:S(2)}, u32[]{:S(2)}) collective-permute-start(bf16[20,128,128]{2,1,0:T(8,128)(2,1)S(1)} %get-tuple-element.99.refs_2_), channel_id=1, source_target_pairs={{0,2},{1,3},{2,0},{3,1},{4,6},{5,7},{6,4},{7,5},{8,10},{9,11},{10,... | collective-permute-start | bytes 1966088 | tf_op jit(solution)/shard_map/ppermute | solution.py:28
  167.7 17.9 %collective-permute-start.37 = (bf16[12,128,128]{2,1,0:T(8,128)(2,1)S(1)}, bf16[12,128,128]{2,1,0:T(8,128)(2,1)S(1)}, u32[]{:S(2)}, u32[]{:S(2)}) collective-permute-start(bf16[12,128,128]{2,1,0:T(8,128)(2,1)S(1)} %get-tuple-element.98.refs_2_), channel_id=1, source_target_pairs={{0,2},{1,3},{2,0},{3,1},{4,6},{5,7},{6,4},{7,5},{8,10},{9,11},{10,... | collective-permute-start | bytes 1179656 | tf_op jit(solution)/shard_map/ppermute | solution.py:28
  (16 other events, 52.4 us)

commit v11 on v10

--- a/solution.py
+++ b/solution.py
@@ -196,7 +196,7 @@
     if not final:
         out_shape += [jax.ShapeDtypeStruct((rows, width), pool.dtype)] * neigh
         out_specs += [vmem] * neigh
-    scratch = [pltpu.SemaphoreType.DMA((blocks + neigh,))]
+    scratch = [pltpu.SemaphoreType.DMA((len(arrived) + (blocks if columns else 0) or 1,))]
     if final:
         scratch += [pltpu.VMEM((rows, count * width), pool.dtype), pltpu.SemaphoreType.DMA((count // group,))]
     if columns:
@@ -241,10 +241,7 @@
                 )
 
     last = layer_count - 1
-    shares = [(0, (8, 8), ((4, 4), (4, 4)))]
-    shares += [(layer, (16,), ((4, 4, 4, 4),)) for layer in range(1, last - 1)]
-    shares += [(last - 1, (12, 4), ((4, 4, 4), (4,)))]
-    shares += [(last, (8,), ((4, 4),)), (last, (5,), ((2, 2, 1),)), (last, (3,), ((2, 1),))]
+    shares = [(0, (8, 8), ((4, 4), (4, 4))), (1, (8, 8), ((4, 4), (4, 4))), (2, (8, 8), ((4, 4), (4, 4))), (last, (8,), ((4, 4),)), (last, (5,), ((2, 2, 1),)), (last, (3,), ((3,),))]
 
     moves = {layer: [] for layer in range(layer_count)}
     for layer, sizes, _ in shares:

time: 192 us -> 191 us (level)
  Pallas kernels: 58.2 us -> 52.5 us
  starting transfers between devices: 49.6 us -> 55 us
  local copies, waits for them, and re-layouts: 5.99 us -> 3.31 us
  waiting for transfers between devices: 75.8 us -> 78.3 us
    pallas_call x6, Pallas kernels: 40 us -> 35 us  [run_blocks(): pl.pallas_call(kernel, out_shape=out_shape, grid_spec=pltpu.PrefetchScala...]
    ppermute x16, starting transfers between devices: 31.1 us -> 35.2 us  [shifted(): return lax.ppermute(block, axis, route)]
    slice x9, local copies, waits for them, and re-layouts: 4.53 us -> 1.86 us  [body(): passed[far] = [tile[start:end] for start, end in zip(starts, starts[1:])]]
    ppermute x28, waiting for transfers between devices: 52.8 us -> 54.8 us  [swapped(): return lax.ppermute(block, 'batch', route)]
  transfers between devices with their start and end apart: 44 -> 44, of which waited for: 22 -> 22; matrix products, arithmetic and copies ran while one was open for 4% -> 2% of each run, Pallas kernels for 29% -> 26%
where the time goes in v11:
time: 191 us; the launch traced here: 190 us
  waiting for transfers between devices  78.3 us (41%)
  starting transfers between devices  55 us (29%)
  Pallas kernels  52.5 us (27%)
  local copies, waits for them, and re-layouts  3.31 us (2%)
    ppermute x28, waiting for transfers between devices, swapped(): return lax.ppermute(block, 'batch', route)  54.8 us
    ppermute x16, starting transfers between devices, shifted(): return lax.ppermute(block, axis, route)  35.2 us
    pallas_call x6, Pallas kernels, run_blocks(): pl.pallas_call(kernel, out_shape=out_shape, grid_spec=pltpu.PrefetchScala...  35 us
    ppermute x16, waiting for transfers between devices, shifted(): return lax.ppermute(block, axis, route)  23.5 us
    ppermute x28, starting transfers between devices, swapped(): return lax.ppermute(block, 'batch', route)  19.8 us
    pallas_call x9, Pallas kernels, cut(): pl.pallas_call(kernel, out_shape=[pltpu.VMEM((count, height, width), tile...  15.9 us
  transfers between devices with their start and end apart: 44, of which 22 were waited for; matrix products, arithmetic and copies ran while one was open for 2% of the time, Pallas kernels for 26%

profile of v11, /device:TPU:0, one launch (start us, length us, event | category | flops | bytes accessed | tf_op | source)
XLA Modules:
  0.0 190.5 jit_solution(17148111037379779951)
XLA Ops:
  1.8 2.6 %collective-permute-start.5 = (bf16[32,128,128]{2,1,0:T(8,128)(2,1)S(1)}, bf16[32,128,128]{2,1,0:T(8,128)(2,1)S(1)}, u32[]{:S(2)}, u32[]{:S(2)}) collective-permute-start(bf16[32,128,128]{2,1,0:T(8,128)(2,1)S(1)} %shard_map.56.refs_6_), channel_id=1, source_target_pairs={{0,2},{1,3},{2,0},{3,1},{4,6},{5,7},{6,4},{7,5},{8,10},{9,11},{10,... | collective-permute-start | bytes 3145736 | tf_op jit(solution)/shard_map/ppermute | solution.py:28
  9.7 2.1 %collective-permute-start.2 = (bf16[256,128]{1,0:T(8,128)(2,1)S(1)}, bf16[256,128]{1,0:T(8,128)(2,1)S(1)}, u32[]{:S(2)}, u32[]{:S(2)}) collective-permute-start(bf16[256,128]{1,0:T(8,128)(2,1)S(1)} %get-tuple-element.62), channel_id=1, source_target_pairs={{24,0},{28,4},{0,8},{4,12},{8,16},{12,20},{16,24},{20,28},{25,1},{... | collective-permute-start | bytes 196616 | tf_op jit(solution)/shard_map/ppermute | solution.py:23
  11.8 2.6 %collective-permute-start = (bf16[256,128]{1,0:T(8,128)(2,1)S(1)}, bf16[256,128]{1,0:T(8,128)(2,1)S(1)}, u32[]{:S(2)}, u32[]{:S(2)}) collective-permute-start(bf16[256,128]{1,0:T(8,128)(2,1)S(1)} %get-tuple-element.60), channel_id=1, source_target_pairs={{16,0},{20,4},{24,8},{28,12},{0,16},{4,20},{8,24},{12,28},{17,1},{... | collective-permute-start | bytes 196616 | tf_op jit(solution)/shard_map/ppermute | solution.py:23
  16.3 3.3 %collective-permute-start.3 = (bf16[256,128]{1,0:T(8,128)(2,1)S(1)}, bf16[256,128]{1,0:T(8,128)(2,1)S(1)}, u32[]{:S(2)}, u32[]{:S(2)}) collective-permute-start(bf16[256,128]{1,0:T(8,128)(2,1)S(1)} %get-tuple-element.64), channel_id=1, source_target_pairs={{4,0},{8,4},{12,8},{16,12},{20,16},{24,20},{28,24},{0,28},{5,1},{9... | collective-permute-start | bytes 196616 | tf_op jit(solution)/shard_map/ppermute | solution.py:23
  22.2 4.4 %collective-permute-done.1.refs_2_ = bf16[256,128]{1,0:T(8,128)(2,1)S(1)} collective-permute-done((bf16[256,128]{1,0:T(8,128)(2,1)S(1)}, bf16[256,128]{1,0:T(8,128)(2,1)S(1)}, u32[]{:S(2)}, u32[]{:S(2)}) %collective-permute-start.1) | collective-permute-done | bytes 65568 | tf_op jit(solution)/shard_map/ppermute | solution.py:23
  32.9 18.1 %collective-permute-done.6.refs_11_ = bf16[32,128,128]{2,1,0:T(8,128)(2,1)} collective-permute-done((bf16[32,128,128]{2,1,0:T(8,128)(2,1)S(1)}, bf16[32,128,128]{2,1,0:T(8,128)(2,1)}, u32[]{:S(2)}, u32[]{:S(2)}) %collective-permute-start.6) | collective-permute-done | bytes 1048608 | tf_op jit(solution)/shard_map/ppermute | solution.py:28
  55.0 10.8 %shard_map.59 = (bf16[68,256,128]{2,1,0:T(8,128)(2,1)S(1)}, bf16[256,128]{1,0:T(8,128)(2,1)S(1)}, bf16[256,128]{1,0:T(8,128)(2,1)S(1)}, bf16[256,128]{1,0:T(8,128)(2,1)S(1)}, bf16[256,128]{1,0:T(8,128)(2,1)S(1)}) custom-call(s32[1040]{0:T(1024)S(1)} %constant_dynamic-update-slice_fusion.table.refs_0_, bf16[256,8192]{1,0:T(8,128)(2,1)} %refs_1_.1, ...), custom_call_target="tpu_custom_call" | custom-call | tf_op jit(solution)/shard_map/pallas_call | solution.py:205
  65.8 2.1 %collective-permute-start.13 = (bf16[256,128]{1,0:T(8,128)(2,1)S(1)}, bf16[256,128]{1,0:T(8,128)(2,1)S(1)}, u32[]{:S(2)}, u32[]{:S(2)}) collective-permute-start(bf16[256,128]{1,0:T(8,128)(2,1)S(1)} %get-tuple-element.73), channel_id=1, source_target_pairs={{24,0},{28,4},{0,8},{4,12},{8,16},{12,20},{16,24},{20,28},{25,1},{... | collective-permute-start | bytes 196616 | tf_op jit(solution)/shard_map/ppermute | solution.py:23
  67.9 2.6 %collective-permute-start.11 = (bf16[256,128]{1,0:T(8,128)(2,1)S(1)}, bf16[256,128]{1,0:T(8,128)(2,1)S(1)}, u32[]{:S(2)}, u32[]{:S(2)}) collective-permute-start(bf16[256,128]{1,0:T(8,128)(2,1)S(1)} %get-tuple-element.71), channel_id=1, source_target_pairs={{16,0},{20,4},{24,8},{28,12},{0,16},{4,20},{8,24},{12,28},{17,1},{... | collective-permute-start | bytes 196616 | tf_op jit(solution)/shard_map/ppermute | solution.py:23
  70.5 2.0 %collective-permute-done.13.refs_3_ = bf16[256,128]{1,0:T(8,128)(2,1)S(1)} collective-permute-done((bf16[256,128]{1,0:T(8,128)(2,1)S(1)}, bf16[256,128]{1,0:T(8,128)(2,1)S(1)}, u32[]{:S(2)}, u32[]{:S(2)}) %collective-permute-start.13) | collective-permute-done | bytes 65568 | tf_op jit(solution)/shard_map/ppermute | solution.py:23
  72.5 3.4 %collective-permute-start.14 = (bf16[256,128]{1,0:T(8,128)(2,1)S(1)}, bf16[256,128]{1,0:T(8,128)(2,1)S(1)}, u32[]{:S(2)}, u32[]{:S(2)}) collective-permute-start(bf16[256,128]{1,0:T(8,128)(2,1)S(1)} %get-tuple-element.75), channel_id=1, source_target_pairs={{4,0},{8,4},{12,8},{16,12},{20,16},{24,20},{28,24},{0,28},{5,1},{9... | collective-permute-start | bytes 196616 | tf_op jit(solution)/shard_map/ppermute | solution.py:23
  78.5 4.4 %collective-permute-done.12.refs_2_ = bf16[256,128]{1,0:T(8,128)(2,1)S(1)} collective-permute-done((bf16[256,128]{1,0:T(8,128)(2,1)S(1)}, bf16[256,128]{1,0:T(8,128)(2,1)S(1)}, u32[]{:S(2)}, u32[]{:S(2)}) %collective-permute-start.12) | collective-permute-done | bytes 65568 | tf_op jit(solution)/shard_map/ppermute | solution.py:23
  87.0 8.8 %collective-permute-done.16.refs_11_ = bf16[32,128,128]{2,1,0:T(8,128)(2,1)S(1)} collective-permute-done((bf16[32,128,128]{2,1,0:T(8,128)(2,1)S(1)}, bf16[32,128,128]{2,1,0:T(8,128)(2,1)S(1)}, u32[]{:S(2)}, u32[]{:S(2)}) %collective-permute-start.16) | collective-permute-done | bytes 1048608 | tf_op jit(solution)/shard_map/ppermute | solution.py:28
  98.7 6.7 %shard_map.62 = (bf16[68,256,128]{2,1,0:T(8,128)(2,1)S(1)}, bf16[68,256,128]{2,1,0:T(8,128)(2,1)S(1)}, bf16[256,128]{1,0:T(8,128)(2,1)S(1)}, bf16[256,128]{1,0:T...) custom-call(s32[1040]{0:T(1024)S(1)} %constant_dynamic-update-slice_, ...), custom_call_target="tpu_custom_call", output_to_operand_aliasing={{1}: (1, {})} | custom-call | tf_op jit(solution)/shard_map/pallas_call | solution.py:205
  105.4 2.1 %collective-permute-start.23 = (bf16[256,128]{1,0:T(8,128)(2,1)S(1)}, bf16[256,128]{1,0:T(8,128)(2,1)S(1)}, u32[]{:S(2)}, u32[]{:S(2)}) collective-permute-start(bf16[256,128]{1,0:T(8,128)(2,1)S(1)} %get-tuple-element.86), channel_id=1, source_target_pairs={{24,0},{28,4},{0,8},{4,12},{8,16},{12,20},{16,24},{20,28},{25,1},{... | collective-permute-start | bytes 196616 | tf_op jit(solution)/shard_map/ppermute | solution.py:23
  107.4 2.6 %collective-permute-start.21 = (bf16[256,128]{1,0:T(8,128)(2,1)S(1)}, bf16[256,128]{1,0:T(8,128)(2,1)S(1)}, u32[]{:S(2)}, u32[]{:S(2)}) collective-permute-start(bf16[256,128]{1,0:T(8,128)(2,1)S(1)} %get-tuple-element.84), channel_id=1, source_target_pairs={{16,0},{20,4},{24,8},{28,12},{0,16},{4,20},{8,24},{12,28},{17,1},{... | collective-permute-start | bytes 196616 | tf_op jit(solution)/shard_map/ppermute | solution.py:23
  110.0 2.0 %collective-permute-done.23.refs_3_ = bf16[256,128]{1,0:T(8,128)(2,1)S(1)} collective-permute-done((bf16[256,128]{1,0:T(8,128)(2,1)S(1)}, bf16[256,128]{1,0:T(8,128)(2,1)S(1)}, u32[]{:S(2)}, u32[]{:S(2)}) %collective-permute-start.23) | collective-permute-done | bytes 65568 | tf_op jit(solution)/shard_map/ppermute | solution.py:23
  112.0 3.4 %collective-permute-start.24 = (bf16[256,128]{1,0:T(8,128)(2,1)S(1)}, bf16[256,128]{1,0:T(8,128)(2,1)S(1)}, u32[]{:S(2)}, u32[]{:S(2)}) collective-permute-start(bf16[256,128]{1,0:T(8,128)(2,1)S(1)} %get-tuple-element.88), channel_id=1, source_target_pairs={{4,0},{8,4},{12,8},{16,12},{20,16},{24,20},{28,24},{0,28},{5,1},{9... | collective-permute-start | bytes 196616 | tf_op jit(solution)/shard_map/ppermute | solution.py:23
  118.3 4.1 %collective-permute-done.22.refs_2_ = bf16[256,128]{1,0:T(8,128)(2,1)S(1)} collective-permute-done((bf16[256,128]{1,0:T(8,128)(2,1)S(1)}, bf16[256,128]{1,0:T(8,128)(2,1)S(1)}, u32[]{:S(2)}, u32[]{:S(2)}) %collective-permute-start.22) | collective-permute-done | bytes 65568 | tf_op jit(solution)/shard_map/ppermute | solution.py:23
  123.1 2.0 %shard_map.66 = (bf16[32,128,128]{2,1,0:T(8,128)(2,1)S(1)}, bf16[20,128,128]{2,1,0:T(8,128)(2,1)S(1)}, bf16[12,128,128]{2,1,0:T(8,128)(2,1)S(1)}) custom-call(bf16[4,64,128,128]{3,2,1,0:T(8,128)(2,1)} %tiles.9), custom_call_target="tpu_custom_call" | custom-call | tf_op jit(solution)/shard_map/pallas_call | solution.py:56
  126.7 14.1 %collective-permute-done.26.refs_11_ = bf16[32,128,128]{2,1,0:T(8,128)(2,1)S(1)} collective-permute-done((bf16[32,128,128]{2,1,0:T(8,128)(2,1)S(1)}, bf16[32,128,128]{2,1,0:T(8,128)(2,1)S(1)}, u32[]{:S(2)}, u32[]{:S(2)}) %collective-permute-start.26) | collective-permute-done | bytes 1048608 | tf_op jit(solution)/shard_map/ppermute | solution.py:28
  143.6 6.7 %shard_map.65 = (bf16[68,256,128]{2,1,0:T(8,128)(2,1)S(1)}, bf16[68,256,128]{2,1,0:T(8,128)(2,1)S(1)}, bf16[256,128]{1,0:T(8,128)(2,1)S(1)}, bf16[256,128]{1,0:T...) custom-call(s32[1040]{0:T(1024)S(1)} %constant_dynamic-update-slice_, ...), custom_call_target="tpu_custom_call", output_to_operand_aliasing={{1}: (1, {})} | custom-call | tf_op jit(solution)/shard_map/pallas_call | solution.py:205
  150.3 2.1 %collective-permute-start.33 = (bf16[256,128]{1,0:T(8,128)(2,1)S(1)}, bf16[256,128]{1,0:T(8,128)(2,1)S(1)}, u32[]{:S(2)}, u32[]{:S(2)}) collective-permute-start(bf16[256,128]{1,0:T(8,128)(2,1)S(1)} %get-tuple-element.99), channel_id=1, source_target_pairs={{24,0},{28,4},{0,8},{4,12},{8,16},{12,20},{16,24},{20,28},{25,1},{... | collective-permute-start | bytes 196616 | tf_op jit(solution)/shard_map/ppermute | solution.py:23
  152.4 2.6 %collective-permute-start.31 = (bf16[256,128]{1,0:T(8,128)(2,1)S(1)}, bf16[256,128]{1,0:T(8,128)(2,1)S(1)}, u32[]{:S(2)}, u32[]{:S(2)}) collective-permute-start(bf16[256,128]{1,0:T(8,128)(2,1)S(1)} %get-tuple-element.97), channel_id=1, source_target_pairs={{16,0},{20,4},{24,8},{28,12},{0,16},{4,20},{8,24},{12,28},{17,1},{... | collective-permute-start | bytes 196616 | tf_op jit(solution)/shard_map/ppermute | solution.py:23
  155.0 2.0 %collective-permute-done.33.refs_3_ = bf16[256,128]{1,0:T(8,128)(2,1)S(1)} collective-permute-done((bf16[256,128]{1,0:T(8,128)(2,1)S(1)}, bf16[256,128]{1,0:T(8,128)(2,1)S(1)}, u32[]{:S(2)}, u32[]{:S(2)}) %collective-permute-start.33) | collective-permute-done | bytes 65568 | tf_op jit(solution)/shard_map/ppermute | solution.py:23
  157.0 3.4 %collective-permute-start.34 = (bf16[256,128]{1,0:T(8,128)(2,1)S(1)}, bf16[256,128]{1,0:T(8,128)(2,1)S(1)}, u32[]{:S(2)}, u32[]{:S(2)}) collective-permute-start(bf16[256,128]{1,0:T(8,128)(2,1)S(1)} %get-tuple-element.101), channel_id=1, source_target_pairs={{4,0},{8,4},{12,8},{16,12},{20,16},{24,20},{28,24},{0,28},{5,1},{9... | collective-permute-start | bytes 196616 | tf_op jit(solution)/shard_map/ppermute | solution.py:23
  162.6 2.0 %shard_map.67 = (bf16[32,128,128]{2,1,0:T(8,128)(2,1)S(1)}, bf16[20,128,128]{2,1,0:T(8,128)(2,1)S(1)}, bf16[12,128,128]{2,1,0:T(8,128)(2,1)S(1)}) custom-call(bf16[4,64,128,128]{3,2,1,0:T(8,128)(2,1)} %collective-permute-done.4.tiles), custom_call_target="tpu_custom_call" | custom-call | tf_op jit(solution)/shard_map/pallas_call | solution.py:56
  164.7 2.7 %collective-permute-done.32.refs_2_ = bf16[256,128]{1,0:T(8,128)(2,1)S(1)} collective-permute-done((bf16[256,128]{1,0:T(8,128)(2,1)S(1)}, bf16[256,128]{1,0:T(8,128)(2,1)S(1)}, u32[]{:S(2)}, u32[]{:S(2)}) %collective-permute-start.32) | collective-permute-done | bytes 65568 | tf_op jit(solution)/shard_map/ppermute | solution.py:23
  170.1 4.7 %shard_map.68 = (bf16[256,8192]{1,0:T(8,128)(2,1)}, bf16[68,256,128]{2,1,0:T(8,128)(2,1)S(1)}) custom-call(s32[1040]{0:T(1024)S(1)} %constant_dynamic-update-slice_fusion.table.refs_0_, bf16[68,256,128]{2,1,0:T(8,128)(2,1)S(1)} %get-tuple-element.95.refs_1_, bf16[256,128]{1,0:T(8,128)(2,1)S(1)} %collective-permute-done.32.refs_2_, ...), custom_call_target="tpu_custom_call", output_to_operand_aliasing={{1}: (1, {})} | custom-call | tf_op jit(solution)/shard_map/pallas_call | solution.py:205
  174.8 3.9 %collective-permute-done.39.refs_4_ = bf16[20,128,128]{2,1,0:T(8,128)(2,1)S(1)} collective-permute-done((bf16[20,128,128]{2,1,0:T(8,128)(2,1)S(1)}, bf16[20,128,128]{2,1,0:T(8,128)(2,1)S(1)}, u32[]{:S(2)}, u32[]{:S(2)}) %collective-permute-start.39) | collective-permute-done | bytes 655392 | tf_op jit(solution)/shard_map/ppermute | solution.py:28
  181.0 3.5 %shard_map.69.refs_7_ = bf16[256,8192]{1,0:T(8,128)(2,1)} custom-call(s32[1040]{0:T(1024)S(1)} %constant_dynamic-update-slice_fusion.table.refs_0_, bf16[68,256,128]{2,1,0:T(8,128)(2,1)S(1)} %get-tuple-element.107.refs_1_, bf16[20,128,128]{2,1,0:T(8,128)(2,1)S(1)} %get-tuple-element.109.refs_2_, ...), custom_call_target="tpu_custom_call", output_to_operand_aliasing={{}: (9, {})} | custom-call | tf_op jit(solution)/shard_map/pallas_call | solution.py:205
  187.7 2.6 %shard_map.70 = bf16[256,8192]{1,0:T(8,128)(2,1)} custom-call(s32[1040]{0:T(1024)S(1)} %constant_dynamic-update-slice_fusion.table.refs_0_, bf16[68,256,128]{2,1,0:T(8,128)(2,1)S(1)} %get-tuple-element.107.refs_1_, bf16[12,128,128]{2,1,0:T(8,128)(2,1)S(1)} %get-tuple-element.108.refs_2_, ...), custom_call_target="tpu_custom_call", output_to_operand_aliasing={{}: (7, {})} | custom-call | tf_op jit(solution)/shard_map/pallas_call | solution.py:205
  (101 shorter events, 49.5 us)
Async XLA Ops:
  0.0 20.4 %collective-permute-start.4 = (bf16[4,64,128,128]{3,2,1,0:T(8,128)(2,1)}, bf16[4,64,128,128]{3,2,1,0:T(8,128)(2,1)}, u32[]{:S(2)}, u32[]{:S(2)}) collective-permute-start(bf16[4,64,128,128]{3,2,1,0:T(8,128)(2,1)} %tiles.9), channel_id=1, source_target_pairs={{0,1},{1,0},{2,3},{3,2},{4,5},{5,4},{6,7},{7,6},{8,9},{9,8},{10,11... | collective-permute-start | bytes 25165832 | tf_op jit(solution)/shard_map/ppermute | solution.py:28
  1.8 26.6 %collective-permute-start.5 = (bf16[32,128,128]{2,1,0:T(8,128)(2,1)S(1)}, bf16[32,128,128]{2,1,0:T(8,128)(2,1)S(1)}, u32[]{:S(2)}, u32[]{:S(2)}) collective-permute-start(bf16[32,128,128]{2,1,0:T(8,128)(2,1)S(1)} %shard_map.56.refs_6_), channel_id=1, source_target_pairs={{0,2},{1,3},{2,0},{3,1},{4,6},{5,7},{6,4},{7,5},{8,10},{9,11},{10,... | collective-permute-start | bytes 3145736 | tf_op jit(solution)/shard_map/ppermute | solution.py:28
  5.8 45.2 %collective-permute-start.6 = (bf16[32,128,128]{2,1,0:T(8,128)(2,1)S(1)}, bf16[32,128,128]{2,1,0:T(8,128)(2,1)}, u32[]{:S(2)}, u32[]{:S(2)}) collective-permute-start(bf16[32,128,128]{2,1,0:T(8,128)(2,1)S(1)} %shard_map.57.refs_7_), channel_id=1, source_target_pairs={{0,2},{1,3},{2,0},{3,1},{4,6},{5,7},{6,4},{7,5},{8,10},{9,11},{10,... | collective-permute-start | bytes 3145736 | tf_op jit(solution)/shard_map/ppermute | solution.py:28
  9.7 6.6 %collective-permute-start.2 = (bf16[256,128]{1,0:T(8,128)(2,1)S(1)}, bf16[256,128]{1,0:T(8,128)(2,1)S(1)}, u32[]{:S(2)}, u32[]{:S(2)}) collective-permute-start(bf16[256,128]{1,0:T(8,128)(2,1)S(1)} %get-tuple-element.62), channel_id=1, source_target_pairs={{24,0},{28,4},{0,8},{4,12},{8,16},{12,20},{16,24},{20,28},{25,1},{... | collective-permute-start | bytes 196616 | tf_op jit(solution)/shard_map/ppermute | solution.py:23
  11.8 7.8 %collective-permute-start = (bf16[256,128]{1,0:T(8,128)(2,1)S(1)}, bf16[256,128]{1,0:T(8,128)(2,1)S(1)}, u32[]{:S(2)}, u32[]{:S(2)}) collective-permute-start(bf16[256,128]{1,0:T(8,128)(2,1)S(1)} %get-tuple-element.60), channel_id=1, source_target_pairs={{16,0},{20,4},{24,8},{28,12},{0,16},{4,20},{8,24},{12,28},{17,1},{... | collective-permute-start | bytes 196616 | tf_op jit(solution)/shard_map/ppermute | solution.py:23
  16.3 5.9 %collective-permute-start.3 = (bf16[256,128]{1,0:T(8,128)(2,1)S(1)}, bf16[256,128]{1,0:T(8,128)(2,1)S(1)}, u32[]{:S(2)}, u32[]{:S(2)}) collective-permute-start(bf16[256,128]{1,0:T(8,128)(2,1)S(1)} %get-tuple-element.64), channel_id=1, source_target_pairs={{4,0},{8,4},{12,8},{16,12},{20,16},{24,20},{28,24},{0,28},{5,1},{9... | collective-permute-start | bytes 196616 | tf_op jit(solution)/shard_map/ppermute | solution.py:23
  19.7 7.0 %collective-permute-start.1 = (bf16[256,128]{1,0:T(8,128)(2,1)S(1)}, bf16[256,128]{1,0:T(8,128)(2,1)S(1)}, u32[]{:S(2)}, u32[]{:S(2)}) collective-permute-start(bf16[256,128]{1,0:T(8,128)(2,1)S(1)} %get-tuple-element.61), channel_id=1, source_target_pairs={{28,0},{0,4},{4,8},{8,12},{12,16},{16,20},{20,24},{24,28},{29,1},{... | collective-permute-start | bytes 196616 | tf_op jit(solution)/shard_map/ppermute | solution.py:23
  28.5 22.5 %collective-permute-start.7 = (bf16[16,128,128]{2,1,0:T(8,128)(2,1)S(1)}, bf16[16,128,128]{2,1,0:T(8,128)(2,1)S(1)}, u32[]{:S(2)}, u32[]{:S(2)}) collective-permute-start(bf16[16,128,128]{2,1,0:T(8,128)(2,1)S(1)} %get-tuple-element.126), channel_id=1, source_target_pairs={{0,1},{1,0},{2,3},{3,2},{4,5},{5,4},{6,7},{7,6},{8,9},{9,8},{10,11... | collective-permute-start | bytes 1572872 | tf_op jit(solution)/shard_map/ppermute | solution.py:28
  28.6 22.4 %collective-permute-start.8 = (bf16[16,128,128]{2,1,0:T(8,128)(2,1)S(1)}, bf16[16,128,128]{2,1,0:T(8,128)(2,1)S(1)}, u32[]{:S(2)}, u32[]{:S(2)}) collective-permute-start(bf16[16,128,128]{2,1,0:T(8,128)(2,1)S(1)} %get-tuple-element.125), channel_id=1, source_target_pairs={{0,1},{1,0},{2,3},{3,2},{4,5},{5,4},{6,7},{7,6},{8,9},{9,8},{10,11... | collective-permute-start | bytes 1572872 | tf_op jit(solution)/shard_map/ppermute | solution.py:28
  30.9 47.6 %collective-permute-start.15 = (bf16[32,128,128]{2,1,0:T(8,128)(2,1)S(1)}, bf16[32,128,128]{2,1,0:T(8,128)(2,1)S(1)}, u32[]{:S(2)}, u32[]{:S(2)}) collective-permute-start(bf16[32,128,128]{2,1,0:T(8,128)(2,1)S(1)} %get-tuple-element.76.refs_6_), channel_id=1, source_target_pairs={{0,2},{1,3},{2,0},{3,1},{4,6},{5,7},{6,4},{7,5},{8,10},{9,11},{10,... | collective-permute-start | bytes 3145736 | tf_op jit(solution)/shard_map/ppermute | solution.py:28
  52.9 43.0 %collective-permute-start.16 = (bf16[32,128,128]{2,1,0:T(8,128)(2,1)S(1)}, bf16[32,128,128]{2,1,0:T(8,128)(2,1)S(1)}, u32[]{:S(2)}, u32[]{:S(2)}) collective-permute-start(bf16[32,128,128]{2,1,0:T(8,128)(2,1)S(1)} %get-tuple-element.77.refs_7_), channel_id=1, source_target_pairs={{0,2},{1,3},{2,0},{3,1},{4,6},{5,7},{6,4},{7,5},{8,10},{9,11},{10,... | collective-permute-start | bytes 3145736 | tf_op jit(solution)/shard_map/ppermute | solution.py:28
  65.8 6.7 %collective-permute-start.13 = (bf16[256,128]{1,0:T(8,128)(2,1)S(1)}, bf16[256,128]{1,0:T(8,128)(2,1)S(1)}, u32[]{:S(2)}, u32[]{:S(2)}) collective-permute-start(bf16[256,128]{1,0:T(8,128)(2,1)S(1)} %get-tuple-element.73), channel_id=1, source_target_pairs={{24,0},{28,4},{0,8},{4,12},{8,16},{12,20},{16,24},{20,28},{25,1},{... | collective-permute-start | bytes 196616 | tf_op jit(solution)/shard_map/ppermute | solution.py:23
  67.9 8.0 %collective-permute-start.11 = (bf16[256,128]{1,0:T(8,128)(2,1)S(1)}, bf16[256,128]{1,0:T(8,128)(2,1)S(1)}, u32[]{:S(2)}, u32[]{:S(2)}) collective-permute-start(bf16[256,128]{1,0:T(8,128)(2,1)S(1)} %get-tuple-element.71), channel_id=1, source_target_pairs={{16,0},{20,4},{24,8},{28,12},{0,16},{4,20},{8,24},{12,28},{17,1},{... | collective-permute-start | bytes 196616 | tf_op jit(solution)/shard_map/ppermute | solution.py:23
  72.5 6.0 %collective-permute-start.14 = (bf16[256,128]{1,0:T(8,128)(2,1)S(1)}, bf16[256,128]{1,0:T(8,128)(2,1)S(1)}, u32[]{:S(2)}, u32[]{:S(2)}) collective-permute-start(bf16[256,128]{1,0:T(8,128)(2,1)S(1)} %get-tuple-element.75), channel_id=1, source_target_pairs={{4,0},{8,4},{12,8},{16,12},{20,16},{24,20},{28,24},{0,28},{5,1},{9... | collective-permute-start | bytes 196616 | tf_op jit(solution)/shard_map/ppermute | solution.py:23
  75.9 7.0 %collective-permute-start.12 = (bf16[256,128]{1,0:T(8,128)(2,1)S(1)}, bf16[256,128]{1,0:T(8,128)(2,1)S(1)}, u32[]{:S(2)}, u32[]{:S(2)}) collective-permute-start(bf16[256,128]{1,0:T(8,128)(2,1)S(1)} %get-tuple-element.72), channel_id=1, source_target_pairs={{28,0},{0,4},{4,8},{8,12},{12,16},{16,20},{20,24},{24,28},{29,1},{... | collective-permute-start | bytes 196616 | tf_op jit(solution)/shard_map/ppermute | solution.py:23
  83.0 12.8 %collective-permute-start.17 = (bf16[16,128,128]{2,1,0:T(8,128)(2,1)S(1)}, bf16[16,128,128]{2,1,0:T(8,128)(2,1)S(1)}, u32[]{:S(2)}, u32[]{:S(2)}) collective-permute-start(bf16[16,128,128]{2,1,0:T(8,128)(2,1)S(1)} %get-tuple-element.122), channel_id=1, source_target_pairs={{0,1},{1,0},{2,3},{3,2},{4,5},{5,4},{6,7},{7,6},{8,9},{9,8},{10,11... | collective-permute-start | bytes 1572872 | tf_op jit(solution)/shard_map/ppermute | solution.py:28
  83.1 12.8 %collective-permute-start.18 = (bf16[16,128,128]{2,1,0:T(8,128)(2,1)S(1)}, bf16[16,128,128]{2,1,0:T(8,128)(2,1)S(1)}, u32[]{:S(2)}, u32[]{:S(2)}) collective-permute-start(bf16[16,128,128]{2,1,0:T(8,128)(2,1)S(1)} %get-tuple-element.121), channel_id=1, source_target_pairs={{0,1},{1,0},{2,3},{3,2},{4,5},{5,4},{6,7},{7,6},{8,9},{9,8},{10,11... | collective-permute-start | bytes 1572872 | tf_op jit(solution)/shard_map/ppermute | solution.py:28
  85.4 32.9 %collective-permute-start.25 = (bf16[32,128,128]{2,1,0:T(8,128)(2,1)S(1)}, bf16[32,128,128]{2,1,0:T(8,128)(2,1)S(1)}, u32[]{:S(2)}, u32[]{:S(2)}) collective-permute-start(bf16[32,128,128]{2,1,0:T(8,128)(2,1)S(1)} %get-tuple-element.89.refs_6_), channel_id=1, source_target_pairs={{0,2},{1,3},{2,0},{3,1},{4,6},{5,7},{6,4},{7,5},{8,10},{9,11},{10,... | collective-permute-start | bytes 3145736 | tf_op jit(solution)/shard_map/ppermute | solution.py:28
  96.5 44.2 %collective-permute-start.26 = (bf16[32,128,128]{2,1,0:T(8,128)(2,1)S(1)}, bf16[32,128,128]{2,1,0:T(8,128)(2,1)S(1)}, u32[]{:S(2)}, u32[]{:S(2)}) collective-permute-start(bf16[32,128,128]{2,1,0:T(8,128)(2,1)S(1)} %get-tuple-element.90.refs_7_), channel_id=1, source_target_pairs={{0,2},{1,3},{2,0},{3,1},{4,6},{5,7},{6,4},{7,5},{8,10},{9,11},{10,... | collective-permute-start | bytes 3145736 | tf_op jit(solution)/shard_map/ppermute | solution.py:28
  105.4 6.7 %collective-permute-start.23 = (bf16[256,128]{1,0:T(8,128)(2,1)S(1)}, bf16[256,128]{1,0:T(8,128)(2,1)S(1)}, u32[]{:S(2)}, u32[]{:S(2)}) collective-permute-start(bf16[256,128]{1,0:T(8,128)(2,1)S(1)} %get-tuple-element.86), channel_id=1, source_target_pairs={{24,0},{28,4},{0,8},{4,12},{8,16},{12,20},{16,24},{20,28},{25,1},{... | collective-permute-start | bytes 196616 | tf_op jit(solution)/shard_map/ppermute | solution.py:23
  107.4 8.0 %collective-permute-start.21 = (bf16[256,128]{1,0:T(8,128)(2,1)S(1)}, bf16[256,128]{1,0:T(8,128)(2,1)S(1)}, u32[]{:S(2)}, u32[]{:S(2)}) collective-permute-start(bf16[256,128]{1,0:T(8,128)(2,1)S(1)} %get-tuple-element.84), channel_id=1, source_target_pairs={{16,0},{20,4},{24,8},{28,12},{0,16},{4,20},{8,24},{12,28},{17,1},{... | collective-permute-start | bytes 196616 | tf_op jit(solution)/shard_map/ppermute | solution.py:23
  112.0 6.3 %collective-permute-start.24 = (bf16[256,128]{1,0:T(8,128)(2,1)S(1)}, bf16[256,128]{1,0:T(8,128)(2,1)S(1)}, u32[]{:S(2)}, u32[]{:S(2)}) collective-permute-start(bf16[256,128]{1,0:T(8,128)(2,1)S(1)} %get-tuple-element.88), channel_id=1, source_target_pairs={{4,0},{8,4},{12,8},{16,12},{20,16},{24,20},{28,24},{0,28},{5,1},{9... | collective-permute-start | bytes 196616 | tf_op jit(solution)/shard_map/ppermute | solution.py:23
  115.4 7.0 %collective-permute-start.22 = (bf16[256,128]{1,0:T(8,128)(2,1)S(1)}, bf16[256,128]{1,0:T(8,128)(2,1)S(1)}, u32[]{:S(2)}, u32[]{:S(2)}) collective-permute-start(bf16[256,128]{1,0:T(8,128)(2,1)S(1)} %get-tuple-element.85), channel_id=1, source_target_pairs={{28,0},{0,4},{4,8},{8,12},{12,16},{16,20},{20,24},{24,28},{29,1},{... | collective-permute-start | bytes 196616 | tf_op jit(solution)/shard_map/ppermute | solution.py:23
  122.5 18.3 %collective-permute-start.27 = (bf16[16,128,128]{2,1,0:T(8,128)(2,1)S(1)}, bf16[16,128,128]{2,1,0:T(8,128)(2,1)S(1)}, u32[]{:S(2)}, u32[]{:S(2)}) collective-permute-start(bf16[16,128,128]{2,1,0:T(8,128)(2,1)S(1)} %get-tuple-element.118), channel_id=1, source_target_pairs={{0,1},{1,0},{2,3},{3,2},{4,5},{5,4},{6,7},{7,6},{8,9},{9,8},{10,11... | collective-permute-start | bytes 1572872 | tf_op jit(solution)/shard_map/ppermute | solution.py:28
  122.6 18.2 %collective-permute-start.28 = (bf16[16,128,128]{2,1,0:T(8,128)(2,1)S(1)}, bf16[16,128,128]{2,1,0:T(8,128)(2,1)S(1)}, u32[]{:S(2)}, u32[]{:S(2)}) collective-permute-start(bf16[16,128,128]{2,1,0:T(8,128)(2,1)S(1)} %get-tuple-element.117), channel_id=1, source_target_pairs={{0,1},{1,0},{2,3},{3,2},{4,5},{5,4},{6,7},{7,6},{8,9},{9,8},{10,11... | collective-permute-start | bytes 1572872 | tf_op jit(solution)/shard_map/ppermute | solution.py:28
  125.1 39.5 %collective-permute-start.35 = (bf16[32,128,128]{2,1,0:T(8,128)(2,1)S(1)}, bf16[32,128,128]{2,1,0:T(8,128)(2,1)S(1)}, u32[]{:S(2)}, u32[]{:S(2)}) collective-permute-start(bf16[32,128,128]{2,1,0:T(8,128)(2,1)S(1)} %get-tuple-element.102.refs_6_), channel_id=1, source_target_pairs={{0,2},{1,3},{2,0},{3,1},{4,6},{5,7},{6,4},{7,5},{8,10},{9,11},{10,... | collective-permute-start | bytes 3145736 | tf_op jit(solution)/shard_map/ppermute | solution.py:28
  150.3 6.7 %collective-permute-start.33 = (bf16[256,128]{1,0:T(8,128)(2,1)S(1)}, bf16[256,128]{1,0:T(8,128)(2,1)S(1)}, u32[]{:S(2)}, u32[]{:S(2)}) collective-permute-start(bf16[256,128]{1,0:T(8,128)(2,1)S(1)} %get-tuple-element.99), channel_id=1, source_target_pairs={{24,0},{28,4},{0,8},{4,12},{8,16},{12,20},{16,24},{20,28},{25,1},{... | collective-permute-start | bytes 196616 | tf_op jit(solution)/shard_map/ppermute | solution.py:23
  152.4 8.0 %collective-permute-start.31 = (bf16[256,128]{1,0:T(8,128)(2,1)S(1)}, bf16[256,128]{1,0:T(8,128)(2,1)S(1)}, u32[]{:S(2)}, u32[]{:S(2)}) collective-permute-start(bf16[256,128]{1,0:T(8,128)(2,1)S(1)} %get-tuple-element.97), channel_id=1, source_target_pairs={{16,0},{20,4},{24,8},{28,12},{0,16},{4,20},{8,24},{12,28},{17,1},{... | collective-permute-start | bytes 196616 | tf_op jit(solution)/shard_map/ppermute | solution.py:23
  157.0 7.7 %collective-permute-start.34 = (bf16[256,128]{1,0:T(8,128)(2,1)S(1)}, bf16[256,128]{1,0:T(8,128)(2,1)S(1)}, u32[]{:S(2)}, u32[]{:S(2)}) collective-permute-start(bf16[256,128]{1,0:T(8,128)(2,1)S(1)} %get-tuple-element.101), channel_id=1, source_target_pairs={{4,0},{8,4},{12,8},{16,12},{20,16},{24,20},{28,24},{0,28},{5,1},{9... | collective-permute-start | bytes 196616 | tf_op jit(solution)/shard_map/ppermute | solution.py:23
  160.4 7.0 %collective-permute-start.32 = (bf16[256,128]{1,0:T(8,128)(2,1)S(1)}, bf16[256,128]{1,0:T(8,128)(2,1)S(1)}, u32[]{:S(2)}, u32[]{:S(2)}) collective-permute-start(bf16[256,128]{1,0:T(8,128)(2,1)S(1)} %get-tuple-element.98), channel_id=1, source_target_pairs={{28,0},{0,4},{4,8},{8,12},{12,16},{16,20},{20,24},{24,28},{29,1},{... | collective-permute-start | bytes 196616 | tf_op jit(solution)/shard_map/ppermute | solution.py:23
  161.1 17.6 %collective-permute-start.39 = (bf16[20,128,128]{2,1,0:T(8,128)(2,1)S(1)}, bf16[20,128,128]{2,1,0:T(8,128)(2,1)S(1)}, u32[]{:S(2)}, u32[]{:S(2)}) collective-permute-start(bf16[20,128,128]{2,1,0:T(8,128)(2,1)S(1)} %get-tuple-element.109.refs_2_), channel_id=1, source_target_pairs={{0,2},{1,3},{2,0},{3,1},{4,6},{5,7},{6,4},{7,5},{8,10},{9,11},{10,... | collective-permute-start | bytes 1966088 | tf_op jit(solution)/shard_map/ppermute | solution.py:28
  168.0 17.9 %collective-permute-start.38 = (bf16[12,128,128]{2,1,0:T(8,128)(2,1)S(1)}, bf16[12,128,128]{2,1,0:T(8,128)(2,1)S(1)}, u32[]{:S(2)}, u32[]{:S(2)}) collective-permute-start(bf16[12,128,128]{2,1,0:T(8,128)(2,1)S(1)} %get-tuple-element.108.refs_2_), channel_id=1, source_target_pairs={{0,2},{1,3},{2,0},{3,1},{4,6},{5,7},{6,4},{7,5},{8,10},{9,11},{10,... | collective-permute-start | bytes 1179656 | tf_op jit(solution)/shard_map/ppermute | solution.py:28
  (16 other events, 74.4 us)

commit v12 on v11

--- a/solution.py
+++ b/solution.py
@@ -163,7 +163,8 @@
             return _
 
         for start, end in zip(cuts, cuts[1:]):
-            lax.fori_loop(start // group, end // group, functools.partial(work, start), None)
+            turns = (end - start) // group
+            lax.fori_loop(start // group, end // group, functools.partial(work, start), None, unroll=turns if final else 1)
         for slot, there in enumerate(outgoing):
             there[...] = result[table[sends + slot]]
         if final:

time: 191 us -> 191 us (level)
  no operation moved by 1% of the time
where the time goes in v12:
time: 191 us; the launch traced here: 190 us
  waiting for transfers between devices  79.5 us (42%)
  starting transfers between devices  55 us (29%)
  Pallas kernels  51.1 us (27%)
  local copies, waits for them, and re-layouts  3.31 us (2%)
    ppermute x28, waiting for transfers between devices, swapped(): return lax.ppermute(block, 'batch', route)  56 us
    ppermute x16, starting transfers between devices, shifted(): return lax.ppermute(block, axis, route)  35.2 us
    pallas_call x6, Pallas kernels, run_blocks(): pl.pallas_call(kernel, out_shape=out_shape, grid_spec=pltpu.PrefetchScala...  33.5 us
    ppermute x16, waiting for transfers between devices, shifted(): return lax.ppermute(block, axis, route)  23.5 us
    ppermute x28, starting transfers between devices, swapped(): return lax.ppermute(block, 'batch', route)  19.8 us
    pallas_call x9, Pallas kernels, cut(): pl.pallas_call(kernel, out_shape=[pltpu.VMEM((count, height, width), tile...  15.9 us
  transfers between devices with their start and end apart: 44, of which 22 were waited for; matrix products, arithmetic and copies ran while one was open for 2% of the time, Pallas kernels for 26%

profile of v12, /device:TPU:0, one launch (start us, length us, event | category | flops | bytes accessed | tf_op | source)
XLA Modules:
  0.0 190.1 jit_solution(15323230250692383826)
XLA Ops:
  1.8 2.6 %collective-permute-start.5 = (bf16[32,128,128]{2,1,0:T(8,128)(2,1)S(1)}, bf16[32,128,128]{2,1,0:T(8,128)(2,1)S(1)}, u32[]{:S(2)}, u32[]{:S(2)}) collective-permute-start(bf16[32,128,128]{2,1,0:T(8,128)(2,1)S(1)} %shard_map.56.refs_6_), channel_id=1, source_target_pairs={{0,2},{1,3},{2,0},{3,1},{4,6},{5,7},{6,4},{7,5},{8,10},{9,11},{10,... | collective-permute-start | bytes 3145736 | tf_op jit(solution)/shard_map/ppermute | solution.py:28
  9.7 2.1 %collective-permute-start.2 = (bf16[256,128]{1,0:T(8,128)(2,1)S(1)}, bf16[256,128]{1,0:T(8,128)(2,1)S(1)}, u32[]{:S(2)}, u32[]{:S(2)}) collective-permute-start(bf16[256,128]{1,0:T(8,128)(2,1)S(1)} %get-tuple-element.62), channel_id=1, source_target_pairs={{24,0},{28,4},{0,8},{4,12},{8,16},{12,20},{16,24},{20,28},{25,1},{... | collective-permute-start | bytes 196616 | tf_op jit(solution)/shard_map/ppermute | solution.py:23
  11.8 2.6 %collective-permute-start = (bf16[256,128]{1,0:T(8,128)(2,1)S(1)}, bf16[256,128]{1,0:T(8,128)(2,1)S(1)}, u32[]{:S(2)}, u32[]{:S(2)}) collective-permute-start(bf16[256,128]{1,0:T(8,128)(2,1)S(1)} %get-tuple-element.60), channel_id=1, source_target_pairs={{16,0},{20,4},{24,8},{28,12},{0,16},{4,20},{8,24},{12,28},{17,1},{... | collective-permute-start | bytes 196616 | tf_op jit(solution)/shard_map/ppermute | solution.py:23
  16.3 3.3 %collective-permute-start.3 = (bf16[256,128]{1,0:T(8,128)(2,1)S(1)}, bf16[256,128]{1,0:T(8,128)(2,1)S(1)}, u32[]{:S(2)}, u32[]{:S(2)}) collective-permute-start(bf16[256,128]{1,0:T(8,128)(2,1)S(1)} %get-tuple-element.64), channel_id=1, source_target_pairs={{4,0},{8,4},{12,8},{16,12},{20,16},{24,20},{28,24},{0,28},{5,1},{9... | collective-permute-start | bytes 196616 | tf_op jit(solution)/shard_map/ppermute | solution.py:23
  22.2 4.4 %collective-permute-done.1.refs_2_ = bf16[256,128]{1,0:T(8,128)(2,1)S(1)} collective-permute-done((bf16[256,128]{1,0:T(8,128)(2,1)S(1)}, bf16[256,128]{1,0:T(8,128)(2,1)S(1)}, u32[]{:S(2)}, u32[]{:S(2)}) %collective-permute-start.1) | collective-permute-done | bytes 65568 | tf_op jit(solution)/shard_map/ppermute | solution.py:23
  32.9 18.1 %collective-permute-done.6.refs_11_ = bf16[32,128,128]{2,1,0:T(8,128)(2,1)} collective-permute-done((bf16[32,128,128]{2,1,0:T(8,128)(2,1)S(1)}, bf16[32,128,128]{2,1,0:T(8,128)(2,1)}, u32[]{:S(2)}, u32[]{:S(2)}) %collective-permute-start.6) | collective-permute-done | bytes 1048608 | tf_op jit(solution)/shard_map/ppermute | solution.py:28
  55.0 10.8 %shard_map.59 = (bf16[68,256,128]{2,1,0:T(8,128)(2,1)S(1)}, bf16[256,128]{1,0:T(8,128)(2,1)S(1)}, bf16[256,128]{1,0:T(8,128)(2,1)S(1)}, bf16[256,128]{1,0:T(8,128)(2,1)S(1)}, bf16[256,128]{1,0:T(8,128)(2,1)S(1)}) custom-call(s32[1040]{0:T(1024)S(1)} %constant_dynamic-update-slice_fusion.table.refs_0_, bf16[256,8192]{1,0:T(8,128)(2,1)} %refs_1_.1, ...), custom_call_target="tpu_custom_call" | custom-call | tf_op jit(solution)/shard_map/pallas_call | solution.py:206
  65.8 2.1 %collective-permute-start.13 = (bf16[256,128]{1,0:T(8,128)(2,1)S(1)}, bf16[256,128]{1,0:T(8,128)(2,1)S(1)}, u32[]{:S(2)}, u32[]{:S(2)}) collective-permute-start(bf16[256,128]{1,0:T(8,128)(2,1)S(1)} %get-tuple-element.73), channel_id=1, source_target_pairs={{24,0},{28,4},{0,8},{4,12},{8,16},{12,20},{16,24},{20,28},{25,1},{... | collective-permute-start | bytes 196616 | tf_op jit(solution)/shard_map/ppermute | solution.py:23
  67.9 2.6 %collective-permute-start.11 = (bf16[256,128]{1,0:T(8,128)(2,1)S(1)}, bf16[256,128]{1,0:T(8,128)(2,1)S(1)}, u32[]{:S(2)}, u32[]{:S(2)}) collective-permute-start(bf16[256,128]{1,0:T(8,128)(2,1)S(1)} %get-tuple-element.71), channel_id=1, source_target_pairs={{16,0},{20,4},{24,8},{28,12},{0,16},{4,20},{8,24},{12,28},{17,1},{... | collective-permute-start | bytes 196616 | tf_op jit(solution)/shard_map/ppermute | solution.py:23
  70.5 2.0 %collective-permute-done.13.refs_3_ = bf16[256,128]{1,0:T(8,128)(2,1)S(1)} collective-permute-done((bf16[256,128]{1,0:T(8,128)(2,1)S(1)}, bf16[256,128]{1,0:T(8,128)(2,1)S(1)}, u32[]{:S(2)}, u32[]{:S(2)}) %collective-permute-start.13) | collective-permute-done | bytes 65568 | tf_op jit(solution)/shard_map/ppermute | solution.py:23
  72.5 3.4 %collective-permute-start.14 = (bf16[256,128]{1,0:T(8,128)(2,1)S(1)}, bf16[256,128]{1,0:T(8,128)(2,1)S(1)}, u32[]{:S(2)}, u32[]{:S(2)}) collective-permute-start(bf16[256,128]{1,0:T(8,128)(2,1)S(1)} %get-tuple-element.75), channel_id=1, source_target_pairs={{4,0},{8,4},{12,8},{16,12},{20,16},{24,20},{28,24},{0,28},{5,1},{9... | collective-permute-start | bytes 196616 | tf_op jit(solution)/shard_map/ppermute | solution.py:23
  78.5 4.4 %collective-permute-done.12.refs_2_ = bf16[256,128]{1,0:T(8,128)(2,1)S(1)} collective-permute-done((bf16[256,128]{1,0:T(8,128)(2,1)S(1)}, bf16[256,128]{1,0:T(8,128)(2,1)S(1)}, u32[]{:S(2)}, u32[]{:S(2)}) %collective-permute-start.12) | collective-permute-done | bytes 65568 | tf_op jit(solution)/shard_map/ppermute | solution.py:23
  87.0 8.8 %collective-permute-done.16.refs_11_ = bf16[32,128,128]{2,1,0:T(8,128)(2,1)S(1)} collective-permute-done((bf16[32,128,128]{2,1,0:T(8,128)(2,1)S(1)}, bf16[32,128,128]{2,1,0:T(8,128)(2,1)S(1)}, u32[]{:S(2)}, u32[]{:S(2)}) %collective-permute-start.16) | collective-permute-done | bytes 1048608 | tf_op jit(solution)/shard_map/ppermute | solution.py:28
  98.7 6.7 %shard_map.62 = (bf16[68,256,128]{2,1,0:T(8,128)(2,1)S(1)}, bf16[68,256,128]{2,1,0:T(8,128)(2,1)S(1)}, bf16[256,128]{1,0:T(8,128)(2,1)S(1)}, bf16[256,128]{1,0:T...) custom-call(s32[1040]{0:T(1024)S(1)} %constant_dynamic-update-slice_, ...), custom_call_target="tpu_custom_call", output_to_operand_aliasing={{1}: (1, {})} | custom-call | tf_op jit(solution)/shard_map/pallas_call | solution.py:206
  105.4 2.1 %collective-permute-start.23 = (bf16[256,128]{1,0:T(8,128)(2,1)S(1)}, bf16[256,128]{1,0:T(8,128)(2,1)S(1)}, u32[]{:S(2)}, u32[]{:S(2)}) collective-permute-start(bf16[256,128]{1,0:T(8,128)(2,1)S(1)} %get-tuple-element.86), channel_id=1, source_target_pairs={{24,0},{28,4},{0,8},{4,12},{8,16},{12,20},{16,24},{20,28},{25,1},{... | collective-permute-start | bytes 196616 | tf_op jit(solution)/shard_map/ppermute | solution.py:23
  107.4 2.6 %collective-permute-start.21 = (bf16[256,128]{1,0:T(8,128)(2,1)S(1)}, bf16[256,128]{1,0:T(8,128)(2,1)S(1)}, u32[]{:S(2)}, u32[]{:S(2)}) collective-permute-start(bf16[256,128]{1,0:T(8,128)(2,1)S(1)} %get-tuple-element.84), channel_id=1, source_target_pairs={{16,0},{20,4},{24,8},{28,12},{0,16},{4,20},{8,24},{12,28},{17,1},{... | collective-permute-start | bytes 196616 | tf_op jit(solution)/shard_map/ppermute | solution.py:23
  112.0 3.4 %collective-permute-start.24 = (bf16[256,128]{1,0:T(8,128)(2,1)S(1)}, bf16[256,128]{1,0:T(8,128)(2,1)S(1)}, u32[]{:S(2)}, u32[]{:S(2)}) collective-permute-start(bf16[256,128]{1,0:T(8,128)(2,1)S(1)} %get-tuple-element.88), channel_id=1, source_target_pairs={{4,0},{8,4},{12,8},{16,12},{20,16},{24,20},{28,24},{0,28},{5,1},{9... | collective-permute-start | bytes 196616 | tf_op jit(solution)/shard_map/ppermute | solution.py:23
  118.3 4.1 %collective-permute-done.22.refs_2_ = bf16[256,128]{1,0:T(8,128)(2,1)S(1)} collective-permute-done((bf16[256,128]{1,0:T(8,128)(2,1)S(1)}, bf16[256,128]{1,0:T(8,128)(2,1)S(1)}, u32[]{:S(2)}, u32[]{:S(2)}) %collective-permute-start.22) | collective-permute-done | bytes 65568 | tf_op jit(solution)/shard_map/ppermute | solution.py:23
  123.1 2.0 %shard_map.66 = (bf16[32,128,128]{2,1,0:T(8,128)(2,1)S(1)}, bf16[20,128,128]{2,1,0:T(8,128)(2,1)S(1)}, bf16[12,128,128]{2,1,0:T(8,128)(2,1)S(1)}) custom-call(bf16[4,64,128,128]{3,2,1,0:T(8,128)(2,1)} %tiles.9), custom_call_target="tpu_custom_call" | custom-call | tf_op jit(solution)/shard_map/pallas_call | solution.py:56
  126.7 14.1 %collective-permute-done.26.refs_11_ = bf16[32,128,128]{2,1,0:T(8,128)(2,1)S(1)} collective-permute-done((bf16[32,128,128]{2,1,0:T(8,128)(2,1)S(1)}, bf16[32,128,128]{2,1,0:T(8,128)(2,1)S(1)}, u32[]{:S(2)}, u32[]{:S(2)}) %collective-permute-start.26) | collective-permute-done | bytes 1048608 | tf_op jit(solution)/shard_map/ppermute | solution.py:28
  143.6 6.7 %shard_map.65 = (bf16[68,256,128]{2,1,0:T(8,128)(2,1)S(1)}, bf16[68,256,128]{2,1,0:T(8,128)(2,1)S(1)}, bf16[256,128]{1,0:T(8,128)(2,1)S(1)}, bf16[256,128]{1,0:T...) custom-call(s32[1040]{0:T(1024)S(1)} %constant_dynamic-update-slice_, ...), custom_call_target="tpu_custom_call", output_to_operand_aliasing={{1}: (1, {})} | custom-call | tf_op jit(solution)/shard_map/pallas_call | solution.py:206
  150.3 2.1 %collective-permute-start.33 = (bf16[256,128]{1,0:T(8,128)(2,1)S(1)}, bf16[256,128]{1,0:T(8,128)(2,1)S(1)}, u32[]{:S(2)}, u32[]{:S(2)}) collective-permute-start(bf16[256,128]{1,0:T(8,128)(2,1)S(1)} %get-tuple-element.99), channel_id=1, source_target_pairs={{24,0},{28,4},{0,8},{4,12},{8,16},{12,20},{16,24},{20,28},{25,1},{... | collective-permute-start | bytes 196616 | tf_op jit(solution)/shard_map/ppermute | solution.py:23
  152.4 2.6 %collective-permute-start.31 = (bf16[256,128]{1,0:T(8,128)(2,1)S(1)}, bf16[256,128]{1,0:T(8,128)(2,1)S(1)}, u32[]{:S(2)}, u32[]{:S(2)}) collective-permute-start(bf16[256,128]{1,0:T(8,128)(2,1)S(1)} %get-tuple-element.97), channel_id=1, source_target_pairs={{16,0},{20,4},{24,8},{28,12},{0,16},{4,20},{8,24},{12,28},{17,1},{... | collective-permute-start | bytes 196616 | tf_op jit(solution)/shard_map/ppermute | solution.py:23
  155.0 2.0 %collective-permute-done.33.refs_3_ = bf16[256,128]{1,0:T(8,128)(2,1)S(1)} collective-permute-done((bf16[256,128]{1,0:T(8,128)(2,1)S(1)}, bf16[256,128]{1,0:T(8,128)(2,1)S(1)}, u32[]{:S(2)}, u32[]{:S(2)}) %collective-permute-start.33) | collective-permute-done | bytes 65568 | tf_op jit(solution)/shard_map/ppermute | solution.py:23
  157.0 3.4 %collective-permute-start.34 = (bf16[256,128]{1,0:T(8,128)(2,1)S(1)}, bf16[256,128]{1,0:T(8,128)(2,1)S(1)}, u32[]{:S(2)}, u32[]{:S(2)}) collective-permute-start(bf16[256,128]{1,0:T(8,128)(2,1)S(1)} %get-tuple-element.101), channel_id=1, source_target_pairs={{4,0},{8,4},{12,8},{16,12},{20,16},{24,20},{28,24},{0,28},{5,1},{9... | collective-permute-start | bytes 196616 | tf_op jit(solution)/shard_map/ppermute | solution.py:23
  162.6 2.0 %shard_map.67 = (bf16[32,128,128]{2,1,0:T(8,128)(2,1)S(1)}, bf16[20,128,128]{2,1,0:T(8,128)(2,1)S(1)}, bf16[12,128,128]{2,1,0:T(8,128)(2,1)S(1)}) custom-call(bf16[4,64,128,128]{3,2,1,0:T(8,128)(2,1)} %collective-permute-done.4.tiles), custom_call_target="tpu_custom_call" | custom-call | tf_op jit(solution)/shard_map/pallas_call | solution.py:56
  164.7 2.7 %collective-permute-done.32.refs_2_ = bf16[256,128]{1,0:T(8,128)(2,1)S(1)} collective-permute-done((bf16[256,128]{1,0:T(8,128)(2,1)S(1)}, bf16[256,128]{1,0:T(8,128)(2,1)S(1)}, u32[]{:S(2)}, u32[]{:S(2)}) %collective-permute-start.32) | collective-permute-done | bytes 65568 | tf_op jit(solution)/shard_map/ppermute | solution.py:23
  170.1 4.2 %shard_map.68 = (bf16[256,8192]{1,0:T(8,128)(2,1)}, bf16[68,256,128]{2,1,0:T(8,128)(2,1)S(1)}) custom-call(s32[1040]{0:T(1024)S(1)} %constant_dynamic-update-slice_fusion.table.refs_0_, bf16[68,256,128]{2,1,0:T(8,128)(2,1)S(1)} %get-tuple-element.95.refs_1_, bf16[256,128]{1,0:T(8,128)(2,1)S(1)} %collective-permute-done.32.refs_2_, ...), custom_call_target="tpu_custom_call", output_to_operand_aliasing={{1}: (1, {})} | custom-call | tf_op jit(solution)/shard_map/pallas_call | solution.py:206
  174.3 4.5 %collective-permute-done.39.refs_4_ = bf16[20,128,128]{2,1,0:T(8,128)(2,1)S(1)} collective-permute-done((bf16[20,128,128]{2,1,0:T(8,128)(2,1)S(1)}, bf16[20,128,128]{2,1,0:T(8,128)(2,1)S(1)}, u32[]{:S(2)}, u32[]{:S(2)}) %collective-permute-start.39) | collective-permute-done | bytes 655392 | tf_op jit(solution)/shard_map/ppermute | solution.py:28
  181.0 2.9 %shard_map.69.refs_7_ = bf16[256,8192]{1,0:T(8,128)(2,1)} custom-call(s32[1040]{0:T(1024)S(1)} %constant_dynamic-update-slice_fusion.table.refs_0_, bf16[68,256,128]{2,1,0:T(8,128)(2,1)S(1)} %get-tuple-element.107.refs_1_, bf16[20,128,128]{2,1,0:T(8,128)(2,1)S(1)} %get-tuple-element.109.refs_2_, ...), custom_call_target="tpu_custom_call", output_to_operand_aliasing={{}: (9, {})} | custom-call | tf_op jit(solution)/shard_map/pallas_call | solution.py:206
  183.9 2.0 %collective-permute-done.38.refs_4_ = bf16[12,128,128]{2,1,0:T(8,128)(2,1)S(1)} collective-permute-done((bf16[12,128,128]{2,1,0:T(8,128)(2,1)S(1)}, bf16[12,128,128]{2,1,0:T(8,128)(2,1)S(1)}, u32[]{:S(2)}, u32[]{:S(2)}) %collective-permute-start.38) | collective-permute-done | bytes 393248 | tf_op jit(solution)/shard_map/ppermute | solution.py:28
  187.7 2.3 %shard_map.70 = bf16[256,8192]{1,0:T(8,128)(2,1)} custom-call(s32[1040]{0:T(1024)S(1)} %constant_dynamic-update-slice_fusion.table.refs_0_, bf16[68,256,128]{2,1,0:T(8,128)(2,1)S(1)} %get-tuple-element.107.refs_1_, bf16[12,128,128]{2,1,0:T(8,128)(2,1)S(1)} %get-tuple-element.108.refs_2_, ...), custom_call_target="tpu_custom_call", output_to_operand_aliasing={{}: (7, {})} | custom-call | tf_op jit(solution)/shard_map/pallas_call | solution.py:206
  (101 shorter events, 50.1 us)
Async XLA Ops:
  0.0 20.4 %collective-permute-start.4 = (bf16[4,64,128,128]{3,2,1,0:T(8,128)(2,1)}, bf16[4,64,128,128]{3,2,1,0:T(8,128)(2,1)}, u32[]{:S(2)}, u32[]{:S(2)}) collective-permute-start(bf16[4,64,128,128]{3,2,1,0:T(8,128)(2,1)} %tiles.9), channel_id=1, source_target_pairs={{0,1},{1,0},{2,3},{3,2},{4,5},{5,4},{6,7},{7,6},{8,9},{9,8},{10,11... | collective-permute-start | bytes 25165832 | tf_op jit(solution)/shard_map/ppermute | solution.py:28
  1.8 26.6 %collective-permute-start.5 = (bf16[32,128,128]{2,1,0:T(8,128)(2,1)S(1)}, bf16[32,128,128]{2,1,0:T(8,128)(2,1)S(1)}, u32[]{:S(2)}, u32[]{:S(2)}) collective-permute-start(bf16[32,128,128]{2,1,0:T(8,128)(2,1)S(1)} %shard_map.56.refs_6_), channel_id=1, source_target_pairs={{0,2},{1,3},{2,0},{3,1},{4,6},{5,7},{6,4},{7,5},{8,10},{9,11},{10,... | collective-permute-start | bytes 3145736 | tf_op jit(solution)/shard_map/ppermute | solution.py:28
  5.8 45.2 %collective-permute-start.6 = (bf16[32,128,128]{2,1,0:T(8,128)(2,1)S(1)}, bf16[32,128,128]{2,1,0:T(8,128)(2,1)}, u32[]{:S(2)}, u32[]{:S(2)}) collective-permute-start(bf16[32,128,128]{2,1,0:T(8,128)(2,1)S(1)} %shard_map.57.refs_7_), channel_id=1, source_target_pairs={{0,2},{1,3},{2,0},{3,1},{4,6},{5,7},{6,4},{7,5},{8,10},{9,11},{10,... | collective-permute-start | bytes 3145736 | tf_op jit(solution)/shard_map/ppermute | solution.py:28
  9.7 6.6 %collective-permute-start.2 = (bf16[256,128]{1,0:T(8,128)(2,1)S(1)}, bf16[256,128]{1,0:T(8,128)(2,1)S(1)}, u32[]{:S(2)}, u32[]{:S(2)}) collective-permute-start(bf16[256,128]{1,0:T(8,128)(2,1)S(1)} %get-tuple-element.62), channel_id=1, source_target_pairs={{24,0},{28,4},{0,8},{4,12},{8,16},{12,20},{16,24},{20,28},{25,1},{... | collective-permute-start | bytes 196616 | tf_op jit(solution)/shard_map/ppermute | solution.py:23
  11.8 7.8 %collective-permute-start = (bf16[256,128]{1,0:T(8,128)(2,1)S(1)}, bf16[256,128]{1,0:T(8,128)(2,1)S(1)}, u32[]{:S(2)}, u32[]{:S(2)}) collective-permute-start(bf16[256,128]{1,0:T(8,128)(2,1)S(1)} %get-tuple-element.60), channel_id=1, source_target_pairs={{16,0},{20,4},{24,8},{28,12},{0,16},{4,20},{8,24},{12,28},{17,1},{... | collective-permute-start | bytes 196616 | tf_op jit(solution)/shard_map/ppermute | solution.py:23
  16.3 5.9 %collective-permute-start.3 = (bf16[256,128]{1,0:T(8,128)(2,1)S(1)}, bf16[256,128]{1,0:T(8,128)(2,1)S(1)}, u32[]{:S(2)}, u32[]{:S(2)}) collective-permute-start(bf16[256,128]{1,0:T(8,128)(2,1)S(1)} %get-tuple-element.64), channel_id=1, source_target_pairs={{4,0},{8,4},{12,8},{16,12},{20,16},{24,20},{28,24},{0,28},{5,1},{9... | collective-permute-start | bytes 196616 | tf_op jit(solution)/shard_map/ppermute | solution.py:23
  19.7 7.0 %collective-permute-start.1 = (bf16[256,128]{1,0:T(8,128)(2,1)S(1)}, bf16[256,128]{1,0:T(8,128)(2,1)S(1)}, u32[]{:S(2)}, u32[]{:S(2)}) collective-permute-start(bf16[256,128]{1,0:T(8,128)(2,1)S(1)} %get-tuple-element.61), channel_id=1, source_target_pairs={{28,0},{0,4},{4,8},{8,12},{12,16},{16,20},{20,24},{24,28},{29,1},{... | collective-permute-start | bytes 196616 | tf_op jit(solution)/shard_map/ppermute | solution.py:23
  28.5 22.5 %collective-permute-start.7 = (bf16[16,128,128]{2,1,0:T(8,128)(2,1)S(1)}, bf16[16,128,128]{2,1,0:T(8,128)(2,1)S(1)}, u32[]{:S(2)}, u32[]{:S(2)}) collective-permute-start(bf16[16,128,128]{2,1,0:T(8,128)(2,1)S(1)} %get-tuple-element.126), channel_id=1, source_target_pairs={{0,1},{1,0},{2,3},{3,2},{4,5},{5,4},{6,7},{7,6},{8,9},{9,8},{10,11... | collective-permute-start | bytes 1572872 | tf_op jit(solution)/shard_map/ppermute | solution.py:28
  28.6 22.4 %collective-permute-start.8 = (bf16[16,128,128]{2,1,0:T(8,128)(2,1)S(1)}, bf16[16,128,128]{2,1,0:T(8,128)(2,1)S(1)}, u32[]{:S(2)}, u32[]{:S(2)}) collective-permute-start(bf16[16,128,128]{2,1,0:T(8,128)(2,1)S(1)} %get-tuple-element.125), channel_id=1, source_target_pairs={{0,1},{1,0},{2,3},{3,2},{4,5},{5,4},{6,7},{7,6},{8,9},{9,8},{10,11... | collective-permute-start | bytes 1572872 | tf_op jit(solution)/shard_map/ppermute | solution.py:28
  30.9 47.6 %collective-permute-start.15 = (bf16[32,128,128]{2,1,0:T(8,128)(2,1)S(1)}, bf16[32,128,128]{2,1,0:T(8,128)(2,1)S(1)}, u32[]{:S(2)}, u32[]{:S(2)}) collective-permute-start(bf16[32,128,128]{2,1,0:T(8,128)(2,1)S(1)} %get-tuple-element.76.refs_6_), channel_id=1, source_target_pairs={{0,2},{1,3},{2,0},{3,1},{4,6},{5,7},{6,4},{7,5},{8,10},{9,11},{10,... | collective-permute-start | bytes 3145736 | tf_op jit(solution)/shard_map/ppermute | solution.py:28
  52.9 43.0 %collective-permute-start.16 = (bf16[32,128,128]{2,1,0:T(8,128)(2,1)S(1)}, bf16[32,128,128]{2,1,0:T(8,128)(2,1)S(1)}, u32[]{:S(2)}, u32[]{:S(2)}) collective-permute-start(bf16[32,128,128]{2,1,0:T(8,128)(2,1)S(1)} %get-tuple-element.77.refs_7_), channel_id=1, source_target_pairs={{0,2},{1,3},{2,0},{3,1},{4,6},{5,7},{6,4},{7,5},{8,10},{9,11},{10,... | collective-permute-start | bytes 3145736 | tf_op jit(solution)/shard_map/ppermute | solution.py:28
  65.8 6.7 %collective-permute-start.13 = (bf16[256,128]{1,0:T(8,128)(2,1)S(1)}, bf16[256,128]{1,0:T(8,128)(2,1)S(1)}, u32[]{:S(2)}, u32[]{:S(2)}) collective-permute-start(bf16[256,128]{1,0:T(8,128)(2,1)S(1)} %get-tuple-element.73), channel_id=1, source_target_pairs={{24,0},{28,4},{0,8},{4,12},{8,16},{12,20},{16,24},{20,28},{25,1},{... | collective-permute-start | bytes 196616 | tf_op jit(solution)/shard_map/ppermute | solution.py:23
  67.9 8.0 %collective-permute-start.11 = (bf16[256,128]{1,0:T(8,128)(2,1)S(1)}, bf16[256,128]{1,0:T(8,128)(2,1)S(1)}, u32[]{:S(2)}, u32[]{:S(2)}) collective-permute-start(bf16[256,128]{1,0:T(8,128)(2,1)S(1)} %get-tuple-element.71), channel_id=1, source_target_pairs={{16,0},{20,4},{24,8},{28,12},{0,16},{4,20},{8,24},{12,28},{17,1},{... | collective-permute-start | bytes 196616 | tf_op jit(solution)/shard_map/ppermute | solution.py:23
  72.5 6.0 %collective-permute-start.14 = (bf16[256,128]{1,0:T(8,128)(2,1)S(1)}, bf16[256,128]{1,0:T(8,128)(2,1)S(1)}, u32[]{:S(2)}, u32[]{:S(2)}) collective-permute-start(bf16[256,128]{1,0:T(8,128)(2,1)S(1)} %get-tuple-element.75), channel_id=1, source_target_pairs={{4,0},{8,4},{12,8},{16,12},{20,16},{24,20},{28,24},{0,28},{5,1},{9... | collective-permute-start | bytes 196616 | tf_op jit(solution)/shard_map/ppermute | solution.py:23
  75.9 7.0 %collective-permute-start.12 = (bf16[256,128]{1,0:T(8,128)(2,1)S(1)}, bf16[256,128]{1,0:T(8,128)(2,1)S(1)}, u32[]{:S(2)}, u32[]{:S(2)}) collective-permute-start(bf16[256,128]{1,0:T(8,128)(2,1)S(1)} %get-tuple-element.72), channel_id=1, source_target_pairs={{28,0},{0,4},{4,8},{8,12},{12,16},{16,20},{20,24},{24,28},{29,1},{... | collective-permute-start | bytes 196616 | tf_op jit(solution)/shard_map/ppermute | solution.py:23
  83.0 12.8 %collective-permute-start.17 = (bf16[16,128,128]{2,1,0:T(8,128)(2,1)S(1)}, bf16[16,128,128]{2,1,0:T(8,128)(2,1)S(1)}, u32[]{:S(2)}, u32[]{:S(2)}) collective-permute-start(bf16[16,128,128]{2,1,0:T(8,128)(2,1)S(1)} %get-tuple-element.122), channel_id=1, source_target_pairs={{0,1},{1,0},{2,3},{3,2},{4,5},{5,4},{6,7},{7,6},{8,9},{9,8},{10,11... | collective-permute-start | bytes 1572872 | tf_op jit(solution)/shard_map/ppermute | solution.py:28
  83.1 12.8 %collective-permute-start.18 = (bf16[16,128,128]{2,1,0:T(8,128)(2,1)S(1)}, bf16[16,128,128]{2,1,0:T(8,128)(2,1)S(1)}, u32[]{:S(2)}, u32[]{:S(2)}) collective-permute-start(bf16[16,128,128]{2,1,0:T(8,128)(2,1)S(1)} %get-tuple-element.121), channel_id=1, source_target_pairs={{0,1},{1,0},{2,3},{3,2},{4,5},{5,4},{6,7},{7,6},{8,9},{9,8},{10,11... | collective-permute-start | bytes 1572872 | tf_op jit(solution)/shard_map/ppermute | solution.py:28
  85.4 32.9 %collective-permute-start.25 = (bf16[32,128,128]{2,1,0:T(8,128)(2,1)S(1)}, bf16[32,128,128]{2,1,0:T(8,128)(2,1)S(1)}, u32[]{:S(2)}, u32[]{:S(2)}) collective-permute-start(bf16[32,128,128]{2,1,0:T(8,128)(2,1)S(1)} %get-tuple-element.89.refs_6_), channel_id=1, source_target_pairs={{0,2},{1,3},{2,0},{3,1},{4,6},{5,7},{6,4},{7,5},{8,10},{9,11},{10,... | collective-permute-start | bytes 3145736 | tf_op jit(solution)/shard_map/ppermute | solution.py:28
  96.5 44.2 %collective-permute-start.26 = (bf16[32,128,128]{2,1,0:T(8,128)(2,1)S(1)}, bf16[32,128,128]{2,1,0:T(8,128)(2,1)S(1)}, u32[]{:S(2)}, u32[]{:S(2)}) collective-permute-start(bf16[32,128,128]{2,1,0:T(8,128)(2,1)S(1)} %get-tuple-element.90.refs_7_), channel_id=1, source_target_pairs={{0,2},{1,3},{2,0},{3,1},{4,6},{5,7},{6,4},{7,5},{8,10},{9,11},{10,... | collective-permute-start | bytes 3145736 | tf_op jit(solution)/shard_map/ppermute | solution.py:28
  105.4 6.7 %collective-permute-start.23 = (bf16[256,128]{1,0:T(8,128)(2,1)S(1)}, bf16[256,128]{1,0:T(8,128)(2,1)S(1)}, u32[]{:S(2)}, u32[]{:S(2)}) collective-permute-start(bf16[256,128]{1,0:T(8,128)(2,1)S(1)} %get-tuple-element.86), channel_id=1, source_target_pairs={{24,0},{28,4},{0,8},{4,12},{8,16},{12,20},{16,24},{20,28},{25,1},{... | collective-permute-start | bytes 196616 | tf_op jit(solution)/shard_map/ppermute | solution.py:23
  107.4 8.0 %collective-permute-start.21 = (bf16[256,128]{1,0:T(8,128)(2,1)S(1)}, bf16[256,128]{1,0:T(8,128)(2,1)S(1)}, u32[]{:S(2)}, u32[]{:S(2)}) collective-permute-start(bf16[256,128]{1,0:T(8,128)(2,1)S(1)} %get-tuple-element.84), channel_id=1, source_target_pairs={{16,0},{20,4},{24,8},{28,12},{0,16},{4,20},{8,24},{12,28},{17,1},{... | collective-permute-start | bytes 196616 | tf_op jit(solution)/shard_map/ppermute | solution.py:23
  112.0 6.3 %collective-permute-start.24 = (bf16[256,128]{1,0:T(8,128)(2,1)S(1)}, bf16[256,128]{1,0:T(8,128)(2,1)S(1)}, u32[]{:S(2)}, u32[]{:S(2)}) collective-permute-start(bf16[256,128]{1,0:T(8,128)(2,1)S(1)} %get-tuple-element.88), channel_id=1, source_target_pairs={{4,0},{8,4},{12,8},{16,12},{20,16},{24,20},{28,24},{0,28},{5,1},{9... | collective-permute-start | bytes 196616 | tf_op jit(solution)/shard_map/ppermute | solution.py:23
  115.4 7.0 %collective-permute-start.22 = (bf16[256,128]{1,0:T(8,128)(2,1)S(1)}, bf16[256,128]{1,0:T(8,128)(2,1)S(1)}, u32[]{:S(2)}, u32[]{:S(2)}) collective-permute-start(bf16[256,128]{1,0:T(8,128)(2,1)S(1)} %get-tuple-element.85), channel_id=1, source_target_pairs={{28,0},{0,4},{4,8},{8,12},{12,16},{16,20},{20,24},{24,28},{29,1},{... | collective-permute-start | bytes 196616 | tf_op jit(solution)/shard_map/ppermute | solution.py:23
  122.5 18.3 %collective-permute-start.27 = (bf16[16,128,128]{2,1,0:T(8,128)(2,1)S(1)}, bf16[16,128,128]{2,1,0:T(8,128)(2,1)S(1)}, u32[]{:S(2)}, u32[]{:S(2)}) collective-permute-start(bf16[16,128,128]{2,1,0:T(8,128)(2,1)S(1)} %get-tuple-element.118), channel_id=1, source_target_pairs={{0,1},{1,0},{2,3},{3,2},{4,5},{5,4},{6,7},{7,6},{8,9},{9,8},{10,11... | collective-permute-start | bytes 1572872 | tf_op jit(solution)/shard_map/ppermute | solution.py:28
  122.6 18.2 %collective-permute-start.28 = (bf16[16,128,128]{2,1,0:T(8,128)(2,1)S(1)}, bf16[16,128,128]{2,1,0:T(8,128)(2,1)S(1)}, u32[]{:S(2)}, u32[]{:S(2)}) collective-permute-start(bf16[16,128,128]{2,1,0:T(8,128)(2,1)S(1)} %get-tuple-element.117), channel_id=1, source_target_pairs={{0,1},{1,0},{2,3},{3,2},{4,5},{5,4},{6,7},{7,6},{8,9},{9,8},{10,11... | collective-permute-start | bytes 1572872 | tf_op jit(solution)/shard_map/ppermute | solution.py:28
  125.1 39.5 %collective-permute-start.35 = (bf16[32,128,128]{2,1,0:T(8,128)(2,1)S(1)}, bf16[32,128,128]{2,1,0:T(8,128)(2,1)S(1)}, u32[]{:S(2)}, u32[]{:S(2)}) collective-permute-start(bf16[32,128,128]{2,1,0:T(8,128)(2,1)S(1)} %get-tuple-element.102.refs_6_), channel_id=1, source_target_pairs={{0,2},{1,3},{2,0},{3,1},{4,6},{5,7},{6,4},{7,5},{8,10},{9,11},{10,... | collective-permute-start | bytes 3145736 | tf_op jit(solution)/shard_map/ppermute | solution.py:28
  150.3 6.7 %collective-permute-start.33 = (bf16[256,128]{1,0:T(8,128)(2,1)S(1)}, bf16[256,128]{1,0:T(8,128)(2,1)S(1)}, u32[]{:S(2)}, u32[]{:S(2)}) collective-permute-start(bf16[256,128]{1,0:T(8,128)(2,1)S(1)} %get-tuple-element.99), channel_id=1, source_target_pairs={{24,0},{28,4},{0,8},{4,12},{8,16},{12,20},{16,24},{20,28},{25,1},{... | collective-permute-start | bytes 196616 | tf_op jit(solution)/shard_map/ppermute | solution.py:23
  152.4 8.0 %collective-permute-start.31 = (bf16[256,128]{1,0:T(8,128)(2,1)S(1)}, bf16[256,128]{1,0:T(8,128)(2,1)S(1)}, u32[]{:S(2)}, u32[]{:S(2)}) collective-permute-start(bf16[256,128]{1,0:T(8,128)(2,1)S(1)} %get-tuple-element.97), channel_id=1, source_target_pairs={{16,0},{20,4},{24,8},{28,12},{0,16},{4,20},{8,24},{12,28},{17,1},{... | collective-permute-start | bytes 196616 | tf_op jit(solution)/shard_map/ppermute | solution.py:23
  157.0 7.7 %collective-permute-start.34 = (bf16[256,128]{1,0:T(8,128)(2,1)S(1)}, bf16[256,128]{1,0:T(8,128)(2,1)S(1)}, u32[]{:S(2)}, u32[]{:S(2)}) collective-permute-start(bf16[256,128]{1,0:T(8,128)(2,1)S(1)} %get-tuple-element.101), channel_id=1, source_target_pairs={{4,0},{8,4},{12,8},{16,12},{20,16},{24,20},{28,24},{0,28},{5,1},{9... | collective-permute-start | bytes 196616 | tf_op jit(solution)/shard_map/ppermute | solution.py:23
  160.4 7.0 %collective-permute-start.32 = (bf16[256,128]{1,0:T(8,128)(2,1)S(1)}, bf16[256,128]{1,0:T(8,128)(2,1)S(1)}, u32[]{:S(2)}, u32[]{:S(2)}) collective-permute-start(bf16[256,128]{1,0:T(8,128)(2,1)S(1)} %get-tuple-element.98), channel_id=1, source_target_pairs={{28,0},{0,4},{4,8},{8,12},{12,16},{16,20},{20,24},{24,28},{29,1},{... | collective-permute-start | bytes 196616 | tf_op jit(solution)/shard_map/ppermute | solution.py:23
  161.1 17.6 %collective-permute-start.39 = (bf16[20,128,128]{2,1,0:T(8,128)(2,1)S(1)}, bf16[20,128,128]{2,1,0:T(8,128)(2,1)S(1)}, u32[]{:S(2)}, u32[]{:S(2)}) collective-permute-start(bf16[20,128,128]{2,1,0:T(8,128)(2,1)S(1)} %get-tuple-element.109.refs_2_), channel_id=1, source_target_pairs={{0,2},{1,3},{2,0},{3,1},{4,6},{5,7},{6,4},{7,5},{8,10},{9,11},{10,... | collective-permute-start | bytes 1966088 | tf_op jit(solution)/shard_map/ppermute | solution.py:28
  168.0 17.9 %collective-permute-start.38 = (bf16[12,128,128]{2,1,0:T(8,128)(2,1)S(1)}, bf16[12,128,128]{2,1,0:T(8,128)(2,1)S(1)}, u32[]{:S(2)}, u32[]{:S(2)}) collective-permute-start(bf16[12,128,128]{2,1,0:T(8,128)(2,1)S(1)} %get-tuple-element.108.refs_2_), channel_id=1, source_target_pairs={{0,2},{1,3},{2,0},{3,1},{4,6},{5,7},{6,4},{7,5},{8,10},{9,11},{10,... | collective-permute-start | bytes 1179656 | tf_op jit(solution)/shard_map/ppermute | solution.py:28
  (16 other events, 74.1 us)

commit v13 on v12

--- a/solution.py
+++ b/solution.py
@@ -242,7 +242,8 @@
                 )
 
     last = layer_count - 1
-    shares = [(0, (8, 8), ((4, 4), (4, 4))), (1, (8, 8), ((4, 4), (4, 4))), (2, (8, 8), ((4, 4), (4, 4))), (last, (8,), ((4, 4),)), (last, (5,), ((2, 2, 1),)), (last, (3,), ((3,),))]
+    shares = [(layer, (8, 8), ((4, 4), (4, 4))) for layer in range(last)]
+    shares += [(last, (9,), ((4, 4, 1),)), (last, (5,), ((2, 1, 1, 1),)), (last, (2,), ((2,),))]
 
     moves = {layer: [] for layer in range(layer_count)}
     for layer, sizes, _ in shares:

time: 191 us -> 190 us (level)
    ppermute x28 -> x30, starting transfers between devices: 19.8 us -> 20.5 us  [swapped(): return lax.ppermute(block, 'batch', route)]
    ppermute x28 -> x30, waiting for transfers between devices: 56 us -> 56.2 us  [swapped(): return lax.ppermute(block, 'batch', route)]
  transfers between devices with their start and end apart: 44 -> 46, of which waited for: 22 -> 25; matrix products, arithmetic and copies ran while one was open for 2% -> 2% of each run, Pallas kernels for 26% -> 26%
where the time goes in v13:
time: 190 us; the launch traced here: 189 us
  waiting for transfers between devices  78.3 us (41%)
  starting transfers between devices  55.7 us (29%)
  Pallas kernels  50.7 us (27%)
  local copies, waits for them, and re-layouts  3.32 us (2%)
    ppermute x30, waiting for transfers between devices, swapped(): return lax.ppermute(block, 'batch', route)  56.2 us
    ppermute x16, starting transfers between devices, shifted(): return lax.ppermute(block, axis, route)  35.2 us
    pallas_call x6, Pallas kernels, run_blocks(): pl.pallas_call(kernel, out_shape=out_shape, grid_spec=pltpu.PrefetchScala...  33.6 us
    ppermute x16, waiting for transfers between devices, shifted(): return lax.ppermute(block, axis, route)  22.1 us
    ppermute x30, starting transfers between devices, swapped(): return lax.ppermute(block, 'batch', route)  20.5 us
    pallas_call x9, Pallas kernels, cut(): pl.pallas_call(kernel, out_shape=[pltpu.VMEM((count, height, width), tile...  15.6 us
  transfers between devices with their start and end apart: 46, of which 25 were waited for; matrix products, arithmetic and copies ran while one was open for 2% of the time, Pallas kernels for 26%

profile of v13, /device:TPU:0, one launch (start us, length us, event | category | flops | bytes accessed | tf_op | source)
XLA Modules:
  0.0 189.4 jit_solution(16594347232470121211)
XLA Ops:
  1.8 2.6 %collective-permute-start.5 = (bf16[32,128,128]{2,1,0:T(8,128)(2,1)S(1)}, bf16[32,128,128]{2,1,0:T(8,128)(2,1)S(1)}, u32[]{:S(2)}, u32[]{:S(2)}) collective-permute-start(bf16[32,128,128]{2,1,0:T(8,128)(2,1)S(1)} %shard_map.56.refs_6_), channel_id=1, source_target_pairs={{0,2},{1,3},{2,0},{3,1},{4,6},{5,7},{6,4},{7,5},{8,10},{9,11},{10,... | collective-permute-start | bytes 3145736 | tf_op jit(solution)/shard_map/ppermute | solution.py:28
  9.7 2.1 %collective-permute-start.2 = (bf16[256,128]{1,0:T(8,128)(2,1)S(1)}, bf16[256,128]{1,0:T(8,128)(2,1)S(1)}, u32[]{:S(2)}, u32[]{:S(2)}) collective-permute-start(bf16[256,128]{1,0:T(8,128)(2,1)S(1)} %get-tuple-element.62), channel_id=1, source_target_pairs={{24,0},{28,4},{0,8},{4,12},{8,16},{12,20},{16,24},{20,28},{25,1},{... | collective-permute-start | bytes 196616 | tf_op jit(solution)/shard_map/ppermute | solution.py:23
  11.8 2.6 %collective-permute-start = (bf16[256,128]{1,0:T(8,128)(2,1)S(1)}, bf16[256,128]{1,0:T(8,128)(2,1)S(1)}, u32[]{:S(2)}, u32[]{:S(2)}) collective-permute-start(bf16[256,128]{1,0:T(8,128)(2,1)S(1)} %get-tuple-element.60), channel_id=1, source_target_pairs={{16,0},{20,4},{24,8},{28,12},{0,16},{4,20},{8,24},{12,28},{17,1},{... | collective-permute-start | bytes 196616 | tf_op jit(solution)/shard_map/ppermute | solution.py:23
  16.3 3.3 %collective-permute-start.3 = (bf16[256,128]{1,0:T(8,128)(2,1)S(1)}, bf16[256,128]{1,0:T(8,128)(2,1)S(1)}, u32[]{:S(2)}, u32[]{:S(2)}) collective-permute-start(bf16[256,128]{1,0:T(8,128)(2,1)S(1)} %get-tuple-element.64), channel_id=1, source_target_pairs={{4,0},{8,4},{12,8},{16,12},{20,16},{24,20},{28,24},{0,28},{5,1},{9... | collective-permute-start | bytes 196616 | tf_op jit(solution)/shard_map/ppermute | solution.py:23
  22.2 4.4 %collective-permute-done.1.refs_2_ = bf16[256,128]{1,0:T(8,128)(2,1)S(1)} collective-permute-done((bf16[256,128]{1,0:T(8,128)(2,1)S(1)}, bf16[256,128]{1,0:T(8,128)(2,1)S(1)}, u32[]{:S(2)}, u32[]{:S(2)}) %collective-permute-start.1) | collective-permute-done | bytes 65568 | tf_op jit(solution)/shard_map/ppermute | solution.py:23
  30.9 2.0 %collective-permute-start.15 = (bf16[32,128,128]{2,1,0:T(8,128)(2,1)S(1)}, bf16[32,128,128]{2,1,0:T(8,128)(2,1)S(1)}, u32[]{:S(2)}, u32[]{:S(2)}) collective-permute-start(bf16[32,128,128]{2,1,0:T(8,128)(2,1)S(1)} %get-tuple-element.76.refs_6_), channel_id=1, source_target_pairs={{0,2},{1,3},{2,0},{3,1},{4,6},{5,7},{6,4},{7,5},{8,10},{9,11},{10,... | collective-permute-start | bytes 3145736 | tf_op jit(solution)/shard_map/ppermute | solution.py:28
  32.9 18.1 %collective-permute-done.6.refs_11_ = bf16[32,128,128]{2,1,0:T(8,128)(2,1)} collective-permute-done((bf16[32,128,128]{2,1,0:T(8,128)(2,1)S(1)}, bf16[32,128,128]{2,1,0:T(8,128)(2,1)}, u32[]{:S(2)}, u32[]{:S(2)}) %collective-permute-start.6) | collective-permute-done | bytes 1048608 | tf_op jit(solution)/shard_map/ppermute | solution.py:28
  52.9 1.9 %collective-permute-start.16 = (bf16[32,128,128]{2,1,0:T(8,128)(2,1)S(1)}, bf16[32,128,128]{2,1,0:T(8,128)(2,1)S(1)}, u32[]{:S(2)}, u32[]{:S(2)}) collective-permute-start(bf16[32,128,128]{2,1,0:T(8,128)(2,1)S(1)} %get-tuple-element.77.refs_7_), channel_id=1, source_target_pairs={{0,2},{1,3},{2,0},{3,1},{4,6},{5,7},{6,4},{7,5},{8,10},{9,11},{10,... | collective-permute-start | bytes 3145736 | tf_op jit(solution)/shard_map/ppermute | solution.py:28
  55.0 10.8 %shard_map.59 = (bf16[68,256,128]{2,1,0:T(8,128)(2,1)S(1)}, bf16[256,128]{1,0:T(8,128)(2,1)S(1)}, bf16[256,128]{1,0:T(8,128)(2,1)S(1)}, bf16[256,128]{1,0:T(8,128)(2,1)S(1)}, bf16[256,128]{1,0:T(8,128)(2,1)S(1)}) custom-call(s32[1040]{0:T(1024)S(1)} %constant_dynamic-update-slice_fusion.table.refs_0_, bf16[256,8192]{1,0:T(8,128)(2,1)} %refs_1_.1, ...), custom_call_target="tpu_custom_call" | custom-call | tf_op jit(solution)/shard_map/pallas_call | solution.py:206
  65.8 2.1 %collective-permute-start.13 = (bf16[256,128]{1,0:T(8,128)(2,1)S(1)}, bf16[256,128]{1,0:T(8,128)(2,1)S(1)}, u32[]{:S(2)}, u32[]{:S(2)}) collective-permute-start(bf16[256,128]{1,0:T(8,128)(2,1)S(1)} %get-tuple-element.73), channel_id=1, source_target_pairs={{24,0},{28,4},{0,8},{4,12},{8,16},{12,20},{16,24},{20,28},{25,1},{... | collective-permute-start | bytes 196616 | tf_op jit(solution)/shard_map/ppermute | solution.py:23
  67.9 2.6 %collective-permute-start.11 = (bf16[256,128]{1,0:T(8,128)(2,1)S(1)}, bf16[256,128]{1,0:T(8,128)(2,1)S(1)}, u32[]{:S(2)}, u32[]{:S(2)}) collective-permute-start(bf16[256,128]{1,0:T(8,128)(2,1)S(1)} %get-tuple-element.71), channel_id=1, source_target_pairs={{16,0},{20,4},{24,8},{28,12},{0,16},{4,20},{8,24},{12,28},{17,1},{... | collective-permute-start | bytes 196616 | tf_op jit(solution)/shard_map/ppermute | solution.py:23
  70.5 2.0 %collective-permute-done.13.refs_3_ = bf16[256,128]{1,0:T(8,128)(2,1)S(1)} collective-permute-done((bf16[256,128]{1,0:T(8,128)(2,1)S(1)}, bf16[256,128]{1,0:T(8,128)(2,1)S(1)}, u32[]{:S(2)}, u32[]{:S(2)}) %collective-permute-start.13) | collective-permute-done | bytes 65568 | tf_op jit(solution)/shard_map/ppermute | solution.py:23
  72.5 3.4 %collective-permute-start.14 = (bf16[256,128]{1,0:T(8,128)(2,1)S(1)}, bf16[256,128]{1,0:T(8,128)(2,1)S(1)}, u32[]{:S(2)}, u32[]{:S(2)}) collective-permute-start(bf16[256,128]{1,0:T(8,128)(2,1)S(1)} %get-tuple-element.75), channel_id=1, source_target_pairs={{4,0},{8,4},{12,8},{16,12},{20,16},{24,20},{28,24},{0,28},{5,1},{9... | collective-permute-start | bytes 196616 | tf_op jit(solution)/shard_map/ppermute | solution.py:23
  78.5 4.4 %collective-permute-done.12.refs_2_ = bf16[256,128]{1,0:T(8,128)(2,1)S(1)} collective-permute-done((bf16[256,128]{1,0:T(8,128)(2,1)S(1)}, bf16[256,128]{1,0:T(8,128)(2,1)S(1)}, u32[]{:S(2)}, u32[]{:S(2)}) %collective-permute-start.12) | collective-permute-done | bytes 65568 | tf_op jit(solution)/shard_map/ppermute | solution.py:23
  87.0 8.8 %collective-permute-done.16.refs_11_ = bf16[32,128,128]{2,1,0:T(8,128)(2,1)S(1)} collective-permute-done((bf16[32,128,128]{2,1,0:T(8,128)(2,1)S(1)}, bf16[32,128,128]{2,1,0:T(8,128)(2,1)S(1)}, u32[]{:S(2)}, u32[]{:S(2)}) %collective-permute-start.16) | collective-permute-done | bytes 1048608 | tf_op jit(solution)/shard_map/ppermute | solution.py:28
  96.5 1.9 %collective-permute-start.26 = (bf16[32,128,128]{2,1,0:T(8,128)(2,1)S(1)}, bf16[32,128,128]{2,1,0:T(8,128)(2,1)S(1)}, u32[]{:S(2)}, u32[]{:S(2)}) collective-permute-start(bf16[32,128,128]{2,1,0:T(8,128)(2,1)S(1)} %get-tuple-element.90.refs_7_), channel_id=1, source_target_pairs={{0,2},{1,3},{2,0},{3,1},{4,6},{5,7},{6,4},{7,5},{8,10},{9,11},{10,... | collective-permute-start | bytes 3145736 | tf_op jit(solution)/shard_map/ppermute | solution.py:28
  98.7 6.7 %shard_map.62 = (bf16[68,256,128]{2,1,0:T(8,128)(2,1)S(1)}, bf16[68,256,128]{2,1,0:T(8,128)(2,1)S(1)}, bf16[256,128]{1,0:T(8,128)(2,1)S(1)}, bf16[256,128]{1,0:T...) custom-call(s32[1040]{0:T(1024)S(1)} %constant_dynamic-update-slice_, ...), custom_call_target="tpu_custom_call", output_to_operand_aliasing={{1}: (1, {})} | custom-call | tf_op jit(solution)/shard_map/pallas_call | solution.py:206
  105.4 2.1 %collective-permute-start.23 = (bf16[256,128]{1,0:T(8,128)(2,1)S(1)}, bf16[256,128]{1,0:T(8,128)(2,1)S(1)}, u32[]{:S(2)}, u32[]{:S(2)}) collective-permute-start(bf16[256,128]{1,0:T(8,128)(2,1)S(1)} %get-tuple-element.86), channel_id=1, source_target_pairs={{24,0},{28,4},{0,8},{4,12},{8,16},{12,20},{16,24},{20,28},{25,1},{... | collective-permute-start | bytes 196616 | tf_op jit(solution)/shard_map/ppermute | solution.py:23
  107.4 2.6 %collective-permute-start.21 = (bf16[256,128]{1,0:T(8,128)(2,1)S(1)}, bf16[256,128]{1,0:T(8,128)(2,1)S(1)}, u32[]{:S(2)}, u32[]{:S(2)}) collective-permute-start(bf16[256,128]{1,0:T(8,128)(2,1)S(1)} %get-tuple-element.84), channel_id=1, source_target_pairs={{16,0},{20,4},{24,8},{28,12},{0,16},{4,20},{8,24},{12,28},{17,1},{... | collective-permute-start | bytes 196616 | tf_op jit(solution)/shard_map/ppermute | solution.py:23
  110.0 2.0 %collective-permute-done.23.refs_3_ = bf16[256,128]{1,0:T(8,128)(2,1)S(1)} collective-permute-done((bf16[256,128]{1,0:T(8,128)(2,1)S(1)}, bf16[256,128]{1,0:T(8,128)(2,1)S(1)}, u32[]{:S(2)}, u32[]{:S(2)}) %collective-permute-start.23) | collective-permute-done | bytes 65568 | tf_op jit(solution)/shard_map/ppermute | solution.py:23
  112.0 3.4 %collective-permute-start.24 = (bf16[256,128]{1,0:T(8,128)(2,1)S(1)}, bf16[256,128]{1,0:T(8,128)(2,1)S(1)}, u32[]{:S(2)}, u32[]{:S(2)}) collective-permute-start(bf16[256,128]{1,0:T(8,128)(2,1)S(1)} %get-tuple-element.88), channel_id=1, source_target_pairs={{4,0},{8,4},{12,8},{16,12},{20,16},{24,20},{28,24},{0,28},{5,1},{9... | collective-permute-start | bytes 196616 | tf_op jit(solution)/shard_map/ppermute | solution.py:23
  118.3 4.1 %collective-permute-done.22.refs_2_ = bf16[256,128]{1,0:T(8,128)(2,1)S(1)} collective-permute-done((bf16[256,128]{1,0:T(8,128)(2,1)S(1)}, bf16[256,128]{1,0:T(8,128)(2,1)S(1)}, u32[]{:S(2)}, u32[]{:S(2)}) %collective-permute-start.22) | collective-permute-done | bytes 65568 | tf_op jit(solution)/shard_map/ppermute | solution.py:23
  126.5 14.2 %collective-permute-done.26.refs_11_ = bf16[32,128,128]{2,1,0:T(8,128)(2,1)S(1)} collective-permute-done((bf16[32,128,128]{2,1,0:T(8,128)(2,1)S(1)}, bf16[32,128,128]{2,1,0:T(8,128)(2,1)S(1)}, u32[]{:S(2)}, u32[]{:S(2)}) %collective-permute-start.26) | collective-permute-done | bytes 1048608 | tf_op jit(solution)/shard_map/ppermute | solution.py:28
  143.6 6.7 %shard_map.65 = (bf16[68,256,128]{2,1,0:T(8,128)(2,1)S(1)}, bf16[68,256,128]{2,1,0:T(8,128)(2,1)S(1)}, bf16[256,128]{1,0:T(8,128)(2,1)S(1)}, bf16[256,128]{1,0:T...) custom-call(s32[1040]{0:T(1024)S(1)} %constant_dynamic-update-slice_, ...), custom_call_target="tpu_custom_call", output_to_operand_aliasing={{1}: (1, {})} | custom-call | tf_op jit(solution)/shard_map/pallas_call | solution.py:206
  150.3 2.1 %collective-permute-start.33 = (bf16[256,128]{1,0:T(8,128)(2,1)S(1)}, bf16[256,128]{1,0:T(8,128)(2,1)S(1)}, u32[]{:S(2)}, u32[]{:S(2)}) collective-permute-start(bf16[256,128]{1,0:T(8,128)(2,1)S(1)} %get-tuple-element.99), channel_id=1, source_target_pairs={{24,0},{28,4},{0,8},{4,12},{8,16},{12,20},{16,24},{20,28},{25,1},{... | collective-permute-start | bytes 196616 | tf_op jit(solution)/shard_map/ppermute | solution.py:23
  152.4 2.6 %collective-permute-start.31 = (bf16[256,128]{1,0:T(8,128)(2,1)S(1)}, bf16[256,128]{1,0:T(8,128)(2,1)S(1)}, u32[]{:S(2)}, u32[]{:S(2)}) collective-permute-start(bf16[256,128]{1,0:T(8,128)(2,1)S(1)} %get-tuple-element.97), channel_id=1, source_target_pairs={{16,0},{20,4},{24,8},{28,12},{0,16},{4,20},{8,24},{12,28},{17,1},{... | collective-permute-start | bytes 196616 | tf_op jit(solution)/shard_map/ppermute | solution.py:23
  155.0 2.0 %collective-permute-done.33.refs_3_ = bf16[256,128]{1,0:T(8,128)(2,1)S(1)} collective-permute-done((bf16[256,128]{1,0:T(8,128)(2,1)S(1)}, bf16[256,128]{1,0:T(8,128)(2,1)S(1)}, u32[]{:S(2)}, u32[]{:S(2)}) %collective-permute-start.33) | collective-permute-done | bytes 65568 | tf_op jit(solution)/shard_map/ppermute | solution.py:23
  157.0 3.4 %collective-permute-start.34 = (bf16[256,128]{1,0:T(8,128)(2,1)S(1)}, bf16[256,128]{1,0:T(8,128)(2,1)S(1)}, u32[]{:S(2)}, u32[]{:S(2)}) collective-permute-start(bf16[256,128]{1,0:T(8,128)(2,1)S(1)} %get-tuple-element.101), channel_id=1, source_target_pairs={{4,0},{8,4},{12,8},{16,12},{20,16},{24,20},{28,24},{0,28},{5,1},{9... | collective-permute-start | bytes 196616 | tf_op jit(solution)/shard_map/ppermute | solution.py:23
  170.4 4.4 %shard_map.68 = (bf16[256,8192]{1,0:T(8,128)(2,1)}, bf16[68,256,128]{2,1,0:T(8,128)(2,1)S(1)}) custom-call(s32[1040]{0:T(1024)S(1)} %constant_dynamic-update-slice_fusion.table.refs_0_, bf16[68,256,128]{2,1,0:T(8,128)(2,1)S(1)} %get-tuple-element.95.refs_1_, bf16[256,128]{1,0:T(8,128)(2,1)S(1)} %collective-permute-done.32.refs_2_, ...), custom_call_target="tpu_custom_call", output_to_operand_aliasing={{1}: (1, {})} | custom-call | tf_op jit(solution)/shard_map/pallas_call | solution.py:206
  174.8 5.3 %collective-permute-done.40.refs_4_ = bf16[20,128,128]{2,1,0:T(8,128)(2,1)S(1)} collective-permute-done((bf16[20,128,128]{2,1,0:T(8,128)(2,1)S(1)}, bf16[20,128,128]{2,1,0:T(8,128)(2,1)S(1)}, u32[]{:S(2)}, u32[]{:S(2)}) %collective-permute-start.40) | collective-permute-done | bytes 655392 | tf_op jit(solution)/shard_map/ppermute | solution.py:28
  182.3 2.9 %shard_map.69.refs_7_ = bf16[256,8192]{1,0:T(8,128)(2,1)} custom-call(s32[1040]{0:T(1024)S(1)} %constant_dynamic-update-slice_fusion.table.refs_0_, bf16[68,256,128]{2,1,0:T(8,128)(2,1)S(1)} %get-tuple-element.107.refs_1_, bf16[20,128,128]{2,1,0:T(8,128)(2,1)S(1)} %get-tuple-element.109.refs_2_, ...), custom_call_target="tpu_custom_call", output_to_operand_aliasing={{}: (10, {})} | custom-call | tf_op jit(solution)/shard_map/pallas_call | solution.py:206
  187.1 2.1 %shard_map.70 = bf16[256,8192]{1,0:T(8,128)(2,1)} custom-call(s32[1040]{0:T(1024)S(1)} %constant_dynamic-update-slice_fusion.table.refs_0_, bf16[68,256,128]{2,1,0:T(8,128)(2,1)S(1)} %get-tuple-element.107.refs_1_, bf16[8,128,128]{2,1,0:T(8,128)(2,1)S(1)} %get-tuple-element.108.refs_2_, ...), custom_call_target="tpu_custom_call", output_to_operand_aliasing={{}: (7, {})} | custom-call | tf_op jit(solution)/shard_map/pallas_call | solution.py:206
  (106 shorter events, 49.1 us)
Async XLA Ops:
  0.0 20.4 %collective-permute-start.4 = (bf16[4,64,128,128]{3,2,1,0:T(8,128)(2,1)}, bf16[4,64,128,128]{3,2,1,0:T(8,128)(2,1)}, u32[]{:S(2)}, u32[]{:S(2)}) collective-permute-start(bf16[4,64,128,128]{3,2,1,0:T(8,128)(2,1)} %tiles.9), channel_id=1, source_target_pairs={{0,1},{1,0},{2,3},{3,2},{4,5},{5,4},{6,7},{7,6},{8,9},{9,8},{10,11... | collective-permute-start | bytes 25165832 | tf_op jit(solution)/shard_map/ppermute | solution.py:28
  1.8 26.6 %collective-permute-start.5 = (bf16[32,128,128]{2,1,0:T(8,128)(2,1)S(1)}, bf16[32,128,128]{2,1,0:T(8,128)(2,1)S(1)}, u32[]{:S(2)}, u32[]{:S(2)}) collective-permute-start(bf16[32,128,128]{2,1,0:T(8,128)(2,1)S(1)} %shard_map.56.refs_6_), channel_id=1, source_target_pairs={{0,2},{1,3},{2,0},{3,1},{4,6},{5,7},{6,4},{7,5},{8,10},{9,11},{10,... | collective-permute-start | bytes 3145736 | tf_op jit(solution)/shard_map/ppermute | solution.py:28
  5.8 45.2 %collective-permute-start.6 = (bf16[32,128,128]{2,1,0:T(8,128)(2,1)S(1)}, bf16[32,128,128]{2,1,0:T(8,128)(2,1)}, u32[]{:S(2)}, u32[]{:S(2)}) collective-permute-start(bf16[32,128,128]{2,1,0:T(8,128)(2,1)S(1)} %shard_map.57.refs_7_), channel_id=1, source_target_pairs={{0,2},{1,3},{2,0},{3,1},{4,6},{5,7},{6,4},{7,5},{8,10},{9,11},{10,... | collective-permute-start | bytes 3145736 | tf_op jit(solution)/shard_map/ppermute | solution.py:28
  9.7 6.6 %collective-permute-start.2 = (bf16[256,128]{1,0:T(8,128)(2,1)S(1)}, bf16[256,128]{1,0:T(8,128)(2,1)S(1)}, u32[]{:S(2)}, u32[]{:S(2)}) collective-permute-start(bf16[256,128]{1,0:T(8,128)(2,1)S(1)} %get-tuple-element.62), channel_id=1, source_target_pairs={{24,0},{28,4},{0,8},{4,12},{8,16},{12,20},{16,24},{20,28},{25,1},{... | collective-permute-start | bytes 196616 | tf_op jit(solution)/shard_map/ppermute | solution.py:23
  11.8 7.8 %collective-permute-start = (bf16[256,128]{1,0:T(8,128)(2,1)S(1)}, bf16[256,128]{1,0:T(8,128)(2,1)S(1)}, u32[]{:S(2)}, u32[]{:S(2)}) collective-permute-start(bf16[256,128]{1,0:T(8,128)(2,1)S(1)} %get-tuple-element.60), channel_id=1, source_target_pairs={{16,0},{20,4},{24,8},{28,12},{0,16},{4,20},{8,24},{12,28},{17,1},{... | collective-permute-start | bytes 196616 | tf_op jit(solution)/shard_map/ppermute | solution.py:23
  16.3 5.9 %collective-permute-start.3 = (bf16[256,128]{1,0:T(8,128)(2,1)S(1)}, bf16[256,128]{1,0:T(8,128)(2,1)S(1)}, u32[]{:S(2)}, u32[]{:S(2)}) collective-permute-start(bf16[256,128]{1,0:T(8,128)(2,1)S(1)} %get-tuple-element.64), channel_id=1, source_target_pairs={{4,0},{8,4},{12,8},{16,12},{20,16},{24,20},{28,24},{0,28},{5,1},{9... | collective-permute-start | bytes 196616 | tf_op jit(solution)/shard_map/ppermute | solution.py:23
  19.7 7.0 %collective-permute-start.1 = (bf16[256,128]{1,0:T(8,128)(2,1)S(1)}, bf16[256,128]{1,0:T(8,128)(2,1)S(1)}, u32[]{:S(2)}, u32[]{:S(2)}) collective-permute-start(bf16[256,128]{1,0:T(8,128)(2,1)S(1)} %get-tuple-element.61), channel_id=1, source_target_pairs={{28,0},{0,4},{4,8},{8,12},{12,16},{16,20},{20,24},{24,28},{29,1},{... | collective-permute-start | bytes 196616 | tf_op jit(solution)/shard_map/ppermute | solution.py:23
  28.5 22.5 %collective-permute-start.7 = (bf16[16,128,128]{2,1,0:T(8,128)(2,1)S(1)}, bf16[16,128,128]{2,1,0:T(8,128)(2,1)S(1)}, u32[]{:S(2)}, u32[]{:S(2)}) collective-permute-start(bf16[16,128,128]{2,1,0:T(8,128)(2,1)S(1)} %get-tuple-element.126), channel_id=1, source_target_pairs={{0,1},{1,0},{2,3},{3,2},{4,5},{5,4},{6,7},{7,6},{8,9},{9,8},{10,11... | collective-permute-start | bytes 1572872 | tf_op jit(solution)/shard_map/ppermute | solution.py:28
  28.6 22.4 %collective-permute-start.8 = (bf16[16,128,128]{2,1,0:T(8,128)(2,1)S(1)}, bf16[16,128,128]{2,1,0:T(8,128)(2,1)S(1)}, u32[]{:S(2)}, u32[]{:S(2)}) collective-permute-start(bf16[16,128,128]{2,1,0:T(8,128)(2,1)S(1)} %get-tuple-element.125), channel_id=1, source_target_pairs={{0,1},{1,0},{2,3},{3,2},{4,5},{5,4},{6,7},{7,6},{8,9},{9,8},{10,11... | collective-permute-start | bytes 1572872 | tf_op jit(solution)/shard_map/ppermute | solution.py:28
  30.9 47.6 %collective-permute-start.15 = (bf16[32,128,128]{2,1,0:T(8,128)(2,1)S(1)}, bf16[32,128,128]{2,1,0:T(8,128)(2,1)S(1)}, u32[]{:S(2)}, u32[]{:S(2)}) collective-permute-start(bf16[32,128,128]{2,1,0:T(8,128)(2,1)S(1)} %get-tuple-element.76.refs_6_), channel_id=1, source_target_pairs={{0,2},{1,3},{2,0},{3,1},{4,6},{5,7},{6,4},{7,5},{8,10},{9,11},{10,... | collective-permute-start | bytes 3145736 | tf_op jit(solution)/shard_map/ppermute | solution.py:28
  52.9 43.0 %collective-permute-start.16 = (bf16[32,128,128]{2,1,0:T(8,128)(2,1)S(1)}, bf16[32,128,128]{2,1,0:T(8,128)(2,1)S(1)}, u32[]{:S(2)}, u32[]{:S(2)}) collective-permute-start(bf16[32,128,128]{2,1,0:T(8,128)(2,1)S(1)} %get-tuple-element.77.refs_7_), channel_id=1, source_target_pairs={{0,2},{1,3},{2,0},{3,1},{4,6},{5,7},{6,4},{7,5},{8,10},{9,11},{10,... | collective-permute-start | bytes 3145736 | tf_op jit(solution)/shard_map/ppermute | solution.py:28
  65.8 6.7 %collective-permute-start.13 = (bf16[256,128]{1,0:T(8,128)(2,1)S(1)}, bf16[256,128]{1,0:T(8,128)(2,1)S(1)}, u32[]{:S(2)}, u32[]{:S(2)}) collective-permute-start(bf16[256,128]{1,0:T(8,128)(2,1)S(1)} %get-tuple-element.73), channel_id=1, source_target_pairs={{24,0},{28,4},{0,8},{4,12},{8,16},{12,20},{16,24},{20,28},{25,1},{... | collective-permute-start | bytes 196616 | tf_op jit(solution)/shard_map/ppermute | solution.py:23
  67.9 8.0 %collective-permute-start.11 = (bf16[256,128]{1,0:T(8,128)(2,1)S(1)}, bf16[256,128]{1,0:T(8,128)(2,1)S(1)}, u32[]{:S(2)}, u32[]{:S(2)}) collective-permute-start(bf16[256,128]{1,0:T(8,128)(2,1)S(1)} %get-tuple-element.71), channel_id=1, source_target_pairs={{16,0},{20,4},{24,8},{28,12},{0,16},{4,20},{8,24},{12,28},{17,1},{... | collective-permute-start | bytes 196616 | tf_op jit(solution)/shard_map/ppermute | solution.py:23
  72.5 6.0 %collective-permute-start.14 = (bf16[256,128]{1,0:T(8,128)(2,1)S(1)}, bf16[256,128]{1,0:T(8,128)(2,1)S(1)}, u32[]{:S(2)}, u32[]{:S(2)}) collective-permute-start(bf16[256,128]{1,0:T(8,128)(2,1)S(1)} %get-tuple-element.75), channel_id=1, source_target_pairs={{4,0},{8,4},{12,8},{16,12},{20,16},{24,20},{28,24},{0,28},{5,1},{9... | collective-permute-start | bytes 196616 | tf_op jit(solution)/shard_map/ppermute | solution.py:23
  75.9 7.0 %collective-permute-start.12 = (bf16[256,128]{1,0:T(8,128)(2,1)S(1)}, bf16[256,128]{1,0:T(8,128)(2,1)S(1)}, u32[]{:S(2)}, u32[]{:S(2)}) collective-permute-start(bf16[256,128]{1,0:T(8,128)(2,1)S(1)} %get-tuple-element.72), channel_id=1, source_target_pairs={{28,0},{0,4},{4,8},{8,12},{12,16},{16,20},{20,24},{24,28},{29,1},{... | collective-permute-start | bytes 196616 | tf_op jit(solution)/shard_map/ppermute | solution.py:23
  83.0 12.8 %collective-permute-start.17 = (bf16[16,128,128]{2,1,0:T(8,128)(2,1)S(1)}, bf16[16,128,128]{2,1,0:T(8,128)(2,1)S(1)}, u32[]{:S(2)}, u32[]{:S(2)}) collective-permute-start(bf16[16,128,128]{2,1,0:T(8,128)(2,1)S(1)} %get-tuple-element.122), channel_id=1, source_target_pairs={{0,1},{1,0},{2,3},{3,2},{4,5},{5,4},{6,7},{7,6},{8,9},{9,8},{10,11... | collective-permute-start | bytes 1572872 | tf_op jit(solution)/shard_map/ppermute | solution.py:28
  83.1 12.8 %collective-permute-start.18 = (bf16[16,128,128]{2,1,0:T(8,128)(2,1)S(1)}, bf16[16,128,128]{2,1,0:T(8,128)(2,1)S(1)}, u32[]{:S(2)}, u32[]{:S(2)}) collective-permute-start(bf16[16,128,128]{2,1,0:T(8,128)(2,1)S(1)} %get-tuple-element.121), channel_id=1, source_target_pairs={{0,1},{1,0},{2,3},{3,2},{4,5},{5,4},{6,7},{7,6},{8,9},{9,8},{10,11... | collective-permute-start | bytes 1572872 | tf_op jit(solution)/shard_map/ppermute | solution.py:28
  85.4 32.9 %collective-permute-start.25 = (bf16[32,128,128]{2,1,0:T(8,128)(2,1)S(1)}, bf16[32,128,128]{2,1,0:T(8,128)(2,1)S(1)}, u32[]{:S(2)}, u32[]{:S(2)}) collective-permute-start(bf16[32,128,128]{2,1,0:T(8,128)(2,1)S(1)} %get-tuple-element.89.refs_6_), channel_id=1, source_target_pairs={{0,2},{1,3},{2,0},{3,1},{4,6},{5,7},{6,4},{7,5},{8,10},{9,11},{10,... | collective-permute-start | bytes 3145736 | tf_op jit(solution)/shard_map/ppermute | solution.py:28
  96.5 44.2 %collective-permute-start.26 = (bf16[32,128,128]{2,1,0:T(8,128)(2,1)S(1)}, bf16[32,128,128]{2,1,0:T(8,128)(2,1)S(1)}, u32[]{:S(2)}, u32[]{:S(2)}) collective-permute-start(bf16[32,128,128]{2,1,0:T(8,128)(2,1)S(1)} %get-tuple-element.90.refs_7_), channel_id=1, source_target_pairs={{0,2},{1,3},{2,0},{3,1},{4,6},{5,7},{6,4},{7,5},{8,10},{9,11},{10,... | collective-permute-start | bytes 3145736 | tf_op jit(solution)/shard_map/ppermute | solution.py:28
  105.4 6.7 %collective-permute-start.23 = (bf16[256,128]{1,0:T(8,128)(2,1)S(1)}, bf16[256,128]{1,0:T(8,128)(2,1)S(1)}, u32[]{:S(2)}, u32[]{:S(2)}) collective-permute-start(bf16[256,128]{1,0:T(8,128)(2,1)S(1)} %get-tuple-element.86), channel_id=1, source_target_pairs={{24,0},{28,4},{0,8},{4,12},{8,16},{12,20},{16,24},{20,28},{25,1},{... | collective-permute-start | bytes 196616 | tf_op jit(solution)/shard_map/ppermute | solution.py:23
  107.4 8.0 %collective-permute-start.21 = (bf16[256,128]{1,0:T(8,128)(2,1)S(1)}, bf16[256,128]{1,0:T(8,128)(2,1)S(1)}, u32[]{:S(2)}, u32[]{:S(2)}) collective-permute-start(bf16[256,128]{1,0:T(8,128)(2,1)S(1)} %get-tuple-element.84), channel_id=1, source_target_pairs={{16,0},{20,4},{24,8},{28,12},{0,16},{4,20},{8,24},{12,28},{17,1},{... | collective-permute-start | bytes 196616 | tf_op jit(solution)/shard_map/ppermute | solution.py:23
  112.0 6.3 %collective-permute-start.24 = (bf16[256,128]{1,0:T(8,128)(2,1)S(1)}, bf16[256,128]{1,0:T(8,128)(2,1)S(1)}, u32[]{:S(2)}, u32[]{:S(2)}) collective-permute-start(bf16[256,128]{1,0:T(8,128)(2,1)S(1)} %get-tuple-element.88), channel_id=1, source_target_pairs={{4,0},{8,4},{12,8},{16,12},{20,16},{24,20},{28,24},{0,28},{5,1},{9... | collective-permute-start | bytes 196616 | tf_op jit(solution)/shard_map/ppermute | solution.py:23
  115.4 7.0 %collective-permute-start.22 = (bf16[256,128]{1,0:T(8,128)(2,1)S(1)}, bf16[256,128]{1,0:T(8,128)(2,1)S(1)}, u32[]{:S(2)}, u32[]{:S(2)}) collective-permute-start(bf16[256,128]{1,0:T(8,128)(2,1)S(1)} %get-tuple-element.85), channel_id=1, source_target_pairs={{28,0},{0,4},{4,8},{8,12},{12,16},{16,20},{20,24},{24,28},{29,1},{... | collective-permute-start | bytes 196616 | tf_op jit(solution)/shard_map/ppermute | solution.py:23
  122.5 18.3 %collective-permute-start.27 = (bf16[16,128,128]{2,1,0:T(8,128)(2,1)S(1)}, bf16[16,128,128]{2,1,0:T(8,128)(2,1)S(1)}, u32[]{:S(2)}, u32[]{:S(2)}) collective-permute-start(bf16[16,128,128]{2,1,0:T(8,128)(2,1)S(1)} %get-tuple-element.118), channel_id=1, source_target_pairs={{0,1},{1,0},{2,3},{3,2},{4,5},{5,4},{6,7},{7,6},{8,9},{9,8},{10,11... | collective-permute-start | bytes 1572872 | tf_op jit(solution)/shard_map/ppermute | solution.py:28
  122.6 18.2 %collective-permute-start.28 = (bf16[16,128,128]{2,1,0:T(8,128)(2,1)S(1)}, bf16[16,128,128]{2,1,0:T(8,128)(2,1)S(1)}, u32[]{:S(2)}, u32[]{:S(2)}) collective-permute-start(bf16[16,128,128]{2,1,0:T(8,128)(2,1)S(1)} %get-tuple-element.117), channel_id=1, source_target_pairs={{0,1},{1,0},{2,3},{3,2},{4,5},{5,4},{6,7},{7,6},{8,9},{9,8},{10,11... | collective-permute-start | bytes 1572872 | tf_op jit(solution)/shard_map/ppermute | solution.py:28
  125.0 41.1 %collective-permute-start.35 = (bf16[36,128,128]{2,1,0:T(8,128)(2,1)S(1)}, bf16[36,128,128]{2,1,0:T(8,128)(2,1)S(1)}, u32[]{:S(2)}, u32[]{:S(2)}) collective-permute-start(bf16[36,128,128]{2,1,0:T(8,128)(2,1)S(1)} %get-tuple-element.102.refs_6_), channel_id=1, source_target_pairs={{0,2},{1,3},{2,0},{3,1},{4,6},{5,7},{6,4},{7,5},{8,10},{9,11},{10,... | collective-permute-start | bytes 3538952 | tf_op jit(solution)/shard_map/ppermute | solution.py:28
  150.3 6.7 %collective-permute-start.33 = (bf16[256,128]{1,0:T(8,128)(2,1)S(1)}, bf16[256,128]{1,0:T(8,128)(2,1)S(1)}, u32[]{:S(2)}, u32[]{:S(2)}) collective-permute-start(bf16[256,128]{1,0:T(8,128)(2,1)S(1)} %get-tuple-element.99), channel_id=1, source_target_pairs={{24,0},{28,4},{0,8},{4,12},{8,16},{12,20},{16,24},{20,28},{25,1},{... | collective-permute-start | bytes 196616 | tf_op jit(solution)/shard_map/ppermute | solution.py:23
  152.4 8.0 %collective-permute-start.31 = (bf16[256,128]{1,0:T(8,128)(2,1)S(1)}, bf16[256,128]{1,0:T(8,128)(2,1)S(1)}, u32[]{:S(2)}, u32[]{:S(2)}) collective-permute-start(bf16[256,128]{1,0:T(8,128)(2,1)S(1)} %get-tuple-element.97), channel_id=1, source_target_pairs={{16,0},{20,4},{24,8},{28,12},{0,16},{4,20},{8,24},{12,28},{17,1},{... | collective-permute-start | bytes 196616 | tf_op jit(solution)/shard_map/ppermute | solution.py:23
  157.0 9.1 %collective-permute-start.34 = (bf16[256,128]{1,0:T(8,128)(2,1)S(1)}, bf16[256,128]{1,0:T(8,128)(2,1)S(1)}, u32[]{:S(2)}, u32[]{:S(2)}) collective-permute-start(bf16[256,128]{1,0:T(8,128)(2,1)S(1)} %get-tuple-element.101), channel_id=1, source_target_pairs={{4,0},{8,4},{12,8},{16,12},{20,16},{24,20},{28,24},{0,28},{5,1},{9... | collective-permute-start | bytes 196616 | tf_op jit(solution)/shard_map/ppermute | solution.py:23
  160.4 7.0 %collective-permute-start.32 = (bf16[256,128]{1,0:T(8,128)(2,1)S(1)}, bf16[256,128]{1,0:T(8,128)(2,1)S(1)}, u32[]{:S(2)}, u32[]{:S(2)}) collective-permute-start(bf16[256,128]{1,0:T(8,128)(2,1)S(1)} %get-tuple-element.98), channel_id=1, source_target_pairs={{28,0},{0,4},{4,8},{8,12},{12,16},{16,20},{20,24},{24,28},{29,1},{... | collective-permute-start | bytes 196616 | tf_op jit(solution)/shard_map/ppermute | solution.py:23
  161.1 19.0 %collective-permute-start.40 = (bf16[20,128,128]{2,1,0:T(8,128)(2,1)S(1)}, bf16[20,128,128]{2,1,0:T(8,128)(2,1)S(1)}, u32[]{:S(2)}, u32[]{:S(2)}) collective-permute-start(bf16[20,128,128]{2,1,0:T(8,128)(2,1)S(1)} %get-tuple-element.109.refs_2_), channel_id=1, source_target_pairs={{0,2},{1,3},{2,0},{3,1},{4,6},{5,7},{6,4},{7,5},{8,10},{9,11},{10,... | collective-permute-start | bytes 1966088 | tf_op jit(solution)/shard_map/ppermute | solution.py:28
  168.2 17.4 %collective-permute-start.39 = (bf16[8,128,128]{2,1,0:T(8,128)(2,1)S(1)}, bf16[8,128,128]{2,1,0:T(8,128)(2,1)S(1)}, u32[]{:S(2)}, u32[]{:S(2)}) collective-permute-start(bf16[8,128,128]{2,1,0:T(8,128)(2,1)S(1)} %get-tuple-element.108.refs_2_), channel_id=1, source_target_pairs={{0,2},{1,3},{2,0},{3,1},{4,6},{5,7},{6,4},{7,5},{8,10},{9,11},{10,... | collective-permute-start | bytes 786440 | tf_op jit(solution)/shard_map/ppermute | solution.py:28
  (18 other events, 76.0 us)

commit v14 on v13

--- a/solution.py
+++ b/solution.py
@@ -102,7 +102,7 @@
     for m in range(fan):
         places[m] = [(part, inside) for part, array in enumerate(tiles[m]) for inside in range(array.shape[0])]
     cuts = [block for block in range(count) if any(places[m][block][1] == 0 for m in range(fan))] + [count]
-    group = math.gcd(8, *cuts)
+    group = math.gcd(2 if final else 8, *cuts)
 
     def kernel(*refs):
         refs = list(refs)

time: 190 us -> 190 us (level)
  no operation moved by 1% of the time
where the time goes in v14:
time: 190 us; the launch traced here: 189 us
  waiting for transfers between devices  78.3 us (41%)
  starting transfers between devices  55.7 us (29%)
  Pallas kernels  50.7 us (27%)
  local copies, waits for them, and re-layouts  3.32 us (2%)
    ppermute x30, waiting for transfers between devices, swapped(): return lax.ppermute(block, 'batch', route)  56.2 us
    ppermute x16, starting transfers between devices, shifted(): return lax.ppermute(block, axis, route)  35.2 us
    pallas_call x6, Pallas kernels, run_blocks(): pl.pallas_call(kernel, out_shape=out_shape, grid_spec=pltpu.PrefetchScala...  33.5 us
    ppermute x16, waiting for transfers between devices, shifted(): return lax.ppermute(block, axis, route)  22.1 us
    ppermute x30, starting transfers between devices, swapped(): return lax.ppermute(block, 'batch', route)  20.5 us
    pallas_call x9, Pallas kernels, cut(): pl.pallas_call(kernel, out_shape=[pltpu.VMEM((count, height, width), tile...  15.6 us
  transfers between devices with their start and end apart: 46, of which 25 were waited for; matrix products, arithmetic and copies ran while one was open for 2% of the time, Pallas kernels for 26%

profile of v14, /device:TPU:0, one launch (start us, length us, event | category | flops | bytes accessed | tf_op | source)
XLA Modules:
  0.0 189.2 jit_solution(9407152471325413718)
XLA Ops:
  1.8 2.6 %collective-permute-start.5 = (bf16[32,128,128]{2,1,0:T(8,128)(2,1)S(1)}, bf16[32,128,128]{2,1,0:T(8,128)(2,1)S(1)}, u32[]{:S(2)}, u32[]{:S(2)}) collective-permute-start(bf16[32,128,128]{2,1,0:T(8,128)(2,1)S(1)} %shard_map.56.refs_6_), channel_id=1, source_target_pairs={{0,2},{1,3},{2,0},{3,1},{4,6},{5,7},{6,4},{7,5},{8,10},{9,11},{10,... | collective-permute-start | bytes 3145736 | tf_op jit(solution)/shard_map/ppermute | solution.py:28
  9.7 2.1 %collective-permute-start.2 = (bf16[256,128]{1,0:T(8,128)(2,1)S(1)}, bf16[256,128]{1,0:T(8,128)(2,1)S(1)}, u32[]{:S(2)}, u32[]{:S(2)}) collective-permute-start(bf16[256,128]{1,0:T(8,128)(2,1)S(1)} %get-tuple-element.62), channel_id=1, source_target_pairs={{24,0},{28,4},{0,8},{4,12},{8,16},{12,20},{16,24},{20,28},{25,1},{... | collective-permute-start | bytes 196616 | tf_op jit(solution)/shard_map/ppermute | solution.py:23
  11.8 2.6 %collective-permute-start = (bf16[256,128]{1,0:T(8,128)(2,1)S(1)}, bf16[256,128]{1,0:T(8,128)(2,1)S(1)}, u32[]{:S(2)}, u32[]{:S(2)}) collective-permute-start(bf16[256,128]{1,0:T(8,128)(2,1)S(1)} %get-tuple-element.60), channel_id=1, source_target_pairs={{16,0},{20,4},{24,8},{28,12},{0,16},{4,20},{8,24},{12,28},{17,1},{... | collective-permute-start | bytes 196616 | tf_op jit(solution)/shard_map/ppermute | solution.py:23
  16.3 3.3 %collective-permute-start.3 = (bf16[256,128]{1,0:T(8,128)(2,1)S(1)}, bf16[256,128]{1,0:T(8,128)(2,1)S(1)}, u32[]{:S(2)}, u32[]{:S(2)}) collective-permute-start(bf16[256,128]{1,0:T(8,128)(2,1)S(1)} %get-tuple-element.64), channel_id=1, source_target_pairs={{4,0},{8,4},{12,8},{16,12},{20,16},{24,20},{28,24},{0,28},{5,1},{9... | collective-permute-start | bytes 196616 | tf_op jit(solution)/shard_map/ppermute | solution.py:23
  22.2 4.4 %collective-permute-done.1.refs_2_ = bf16[256,128]{1,0:T(8,128)(2,1)S(1)} collective-permute-done((bf16[256,128]{1,0:T(8,128)(2,1)S(1)}, bf16[256,128]{1,0:T(8,128)(2,1)S(1)}, u32[]{:S(2)}, u32[]{:S(2)}) %collective-permute-start.1) | collective-permute-done | bytes 65568 | tf_op jit(solution)/shard_map/ppermute | solution.py:23
  30.9 2.0 %collective-permute-start.15 = (bf16[32,128,128]{2,1,0:T(8,128)(2,1)S(1)}, bf16[32,128,128]{2,1,0:T(8,128)(2,1)S(1)}, u32[]{:S(2)}, u32[]{:S(2)}) collective-permute-start(bf16[32,128,128]{2,1,0:T(8,128)(2,1)S(1)} %get-tuple-element.76.refs_6_), channel_id=1, source_target_pairs={{0,2},{1,3},{2,0},{3,1},{4,6},{5,7},{6,4},{7,5},{8,10},{9,11},{10,... | collective-permute-start | bytes 3145736 | tf_op jit(solution)/shard_map/ppermute | solution.py:28
  32.9 18.1 %collective-permute-done.6.refs_11_ = bf16[32,128,128]{2,1,0:T(8,128)(2,1)} collective-permute-done((bf16[32,128,128]{2,1,0:T(8,128)(2,1)S(1)}, bf16[32,128,128]{2,1,0:T(8,128)(2,1)}, u32[]{:S(2)}, u32[]{:S(2)}) %collective-permute-start.6) | collective-permute-done | bytes 1048608 | tf_op jit(solution)/shard_map/ppermute | solution.py:28
  52.9 1.9 %collective-permute-start.16 = (bf16[32,128,128]{2,1,0:T(8,128)(2,1)S(1)}, bf16[32,128,128]{2,1,0:T(8,128)(2,1)S(1)}, u32[]{:S(2)}, u32[]{:S(2)}) collective-permute-start(bf16[32,128,128]{2,1,0:T(8,128)(2,1)S(1)} %get-tuple-element.77.refs_7_), channel_id=1, source_target_pairs={{0,2},{1,3},{2,0},{3,1},{4,6},{5,7},{6,4},{7,5},{8,10},{9,11},{10,... | collective-permute-start | bytes 3145736 | tf_op jit(solution)/shard_map/ppermute | solution.py:28
  55.0 10.8 %shard_map.59 = (bf16[68,256,128]{2,1,0:T(8,128)(2,1)S(1)}, bf16[256,128]{1,0:T(8,128)(2,1)S(1)}, bf16[256,128]{1,0:T(8,128)(2,1)S(1)}, bf16[256,128]{1,0:T(8,128)(2,1)S(1)}, bf16[256,128]{1,0:T(8,128)(2,1)S(1)}) custom-call(s32[1040]{0:T(1024)S(1)} %constant_dynamic-update-slice_fusion.table.refs_0_, bf16[256,8192]{1,0:T(8,128)(2,1)} %refs_1_.1, ...), custom_call_target="tpu_custom_call" | custom-call | tf_op jit(solution)/shard_map/pallas_call | solution.py:206
  65.8 2.1 %collective-permute-start.13 = (bf16[256,128]{1,0:T(8,128)(2,1)S(1)}, bf16[256,128]{1,0:T(8,128)(2,1)S(1)}, u32[]{:S(2)}, u32[]{:S(2)}) collective-permute-start(bf16[256,128]{1,0:T(8,128)(2,1)S(1)} %get-tuple-element.73), channel_id=1, source_target_pairs={{24,0},{28,4},{0,8},{4,12},{8,16},{12,20},{16,24},{20,28},{25,1},{... | collective-permute-start | bytes 196616 | tf_op jit(solution)/shard_map/ppermute | solution.py:23
  67.9 2.6 %collective-permute-start.11 = (bf16[256,128]{1,0:T(8,128)(2,1)S(1)}, bf16[256,128]{1,0:T(8,128)(2,1)S(1)}, u32[]{:S(2)}, u32[]{:S(2)}) collective-permute-start(bf16[256,128]{1,0:T(8,128)(2,1)S(1)} %get-tuple-element.71), channel_id=1, source_target_pairs={{16,0},{20,4},{24,8},{28,12},{0,16},{4,20},{8,24},{12,28},{17,1},{... | collective-permute-start | bytes 196616 | tf_op jit(solution)/shard_map/ppermute | solution.py:23
  70.5 2.0 %collective-permute-done.13.refs_3_ = bf16[256,128]{1,0:T(8,128)(2,1)S(1)} collective-permute-done((bf16[256,128]{1,0:T(8,128)(2,1)S(1)}, bf16[256,128]{1,0:T(8,128)(2,1)S(1)}, u32[]{:S(2)}, u32[]{:S(2)}) %collective-permute-start.13) | collective-permute-done | bytes 65568 | tf_op jit(solution)/shard_map/ppermute | solution.py:23
  72.5 3.4 %collective-permute-start.14 = (bf16[256,128]{1,0:T(8,128)(2,1)S(1)}, bf16[256,128]{1,0:T(8,128)(2,1)S(1)}, u32[]{:S(2)}, u32[]{:S(2)}) collective-permute-start(bf16[256,128]{1,0:T(8,128)(2,1)S(1)} %get-tuple-element.75), channel_id=1, source_target_pairs={{4,0},{8,4},{12,8},{16,12},{20,16},{24,20},{28,24},{0,28},{5,1},{9... | collective-permute-start | bytes 196616 | tf_op jit(solution)/shard_map/ppermute | solution.py:23
  78.5 4.4 %collective-permute-done.12.refs_2_ = bf16[256,128]{1,0:T(8,128)(2,1)S(1)} collective-permute-done((bf16[256,128]{1,0:T(8,128)(2,1)S(1)}, bf16[256,128]{1,0:T(8,128)(2,1)S(1)}, u32[]{:S(2)}, u32[]{:S(2)}) %collective-permute-start.12) | collective-permute-done | bytes 65568 | tf_op jit(solution)/shard_map/ppermute | solution.py:23
  87.0 8.8 %collective-permute-done.16.refs_11_ = bf16[32,128,128]{2,1,0:T(8,128)(2,1)S(1)} collective-permute-done((bf16[32,128,128]{2,1,0:T(8,128)(2,1)S(1)}, bf16[32,128,128]{2,1,0:T(8,128)(2,1)S(1)}, u32[]{:S(2)}, u32[]{:S(2)}) %collective-permute-start.16) | collective-permute-done | bytes 1048608 | tf_op jit(solution)/shard_map/ppermute | solution.py:28
  96.5 1.9 %collective-permute-start.26 = (bf16[32,128,128]{2,1,0:T(8,128)(2,1)S(1)}, bf16[32,128,128]{2,1,0:T(8,128)(2,1)S(1)}, u32[]{:S(2)}, u32[]{:S(2)}) collective-permute-start(bf16[32,128,128]{2,1,0:T(8,128)(2,1)S(1)} %get-tuple-element.90.refs_7_), channel_id=1, source_target_pairs={{0,2},{1,3},{2,0},{3,1},{4,6},{5,7},{6,4},{7,5},{8,10},{9,11},{10,... | collective-permute-start | bytes 3145736 | tf_op jit(solution)/shard_map/ppermute | solution.py:28
  98.7 6.7 %shard_map.62 = (bf16[68,256,128]{2,1,0:T(8,128)(2,1)S(1)}, bf16[68,256,128]{2,1,0:T(8,128)(2,1)S(1)}, bf16[256,128]{1,0:T(8,128)(2,1)S(1)}, bf16[256,128]{1,0:T...) custom-call(s32[1040]{0:T(1024)S(1)} %constant_dynamic-update-slice_, ...), custom_call_target="tpu_custom_call", output_to_operand_aliasing={{1}: (1, {})} | custom-call | tf_op jit(solution)/shard_map/pallas_call | solution.py:206
  105.4 2.1 %collective-permute-start.23 = (bf16[256,128]{1,0:T(8,128)(2,1)S(1)}, bf16[256,128]{1,0:T(8,128)(2,1)S(1)}, u32[]{:S(2)}, u32[]{:S(2)}) collective-permute-start(bf16[256,128]{1,0:T(8,128)(2,1)S(1)} %get-tuple-element.86), channel_id=1, source_target_pairs={{24,0},{28,4},{0,8},{4,12},{8,16},{12,20},{16,24},{20,28},{25,1},{... | collective-permute-start | bytes 196616 | tf_op jit(solution)/shard_map/ppermute | solution.py:23
  107.4 2.6 %collective-permute-start.21 = (bf16[256,128]{1,0:T(8,128)(2,1)S(1)}, bf16[256,128]{1,0:T(8,128)(2,1)S(1)}, u32[]{:S(2)}, u32[]{:S(2)}) collective-permute-start(bf16[256,128]{1,0:T(8,128)(2,1)S(1)} %get-tuple-element.84), channel_id=1, source_target_pairs={{16,0},{20,4},{24,8},{28,12},{0,16},{4,20},{8,24},{12,28},{17,1},{... | collective-permute-start | bytes 196616 | tf_op jit(solution)/shard_map/ppermute | solution.py:23
  110.0 2.0 %collective-permute-done.23.refs_3_ = bf16[256,128]{1,0:T(8,128)(2,1)S(1)} collective-permute-done((bf16[256,128]{1,0:T(8,128)(2,1)S(1)}, bf16[256,128]{1,0:T(8,128)(2,1)S(1)}, u32[]{:S(2)}, u32[]{:S(2)}) %collective-permute-start.23) | collective-permute-done | bytes 65568 | tf_op jit(solution)/shard_map/ppermute | solution.py:23
  112.0 3.4 %collective-permute-start.24 = (bf16[256,128]{1,0:T(8,128)(2,1)S(1)}, bf16[256,128]{1,0:T(8,128)(2,1)S(1)}, u32[]{:S(2)}, u32[]{:S(2)}) collective-permute-start(bf16[256,128]{1,0:T(8,128)(2,1)S(1)} %get-tuple-element.88), channel_id=1, source_target_pairs={{4,0},{8,4},{12,8},{16,12},{20,16},{24,20},{28,24},{0,28},{5,1},{9... | collective-permute-start | bytes 196616 | tf_op jit(solution)/shard_map/ppermute | solution.py:23
  118.3 4.1 %collective-permute-done.22.refs_2_ = bf16[256,128]{1,0:T(8,128)(2,1)S(1)} collective-permute-done((bf16[256,128]{1,0:T(8,128)(2,1)S(1)}, bf16[256,128]{1,0:T(8,128)(2,1)S(1)}, u32[]{:S(2)}, u32[]{:S(2)}) %collective-permute-start.22) | collective-permute-done | bytes 65568 | tf_op jit(solution)/shard_map/ppermute | solution.py:23
  126.5 14.2 %collective-permute-done.26.refs_11_ = bf16[32,128,128]{2,1,0:T(8,128)(2,1)S(1)} collective-permute-done((bf16[32,128,128]{2,1,0:T(8,128)(2,1)S(1)}, bf16[32,128,128]{2,1,0:T(8,128)(2,1)S(1)}, u32[]{:S(2)}, u32[]{:S(2)}) %collective-permute-start.26) | collective-permute-done | bytes 1048608 | tf_op jit(solution)/shard_map/ppermute | solution.py:28
  143.6 6.7 %shard_map.65 = (bf16[68,256,128]{2,1,0:T(8,128)(2,1)S(1)}, bf16[68,256,128]{2,1,0:T(8,128)(2,1)S(1)}, bf16[256,128]{1,0:T(8,128)(2,1)S(1)}, bf16[256,128]{1,0:T...) custom-call(s32[1040]{0:T(1024)S(1)} %constant_dynamic-update-slice_, ...), custom_call_target="tpu_custom_call", output_to_operand_aliasing={{1}: (1, {})} | custom-call | tf_op jit(solution)/shard_map/pallas_call | solution.py:206
  150.3 2.1 %collective-permute-start.33 = (bf16[256,128]{1,0:T(8,128)(2,1)S(1)}, bf16[256,128]{1,0:T(8,128)(2,1)S(1)}, u32[]{:S(2)}, u32[]{:S(2)}) collective-permute-start(bf16[256,128]{1,0:T(8,128)(2,1)S(1)} %get-tuple-element.99), channel_id=1, source_target_pairs={{24,0},{28,4},{0,8},{4,12},{8,16},{12,20},{16,24},{20,28},{25,1},{... | collective-permute-start | bytes 196616 | tf_op jit(solution)/shard_map/ppermute | solution.py:23
  152.4 2.6 %collective-permute-start.31 = (bf16[256,128]{1,0:T(8,128)(2,1)S(1)}, bf16[256,128]{1,0:T(8,128)(2,1)S(1)}, u32[]{:S(2)}, u32[]{:S(2)}) collective-permute-start(bf16[256,128]{1,0:T(8,128)(2,1)S(1)} %get-tuple-element.97), channel_id=1, source_target_pairs={{16,0},{20,4},{24,8},{28,12},{0,16},{4,20},{8,24},{12,28},{17,1},{... | collective-permute-start | bytes 196616 | tf_op jit(solution)/shard_map/ppermute | solution.py:23
  155.0 2.0 %collective-permute-done.33.refs_3_ = bf16[256,128]{1,0:T(8,128)(2,1)S(1)} collective-permute-done((bf16[256,128]{1,0:T(8,128)(2,1)S(1)}, bf16[256,128]{1,0:T(8,128)(2,1)S(1)}, u32[]{:S(2)}, u32[]{:S(2)}) %collective-permute-start.33) | collective-permute-done | bytes 65568 | tf_op jit(solution)/shard_map/ppermute | solution.py:23
  157.0 3.4 %collective-permute-start.34 = (bf16[256,128]{1,0:T(8,128)(2,1)S(1)}, bf16[256,128]{1,0:T(8,128)(2,1)S(1)}, u32[]{:S(2)}, u32[]{:S(2)}) collective-permute-start(bf16[256,128]{1,0:T(8,128)(2,1)S(1)} %get-tuple-element.101), channel_id=1, source_target_pairs={{4,0},{8,4},{12,8},{16,12},{20,16},{24,20},{28,24},{0,28},{5,1},{9... | collective-permute-start | bytes 196616 | tf_op jit(solution)/shard_map/ppermute | solution.py:23
  170.4 4.4 %shard_map.68 = (bf16[256,8192]{1,0:T(8,128)(2,1)}, bf16[68,256,128]{2,1,0:T(8,128)(2,1)S(1)}) custom-call(s32[1040]{0:T(1024)S(1)} %constant_dynamic-update-slice_fusion.table.refs_0_, bf16[68,256,128]{2,1,0:T(8,128)(2,1)S(1)} %get-tuple-element.95.refs_1_, bf16[256,128]{1,0:T(8,128)(2,1)S(1)} %collective-permute-done.32.refs_2_, ...), custom_call_target="tpu_custom_call", output_to_operand_aliasing={{1}: (1, {})} | custom-call | tf_op jit(solution)/shard_map/pallas_call | solution.py:206
  174.8 5.3 %collective-permute-done.40.refs_4_ = bf16[20,128,128]{2,1,0:T(8,128)(2,1)S(1)} collective-permute-done((bf16[20,128,128]{2,1,0:T(8,128)(2,1)S(1)}, bf16[20,128,128]{2,1,0:T(8,128)(2,1)S(1)}, u32[]{:S(2)}, u32[]{:S(2)}) %collective-permute-start.40) | collective-permute-done | bytes 655392 | tf_op jit(solution)/shard_map/ppermute | solution.py:28
  182.3 2.9 %shard_map.69.refs_7_ = bf16[256,8192]{1,0:T(8,128)(2,1)} custom-call(s32[1040]{0:T(1024)S(1)} %constant_dynamic-update-slice_fusion.table.refs_0_, bf16[68,256,128]{2,1,0:T(8,128)(2,1)S(1)} %get-tuple-element.107.refs_1_, bf16[20,128,128]{2,1,0:T(8,128)(2,1)S(1)} %get-tuple-element.109.refs_2_, ...), custom_call_target="tpu_custom_call", output_to_operand_aliasing={{}: (10, {})} | custom-call | tf_op jit(solution)/shard_map/pallas_call | solution.py:206
  187.1 2.0 %shard_map.70 = bf16[256,8192]{1,0:T(8,128)(2,1)} custom-call(s32[1040]{0:T(1024)S(1)} %constant_dynamic-update-slice_fusion.table.refs_0_, bf16[68,256,128]{2,1,0:T(8,128)(2,1)S(1)} %get-tuple-element.107.refs_1_, bf16[8,128,128]{2,1,0:T(8,128)(2,1)S(1)} %get-tuple-element.108.refs_2_, ...), custom_call_target="tpu_custom_call", output_to_operand_aliasing={{}: (7, {})} | custom-call | tf_op jit(solution)/shard_map/pallas_call | solution.py:206
  (106 shorter events, 49.1 us)
Async XLA Ops:
  0.0 20.4 %collective-permute-start.4 = (bf16[4,64,128,128]{3,2,1,0:T(8,128)(2,1)}, bf16[4,64,128,128]{3,2,1,0:T(8,128)(2,1)}, u32[]{:S(2)}, u32[]{:S(2)}) collective-permute-start(bf16[4,64,128,128]{3,2,1,0:T(8,128)(2,1)} %tiles.9), channel_id=1, source_target_pairs={{0,1},{1,0},{2,3},{3,2},{4,5},{5,4},{6,7},{7,6},{8,9},{9,8},{10,11... | collective-permute-start | bytes 25165832 | tf_op jit(solution)/shard_map/ppermute | solution.py:28
  1.8 26.6 %collective-permute-start.5 = (bf16[32,128,128]{2,1,0:T(8,128)(2,1)S(1)}, bf16[32,128,128]{2,1,0:T(8,128)(2,1)S(1)}, u32[]{:S(2)}, u32[]{:S(2)}) collective-permute-start(bf16[32,128,128]{2,1,0:T(8,128)(2,1)S(1)} %shard_map.56.refs_6_), channel_id=1, source_target_pairs={{0,2},{1,3},{2,0},{3,1},{4,6},{5,7},{6,4},{7,5},{8,10},{9,11},{10,... | collective-permute-start | bytes 3145736 | tf_op jit(solution)/shard_map/ppermute | solution.py:28
  5.8 45.2 %collective-permute-start.6 = (bf16[32,128,128]{2,1,0:T(8,128)(2,1)S(1)}, bf16[32,128,128]{2,1,0:T(8,128)(2,1)}, u32[]{:S(2)}, u32[]{:S(2)}) collective-permute-start(bf16[32,128,128]{2,1,0:T(8,128)(2,1)S(1)} %shard_map.57.refs_7_), channel_id=1, source_target_pairs={{0,2},{1,3},{2,0},{3,1},{4,6},{5,7},{6,4},{7,5},{8,10},{9,11},{10,... | collective-permute-start | bytes 3145736 | tf_op jit(solution)/shard_map/ppermute | solution.py:28
  9.7 6.6 %collective-permute-start.2 = (bf16[256,128]{1,0:T(8,128)(2,1)S(1)}, bf16[256,128]{1,0:T(8,128)(2,1)S(1)}, u32[]{:S(2)}, u32[]{:S(2)}) collective-permute-start(bf16[256,128]{1,0:T(8,128)(2,1)S(1)} %get-tuple-element.62), channel_id=1, source_target_pairs={{24,0},{28,4},{0,8},{4,12},{8,16},{12,20},{16,24},{20,28},{25,1},{... | collective-permute-start | bytes 196616 | tf_op jit(solution)/shard_map/ppermute | solution.py:23
  11.8 7.8 %collective-permute-start = (bf16[256,128]{1,0:T(8,128)(2,1)S(1)}, bf16[256,128]{1,0:T(8,128)(2,1)S(1)}, u32[]{:S(2)}, u32[]{:S(2)}) collective-permute-start(bf16[256,128]{1,0:T(8,128)(2,1)S(1)} %get-tuple-element.60), channel_id=1, source_target_pairs={{16,0},{20,4},{24,8},{28,12},{0,16},{4,20},{8,24},{12,28},{17,1},{... | collective-permute-start | bytes 196616 | tf_op jit(solution)/shard_map/ppermute | solution.py:23
  16.3 5.9 %collective-permute-start.3 = (bf16[256,128]{1,0:T(8,128)(2,1)S(1)}, bf16[256,128]{1,0:T(8,128)(2,1)S(1)}, u32[]{:S(2)}, u32[]{:S(2)}) collective-permute-start(bf16[256,128]{1,0:T(8,128)(2,1)S(1)} %get-tuple-element.64), channel_id=1, source_target_pairs={{4,0},{8,4},{12,8},{16,12},{20,16},{24,20},{28,24},{0,28},{5,1},{9... | collective-permute-start | bytes 196616 | tf_op jit(solution)/shard_map/ppermute | solution.py:23
  19.7 7.0 %collective-permute-start.1 = (bf16[256,128]{1,0:T(8,128)(2,1)S(1)}, bf16[256,128]{1,0:T(8,128)(2,1)S(1)}, u32[]{:S(2)}, u32[]{:S(2)}) collective-permute-start(bf16[256,128]{1,0:T(8,128)(2,1)S(1)} %get-tuple-element.61), channel_id=1, source_target_pairs={{28,0},{0,4},{4,8},{8,12},{12,16},{16,20},{20,24},{24,28},{29,1},{... | collective-permute-start | bytes 196616 | tf_op jit(solution)/shard_map/ppermute | solution.py:23
  28.5 22.5 %collective-permute-start.7 = (bf16[16,128,128]{2,1,0:T(8,128)(2,1)S(1)}, bf16[16,128,128]{2,1,0:T(8,128)(2,1)S(1)}, u32[]{:S(2)}, u32[]{:S(2)}) collective-permute-start(bf16[16,128,128]{2,1,0:T(8,128)(2,1)S(1)} %get-tuple-element.126), channel_id=1, source_target_pairs={{0,1},{1,0},{2,3},{3,2},{4,5},{5,4},{6,7},{7,6},{8,9},{9,8},{10,11... | collective-permute-start | bytes 1572872 | tf_op jit(solution)/shard_map/ppermute | solution.py:28
  28.6 22.4 %collective-permute-start.8 = (bf16[16,128,128]{2,1,0:T(8,128)(2,1)S(1)}, bf16[16,128,128]{2,1,0:T(8,128)(2,1)S(1)}, u32[]{:S(2)}, u32[]{:S(2)}) collective-permute-start(bf16[16,128,128]{2,1,0:T(8,128)(2,1)S(1)} %get-tuple-element.125), channel_id=1, source_target_pairs={{0,1},{1,0},{2,3},{3,2},{4,5},{5,4},{6,7},{7,6},{8,9},{9,8},{10,11... | collective-permute-start | bytes 1572872 | tf_op jit(solution)/shard_map/ppermute | solution.py:28
  30.9 47.6 %collective-permute-start.15 = (bf16[32,128,128]{2,1,0:T(8,128)(2,1)S(1)}, bf16[32,128,128]{2,1,0:T(8,128)(2,1)S(1)}, u32[]{:S(2)}, u32[]{:S(2)}) collective-permute-start(bf16[32,128,128]{2,1,0:T(8,128)(2,1)S(1)} %get-tuple-element.76.refs_6_), channel_id=1, source_target_pairs={{0,2},{1,3},{2,0},{3,1},{4,6},{5,7},{6,4},{7,5},{8,10},{9,11},{10,... | collective-permute-start | bytes 3145736 | tf_op jit(solution)/shard_map/ppermute | solution.py:28
  52.9 43.0 %collective-permute-start.16 = (bf16[32,128,128]{2,1,0:T(8,128)(2,1)S(1)}, bf16[32,128,128]{2,1,0:T(8,128)(2,1)S(1)}, u32[]{:S(2)}, u32[]{:S(2)}) collective-permute-start(bf16[32,128,128]{2,1,0:T(8,128)(2,1)S(1)} %get-tuple-element.77.refs_7_), channel_id=1, source_target_pairs={{0,2},{1,3},{2,0},{3,1},{4,6},{5,7},{6,4},{7,5},{8,10},{9,11},{10,... | collective-permute-start | bytes 3145736 | tf_op jit(solution)/shard_map/ppermute | solution.py:28
  65.8 6.7 %collective-permute-start.13 = (bf16[256,128]{1,0:T(8,128)(2,1)S(1)}, bf16[256,128]{1,0:T(8,128)(2,1)S(1)}, u32[]{:S(2)}, u32[]{:S(2)}) collective-permute-start(bf16[256,128]{1,0:T(8,128)(2,1)S(1)} %get-tuple-element.73), channel_id=1, source_target_pairs={{24,0},{28,4},{0,8},{4,12},{8,16},{12,20},{16,24},{20,28},{25,1},{... | collective-permute-start | bytes 196616 | tf_op jit(solution)/shard_map/ppermute | solution.py:23
  67.9 8.0 %collective-permute-start.11 = (bf16[256,128]{1,0:T(8,128)(2,1)S(1)}, bf16[256,128]{1,0:T(8,128)(2,1)S(1)}, u32[]{:S(2)}, u32[]{:S(2)}) collective-permute-start(bf16[256,128]{1,0:T(8,128)(2,1)S(1)} %get-tuple-element.71), channel_id=1, source_target_pairs={{16,0},{20,4},{24,8},{28,12},{0,16},{4,20},{8,24},{12,28},{17,1},{... | collective-permute-start | bytes 196616 | tf_op jit(solution)/shard_map/ppermute | solution.py:23
  72.5 6.0 %collective-permute-start.14 = (bf16[256,128]{1,0:T(8,128)(2,1)S(1)}, bf16[256,128]{1,0:T(8,128)(2,1)S(1)}, u32[]{:S(2)}, u32[]{:S(2)}) collective-permute-start(bf16[256,128]{1,0:T(8,128)(2,1)S(1)} %get-tuple-element.75), channel_id=1, source_target_pairs={{4,0},{8,4},{12,8},{16,12},{20,16},{24,20},{28,24},{0,28},{5,1},{9... | collective-permute-start | bytes 196616 | tf_op jit(solution)/shard_map/ppermute | solution.py:23
  75.9 7.0 %collective-permute-start.12 = (bf16[256,128]{1,0:T(8,128)(2,1)S(1)}, bf16[256,128]{1,0:T(8,128)(2,1)S(1)}, u32[]{:S(2)}, u32[]{:S(2)}) collective-permute-start(bf16[256,128]{1,0:T(8,128)(2,1)S(1)} %get-tuple-element.72), channel_id=1, source_target_pairs={{28,0},{0,4},{4,8},{8,12},{12,16},{16,20},{20,24},{24,28},{29,1},{... | collective-permute-start | bytes 196616 | tf_op jit(solution)/shard_map/ppermute | solution.py:23
  83.0 12.8 %collective-permute-start.17 = (bf16[16,128,128]{2,1,0:T(8,128)(2,1)S(1)}, bf16[16,128,128]{2,1,0:T(8,128)(2,1)S(1)}, u32[]{:S(2)}, u32[]{:S(2)}) collective-permute-start(bf16[16,128,128]{2,1,0:T(8,128)(2,1)S(1)} %get-tuple-element.122), channel_id=1, source_target_pairs={{0,1},{1,0},{2,3},{3,2},{4,5},{5,4},{6,7},{7,6},{8,9},{9,8},{10,11... | collective-permute-start | bytes 1572872 | tf_op jit(solution)/shard_map/ppermute | solution.py:28
  83.1 12.8 %collective-permute-start.18 = (bf16[16,128,128]{2,1,0:T(8,128)(2,1)S(1)}, bf16[16,128,128]{2,1,0:T(8,128)(2,1)S(1)}, u32[]{:S(2)}, u32[]{:S(2)}) collective-permute-start(bf16[16,128,128]{2,1,0:T(8,128)(2,1)S(1)} %get-tuple-element.121), channel_id=1, source_target_pairs={{0,1},{1,0},{2,3},{3,2},{4,5},{5,4},{6,7},{7,6},{8,9},{9,8},{10,11... | collective-permute-start | bytes 1572872 | tf_op jit(solution)/shard_map/ppermute | solution.py:28
  85.4 32.9 %collective-permute-start.25 = (bf16[32,128,128]{2,1,0:T(8,128)(2,1)S(1)}, bf16[32,128,128]{2,1,0:T(8,128)(2,1)S(1)}, u32[]{:S(2)}, u32[]{:S(2)}) collective-permute-start(bf16[32,128,128]{2,1,0:T(8,128)(2,1)S(1)} %get-tuple-element.89.refs_6_), channel_id=1, source_target_pairs={{0,2},{1,3},{2,0},{3,1},{4,6},{5,7},{6,4},{7,5},{8,10},{9,11},{10,... | collective-permute-start | bytes 3145736 | tf_op jit(solution)/shard_map/ppermute | solution.py:28
  96.5 44.2 %collective-permute-start.26 = (bf16[32,128,128]{2,1,0:T(8,128)(2,1)S(1)}, bf16[32,128,128]{2,1,0:T(8,128)(2,1)S(1)}, u32[]{:S(2)}, u32[]{:S(2)}) collective-permute-start(bf16[32,128,128]{2,1,0:T(8,128)(2,1)S(1)} %get-tuple-element.90.refs_7_), channel_id=1, source_target_pairs={{0,2},{1,3},{2,0},{3,1},{4,6},{5,7},{6,4},{7,5},{8,10},{9,11},{10,... | collective-permute-start | bytes 3145736 | tf_op jit(solution)/shard_map/ppermute | solution.py:28
  105.4 6.7 %collective-permute-start.23 = (bf16[256,128]{1,0:T(8,128)(2,1)S(1)}, bf16[256,128]{1,0:T(8,128)(2,1)S(1)}, u32[]{:S(2)}, u32[]{:S(2)}) collective-permute-start(bf16[256,128]{1,0:T(8,128)(2,1)S(1)} %get-tuple-element.86), channel_id=1, source_target_pairs={{24,0},{28,4},{0,8},{4,12},{8,16},{12,20},{16,24},{20,28},{25,1},{... | collective-permute-start | bytes 196616 | tf_op jit(solution)/shard_map/ppermute | solution.py:23
  107.4 8.0 %collective-permute-start.21 = (bf16[256,128]{1,0:T(8,128)(2,1)S(1)}, bf16[256,128]{1,0:T(8,128)(2,1)S(1)}, u32[]{:S(2)}, u32[]{:S(2)}) collective-permute-start(bf16[256,128]{1,0:T(8,128)(2,1)S(1)} %get-tuple-element.84), channel_id=1, source_target_pairs={{16,0},{20,4},{24,8},{28,12},{0,16},{4,20},{8,24},{12,28},{17,1},{... | collective-permute-start | bytes 196616 | tf_op jit(solution)/shard_map/ppermute | solution.py:23
  112.0 6.3 %collective-permute-start.24 = (bf16[256,128]{1,0:T(8,128)(2,1)S(1)}, bf16[256,128]{1,0:T(8,128)(2,1)S(1)}, u32[]{:S(2)}, u32[]{:S(2)}) collective-permute-start(bf16[256,128]{1,0:T(8,128)(2,1)S(1)} %get-tuple-element.88), channel_id=1, source_target_pairs={{4,0},{8,4},{12,8},{16,12},{20,16},{24,20},{28,24},{0,28},{5,1},{9... | collective-permute-start | bytes 196616 | tf_op jit(solution)/shard_map/ppermute | solution.py:23
  115.4 7.0 %collective-permute-start.22 = (bf16[256,128]{1,0:T(8,128)(2,1)S(1)}, bf16[256,128]{1,0:T(8,128)(2,1)S(1)}, u32[]{:S(2)}, u32[]{:S(2)}) collective-permute-start(bf16[256,128]{1,0:T(8,128)(2,1)S(1)} %get-tuple-element.85), channel_id=1, source_target_pairs={{28,0},{0,4},{4,8},{8,12},{12,16},{16,20},{20,24},{24,28},{29,1},{... | collective-permute-start | bytes 196616 | tf_op jit(solution)/shard_map/ppermute | solution.py:23
  122.5 18.3 %collective-permute-start.27 = (bf16[16,128,128]{2,1,0:T(8,128)(2,1)S(1)}, bf16[16,128,128]{2,1,0:T(8,128)(2,1)S(1)}, u32[]{:S(2)}, u32[]{:S(2)}) collective-permute-start(bf16[16,128,128]{2,1,0:T(8,128)(2,1)S(1)} %get-tuple-element.118), channel_id=1, source_target_pairs={{0,1},{1,0},{2,3},{3,2},{4,5},{5,4},{6,7},{7,6},{8,9},{9,8},{10,11... | collective-permute-start | bytes 1572872 | tf_op jit(solution)/shard_map/ppermute | solution.py:28
  122.6 18.2 %collective-permute-start.28 = (bf16[16,128,128]{2,1,0:T(8,128)(2,1)S(1)}, bf16[16,128,128]{2,1,0:T(8,128)(2,1)S(1)}, u32[]{:S(2)}, u32[]{:S(2)}) collective-permute-start(bf16[16,128,128]{2,1,0:T(8,128)(2,1)S(1)} %get-tuple-element.117), channel_id=1, source_target_pairs={{0,1},{1,0},{2,3},{3,2},{4,5},{5,4},{6,7},{7,6},{8,9},{9,8},{10,11... | collective-permute-start | bytes 1572872 | tf_op jit(solution)/shard_map/ppermute | solution.py:28
  125.0 41.1 %collective-permute-start.35 = (bf16[36,128,128]{2,1,0:T(8,128)(2,1)S(1)}, bf16[36,128,128]{2,1,0:T(8,128)(2,1)S(1)}, u32[]{:S(2)}, u32[]{:S(2)}) collective-permute-start(bf16[36,128,128]{2,1,0:T(8,128)(2,1)S(1)} %get-tuple-element.102.refs_6_), channel_id=1, source_target_pairs={{0,2},{1,3},{2,0},{3,1},{4,6},{5,7},{6,4},{7,5},{8,10},{9,11},{10,... | collective-permute-start | bytes 3538952 | tf_op jit(solution)/shard_map/ppermute | solution.py:28
  150.3 6.7 %collective-permute-start.33 = (bf16[256,128]{1,0:T(8,128)(2,1)S(1)}, bf16[256,128]{1,0:T(8,128)(2,1)S(1)}, u32[]{:S(2)}, u32[]{:S(2)}) collective-permute-start(bf16[256,128]{1,0:T(8,128)(2,1)S(1)} %get-tuple-element.99), channel_id=1, source_target_pairs={{24,0},{28,4},{0,8},{4,12},{8,16},{12,20},{16,24},{20,28},{25,1},{... | collective-permute-start | bytes 196616 | tf_op jit(solution)/shard_map/ppermute | solution.py:23
  152.4 8.0 %collective-permute-start.31 = (bf16[256,128]{1,0:T(8,128)(2,1)S(1)}, bf16[256,128]{1,0:T(8,128)(2,1)S(1)}, u32[]{:S(2)}, u32[]{:S(2)}) collective-permute-start(bf16[256,128]{1,0:T(8,128)(2,1)S(1)} %get-tuple-element.97), channel_id=1, source_target_pairs={{16,0},{20,4},{24,8},{28,12},{0,16},{4,20},{8,24},{12,28},{17,1},{... | collective-permute-start | bytes 196616 | tf_op jit(solution)/shard_map/ppermute | solution.py:23
  157.0 9.1 %collective-permute-start.34 = (bf16[256,128]{1,0:T(8,128)(2,1)S(1)}, bf16[256,128]{1,0:T(8,128)(2,1)S(1)}, u32[]{:S(2)}, u32[]{:S(2)}) collective-permute-start(bf16[256,128]{1,0:T(8,128)(2,1)S(1)} %get-tuple-element.101), channel_id=1, source_target_pairs={{4,0},{8,4},{12,8},{16,12},{20,16},{24,20},{28,24},{0,28},{5,1},{9... | collective-permute-start | bytes 196616 | tf_op jit(solution)/shard_map/ppermute | solution.py:23
  160.4 7.0 %collective-permute-start.32 = (bf16[256,128]{1,0:T(8,128)(2,1)S(1)}, bf16[256,128]{1,0:T(8,128)(2,1)S(1)}, u32[]{:S(2)}, u32[]{:S(2)}) collective-permute-start(bf16[256,128]{1,0:T(8,128)(2,1)S(1)} %get-tuple-element.98), channel_id=1, source_target_pairs={{28,0},{0,4},{4,8},{8,12},{12,16},{16,20},{20,24},{24,28},{29,1},{... | collective-permute-start | bytes 196616 | tf_op jit(solution)/shard_map/ppermute | solution.py:23
  161.1 19.0 %collective-permute-start.40 = (bf16[20,128,128]{2,1,0:T(8,128)(2,1)S(1)}, bf16[20,128,128]{2,1,0:T(8,128)(2,1)S(1)}, u32[]{:S(2)}, u32[]{:S(2)}) collective-permute-start(bf16[20,128,128]{2,1,0:T(8,128)(2,1)S(1)} %get-tuple-element.109.refs_2_), channel_id=1, source_target_pairs={{0,2},{1,3},{2,0},{3,1},{4,6},{5,7},{6,4},{7,5},{8,10},{9,11},{10,... | collective-permute-start | bytes 1966088 | tf_op jit(solution)/shard_map/ppermute | solution.py:28
  168.2 17.4 %collective-permute-start.39 = (bf16[8,128,128]{2,1,0:T(8,128)(2,1)S(1)}, bf16[8,128,128]{2,1,0:T(8,128)(2,1)S(1)}, u32[]{:S(2)}, u32[]{:S(2)}) collective-permute-start(bf16[8,128,128]{2,1,0:T(8,128)(2,1)S(1)} %get-tuple-element.108.refs_2_), channel_id=1, source_target_pairs={{0,2},{1,3},{2,0},{3,1},{4,6},{5,7},{6,4},{7,5},{8,10},{9,11},{10,... | collective-permute-start | bytes 786440 | tf_op jit(solution)/shard_map/ppermute | solution.py:28
  (18 other events, 75.9 us)

commit v15 on v14

--- a/solution.py
+++ b/solution.py
@@ -10,7 +10,7 @@
 
 TURNS = (3, 1, 0, 2)
 BOUNDARY = 2
-CUTS = 16
+CUTS = 8
 NEIGH = 4
 VMEM_LIMIT = 16 * 2**20
 LAYER_LIMIT = 20 * 2**20

time: 190 us -> 190 us (level)
  transfers between devices with their start and end apart: 46 -> 46, of which waited for: 25 -> 25; matrix products, arithmetic and copies ran while one was open for 2% -> 2% of each run, Pallas kernels for 26% -> 25%
where the time goes in v15:
time: 190 us; the launch traced here: 189 us
  waiting for transfers between devices  79.2 us (42%)
  starting transfers between devices  55.6 us (29%)
  Pallas kernels  49.7 us (26%)
  local copies, waits for them, and re-layouts  3.32 us (2%)
    ppermute x30, waiting for transfers between devices, swapped(): return lax.ppermute(block, 'batch', route)  56.9 us
    ppermute x16, starting transfers between devices, shifted(): return lax.ppermute(block, axis, route)  35.2 us
    pallas_call x6, Pallas kernels, run_blocks(): pl.pallas_call(kernel, out_shape=out_shape, grid_spec=pltpu.PrefetchScala...  33.5 us
    ppermute x16, waiting for transfers between devices, shifted(): return lax.ppermute(block, axis, route)  22.3 us
    ppermute x30, starting transfers between devices, swapped(): return lax.ppermute(block, 'batch', route)  20.4 us
    pallas_call x9, Pallas kernels, cut(): pl.pallas_call(kernel, out_shape=[pltpu.VMEM((count, height, width), tile...  14.6 us
  transfers between devices with their start and end apart: 46, of which 25 were waited for; matrix products, arithmetic and copies ran while one was open for 2% of the time, Pallas kernels for 25%

profile of v15, /device:TPU:0, one launch (start us, length us, event | category | flops | bytes accessed | tf_op | source)
XLA Modules:
  0.0 189.2 jit_solution(12116785488379239589)
XLA Ops:
  1.8 2.6 %collective-permute-start.5 = (bf16[32,128,128]{2,1,0:T(8,128)(2,1)S(1)}, bf16[32,128,128]{2,1,0:T(8,128)(2,1)S(1)}, u32[]{:S(2)}, u32[]{:S(2)}) collective-permute-start(bf16[32,128,128]{2,1,0:T(8,128)(2,1)S(1)} %shard_map.56.refs_6_), channel_id=1, source_target_pairs={{0,2},{1,3},{2,0},{3,1},{4,6},{5,7},{6,4},{7,5},{8,10},{9,11},{10,... | collective-permute-start | bytes 3145736 | tf_op jit(solution)/shard_map/ppermute | solution.py:28
  9.7 2.1 %collective-permute-start.2 = (bf16[256,128]{1,0:T(8,128)(2,1)S(1)}, bf16[256,128]{1,0:T(8,128)(2,1)S(1)}, u32[]{:S(2)}, u32[]{:S(2)}) collective-permute-start(bf16[256,128]{1,0:T(8,128)(2,1)S(1)} %get-tuple-element.62), channel_id=1, source_target_pairs={{24,0},{28,4},{0,8},{4,12},{8,16},{12,20},{16,24},{20,28},{25,1},{... | collective-permute-start | bytes 196616 | tf_op jit(solution)/shard_map/ppermute | solution.py:23
  11.8 2.6 %collective-permute-start = (bf16[256,128]{1,0:T(8,128)(2,1)S(1)}, bf16[256,128]{1,0:T(8,128)(2,1)S(1)}, u32[]{:S(2)}, u32[]{:S(2)}) collective-permute-start(bf16[256,128]{1,0:T(8,128)(2,1)S(1)} %get-tuple-element.60), channel_id=1, source_target_pairs={{16,0},{20,4},{24,8},{28,12},{0,16},{4,20},{8,24},{12,28},{17,1},{... | collective-permute-start | bytes 196616 | tf_op jit(solution)/shard_map/ppermute | solution.py:23
  16.3 3.3 %collective-permute-start.3 = (bf16[256,128]{1,0:T(8,128)(2,1)S(1)}, bf16[256,128]{1,0:T(8,128)(2,1)S(1)}, u32[]{:S(2)}, u32[]{:S(2)}) collective-permute-start(bf16[256,128]{1,0:T(8,128)(2,1)S(1)} %get-tuple-element.64), channel_id=1, source_target_pairs={{4,0},{8,4},{12,8},{16,12},{20,16},{24,20},{28,24},{0,28},{5,1},{9... | collective-permute-start | bytes 196616 | tf_op jit(solution)/shard_map/ppermute | solution.py:23
  22.1 4.5 %collective-permute-done.1.refs_2_ = bf16[256,128]{1,0:T(8,128)(2,1)S(1)} collective-permute-done((bf16[256,128]{1,0:T(8,128)(2,1)S(1)}, bf16[256,128]{1,0:T(8,128)(2,1)S(1)}, u32[]{:S(2)}, u32[]{:S(2)}) %collective-permute-start.1) | collective-permute-done | bytes 65568 | tf_op jit(solution)/shard_map/ppermute | solution.py:23
  30.8 2.0 %collective-permute-start.15 = (bf16[32,128,128]{2,1,0:T(8,128)(2,1)S(1)}, bf16[32,128,128]{2,1,0:T(8,128)(2,1)S(1)}, u32[]{:S(2)}, u32[]{:S(2)}) collective-permute-start(bf16[32,128,128]{2,1,0:T(8,128)(2,1)S(1)} %get-tuple-element.76.refs_6_), channel_id=1, source_target_pairs={{0,2},{1,3},{2,0},{3,1},{4,6},{5,7},{6,4},{7,5},{8,10},{9,11},{10,... | collective-permute-start | bytes 3145736 | tf_op jit(solution)/shard_map/ppermute | solution.py:28
  32.8 18.2 %collective-permute-done.6.refs_11_ = bf16[32,128,128]{2,1,0:T(8,128)(2,1)} collective-permute-done((bf16[32,128,128]{2,1,0:T(8,128)(2,1)S(1)}, bf16[32,128,128]{2,1,0:T(8,128)(2,1)}, u32[]{:S(2)}, u32[]{:S(2)}) %collective-permute-start.6) | collective-permute-done | bytes 1048608 | tf_op jit(solution)/shard_map/ppermute | solution.py:28
  52.8 1.9 %collective-permute-start.16 = (bf16[32,128,128]{2,1,0:T(8,128)(2,1)S(1)}, bf16[32,128,128]{2,1,0:T(8,128)(2,1)S(1)}, u32[]{:S(2)}, u32[]{:S(2)}) collective-permute-start(bf16[32,128,128]{2,1,0:T(8,128)(2,1)S(1)} %get-tuple-element.77.refs_7_), channel_id=1, source_target_pairs={{0,2},{1,3},{2,0},{3,1},{4,6},{5,7},{6,4},{7,5},{8,10},{9,11},{10,... | collective-permute-start | bytes 3145736 | tf_op jit(solution)/shard_map/ppermute | solution.py:28
  55.0 10.8 %shard_map.59 = (bf16[68,256,128]{2,1,0:T(8,128)(2,1)S(1)}, bf16[256,128]{1,0:T(8,128)(2,1)S(1)}, bf16[256,128]{1,0:T(8,128)(2,1)S(1)}, bf16[256,128]{1,0:T(8,128)(2,1)S(1)}, bf16[256,128]{1,0:T(8,128)(2,1)S(1)}) custom-call(s32[1040]{0:T(1024)S(1)} %constant_dynamic-update-slice_fusion.table.refs_0_, bf16[256,8192]{1,0:T(8,128)(2,1)} %refs_1_.1, ...), custom_call_target="tpu_custom_call" | custom-call | tf_op jit(solution)/shard_map/pallas_call | solution.py:206
  65.8 2.1 %collective-permute-start.13 = (bf16[256,128]{1,0:T(8,128)(2,1)S(1)}, bf16[256,128]{1,0:T(8,128)(2,1)S(1)}, u32[]{:S(2)}, u32[]{:S(2)}) collective-permute-start(bf16[256,128]{1,0:T(8,128)(2,1)S(1)} %get-tuple-element.73), channel_id=1, source_target_pairs={{24,0},{28,4},{0,8},{4,12},{8,16},{12,20},{16,24},{20,28},{25,1},{... | collective-permute-start | bytes 196616 | tf_op jit(solution)/shard_map/ppermute | solution.py:23
  67.9 2.6 %collective-permute-start.11 = (bf16[256,128]{1,0:T(8,128)(2,1)S(1)}, bf16[256,128]{1,0:T(8,128)(2,1)S(1)}, u32[]{:S(2)}, u32[]{:S(2)}) collective-permute-start(bf16[256,128]{1,0:T(8,128)(2,1)S(1)} %get-tuple-element.71), channel_id=1, source_target_pairs={{16,0},{20,4},{24,8},{28,12},{0,16},{4,20},{8,24},{12,28},{17,1},{... | collective-permute-start | bytes 196616 | tf_op jit(solution)/shard_map/ppermute | solution.py:23
  70.5 2.0 %collective-permute-done.13.refs_3_ = bf16[256,128]{1,0:T(8,128)(2,1)S(1)} collective-permute-done((bf16[256,128]{1,0:T(8,128)(2,1)S(1)}, bf16[256,128]{1,0:T(8,128)(2,1)S(1)}, u32[]{:S(2)}, u32[]{:S(2)}) %collective-permute-start.13) | collective-permute-done | bytes 65568 | tf_op jit(solution)/shard_map/ppermute | solution.py:23
  72.5 3.4 %collective-permute-start.14 = (bf16[256,128]{1,0:T(8,128)(2,1)S(1)}, bf16[256,128]{1,0:T(8,128)(2,1)S(1)}, u32[]{:S(2)}, u32[]{:S(2)}) collective-permute-start(bf16[256,128]{1,0:T(8,128)(2,1)S(1)} %get-tuple-element.75), channel_id=1, source_target_pairs={{4,0},{8,4},{12,8},{16,12},{20,16},{24,20},{28,24},{0,28},{5,1},{9... | collective-permute-start | bytes 196616 | tf_op jit(solution)/shard_map/ppermute | solution.py:23
  78.4 4.5 %collective-permute-done.12.refs_2_ = bf16[256,128]{1,0:T(8,128)(2,1)S(1)} collective-permute-done((bf16[256,128]{1,0:T(8,128)(2,1)S(1)}, bf16[256,128]{1,0:T(8,128)(2,1)S(1)}, u32[]{:S(2)}, u32[]{:S(2)}) %collective-permute-start.12) | collective-permute-done | bytes 65568 | tf_op jit(solution)/shard_map/ppermute | solution.py:23
  86.9 8.9 %collective-permute-done.16.refs_11_ = bf16[32,128,128]{2,1,0:T(8,128)(2,1)S(1)} collective-permute-done((bf16[32,128,128]{2,1,0:T(8,128)(2,1)S(1)}, bf16[32,128,128]{2,1,0:T(8,128)(2,1)S(1)}, u32[]{:S(2)}, u32[]{:S(2)}) %collective-permute-start.16) | collective-permute-done | bytes 1048608 | tf_op jit(solution)/shard_map/ppermute | solution.py:28
  96.5 1.9 %collective-permute-start.26 = (bf16[32,128,128]{2,1,0:T(8,128)(2,1)S(1)}, bf16[32,128,128]{2,1,0:T(8,128)(2,1)S(1)}, u32[]{:S(2)}, u32[]{:S(2)}) collective-permute-start(bf16[32,128,128]{2,1,0:T(8,128)(2,1)S(1)} %get-tuple-element.90.refs_7_), channel_id=1, source_target_pairs={{0,2},{1,3},{2,0},{3,1},{4,6},{5,7},{6,4},{7,5},{8,10},{9,11},{10,... | collective-permute-start | bytes 3145736 | tf_op jit(solution)/shard_map/ppermute | solution.py:28
  98.7 6.7 %shard_map.62 = (bf16[68,256,128]{2,1,0:T(8,128)(2,1)S(1)}, bf16[68,256,128]{2,1,0:T(8,128)(2,1)S(1)}, bf16[256,128]{1,0:T(8,128)(2,1)S(1)}, bf16[256,128]{1,0:T...) custom-call(s32[1040]{0:T(1024)S(1)} %constant_dynamic-update-slice_, ...), custom_call_target="tpu_custom_call", output_to_operand_aliasing={{1}: (1, {})} | custom-call | tf_op jit(solution)/shard_map/pallas_call | solution.py:206
  105.3 2.1 %collective-permute-start.23 = (bf16[256,128]{1,0:T(8,128)(2,1)S(1)}, bf16[256,128]{1,0:T(8,128)(2,1)S(1)}, u32[]{:S(2)}, u32[]{:S(2)}) collective-permute-start(bf16[256,128]{1,0:T(8,128)(2,1)S(1)} %get-tuple-element.86), channel_id=1, source_target_pairs={{24,0},{28,4},{0,8},{4,12},{8,16},{12,20},{16,24},{20,28},{25,1},{... | collective-permute-start | bytes 196616 | tf_op jit(solution)/shard_map/ppermute | solution.py:23
  107.4 2.6 %collective-permute-start.21 = (bf16[256,128]{1,0:T(8,128)(2,1)S(1)}, bf16[256,128]{1,0:T(8,128)(2,1)S(1)}, u32[]{:S(2)}, u32[]{:S(2)}) collective-permute-start(bf16[256,128]{1,0:T(8,128)(2,1)S(1)} %get-tuple-element.84), channel_id=1, source_target_pairs={{16,0},{20,4},{24,8},{28,12},{0,16},{4,20},{8,24},{12,28},{17,1},{... | collective-permute-start | bytes 196616 | tf_op jit(solution)/shard_map/ppermute | solution.py:23
  110.0 2.0 %collective-permute-done.23.refs_3_ = bf16[256,128]{1,0:T(8,128)(2,1)S(1)} collective-permute-done((bf16[256,128]{1,0:T(8,128)(2,1)S(1)}, bf16[256,128]{1,0:T(8,128)(2,1)S(1)}, u32[]{:S(2)}, u32[]{:S(2)}) %collective-permute-start.23) | collective-permute-done | bytes 65568 | tf_op jit(solution)/shard_map/ppermute | solution.py:23
  112.0 3.4 %collective-permute-start.24 = (bf16[256,128]{1,0:T(8,128)(2,1)S(1)}, bf16[256,128]{1,0:T(8,128)(2,1)S(1)}, u32[]{:S(2)}, u32[]{:S(2)}) collective-permute-start(bf16[256,128]{1,0:T(8,128)(2,1)S(1)} %get-tuple-element.88), channel_id=1, source_target_pairs={{4,0},{8,4},{12,8},{16,12},{20,16},{24,20},{28,24},{0,28},{5,1},{9... | collective-permute-start | bytes 196616 | tf_op jit(solution)/shard_map/ppermute | solution.py:23
  118.3 4.1 %collective-permute-done.22.refs_2_ = bf16[256,128]{1,0:T(8,128)(2,1)S(1)} collective-permute-done((bf16[256,128]{1,0:T(8,128)(2,1)S(1)}, bf16[256,128]{1,0:T(8,128)(2,1)S(1)}, u32[]{:S(2)}, u32[]{:S(2)}) %collective-permute-start.22) | collective-permute-done | bytes 65568 | tf_op jit(solution)/shard_map/ppermute | solution.py:23
  126.3 14.5 %collective-permute-done.26.refs_11_ = bf16[32,128,128]{2,1,0:T(8,128)(2,1)S(1)} collective-permute-done((bf16[32,128,128]{2,1,0:T(8,128)(2,1)S(1)}, bf16[32,128,128]{2,1,0:T(8,128)(2,1)S(1)}, u32[]{:S(2)}, u32[]{:S(2)}) %collective-permute-start.26) | collective-permute-done | bytes 1048608 | tf_op jit(solution)/shard_map/ppermute | solution.py:28
  143.6 6.7 %shard_map.65 = (bf16[68,256,128]{2,1,0:T(8,128)(2,1)S(1)}, bf16[68,256,128]{2,1,0:T(8,128)(2,1)S(1)}, bf16[256,128]{1,0:T(8,128)(2,1)S(1)}, bf16[256,128]{1,0:T...) custom-call(s32[1040]{0:T(1024)S(1)} %constant_dynamic-update-slice_, ...), custom_call_target="tpu_custom_call", output_to_operand_aliasing={{1}: (1, {})} | custom-call | tf_op jit(solution)/shard_map/pallas_call | solution.py:206
  150.3 2.1 %collective-permute-start.33 = (bf16[256,128]{1,0:T(8,128)(2,1)S(1)}, bf16[256,128]{1,0:T(8,128)(2,1)S(1)}, u32[]{:S(2)}, u32[]{:S(2)}) collective-permute-start(bf16[256,128]{1,0:T(8,128)(2,1)S(1)} %get-tuple-element.99), channel_id=1, source_target_pairs={{24,0},{28,4},{0,8},{4,12},{8,16},{12,20},{16,24},{20,28},{25,1},{... | collective-permute-start | bytes 196616 | tf_op jit(solution)/shard_map/ppermute | solution.py:23
  152.4 2.6 %collective-permute-start.31 = (bf16[256,128]{1,0:T(8,128)(2,1)S(1)}, bf16[256,128]{1,0:T(8,128)(2,1)S(1)}, u32[]{:S(2)}, u32[]{:S(2)}) collective-permute-start(bf16[256,128]{1,0:T(8,128)(2,1)S(1)} %get-tuple-element.97), channel_id=1, source_target_pairs={{16,0},{20,4},{24,8},{28,12},{0,16},{4,20},{8,24},{12,28},{17,1},{... | collective-permute-start | bytes 196616 | tf_op jit(solution)/shard_map/ppermute | solution.py:23
  155.0 2.0 %collective-permute-done.33.refs_3_ = bf16[256,128]{1,0:T(8,128)(2,1)S(1)} collective-permute-done((bf16[256,128]{1,0:T(8,128)(2,1)S(1)}, bf16[256,128]{1,0:T(8,128)(2,1)S(1)}, u32[]{:S(2)}, u32[]{:S(2)}) %collective-permute-start.33) | collective-permute-done | bytes 65568 | tf_op jit(solution)/shard_map/ppermute | solution.py:23
  157.0 3.4 %collective-permute-start.34 = (bf16[256,128]{1,0:T(8,128)(2,1)S(1)}, bf16[256,128]{1,0:T(8,128)(2,1)S(1)}, u32[]{:S(2)}, u32[]{:S(2)}) collective-permute-start(bf16[256,128]{1,0:T(8,128)(2,1)S(1)} %get-tuple-element.101), channel_id=1, source_target_pairs={{4,0},{8,4},{12,8},{16,12},{20,16},{24,20},{28,24},{0,28},{5,1},{9... | collective-permute-start | bytes 196616 | tf_op jit(solution)/shard_map/ppermute | solution.py:23
  170.3 4.4 %shard_map.68 = (bf16[256,8192]{1,0:T(8,128)(2,1)}, bf16[68,256,128]{2,1,0:T(8,128)(2,1)S(1)}) custom-call(s32[1040]{0:T(1024)S(1)} %constant_dynamic-update-slice_fusion.table.refs_0_, bf16[68,256,128]{2,1,0:T(8,128)(2,1)S(1)} %get-tuple-element.95.refs_1_, bf16[256,128]{1,0:T(8,128)(2,1)S(1)} %collective-permute-done.32.refs_2_, ...), custom_call_target="tpu_custom_call", output_to_operand_aliasing={{1}: (1, {})} | custom-call | tf_op jit(solution)/shard_map/pallas_call | solution.py:206
  174.8 5.3 %collective-permute-done.40.refs_4_ = bf16[20,128,128]{2,1,0:T(8,128)(2,1)S(1)} collective-permute-done((bf16[20,128,128]{2,1,0:T(8,128)(2,1)S(1)}, bf16[20,128,128]{2,1,0:T(8,128)(2,1)S(1)}, u32[]{:S(2)}, u32[]{:S(2)}) %collective-permute-start.40) | collective-permute-done | bytes 655392 | tf_op jit(solution)/shard_map/ppermute | solution.py:28
  182.3 2.9 %shard_map.69.refs_7_ = bf16[256,8192]{1,0:T(8,128)(2,1)} custom-call(s32[1040]{0:T(1024)S(1)} %constant_dynamic-update-slice_fusion.table.refs_0_, bf16[68,256,128]{2,1,0:T(8,128)(2,1)S(1)} %get-tuple-element.107.refs_1_, bf16[20,128,128]{2,1,0:T(8,128)(2,1)S(1)} %get-tuple-element.109.refs_2_, ...), custom_call_target="tpu_custom_call", output_to_operand_aliasing={{}: (10, {})} | custom-call | tf_op jit(solution)/shard_map/pallas_call | solution.py:206
  187.0 2.0 %shard_map.70 = bf16[256,8192]{1,0:T(8,128)(2,1)} custom-call(s32[1040]{0:T(1024)S(1)} %constant_dynamic-update-slice_fusion.table.refs_0_, bf16[68,256,128]{2,1,0:T(8,128)(2,1)S(1)} %get-tuple-element.107.refs_1_, bf16[8,128,128]{2,1,0:T(8,128)(2,1)S(1)} %get-tuple-element.108.refs_2_, ...), custom_call_target="tpu_custom_call", output_to_operand_aliasing={{}: (7, {})} | custom-call | tf_op jit(solution)/shard_map/pallas_call | solution.py:206
  (106 shorter events, 48.4 us)
Async XLA Ops:
  0.0 20.3 %collective-permute-start.4 = (bf16[4,64,128,128]{3,2,1,0:T(8,128)(2,1)}, bf16[4,64,128,128]{3,2,1,0:T(8,128)(2,1)}, u32[]{:S(2)}, u32[]{:S(2)}) collective-permute-start(bf16[4,64,128,128]{3,2,1,0:T(8,128)(2,1)} %tiles.9), channel_id=1, source_target_pairs={{0,1},{1,0},{2,3},{3,2},{4,5},{5,4},{6,7},{7,6},{8,9},{9,8},{10,11... | collective-permute-start | bytes 25165832 | tf_op jit(solution)/shard_map/ppermute | solution.py:28
  1.8 26.6 %collective-permute-start.5 = (bf16[32,128,128]{2,1,0:T(8,128)(2,1)S(1)}, bf16[32,128,128]{2,1,0:T(8,128)(2,1)S(1)}, u32[]{:S(2)}, u32[]{:S(2)}) collective-permute-start(bf16[32,128,128]{2,1,0:T(8,128)(2,1)S(1)} %shard_map.56.refs_6_), channel_id=1, source_target_pairs={{0,2},{1,3},{2,0},{3,1},{4,6},{5,7},{6,4},{7,5},{8,10},{9,11},{10,... | collective-permute-start | bytes 3145736 | tf_op jit(solution)/shard_map/ppermute | solution.py:28
  5.7 45.2 %collective-permute-start.6 = (bf16[32,128,128]{2,1,0:T(8,128)(2,1)S(1)}, bf16[32,128,128]{2,1,0:T(8,128)(2,1)}, u32[]{:S(2)}, u32[]{:S(2)}) collective-permute-start(bf16[32,128,128]{2,1,0:T(8,128)(2,1)S(1)} %shard_map.57.refs_7_), channel_id=1, source_target_pairs={{0,2},{1,3},{2,0},{3,1},{4,6},{5,7},{6,4},{7,5},{8,10},{9,11},{10,... | collective-permute-start | bytes 3145736 | tf_op jit(solution)/shard_map/ppermute | solution.py:28
  9.7 6.6 %collective-permute-start.2 = (bf16[256,128]{1,0:T(8,128)(2,1)S(1)}, bf16[256,128]{1,0:T(8,128)(2,1)S(1)}, u32[]{:S(2)}, u32[]{:S(2)}) collective-permute-start(bf16[256,128]{1,0:T(8,128)(2,1)S(1)} %get-tuple-element.62), channel_id=1, source_target_pairs={{24,0},{28,4},{0,8},{4,12},{8,16},{12,20},{16,24},{20,28},{25,1},{... | collective-permute-start | bytes 196616 | tf_op jit(solution)/shard_map/ppermute | solution.py:23
  11.8 7.8 %collective-permute-start = (bf16[256,128]{1,0:T(8,128)(2,1)S(1)}, bf16[256,128]{1,0:T(8,128)(2,1)S(1)}, u32[]{:S(2)}, u32[]{:S(2)}) collective-permute-start(bf16[256,128]{1,0:T(8,128)(2,1)S(1)} %get-tuple-element.60), channel_id=1, source_target_pairs={{16,0},{20,4},{24,8},{28,12},{0,16},{4,20},{8,24},{12,28},{17,1},{... | collective-permute-start | bytes 196616 | tf_op jit(solution)/shard_map/ppermute | solution.py:23
  16.3 5.8 %collective-permute-start.3 = (bf16[256,128]{1,0:T(8,128)(2,1)S(1)}, bf16[256,128]{1,0:T(8,128)(2,1)S(1)}, u32[]{:S(2)}, u32[]{:S(2)}) collective-permute-start(bf16[256,128]{1,0:T(8,128)(2,1)S(1)} %get-tuple-element.64), channel_id=1, source_target_pairs={{4,0},{8,4},{12,8},{16,12},{20,16},{24,20},{28,24},{0,28},{5,1},{9... | collective-permute-start | bytes 196616 | tf_op jit(solution)/shard_map/ppermute | solution.py:23
  19.6 7.0 %collective-permute-start.1 = (bf16[256,128]{1,0:T(8,128)(2,1)S(1)}, bf16[256,128]{1,0:T(8,128)(2,1)S(1)}, u32[]{:S(2)}, u32[]{:S(2)}) collective-permute-start(bf16[256,128]{1,0:T(8,128)(2,1)S(1)} %get-tuple-element.61), channel_id=1, source_target_pairs={{28,0},{0,4},{4,8},{8,12},{12,16},{16,20},{20,24},{24,28},{29,1},{... | collective-permute-start | bytes 196616 | tf_op jit(solution)/shard_map/ppermute | solution.py:23
  28.5 22.5 %collective-permute-start.7 = (bf16[16,128,128]{2,1,0:T(8,128)(2,1)S(1)}, bf16[16,128,128]{2,1,0:T(8,128)(2,1)S(1)}, u32[]{:S(2)}, u32[]{:S(2)}) collective-permute-start(bf16[16,128,128]{2,1,0:T(8,128)(2,1)S(1)} %get-tuple-element.126), channel_id=1, source_target_pairs={{0,1},{1,0},{2,3},{3,2},{4,5},{5,4},{6,7},{7,6},{8,9},{9,8},{10,11... | collective-permute-start | bytes 1572872 | tf_op jit(solution)/shard_map/ppermute | solution.py:28
  28.6 22.4 %collective-permute-start.8 = (bf16[16,128,128]{2,1,0:T(8,128)(2,1)S(1)}, bf16[16,128,128]{2,1,0:T(8,128)(2,1)S(1)}, u32[]{:S(2)}, u32[]{:S(2)}) collective-permute-start(bf16[16,128,128]{2,1,0:T(8,128)(2,1)S(1)} %get-tuple-element.125), channel_id=1, source_target_pairs={{0,1},{1,0},{2,3},{3,2},{4,5},{5,4},{6,7},{7,6},{8,9},{9,8},{10,11... | collective-permute-start | bytes 1572872 | tf_op jit(solution)/shard_map/ppermute | solution.py:28
  30.8 47.6 %collective-permute-start.15 = (bf16[32,128,128]{2,1,0:T(8,128)(2,1)S(1)}, bf16[32,128,128]{2,1,0:T(8,128)(2,1)S(1)}, u32[]{:S(2)}, u32[]{:S(2)}) collective-permute-start(bf16[32,128,128]{2,1,0:T(8,128)(2,1)S(1)} %get-tuple-element.76.refs_6_), channel_id=1, source_target_pairs={{0,2},{1,3},{2,0},{3,1},{4,6},{5,7},{6,4},{7,5},{8,10},{9,11},{10,... | collective-permute-start | bytes 3145736 | tf_op jit(solution)/shard_map/ppermute | solution.py:28
  52.8 43.0 %collective-permute-start.16 = (bf16[32,128,128]{2,1,0:T(8,128)(2,1)S(1)}, bf16[32,128,128]{2,1,0:T(8,128)(2,1)S(1)}, u32[]{:S(2)}, u32[]{:S(2)}) collective-permute-start(bf16[32,128,128]{2,1,0:T(8,128)(2,1)S(1)} %get-tuple-element.77.refs_7_), channel_id=1, source_target_pairs={{0,2},{1,3},{2,0},{3,1},{4,6},{5,7},{6,4},{7,5},{8,10},{9,11},{10,... | collective-permute-start | bytes 3145736 | tf_op jit(solution)/shard_map/ppermute | solution.py:28
  65.8 6.7 %collective-permute-start.13 = (bf16[256,128]{1,0:T(8,128)(2,1)S(1)}, bf16[256,128]{1,0:T(8,128)(2,1)S(1)}, u32[]{:S(2)}, u32[]{:S(2)}) collective-permute-start(bf16[256,128]{1,0:T(8,128)(2,1)S(1)} %get-tuple-element.73), channel_id=1, source_target_pairs={{24,0},{28,4},{0,8},{4,12},{8,16},{12,20},{16,24},{20,28},{25,1},{... | collective-permute-start | bytes 196616 | tf_op jit(solution)/shard_map/ppermute | solution.py:23
  67.9 8.0 %collective-permute-start.11 = (bf16[256,128]{1,0:T(8,128)(2,1)S(1)}, bf16[256,128]{1,0:T(8,128)(2,1)S(1)}, u32[]{:S(2)}, u32[]{:S(2)}) collective-permute-start(bf16[256,128]{1,0:T(8,128)(2,1)S(1)} %get-tuple-element.71), channel_id=1, source_target_pairs={{16,0},{20,4},{24,8},{28,12},{0,16},{4,20},{8,24},{12,28},{17,1},{... | collective-permute-start | bytes 196616 | tf_op jit(solution)/shard_map/ppermute | solution.py:23
  72.5 5.9 %collective-permute-start.14 = (bf16[256,128]{1,0:T(8,128)(2,1)S(1)}, bf16[256,128]{1,0:T(8,128)(2,1)S(1)}, u32[]{:S(2)}, u32[]{:S(2)}) collective-permute-start(bf16[256,128]{1,0:T(8,128)(2,1)S(1)} %get-tuple-element.75), channel_id=1, source_target_pairs={{4,0},{8,4},{12,8},{16,12},{20,16},{24,20},{28,24},{0,28},{5,1},{9... | collective-permute-start | bytes 196616 | tf_op jit(solution)/shard_map/ppermute | solution.py:23
  75.9 7.0 %collective-permute-start.12 = (bf16[256,128]{1,0:T(8,128)(2,1)S(1)}, bf16[256,128]{1,0:T(8,128)(2,1)S(1)}, u32[]{:S(2)}, u32[]{:S(2)}) collective-permute-start(bf16[256,128]{1,0:T(8,128)(2,1)S(1)} %get-tuple-element.72), channel_id=1, source_target_pairs={{28,0},{0,4},{4,8},{8,12},{12,16},{16,20},{20,24},{24,28},{29,1},{... | collective-permute-start | bytes 196616 | tf_op jit(solution)/shard_map/ppermute | solution.py:23
  83.0 12.8 %collective-permute-start.17 = (bf16[16,128,128]{2,1,0:T(8,128)(2,1)S(1)}, bf16[16,128,128]{2,1,0:T(8,128)(2,1)S(1)}, u32[]{:S(2)}, u32[]{:S(2)}) collective-permute-start(bf16[16,128,128]{2,1,0:T(8,128)(2,1)S(1)} %get-tuple-element.122), channel_id=1, source_target_pairs={{0,1},{1,0},{2,3},{3,2},{4,5},{5,4},{6,7},{7,6},{8,9},{9,8},{10,11... | collective-permute-start | bytes 1572872 | tf_op jit(solution)/shard_map/ppermute | solution.py:28
  83.1 12.7 %collective-permute-start.18 = (bf16[16,128,128]{2,1,0:T(8,128)(2,1)S(1)}, bf16[16,128,128]{2,1,0:T(8,128)(2,1)S(1)}, u32[]{:S(2)}, u32[]{:S(2)}) collective-permute-start(bf16[16,128,128]{2,1,0:T(8,128)(2,1)S(1)} %get-tuple-element.121), channel_id=1, source_target_pairs={{0,1},{1,0},{2,3},{3,2},{4,5},{5,4},{6,7},{7,6},{8,9},{9,8},{10,11... | collective-permute-start | bytes 1572872 | tf_op jit(solution)/shard_map/ppermute | solution.py:28
  85.3 33.0 %collective-permute-start.25 = (bf16[32,128,128]{2,1,0:T(8,128)(2,1)S(1)}, bf16[32,128,128]{2,1,0:T(8,128)(2,1)S(1)}, u32[]{:S(2)}, u32[]{:S(2)}) collective-permute-start(bf16[32,128,128]{2,1,0:T(8,128)(2,1)S(1)} %get-tuple-element.89.refs_6_), channel_id=1, source_target_pairs={{0,2},{1,3},{2,0},{3,1},{4,6},{5,7},{6,4},{7,5},{8,10},{9,11},{10,... | collective-permute-start | bytes 3145736 | tf_op jit(solution)/shard_map/ppermute | solution.py:28
  96.5 44.2 %collective-permute-start.26 = (bf16[32,128,128]{2,1,0:T(8,128)(2,1)S(1)}, bf16[32,128,128]{2,1,0:T(8,128)(2,1)S(1)}, u32[]{:S(2)}, u32[]{:S(2)}) collective-permute-start(bf16[32,128,128]{2,1,0:T(8,128)(2,1)S(1)} %get-tuple-element.90.refs_7_), channel_id=1, source_target_pairs={{0,2},{1,3},{2,0},{3,1},{4,6},{5,7},{6,4},{7,5},{8,10},{9,11},{10,... | collective-permute-start | bytes 3145736 | tf_op jit(solution)/shard_map/ppermute | solution.py:28
  105.3 6.7 %collective-permute-start.23 = (bf16[256,128]{1,0:T(8,128)(2,1)S(1)}, bf16[256,128]{1,0:T(8,128)(2,1)S(1)}, u32[]{:S(2)}, u32[]{:S(2)}) collective-permute-start(bf16[256,128]{1,0:T(8,128)(2,1)S(1)} %get-tuple-element.86), channel_id=1, source_target_pairs={{24,0},{28,4},{0,8},{4,12},{8,16},{12,20},{16,24},{20,28},{25,1},{... | collective-permute-start | bytes 196616 | tf_op jit(solution)/shard_map/ppermute | solution.py:23
  107.4 8.0 %collective-permute-start.21 = (bf16[256,128]{1,0:T(8,128)(2,1)S(1)}, bf16[256,128]{1,0:T(8,128)(2,1)S(1)}, u32[]{:S(2)}, u32[]{:S(2)}) collective-permute-start(bf16[256,128]{1,0:T(8,128)(2,1)S(1)} %get-tuple-element.84), channel_id=1, source_target_pairs={{16,0},{20,4},{24,8},{28,12},{0,16},{4,20},{8,24},{12,28},{17,1},{... | collective-permute-start | bytes 196616 | tf_op jit(solution)/shard_map/ppermute | solution.py:23
  112.0 6.3 %collective-permute-start.24 = (bf16[256,128]{1,0:T(8,128)(2,1)S(1)}, bf16[256,128]{1,0:T(8,128)(2,1)S(1)}, u32[]{:S(2)}, u32[]{:S(2)}) collective-permute-start(bf16[256,128]{1,0:T(8,128)(2,1)S(1)} %get-tuple-element.88), channel_id=1, source_target_pairs={{4,0},{8,4},{12,8},{16,12},{20,16},{24,20},{28,24},{0,28},{5,1},{9... | collective-permute-start | bytes 196616 | tf_op jit(solution)/shard_map/ppermute | solution.py:23
  115.4 7.0 %collective-permute-start.22 = (bf16[256,128]{1,0:T(8,128)(2,1)S(1)}, bf16[256,128]{1,0:T(8,128)(2,1)S(1)}, u32[]{:S(2)}, u32[]{:S(2)}) collective-permute-start(bf16[256,128]{1,0:T(8,128)(2,1)S(1)} %get-tuple-element.85), channel_id=1, source_target_pairs={{28,0},{0,4},{4,8},{8,12},{12,16},{16,20},{20,24},{24,28},{29,1},{... | collective-permute-start | bytes 196616 | tf_op jit(solution)/shard_map/ppermute | solution.py:23
  122.5 18.3 %collective-permute-start.27 = (bf16[16,128,128]{2,1,0:T(8,128)(2,1)S(1)}, bf16[16,128,128]{2,1,0:T(8,128)(2,1)S(1)}, u32[]{:S(2)}, u32[]{:S(2)}) collective-permute-start(bf16[16,128,128]{2,1,0:T(8,128)(2,1)S(1)} %get-tuple-element.118), channel_id=1, source_target_pairs={{0,1},{1,0},{2,3},{3,2},{4,5},{5,4},{6,7},{7,6},{8,9},{9,8},{10,11... | collective-permute-start | bytes 1572872 | tf_op jit(solution)/shard_map/ppermute | solution.py:28
  122.6 18.2 %collective-permute-start.28 = (bf16[16,128,128]{2,1,0:T(8,128)(2,1)S(1)}, bf16[16,128,128]{2,1,0:T(8,128)(2,1)S(1)}, u32[]{:S(2)}, u32[]{:S(2)}) collective-permute-start(bf16[16,128,128]{2,1,0:T(8,128)(2,1)S(1)} %get-tuple-element.117), channel_id=1, source_target_pairs={{0,1},{1,0},{2,3},{3,2},{4,5},{5,4},{6,7},{7,6},{8,9},{9,8},{10,11... | collective-permute-start | bytes 1572872 | tf_op jit(solution)/shard_map/ppermute | solution.py:28
  124.7 41.3 %collective-permute-start.35 = (bf16[36,128,128]{2,1,0:T(8,128)(2,1)S(1)}, bf16[36,128,128]{2,1,0:T(8,128)(2,1)S(1)}, u32[]{:S(2)}, u32[]{:S(2)}) collective-permute-start(bf16[36,128,128]{2,1,0:T(8,128)(2,1)S(1)} %get-tuple-element.102.refs_6_), channel_id=1, source_target_pairs={{0,2},{1,3},{2,0},{3,1},{4,6},{5,7},{6,4},{7,5},{8,10},{9,11},{10,... | collective-permute-start | bytes 3538952 | tf_op jit(solution)/shard_map/ppermute | solution.py:28
  150.3 6.7 %collective-permute-start.33 = (bf16[256,128]{1,0:T(8,128)(2,1)S(1)}, bf16[256,128]{1,0:T(8,128)(2,1)S(1)}, u32[]{:S(2)}, u32[]{:S(2)}) collective-permute-start(bf16[256,128]{1,0:T(8,128)(2,1)S(1)} %get-tuple-element.99), channel_id=1, source_target_pairs={{24,0},{28,4},{0,8},{4,12},{8,16},{12,20},{16,24},{20,28},{25,1},{... | collective-permute-start | bytes 196616 | tf_op jit(solution)/shard_map/ppermute | solution.py:23
  152.4 8.0 %collective-permute-start.31 = (bf16[256,128]{1,0:T(8,128)(2,1)S(1)}, bf16[256,128]{1,0:T(8,128)(2,1)S(1)}, u32[]{:S(2)}, u32[]{:S(2)}) collective-permute-start(bf16[256,128]{1,0:T(8,128)(2,1)S(1)} %get-tuple-element.97), channel_id=1, source_target_pairs={{16,0},{20,4},{24,8},{28,12},{0,16},{4,20},{8,24},{12,28},{17,1},{... | collective-permute-start | bytes 196616 | tf_op jit(solution)/shard_map/ppermute | solution.py:23
  157.0 9.1 %collective-permute-start.34 = (bf16[256,128]{1,0:T(8,128)(2,1)S(1)}, bf16[256,128]{1,0:T(8,128)(2,1)S(1)}, u32[]{:S(2)}, u32[]{:S(2)}) collective-permute-start(bf16[256,128]{1,0:T(8,128)(2,1)S(1)} %get-tuple-element.101), channel_id=1, source_target_pairs={{4,0},{8,4},{12,8},{16,12},{20,16},{24,20},{28,24},{0,28},{5,1},{9... | collective-permute-start | bytes 196616 | tf_op jit(solution)/shard_map/ppermute | solution.py:23
  160.4 7.0 %collective-permute-start.32 = (bf16[256,128]{1,0:T(8,128)(2,1)S(1)}, bf16[256,128]{1,0:T(8,128)(2,1)S(1)}, u32[]{:S(2)}, u32[]{:S(2)}) collective-permute-start(bf16[256,128]{1,0:T(8,128)(2,1)S(1)} %get-tuple-element.98), channel_id=1, source_target_pairs={{28,0},{0,4},{4,8},{8,12},{12,16},{16,20},{20,24},{24,28},{29,1},{... | collective-permute-start | bytes 196616 | tf_op jit(solution)/shard_map/ppermute | solution.py:23
  161.1 19.0 %collective-permute-start.40 = (bf16[20,128,128]{2,1,0:T(8,128)(2,1)S(1)}, bf16[20,128,128]{2,1,0:T(8,128)(2,1)S(1)}, u32[]{:S(2)}, u32[]{:S(2)}) collective-permute-start(bf16[20,128,128]{2,1,0:T(8,128)(2,1)S(1)} %get-tuple-element.109.refs_2_), channel_id=1, source_target_pairs={{0,2},{1,3},{2,0},{3,1},{4,6},{5,7},{6,4},{7,5},{8,10},{9,11},{10,... | collective-permute-start | bytes 1966088 | tf_op jit(solution)/shard_map/ppermute | solution.py:28
  168.2 17.4 %collective-permute-start.39 = (bf16[8,128,128]{2,1,0:T(8,128)(2,1)S(1)}, bf16[8,128,128]{2,1,0:T(8,128)(2,1)S(1)}, u32[]{:S(2)}, u32[]{:S(2)}) collective-permute-start(bf16[8,128,128]{2,1,0:T(8,128)(2,1)S(1)} %get-tuple-element.108.refs_2_), channel_id=1, source_target_pairs={{0,2},{1,3},{2,0},{3,1},{4,6},{5,7},{6,4},{7,5},{8,10},{9,11},{10,... | collective-permute-start | bytes 786440 | tf_op jit(solution)/shard_map/ppermute | solution.py:28
  (18 other events, 75.8 us)

commit v16 on v15

--- a/solution.py
+++ b/solution.py
@@ -146,11 +146,16 @@
                 for m in range(fan):
                     place, inside = places[m][start]
                     weights.append(tile_refs[m][place][block - start + inside])
-                summed = jnp.dot(
-                    jnp.concatenate([inputs[table[base + m]] for m in range(fan)], axis=1),
-                    jnp.concatenate(weights, axis=0),
-                    preferred_element_type=jnp.float32,
-                )
+                panel = [inputs[table[base + m]] for m in range(fan)]
+                halves = [
+                    jnp.dot(
+                        jnp.concatenate(panel[half], axis=1),
+                        jnp.concatenate(weights[half], axis=0),
+                        preferred_element_type=jnp.float32,
+                    )
+                    for half in (slice(0, fan // 2), slice(fan // 2, fan))
+                ]
+                summed = halves[0] + halves[1]
                 place = pl.multiple_of((first + block) * width, width)
                 summed = summed + bias[layer : layer + 1, pl.ds(place, width)]
                 summed = jnp.maximum(summed, 0.0).astype(result.dtype)

time: 190 us -> 190 us (level)
  no operation moved by 1% of the time
where the time goes in v16:
time: 190 us; the launch traced here: 189 us
  waiting for transfers between devices  79.2 us (42%)
  starting transfers between devices  55.7 us (29%)
  Pallas kernels  49.7 us (26%)
  local copies, waits for them, and re-layouts  3.32 us (2%)
    ppermute x30, waiting for transfers between devices, swapped(): return lax.ppermute(block, 'batch', route)  56.9 us
    ppermute x16, starting transfers between devices, shifted(): return lax.ppermute(block, axis, route)  35.2 us
    pallas_call x6, Pallas kernels, run_blocks(): pl.pallas_call(kernel, out_shape=out_shape, grid_spec=pltpu.PrefetchScala...  33.5 us
    ppermute x16, waiting for transfers between devices, shifted(): return lax.ppermute(block, axis, route)  22.3 us
    ppermute x30, starting transfers between devices, swapped(): return lax.ppermute(block, 'batch', route)  20.4 us
    pallas_call x9, Pallas kernels, cut(): pl.pallas_call(kernel, out_shape=[pltpu.VMEM((count, height, width), tile...  14.6 us
  transfers between devices with their start and end apart: 46, of which 25 were waited for; matrix products, arithmetic and copies ran while one was open for 2% of the time, Pallas kernels for 25%

profile of v16, /device:TPU:0, one launch (start us, length us, event | category | flops | bytes accessed | tf_op | source)
XLA Modules:
  0.0 189.2 jit_solution(12533858880652202369)
XLA Ops:
  1.8 2.6 %collective-permute-start.5 = (bf16[32,128,128]{2,1,0:T(8,128)(2,1)S(1)}, bf16[32,128,128]{2,1,0:T(8,128)(2,1)S(1)}, u32[]{:S(2)}, u32[]{:S(2)}) collective-permute-start(bf16[32,128,128]{2,1,0:T(8,128)(2,1)S(1)} %shard_map.56.refs_6_), channel_id=1, source_target_pairs={{0,2},{1,3},{2,0},{3,1},{4,6},{5,7},{6,4},{7,5},{8,10},{9,11},{10,... | collective-permute-start | bytes 3145736 | tf_op jit(solution)/shard_map/ppermute | solution.py:28
  9.7 2.1 %collective-permute-start.2 = (bf16[256,128]{1,0:T(8,128)(2,1)S(1)}, bf16[256,128]{1,0:T(8,128)(2,1)S(1)}, u32[]{:S(2)}, u32[]{:S(2)}) collective-permute-start(bf16[256,128]{1,0:T(8,128)(2,1)S(1)} %get-tuple-element.62), channel_id=1, source_target_pairs={{24,0},{28,4},{0,8},{4,12},{8,16},{12,20},{16,24},{20,28},{25,1},{... | collective-permute-start | bytes 196616 | tf_op jit(solution)/shard_map/ppermute | solution.py:23
  11.8 2.6 %collective-permute-start = (bf16[256,128]{1,0:T(8,128)(2,1)S(1)}, bf16[256,128]{1,0:T(8,128)(2,1)S(1)}, u32[]{:S(2)}, u32[]{:S(2)}) collective-permute-start(bf16[256,128]{1,0:T(8,128)(2,1)S(1)} %get-tuple-element.60), channel_id=1, source_target_pairs={{16,0},{20,4},{24,8},{28,12},{0,16},{4,20},{8,24},{12,28},{17,1},{... | collective-permute-start | bytes 196616 | tf_op jit(solution)/shard_map/ppermute | solution.py:23
  16.3 3.3 %collective-permute-start.3 = (bf16[256,128]{1,0:T(8,128)(2,1)S(1)}, bf16[256,128]{1,0:T(8,128)(2,1)S(1)}, u32[]{:S(2)}, u32[]{:S(2)}) collective-permute-start(bf16[256,128]{1,0:T(8,128)(2,1)S(1)} %get-tuple-element.64), channel_id=1, source_target_pairs={{4,0},{8,4},{12,8},{16,12},{20,16},{24,20},{28,24},{0,28},{5,1},{9... | collective-permute-start | bytes 196616 | tf_op jit(solution)/shard_map/ppermute | solution.py:23
  22.1 4.5 %collective-permute-done.1.refs_2_ = bf16[256,128]{1,0:T(8,128)(2,1)S(1)} collective-permute-done((bf16[256,128]{1,0:T(8,128)(2,1)S(1)}, bf16[256,128]{1,0:T(8,128)(2,1)S(1)}, u32[]{:S(2)}, u32[]{:S(2)}) %collective-permute-start.1) | collective-permute-done | bytes 65568 | tf_op jit(solution)/shard_map/ppermute | solution.py:23
  30.8 2.0 %collective-permute-start.15 = (bf16[32,128,128]{2,1,0:T(8,128)(2,1)S(1)}, bf16[32,128,128]{2,1,0:T(8,128)(2,1)S(1)}, u32[]{:S(2)}, u32[]{:S(2)}) collective-permute-start(bf16[32,128,128]{2,1,0:T(8,128)(2,1)S(1)} %get-tuple-element.76.refs_6_), channel_id=1, source_target_pairs={{0,2},{1,3},{2,0},{3,1},{4,6},{5,7},{6,4},{7,5},{8,10},{9,11},{10,... | collective-permute-start | bytes 3145736 | tf_op jit(solution)/shard_map/ppermute | solution.py:28
  32.8 18.2 %collective-permute-done.6.refs_11_ = bf16[32,128,128]{2,1,0:T(8,128)(2,1)} collective-permute-done((bf16[32,128,128]{2,1,0:T(8,128)(2,1)S(1)}, bf16[32,128,128]{2,1,0:T(8,128)(2,1)}, u32[]{:S(2)}, u32[]{:S(2)}) %collective-permute-start.6) | collective-permute-done | bytes 1048608 | tf_op jit(solution)/shard_map/ppermute | solution.py:28
  52.8 1.9 %collective-permute-start.16 = (bf16[32,128,128]{2,1,0:T(8,128)(2,1)S(1)}, bf16[32,128,128]{2,1,0:T(8,128)(2,1)S(1)}, u32[]{:S(2)}, u32[]{:S(2)}) collective-permute-start(bf16[32,128,128]{2,1,0:T(8,128)(2,1)S(1)} %get-tuple-element.77.refs_7_), channel_id=1, source_target_pairs={{0,2},{1,3},{2,0},{3,1},{4,6},{5,7},{6,4},{7,5},{8,10},{9,11},{10,... | collective-permute-start | bytes 3145736 | tf_op jit(solution)/shard_map/ppermute | solution.py:28
  55.0 10.9 %shard_map.59 = (bf16[68,256,128]{2,1,0:T(8,128)(2,1)S(1)}, bf16[256,128]{1,0:T(8,128)(2,1)S(1)}, bf16[256,128]{1,0:T(8,128)(2,1)S(1)}, bf16[256,128]{1,0:T(8,128)(2,1)S(1)}, bf16[256,128]{1,0:T(8,128)(2,1)S(1)}) custom-call(s32[1040]{0:T(1024)S(1)} %constant_dynamic-update-slice_fusion.table.refs_0_, bf16[256,8192]{1,0:T(8,128)(2,1)} %refs_1_.1, ...), custom_call_target="tpu_custom_call" | custom-call | tf_op jit(solution)/shard_map/pallas_call | solution.py:211
  65.9 2.1 %collective-permute-start.13 = (bf16[256,128]{1,0:T(8,128)(2,1)S(1)}, bf16[256,128]{1,0:T(8,128)(2,1)S(1)}, u32[]{:S(2)}, u32[]{:S(2)}) collective-permute-start(bf16[256,128]{1,0:T(8,128)(2,1)S(1)} %get-tuple-element.73), channel_id=1, source_target_pairs={{24,0},{28,4},{0,8},{4,12},{8,16},{12,20},{16,24},{20,28},{25,1},{... | collective-permute-start | bytes 196616 | tf_op jit(solution)/shard_map/ppermute | solution.py:23
  67.9 2.6 %collective-permute-start.11 = (bf16[256,128]{1,0:T(8,128)(2,1)S(1)}, bf16[256,128]{1,0:T(8,128)(2,1)S(1)}, u32[]{:S(2)}, u32[]{:S(2)}) collective-permute-start(bf16[256,128]{1,0:T(8,128)(2,1)S(1)} %get-tuple-element.71), channel_id=1, source_target_pairs={{16,0},{20,4},{24,8},{28,12},{0,16},{4,20},{8,24},{12,28},{17,1},{... | collective-permute-start | bytes 196616 | tf_op jit(solution)/shard_map/ppermute | solution.py:23
  70.5 2.0 %collective-permute-done.13.refs_3_ = bf16[256,128]{1,0:T(8,128)(2,1)S(1)} collective-permute-done((bf16[256,128]{1,0:T(8,128)(2,1)S(1)}, bf16[256,128]{1,0:T(8,128)(2,1)S(1)}, u32[]{:S(2)}, u32[]{:S(2)}) %collective-permute-start.13) | collective-permute-done | bytes 65568 | tf_op jit(solution)/shard_map/ppermute | solution.py:23
  72.5 3.4 %collective-permute-start.14 = (bf16[256,128]{1,0:T(8,128)(2,1)S(1)}, bf16[256,128]{1,0:T(8,128)(2,1)S(1)}, u32[]{:S(2)}, u32[]{:S(2)}) collective-permute-start(bf16[256,128]{1,0:T(8,128)(2,1)S(1)} %get-tuple-element.75), channel_id=1, source_target_pairs={{4,0},{8,4},{12,8},{16,12},{20,16},{24,20},{28,24},{0,28},{5,1},{9... | collective-permute-start | bytes 196616 | tf_op jit(solution)/shard_map/ppermute | solution.py:23
  78.4 4.5 %collective-permute-done.12.refs_2_ = bf16[256,128]{1,0:T(8,128)(2,1)S(1)} collective-permute-done((bf16[256,128]{1,0:T(8,128)(2,1)S(1)}, bf16[256,128]{1,0:T(8,128)(2,1)S(1)}, u32[]{:S(2)}, u32[]{:S(2)}) %collective-permute-start.12) | collective-permute-done | bytes 65568 | tf_op jit(solution)/shard_map/ppermute | solution.py:23
  86.9 8.9 %collective-permute-done.16.refs_11_ = bf16[32,128,128]{2,1,0:T(8,128)(2,1)S(1)} collective-permute-done((bf16[32,128,128]{2,1,0:T(8,128)(2,1)S(1)}, bf16[32,128,128]{2,1,0:T(8,128)(2,1)S(1)}, u32[]{:S(2)}, u32[]{:S(2)}) %collective-permute-start.16) | collective-permute-done | bytes 1048608 | tf_op jit(solution)/shard_map/ppermute | solution.py:28
  96.5 1.9 %collective-permute-start.26 = (bf16[32,128,128]{2,1,0:T(8,128)(2,1)S(1)}, bf16[32,128,128]{2,1,0:T(8,128)(2,1)S(1)}, u32[]{:S(2)}, u32[]{:S(2)}) collective-permute-start(bf16[32,128,128]{2,1,0:T(8,128)(2,1)S(1)} %get-tuple-element.90.refs_7_), channel_id=1, source_target_pairs={{0,2},{1,3},{2,0},{3,1},{4,6},{5,7},{6,4},{7,5},{8,10},{9,11},{10,... | collective-permute-start | bytes 3145736 | tf_op jit(solution)/shard_map/ppermute | solution.py:28
  98.7 6.7 %shard_map.62 = (bf16[68,256,128]{2,1,0:T(8,128)(2,1)S(1)}, bf16[68,256,128]{2,1,0:T(8,128)(2,1)S(1)}, bf16[256,128]{1,0:T(8,128)(2,1)S(1)}, bf16[256,128]{1,0:T...) custom-call(s32[1040]{0:T(1024)S(1)} %constant_dynamic-update-slice_, ...), custom_call_target="tpu_custom_call", output_to_operand_aliasing={{1}: (1, {})} | custom-call | tf_op jit(solution)/shard_map/pallas_call | solution.py:211
  105.3 2.1 %collective-permute-start.23 = (bf16[256,128]{1,0:T(8,128)(2,1)S(1)}, bf16[256,128]{1,0:T(8,128)(2,1)S(1)}, u32[]{:S(2)}, u32[]{:S(2)}) collective-permute-start(bf16[256,128]{1,0:T(8,128)(2,1)S(1)} %get-tuple-element.86), channel_id=1, source_target_pairs={{24,0},{28,4},{0,8},{4,12},{8,16},{12,20},{16,24},{20,28},{25,1},{... | collective-permute-start | bytes 196616 | tf_op jit(solution)/shard_map/ppermute | solution.py:23
  107.4 2.6 %collective-permute-start.21 = (bf16[256,128]{1,0:T(8,128)(2,1)S(1)}, bf16[256,128]{1,0:T(8,128)(2,1)S(1)}, u32[]{:S(2)}, u32[]{:S(2)}) collective-permute-start(bf16[256,128]{1,0:T(8,128)(2,1)S(1)} %get-tuple-element.84), channel_id=1, source_target_pairs={{16,0},{20,4},{24,8},{28,12},{0,16},{4,20},{8,24},{12,28},{17,1},{... | collective-permute-start | bytes 196616 | tf_op jit(solution)/shard_map/ppermute | solution.py:23
  110.0 2.0 %collective-permute-done.23.refs_3_ = bf16[256,128]{1,0:T(8,128)(2,1)S(1)} collective-permute-done((bf16[256,128]{1,0:T(8,128)(2,1)S(1)}, bf16[256,128]{1,0:T(8,128)(2,1)S(1)}, u32[]{:S(2)}, u32[]{:S(2)}) %collective-permute-start.23) | collective-permute-done | bytes 65568 | tf_op jit(solution)/shard_map/ppermute | solution.py:23
  112.0 3.4 %collective-permute-start.24 = (bf16[256,128]{1,0:T(8,128)(2,1)S(1)}, bf16[256,128]{1,0:T(8,128)(2,1)S(1)}, u32[]{:S(2)}, u32[]{:S(2)}) collective-permute-start(bf16[256,128]{1,0:T(8,128)(2,1)S(1)} %get-tuple-element.88), channel_id=1, source_target_pairs={{4,0},{8,4},{12,8},{16,12},{20,16},{24,20},{28,24},{0,28},{5,1},{9... | collective-permute-start | bytes 196616 | tf_op jit(solution)/shard_map/ppermute | solution.py:23
  118.3 4.1 %collective-permute-done.22.refs_2_ = bf16[256,128]{1,0:T(8,128)(2,1)S(1)} collective-permute-done((bf16[256,128]{1,0:T(8,128)(2,1)S(1)}, bf16[256,128]{1,0:T(8,128)(2,1)S(1)}, u32[]{:S(2)}, u32[]{:S(2)}) %collective-permute-start.22) | collective-permute-done | bytes 65568 | tf_op jit(solution)/shard_map/ppermute | solution.py:23
  126.3 14.5 %collective-permute-done.26.refs_11_ = bf16[32,128,128]{2,1,0:T(8,128)(2,1)S(1)} collective-permute-done((bf16[32,128,128]{2,1,0:T(8,128)(2,1)S(1)}, bf16[32,128,128]{2,1,0:T(8,128)(2,1)S(1)}, u32[]{:S(2)}, u32[]{:S(2)}) %collective-permute-start.26) | collective-permute-done | bytes 1048608 | tf_op jit(solution)/shard_map/ppermute | solution.py:28
  143.6 6.7 %shard_map.65 = (bf16[68,256,128]{2,1,0:T(8,128)(2,1)S(1)}, bf16[68,256,128]{2,1,0:T(8,128)(2,1)S(1)}, bf16[256,128]{1,0:T(8,128)(2,1)S(1)}, bf16[256,128]{1,0:T...) custom-call(s32[1040]{0:T(1024)S(1)} %constant_dynamic-update-slice_, ...), custom_call_target="tpu_custom_call", output_to_operand_aliasing={{1}: (1, {})} | custom-call | tf_op jit(solution)/shard_map/pallas_call | solution.py:211
  150.3 2.1 %collective-permute-start.33 = (bf16[256,128]{1,0:T(8,128)(2,1)S(1)}, bf16[256,128]{1,0:T(8,128)(2,1)S(1)}, u32[]{:S(2)}, u32[]{:S(2)}) collective-permute-start(bf16[256,128]{1,0:T(8,128)(2,1)S(1)} %get-tuple-element.99), channel_id=1, source_target_pairs={{24,0},{28,4},{0,8},{4,12},{8,16},{12,20},{16,24},{20,28},{25,1},{... | collective-permute-start | bytes 196616 | tf_op jit(solution)/shard_map/ppermute | solution.py:23
  152.4 2.6 %collective-permute-start.31 = (bf16[256,128]{1,0:T(8,128)(2,1)S(1)}, bf16[256,128]{1,0:T(8,128)(2,1)S(1)}, u32[]{:S(2)}, u32[]{:S(2)}) collective-permute-start(bf16[256,128]{1,0:T(8,128)(2,1)S(1)} %get-tuple-element.97), channel_id=1, source_target_pairs={{16,0},{20,4},{24,8},{28,12},{0,16},{4,20},{8,24},{12,28},{17,1},{... | collective-permute-start | bytes 196616 | tf_op jit(solution)/shard_map/ppermute | solution.py:23
  155.0 2.0 %collective-permute-done.33.refs_3_ = bf16[256,128]{1,0:T(8,128)(2,1)S(1)} collective-permute-done((bf16[256,128]{1,0:T(8,128)(2,1)S(1)}, bf16[256,128]{1,0:T(8,128)(2,1)S(1)}, u32[]{:S(2)}, u32[]{:S(2)}) %collective-permute-start.33) | collective-permute-done | bytes 65568 | tf_op jit(solution)/shard_map/ppermute | solution.py:23
  157.0 3.4 %collective-permute-start.34 = (bf16[256,128]{1,0:T(8,128)(2,1)S(1)}, bf16[256,128]{1,0:T(8,128)(2,1)S(1)}, u32[]{:S(2)}, u32[]{:S(2)}) collective-permute-start(bf16[256,128]{1,0:T(8,128)(2,1)S(1)} %get-tuple-element.101), channel_id=1, source_target_pairs={{4,0},{8,4},{12,8},{16,12},{20,16},{24,20},{28,24},{0,28},{5,1},{9... | collective-permute-start | bytes 196616 | tf_op jit(solution)/shard_map/ppermute | solution.py:23
  170.3 4.4 %shard_map.68 = (bf16[256,8192]{1,0:T(8,128)(2,1)}, bf16[68,256,128]{2,1,0:T(8,128)(2,1)S(1)}) custom-call(s32[1040]{0:T(1024)S(1)} %constant_dynamic-update-slice_fusion.table.refs_0_, bf16[68,256,128]{2,1,0:T(8,128)(2,1)S(1)} %get-tuple-element.95.refs_1_, bf16[256,128]{1,0:T(8,128)(2,1)S(1)} %collective-permute-done.32.refs_2_, ...), custom_call_target="tpu_custom_call", output_to_operand_aliasing={{1}: (1, {})} | custom-call | tf_op jit(solution)/shard_map/pallas_call | solution.py:211
  174.8 5.3 %collective-permute-done.40.refs_4_ = bf16[20,128,128]{2,1,0:T(8,128)(2,1)S(1)} collective-permute-done((bf16[20,128,128]{2,1,0:T(8,128)(2,1)S(1)}, bf16[20,128,128]{2,1,0:T(8,128)(2,1)S(1)}, u32[]{:S(2)}, u32[]{:S(2)}) %collective-permute-start.40) | collective-permute-done | bytes 655392 | tf_op jit(solution)/shard_map/ppermute | solution.py:28
  182.3 2.9 %shard_map.69.refs_7_ = bf16[256,8192]{1,0:T(8,128)(2,1)} custom-call(s32[1040]{0:T(1024)S(1)} %constant_dynamic-update-slice_fusion.table.refs_0_, bf16[68,256,128]{2,1,0:T(8,128)(2,1)S(1)} %get-tuple-element.107.refs_1_, bf16[20,128,128]{2,1,0:T(8,128)(2,1)S(1)} %get-tuple-element.109.refs_2_, ...), custom_call_target="tpu_custom_call", output_to_operand_aliasing={{}: (10, {})} | custom-call | tf_op jit(solution)/shard_map/pallas_call | solution.py:211
  187.0 2.0 %shard_map.70 = bf16[256,8192]{1,0:T(8,128)(2,1)} custom-call(s32[1040]{0:T(1024)S(1)} %constant_dynamic-update-slice_fusion.table.refs_0_, bf16[68,256,128]{2,1,0:T(8,128)(2,1)S(1)} %get-tuple-element.107.refs_1_, bf16[8,128,128]{2,1,0:T(8,128)(2,1)S(1)} %get-tuple-element.108.refs_2_, ...), custom_call_target="tpu_custom_call", output_to_operand_aliasing={{}: (7, {})} | custom-call | tf_op jit(solution)/shard_map/pallas_call | solution.py:211
  (106 shorter events, 48.4 us)
Async XLA Ops:
  0.0 20.3 %collective-permute-start.4 = (bf16[4,64,128,128]{3,2,1,0:T(8,128)(2,1)}, bf16[4,64,128,128]{3,2,1,0:T(8,128)(2,1)}, u32[]{:S(2)}, u32[]{:S(2)}) collective-permute-start(bf16[4,64,128,128]{3,2,1,0:T(8,128)(2,1)} %tiles.9), channel_id=1, source_target_pairs={{0,1},{1,0},{2,3},{3,2},{4,5},{5,4},{6,7},{7,6},{8,9},{9,8},{10,11... | collective-permute-start | bytes 25165832 | tf_op jit(solution)/shard_map/ppermute | solution.py:28
  1.8 26.6 %collective-permute-start.5 = (bf16[32,128,128]{2,1,0:T(8,128)(2,1)S(1)}, bf16[32,128,128]{2,1,0:T(8,128)(2,1)S(1)}, u32[]{:S(2)}, u32[]{:S(2)}) collective-permute-start(bf16[32,128,128]{2,1,0:T(8,128)(2,1)S(1)} %shard_map.56.refs_6_), channel_id=1, source_target_pairs={{0,2},{1,3},{2,0},{3,1},{4,6},{5,7},{6,4},{7,5},{8,10},{9,11},{10,... | collective-permute-start | bytes 3145736 | tf_op jit(solution)/shard_map/ppermute | solution.py:28
  5.7 45.2 %collective-permute-start.6 = (bf16[32,128,128]{2,1,0:T(8,128)(2,1)S(1)}, bf16[32,128,128]{2,1,0:T(8,128)(2,1)}, u32[]{:S(2)}, u32[]{:S(2)}) collective-permute-start(bf16[32,128,128]{2,1,0:T(8,128)(2,1)S(1)} %shard_map.57.refs_7_), channel_id=1, source_target_pairs={{0,2},{1,3},{2,0},{3,1},{4,6},{5,7},{6,4},{7,5},{8,10},{9,11},{10,... | collective-permute-start | bytes 3145736 | tf_op jit(solution)/shard_map/ppermute | solution.py:28
  9.7 6.6 %collective-permute-start.2 = (bf16[256,128]{1,0:T(8,128)(2,1)S(1)}, bf16[256,128]{1,0:T(8,128)(2,1)S(1)}, u32[]{:S(2)}, u32[]{:S(2)}) collective-permute-start(bf16[256,128]{1,0:T(8,128)(2,1)S(1)} %get-tuple-element.62), channel_id=1, source_target_pairs={{24,0},{28,4},{0,8},{4,12},{8,16},{12,20},{16,24},{20,28},{25,1},{... | collective-permute-start | bytes 196616 | tf_op jit(solution)/shard_map/ppermute | solution.py:23
  11.8 7.8 %collective-permute-start = (bf16[256,128]{1,0:T(8,128)(2,1)S(1)}, bf16[256,128]{1,0:T(8,128)(2,1)S(1)}, u32[]{:S(2)}, u32[]{:S(2)}) collective-permute-start(bf16[256,128]{1,0:T(8,128)(2,1)S(1)} %get-tuple-element.60), channel_id=1, source_target_pairs={{16,0},{20,4},{24,8},{28,12},{0,16},{4,20},{8,24},{12,28},{17,1},{... | collective-permute-start | bytes 196616 | tf_op jit(solution)/shard_map/ppermute | solution.py:23
  16.3 5.8 %collective-permute-start.3 = (bf16[256,128]{1,0:T(8,128)(2,1)S(1)}, bf16[256,128]{1,0:T(8,128)(2,1)S(1)}, u32[]{:S(2)}, u32[]{:S(2)}) collective-permute-start(bf16[256,128]{1,0:T(8,128)(2,1)S(1)} %get-tuple-element.64), channel_id=1, source_target_pairs={{4,0},{8,4},{12,8},{16,12},{20,16},{24,20},{28,24},{0,28},{5,1},{9... | collective-permute-start | bytes 196616 | tf_op jit(solution)/shard_map/ppermute | solution.py:23
  19.6 7.0 %collective-permute-start.1 = (bf16[256,128]{1,0:T(8,128)(2,1)S(1)}, bf16[256,128]{1,0:T(8,128)(2,1)S(1)}, u32[]{:S(2)}, u32[]{:S(2)}) collective-permute-start(bf16[256,128]{1,0:T(8,128)(2,1)S(1)} %get-tuple-element.61), channel_id=1, source_target_pairs={{28,0},{0,4},{4,8},{8,12},{12,16},{16,20},{20,24},{24,28},{29,1},{... | collective-permute-start | bytes 196616 | tf_op jit(solution)/shard_map/ppermute | solution.py:23
  28.5 22.5 %collective-permute-start.7 = (bf16[16,128,128]{2,1,0:T(8,128)(2,1)S(1)}, bf16[16,128,128]{2,1,0:T(8,128)(2,1)S(1)}, u32[]{:S(2)}, u32[]{:S(2)}) collective-permute-start(bf16[16,128,128]{2,1,0:T(8,128)(2,1)S(1)} %get-tuple-element.126), channel_id=1, source_target_pairs={{0,1},{1,0},{2,3},{3,2},{4,5},{5,4},{6,7},{7,6},{8,9},{9,8},{10,11... | collective-permute-start | bytes 1572872 | tf_op jit(solution)/shard_map/ppermute | solution.py:28
  28.6 22.4 %collective-permute-start.8 = (bf16[16,128,128]{2,1,0:T(8,128)(2,1)S(1)}, bf16[16,128,128]{2,1,0:T(8,128)(2,1)S(1)}, u32[]{:S(2)}, u32[]{:S(2)}) collective-permute-start(bf16[16,128,128]{2,1,0:T(8,128)(2,1)S(1)} %get-tuple-element.125), channel_id=1, source_target_pairs={{0,1},{1,0},{2,3},{3,2},{4,5},{5,4},{6,7},{7,6},{8,9},{9,8},{10,11... | collective-permute-start | bytes 1572872 | tf_op jit(solution)/shard_map/ppermute | solution.py:28
  30.8 47.6 %collective-permute-start.15 = (bf16[32,128,128]{2,1,0:T(8,128)(2,1)S(1)}, bf16[32,128,128]{2,1,0:T(8,128)(2,1)S(1)}, u32[]{:S(2)}, u32[]{:S(2)}) collective-permute-start(bf16[32,128,128]{2,1,0:T(8,128)(2,1)S(1)} %get-tuple-element.76.refs_6_), channel_id=1, source_target_pairs={{0,2},{1,3},{2,0},{3,1},{4,6},{5,7},{6,4},{7,5},{8,10},{9,11},{10,... | collective-permute-start | bytes 3145736 | tf_op jit(solution)/shard_map/ppermute | solution.py:28
  52.8 43.0 %collective-permute-start.16 = (bf16[32,128,128]{2,1,0:T(8,128)(2,1)S(1)}, bf16[32,128,128]{2,1,0:T(8,128)(2,1)S(1)}, u32[]{:S(2)}, u32[]{:S(2)}) collective-permute-start(bf16[32,128,128]{2,1,0:T(8,128)(2,1)S(1)} %get-tuple-element.77.refs_7_), channel_id=1, source_target_pairs={{0,2},{1,3},{2,0},{3,1},{4,6},{5,7},{6,4},{7,5},{8,10},{9,11},{10,... | collective-permute-start | bytes 3145736 | tf_op jit(solution)/shard_map/ppermute | solution.py:28
  65.9 6.7 %collective-permute-start.13 = (bf16[256,128]{1,0:T(8,128)(2,1)S(1)}, bf16[256,128]{1,0:T(8,128)(2,1)S(1)}, u32[]{:S(2)}, u32[]{:S(2)}) collective-permute-start(bf16[256,128]{1,0:T(8,128)(2,1)S(1)} %get-tuple-element.73), channel_id=1, source_target_pairs={{24,0},{28,4},{0,8},{4,12},{8,16},{12,20},{16,24},{20,28},{25,1},{... | collective-permute-start | bytes 196616 | tf_op jit(solution)/shard_map/ppermute | solution.py:23
  67.9 8.0 %collective-permute-start.11 = (bf16[256,128]{1,0:T(8,128)(2,1)S(1)}, bf16[256,128]{1,0:T(8,128)(2,1)S(1)}, u32[]{:S(2)}, u32[]{:S(2)}) collective-permute-start(bf16[256,128]{1,0:T(8,128)(2,1)S(1)} %get-tuple-element.71), channel_id=1, source_target_pairs={{16,0},{20,4},{24,8},{28,12},{0,16},{4,20},{8,24},{12,28},{17,1},{... | collective-permute-start | bytes 196616 | tf_op jit(solution)/shard_map/ppermute | solution.py:23
  72.5 5.9 %collective-permute-start.14 = (bf16[256,128]{1,0:T(8,128)(2,1)S(1)}, bf16[256,128]{1,0:T(8,128)(2,1)S(1)}, u32[]{:S(2)}, u32[]{:S(2)}) collective-permute-start(bf16[256,128]{1,0:T(8,128)(2,1)S(1)} %get-tuple-element.75), channel_id=1, source_target_pairs={{4,0},{8,4},{12,8},{16,12},{20,16},{24,20},{28,24},{0,28},{5,1},{9... | collective-permute-start | bytes 196616 | tf_op jit(solution)/shard_map/ppermute | solution.py:23
  75.9 7.0 %collective-permute-start.12 = (bf16[256,128]{1,0:T(8,128)(2,1)S(1)}, bf16[256,128]{1,0:T(8,128)(2,1)S(1)}, u32[]{:S(2)}, u32[]{:S(2)}) collective-permute-start(bf16[256,128]{1,0:T(8,128)(2,1)S(1)} %get-tuple-element.72), channel_id=1, source_target_pairs={{28,0},{0,4},{4,8},{8,12},{12,16},{16,20},{20,24},{24,28},{29,1},{... | collective-permute-start | bytes 196616 | tf_op jit(solution)/shard_map/ppermute | solution.py:23
  83.0 12.8 %collective-permute-start.17 = (bf16[16,128,128]{2,1,0:T(8,128)(2,1)S(1)}, bf16[16,128,128]{2,1,0:T(8,128)(2,1)S(1)}, u32[]{:S(2)}, u32[]{:S(2)}) collective-permute-start(bf16[16,128,128]{2,1,0:T(8,128)(2,1)S(1)} %get-tuple-element.122), channel_id=1, source_target_pairs={{0,1},{1,0},{2,3},{3,2},{4,5},{5,4},{6,7},{7,6},{8,9},{9,8},{10,11... | collective-permute-start | bytes 1572872 | tf_op jit(solution)/shard_map/ppermute | solution.py:28
  83.1 12.7 %collective-permute-start.18 = (bf16[16,128,128]{2,1,0:T(8,128)(2,1)S(1)}, bf16[16,128,128]{2,1,0:T(8,128)(2,1)S(1)}, u32[]{:S(2)}, u32[]{:S(2)}) collective-permute-start(bf16[16,128,128]{2,1,0:T(8,128)(2,1)S(1)} %get-tuple-element.121), channel_id=1, source_target_pairs={{0,1},{1,0},{2,3},{3,2},{4,5},{5,4},{6,7},{7,6},{8,9},{9,8},{10,11... | collective-permute-start | bytes 1572872 | tf_op jit(solution)/shard_map/ppermute | solution.py:28
  85.3 32.9 %collective-permute-start.25 = (bf16[32,128,128]{2,1,0:T(8,128)(2,1)S(1)}, bf16[32,128,128]{2,1,0:T(8,128)(2,1)S(1)}, u32[]{:S(2)}, u32[]{:S(2)}) collective-permute-start(bf16[32,128,128]{2,1,0:T(8,128)(2,1)S(1)} %get-tuple-element.89.refs_6_), channel_id=1, source_target_pairs={{0,2},{1,3},{2,0},{3,1},{4,6},{5,7},{6,4},{7,5},{8,10},{9,11},{10,... | collective-permute-start | bytes 3145736 | tf_op jit(solution)/shard_map/ppermute | solution.py:28
  96.5 44.2 %collective-permute-start.26 = (bf16[32,128,128]{2,1,0:T(8,128)(2,1)S(1)}, bf16[32,128,128]{2,1,0:T(8,128)(2,1)S(1)}, u32[]{:S(2)}, u32[]{:S(2)}) collective-permute-start(bf16[32,128,128]{2,1,0:T(8,128)(2,1)S(1)} %get-tuple-element.90.refs_7_), channel_id=1, source_target_pairs={{0,2},{1,3},{2,0},{3,1},{4,6},{5,7},{6,4},{7,5},{8,10},{9,11},{10,... | collective-permute-start | bytes 3145736 | tf_op jit(solution)/shard_map/ppermute | solution.py:28
  105.3 6.7 %collective-permute-start.23 = (bf16[256,128]{1,0:T(8,128)(2,1)S(1)}, bf16[256,128]{1,0:T(8,128)(2,1)S(1)}, u32[]{:S(2)}, u32[]{:S(2)}) collective-permute-start(bf16[256,128]{1,0:T(8,128)(2,1)S(1)} %get-tuple-element.86), channel_id=1, source_target_pairs={{24,0},{28,4},{0,8},{4,12},{8,16},{12,20},{16,24},{20,28},{25,1},{... | collective-permute-start | bytes 196616 | tf_op jit(solution)/shard_map/ppermute | solution.py:23
  107.4 8.0 %collective-permute-start.21 = (bf16[256,128]{1,0:T(8,128)(2,1)S(1)}, bf16[256,128]{1,0:T(8,128)(2,1)S(1)}, u32[]{:S(2)}, u32[]{:S(2)}) collective-permute-start(bf16[256,128]{1,0:T(8,128)(2,1)S(1)} %get-tuple-element.84), channel_id=1, source_target_pairs={{16,0},{20,4},{24,8},{28,12},{0,16},{4,20},{8,24},{12,28},{17,1},{... | collective-permute-start | bytes 196616 | tf_op jit(solution)/shard_map/ppermute | solution.py:23
  112.0 6.3 %collective-permute-start.24 = (bf16[256,128]{1,0:T(8,128)(2,1)S(1)}, bf16[256,128]{1,0:T(8,128)(2,1)S(1)}, u32[]{:S(2)}, u32[]{:S(2)}) collective-permute-start(bf16[256,128]{1,0:T(8,128)(2,1)S(1)} %get-tuple-element.88), channel_id=1, source_target_pairs={{4,0},{8,4},{12,8},{16,12},{20,16},{24,20},{28,24},{0,28},{5,1},{9... | collective-permute-start | bytes 196616 | tf_op jit(solution)/shard_map/ppermute | solution.py:23
  115.4 7.0 %collective-permute-start.22 = (bf16[256,128]{1,0:T(8,128)(2,1)S(1)}, bf16[256,128]{1,0:T(8,128)(2,1)S(1)}, u32[]{:S(2)}, u32[]{:S(2)}) collective-permute-start(bf16[256,128]{1,0:T(8,128)(2,1)S(1)} %get-tuple-element.85), channel_id=1, source_target_pairs={{28,0},{0,4},{4,8},{8,12},{12,16},{16,20},{20,24},{24,28},{29,1},{... | collective-permute-start | bytes 196616 | tf_op jit(solution)/shard_map/ppermute | solution.py:23
  122.5 18.3 %collective-permute-start.27 = (bf16[16,128,128]{2,1,0:T(8,128)(2,1)S(1)}, bf16[16,128,128]{2,1,0:T(8,128)(2,1)S(1)}, u32[]{:S(2)}, u32[]{:S(2)}) collective-permute-start(bf16[16,128,128]{2,1,0:T(8,128)(2,1)S(1)} %get-tuple-element.118), channel_id=1, source_target_pairs={{0,1},{1,0},{2,3},{3,2},{4,5},{5,4},{6,7},{7,6},{8,9},{9,8},{10,11... | collective-permute-start | bytes 1572872 | tf_op jit(solution)/shard_map/ppermute | solution.py:28
  122.6 18.2 %collective-permute-start.28 = (bf16[16,128,128]{2,1,0:T(8,128)(2,1)S(1)}, bf16[16,128,128]{2,1,0:T(8,128)(2,1)S(1)}, u32[]{:S(2)}, u32[]{:S(2)}) collective-permute-start(bf16[16,128,128]{2,1,0:T(8,128)(2,1)S(1)} %get-tuple-element.117), channel_id=1, source_target_pairs={{0,1},{1,0},{2,3},{3,2},{4,5},{5,4},{6,7},{7,6},{8,9},{9,8},{10,11... | collective-permute-start | bytes 1572872 | tf_op jit(solution)/shard_map/ppermute | solution.py:28
  124.7 41.3 %collective-permute-start.35 = (bf16[36,128,128]{2,1,0:T(8,128)(2,1)S(1)}, bf16[36,128,128]{2,1,0:T(8,128)(2,1)S(1)}, u32[]{:S(2)}, u32[]{:S(2)}) collective-permute-start(bf16[36,128,128]{2,1,0:T(8,128)(2,1)S(1)} %get-tuple-element.102.refs_6_), channel_id=1, source_target_pairs={{0,2},{1,3},{2,0},{3,1},{4,6},{5,7},{6,4},{7,5},{8,10},{9,11},{10,... | collective-permute-start | bytes 3538952 | tf_op jit(solution)/shard_map/ppermute | solution.py:28
  150.3 6.7 %collective-permute-start.33 = (bf16[256,128]{1,0:T(8,128)(2,1)S(1)}, bf16[256,128]{1,0:T(8,128)(2,1)S(1)}, u32[]{:S(2)}, u32[]{:S(2)}) collective-permute-start(bf16[256,128]{1,0:T(8,128)(2,1)S(1)} %get-tuple-element.99), channel_id=1, source_target_pairs={{24,0},{28,4},{0,8},{4,12},{8,16},{12,20},{16,24},{20,28},{25,1},{... | collective-permute-start | bytes 196616 | tf_op jit(solution)/shard_map/ppermute | solution.py:23
  152.4 8.0 %collective-permute-start.31 = (bf16[256,128]{1,0:T(8,128)(2,1)S(1)}, bf16[256,128]{1,0:T(8,128)(2,1)S(1)}, u32[]{:S(2)}, u32[]{:S(2)}) collective-permute-start(bf16[256,128]{1,0:T(8,128)(2,1)S(1)} %get-tuple-element.97), channel_id=1, source_target_pairs={{16,0},{20,4},{24,8},{28,12},{0,16},{4,20},{8,24},{12,28},{17,1},{... | collective-permute-start | bytes 196616 | tf_op jit(solution)/shard_map/ppermute | solution.py:23
  157.0 9.1 %collective-permute-start.34 = (bf16[256,128]{1,0:T(8,128)(2,1)S(1)}, bf16[256,128]{1,0:T(8,128)(2,1)S(1)}, u32[]{:S(2)}, u32[]{:S(2)}) collective-permute-start(bf16[256,128]{1,0:T(8,128)(2,1)S(1)} %get-tuple-element.101), channel_id=1, source_target_pairs={{4,0},{8,4},{12,8},{16,12},{20,16},{24,20},{28,24},{0,28},{5,1},{9... | collective-permute-start | bytes 196616 | tf_op jit(solution)/shard_map/ppermute | solution.py:23
  160.4 7.0 %collective-permute-start.32 = (bf16[256,128]{1,0:T(8,128)(2,1)S(1)}, bf16[256,128]{1,0:T(8,128)(2,1)S(1)}, u32[]{:S(2)}, u32[]{:S(2)}) collective-permute-start(bf16[256,128]{1,0:T(8,128)(2,1)S(1)} %get-tuple-element.98), channel_id=1, source_target_pairs={{28,0},{0,4},{4,8},{8,12},{12,16},{16,20},{20,24},{24,28},{29,1},{... | collective-permute-start | bytes 196616 | tf_op jit(solution)/shard_map/ppermute | solution.py:23
  161.1 19.0 %collective-permute-start.40 = (bf16[20,128,128]{2,1,0:T(8,128)(2,1)S(1)}, bf16[20,128,128]{2,1,0:T(8,128)(2,1)S(1)}, u32[]{:S(2)}, u32[]{:S(2)}) collective-permute-start(bf16[20,128,128]{2,1,0:T(8,128)(2,1)S(1)} %get-tuple-element.109.refs_2_), channel_id=1, source_target_pairs={{0,2},{1,3},{2,0},{3,1},{4,6},{5,7},{6,4},{7,5},{8,10},{9,11},{10,... | collective-permute-start | bytes 1966088 | tf_op jit(solution)/shard_map/ppermute | solution.py:28
  168.2 17.3 %collective-permute-start.39 = (bf16[8,128,128]{2,1,0:T(8,128)(2,1)S(1)}, bf16[8,128,128]{2,1,0:T(8,128)(2,1)S(1)}, u32[]{:S(2)}, u32[]{:S(2)}) collective-permute-start(bf16[8,128,128]{2,1,0:T(8,128)(2,1)S(1)} %get-tuple-element.108.refs_2_), channel_id=1, source_target_pairs={{0,2},{1,3},{2,0},{3,1},{4,6},{5,7},{6,4},{7,5},{8,10},{9,11},{10,... | collective-permute-start | bytes 786440 | tf_op jit(solution)/shard_map/ppermute | solution.py:28
  (18 other events, 75.8 us)
